TPU v7x, 32 devices: a whole 2x2x4 slice. The times are simulated.
32 devices in a mesh: rad: 2 (over x), az: 16 (over z, y, core).
Axes of the slice: x: 2, y: 2, z: 4, core: 2. Of those that a mesh axis runs over, the one named last changes fastest.
Arguments:
- fields: float32 [7, 32, 256, 128], P(None, 'rad', 'az'), may hold values from -6 to 6
- density: float32 [32, 256, 128], P('rad', 'az'), may hold values from 0.3 to 3
- shift_int: int32 [32], P('rad'), may hold values from 0 to 255
- frac_num: int32 [32], P('rad'), may hold values from 0 to 63
- boundary_shift: int32 [1], replicated, may hold values from 0 to 255
Outputs:
- new_fields: float32 [7, 32, 256, 128], P(None, 'rad', 'az')
- new_density: float32 [32, 256, 128], P('rad', 'az')
All inputs are finite; a program needn't handle non-finite values.
Results may differ from a plain program's by a relative error of at most 0.00002.
Values sent between devices are 32-bit elements; how exact they have to be, the bound alone decides.
No kernel may reach another device: no remote copies, remote signals or barrier semaphores. Data moves between devices by JAX's collectives and lax.ppermute only.
A program may use at most 64 MiB of HBM per device.

v0:
```python
import jax
import jax.numpy as jnp
from jax import lax
from jax.sharding import PartitionSpec as P

FRAC_DEN = 64


shear_jump = 1.5
visc_step = 0.05
field_floor = 0.25


def passed_along(value, axis, steps):
    count = lax.axis_size(axis)
    pairs = [(source, (source + steps) % count) for source in range(count)]
    return lax.ppermute(value, axis, pairs)


def extended(cells, sides, width):
    for axis, dim in sides:
        count = lax.axis_size(axis)
        head = lax.slice_in_dim(cells, 0, width, axis=dim)
        tail = lax.slice_in_dim(cells, cells.shape[dim] - width, cells.shape[dim], axis=dim)
        cells = jnp.concatenate(
            [
                lax.ppermute(tail, axis, [(i, (i + 1) % count) for i in range(count)]),
                cells,
                lax.ppermute(head, axis, [((i + 1) % count, i) for i in range(count)]),
            ],
            axis=dim,
        )
    return cells


def vertical_slope(values):
    padded = jnp.concatenate([values[..., :1], values, values[..., -1:]], axis=-1)
    return (padded[..., 2:] - padded[..., :-2]) * 0.5


def field_stress(padded):
    velocity = padded[1:4]
    grad_x = (velocity[:, 2:, 1:-1] - velocity[:, :-2, 1:-1]) * 0.5
    grad_y = (velocity[:, 1:-1, 2:] - velocity[:, 1:-1, :-2]) * 0.5
    interior = padded[:, 1:-1, 1:-1]
    grad_z = vertical_slope(interior[1:4])
    magnet = interior[4:7]
    mag_square = magnet[0] * magnet[0] + magnet[1] * magnet[1] + magnet[2] * magnet[2]
    unit_field = magnet / jnp.sqrt(jnp.maximum(mag_square, field_floor))
    slopes = (grad_x, grad_y, grad_z)
    aligned = jnp.zeros_like(mag_square)
    for first_axis in range(3):
        for second_axis in range(3):
            aligned = (
                aligned
                + unit_field[first_axis] * unit_field[second_axis] * slopes[second_axis][first_axis]
            )
    velocity_div = grad_x[0] + grad_y[1] + grad_z[2]
    anisotropy = aligned - velocity_div / 3.0
    pressure_gap = 3.0 * visc_step * interior[0] * anisotropy
    tensor = jnp.stack(
        [
            pressure_gap * (unit_field[0] * unit_field[0] - 1.0 / 3.0),
            pressure_gap * (unit_field[1] * unit_field[1] - 1.0 / 3.0),
            pressure_gap * (unit_field[2] * unit_field[2] - 1.0 / 3.0),
            pressure_gap * unit_field[0] * unit_field[1],
            pressure_gap * unit_field[0] * unit_field[2],
            pressure_gap * unit_field[1] * unit_field[2],
        ]
    )
    return (tensor, pressure_gap * anisotropy)


def divergence(padded):
    interior = padded[:, 1:-1, 1:-1]

    def along_x(component):
        return (padded[component, 2:, 1:-1] - padded[component, :-2, 1:-1]) * 0.5

    def along_y(component):
        return (padded[component, 1:-1, 2:] - padded[component, 1:-1, :-2]) * 0.5

    vertical = vertical_slope(interior)
    force_x = along_x(0) + along_y(3) + vertical[4]
    force_y = along_x(3) + along_y(1) + vertical[5]
    force_z = along_x(4) + along_y(5) + vertical[2]
    return jnp.stack([force_x, force_y, force_z])


def fromm_blend(back_two, back_one, centre, ahead_one, fraction):
    slope_here = (ahead_one - back_one) * 0.5
    slope_back = (centre - back_two) * 0.5
    return (
        centre
        + fraction * (back_one - centre)
        + fraction * (1.0 - fraction) * 0.5 * (slope_back - slope_here)
    )


def roll_by_rows(values, amounts, row_dim, roll_dim, limit):
    digits = max(int(limit - 1).bit_length(), 1)
    shape_mask = [1] * values.ndim
    shape_mask[row_dim] = values.shape[row_dim]
    result = values
    for bit_place in range(digits):
        chosen = (amounts >> bit_place & 1 == 1).reshape(shape_mask)
        result = jnp.where(chosen, jnp.roll(result, 2**bit_place, axis=roll_dim), result)
    return result


def roll_strips(strips, amounts):
    az_cells = strips.shape[3]
    blocks = amounts // az_cells
    remainder = amounts % az_cells
    places = lax.axis_size("az").bit_length() - 1
    rolled = strips
    for bit_place in range(places):
        shifted = passed_along(rolled, "az", 2**bit_place)
        chosen = blocks >> bit_place & 1 == 1
        rolled = jnp.where(chosen[:, None, None, None, None], shifted, rolled)
    before = passed_along(rolled, "az", 1)
    joined = jnp.concatenate([before, rolled], axis=3)
    moved = roll_by_rows(joined, remainder, 0, 3, az_cells)
    return moved[:, :, :, az_cells:]


def extend(block_data, cells_wide, jump_row, shear_cells):
    cycle_index = lax.axis_index("rad")
    cycle_count = lax.axis_size("rad")
    total_az = block_data.shape[2] * lax.axis_size("az")
    down_amount = jnp.where(cycle_index == 0, (total_az - shear_cells) % total_az, 0)
    up_amount = jnp.where(cycle_index == cycle_count - 1, shear_cells, 0)
    strips = jnp.stack([block_data[:, :cells_wide], block_data[:, -cells_wide:]])
    amounts = jnp.stack([down_amount, up_amount])
    rolled = roll_strips(strips, amounts)
    if jump_row is not None:
        jump_terms = jnp.stack(
            [
                jnp.where(cycle_index == 0, -shear_jump, 0.0),
                jnp.where(cycle_index == cycle_count - 1, shear_jump, 0.0),
            ]
        ).astype(jnp.float32)
        marker = (jnp.arange(block_data.shape[0]) == jump_row).astype(jnp.float32)
        rolled = rolled + (jump_terms[:, None] * marker[None, :])[:, :, None, None, None]
    rim_pair = jnp.concatenate([rolled[0], rolled[1]], axis=1)
    ghosts = extended(rim_pair, (("rad", 1),), cells_wide)
    widened = jnp.concatenate([ghosts[:, :cells_wide], block_data, ghosts[:, -cells_wide:]], axis=1)
    return extended(widened, (("az", 2),), cells_wide)


def remap_shifts(updated, shift_int, frac_num):
    az_cells = updated.shape[2]
    blocks = shift_int // az_cells
    remainder = shift_int % az_cells
    places = lax.axis_size("az").bit_length() - 1
    rolled = updated
    for bit_place in range(places):
        shifted = passed_along(rolled, "az", 2**bit_place)
        chosen = blocks >> bit_place & 1 == 1
        rolled = jnp.where(chosen[None, :, None, None], shifted, rolled)
    before = passed_along(rolled, "az", 1)
    joined = jnp.concatenate([before, rolled], axis=2)
    aligned = roll_by_rows(joined, remainder, 1, 2, az_cells)[:, :, az_cells:]
    padded = extended(aligned, (("az", 2),), 2)
    fraction = (frac_num.astype(jnp.float32) / FRAC_DEN)[None, :, None, None]
    return fromm_blend(
        padded[:, :, 0:az_cells],
        padded[:, :, 1 : az_cells + 1],
        padded[:, :, 2 : az_cells + 2],
        padded[:, :, 3 : az_cells + 3],
        fraction,
    )


def local(fields, density, shift_int, frac_num, boundary_shift):
    stacked = jnp.concatenate([density[None], fields], axis=0)
    shear_cells = boundary_shift[0]
    padded = extend(stacked, 1, 2, shear_cells)
    tensor, heating = field_stress(padded)
    tensor_pad = extend(tensor, 1, None, shear_cells)
    force_terms = divergence(tensor_pad)
    updated = jnp.concatenate(
        [
            stacked[0:1],
            stacked[1:4] + force_terms / stacked[0],
            stacked[4:7],
            (stacked[7] + heating)[None],
        ],
        axis=0,
    )
    result = remap_shifts(updated, shift_int, frac_num)
    return (result[1:], result[0])


def solution(mesh):
    in_specs = (P(None, "rad", "az", None), P("rad", "az", None), P("rad"), P("rad"), P())
    out_specs = (P(None, "rad", "az", None), P("rad", "az", None))
    return jax.shard_map(local, mesh=mesh, in_specs=in_specs, out_specs=out_specs, check_vma=False)
```

profile of v0, /device:TPU:0, one launch (start us, length us, event | category | flops | bytes accessed | tf_op | source)
XLA Modules:
  0.0 234.6 jit_solution(13050447340616291767)
XLA Ops:
  0.6 0.9 fusion.53
  2.9 6.8 %collective-permute-done = f32[2,8,1,16,128]{4,3,1,2,0:T(8,128)S(1)} collective-permute-done((f32[2,8,1,16,128]{4,3,1,2,0:T(8,128)S(1)}, f32[2,8,1,16,128]{4,3,1,2,0:T(8,128)S(1)}, u32[]{:S(2)}, u32[]{:S(2)}) %collective-permute-start) | collective-permute-done | bytes 131104 | tf_op jit(solution)/shard_map/ppermute | solution.py:17
  9.8 9.0 %collective-permute-done.1 = f32[2,8,1,16,128]{4,3,1,2,0:T(8,128)S(1)} collective-permute-done((f32[2,8,1,16,128]{4,3,1,2,0:T(8,128)S(1)}, f32[2,8,1,16,128]{4,3,1,2,0:T(8,128)S(1)}, u32[]{:S(2)}, u32[]{:S(2)}) %collective-permute-start.1) | collective-permute-done | bytes 131104 | tf_op jit(solution)/shard_map/ppermute | solution.py:17
  19.0 6.7 %collective-permute-done.2 = f32[2,8,1,16,128]{4,3,1,2,0:T(8,128)S(1)} collective-permute-done((f32[2,8,1,16,128]{4,3,1,2,0:T(8,128)S(1)}, f32[2,8,1,16,128]{4,3,1,2,0:T(8,128)S(1)}, u32[]{:S(2)}, u32[]{:S(2)}) %collective-permute-start.2) | collective-permute-done | bytes 131104 | tf_op jit(solution)/shard_map/ppermute | solution.py:17
  26.0 5.8 %collective-permute-done.3 = f32[2,8,1,16,128]{4,3,1,2,0:T(8,128)S(1)} collective-permute-done((f32[2,8,1,16,128]{4,3,1,2,0:T(8,128)S(1)}, f32[2,8,1,16,128]{4,3,1,2,0:T(8,128)S(1)}, u32[]{:S(2)}, u32[]{:S(2)}) %collective-permute-start.3) | collective-permute-done | bytes 131104 | tf_op jit(solution)/shard_map/ppermute | solution.py:17
  32.0 7.0 %collective-permute-done.4 = f32[2,8,1,16,128]{4,3,1,2,0:T(8,128)S(1)} collective-permute-done((f32[2,8,1,16,128]{4,3,1,2,0:T(8,128)S(1)}, f32[2,8,1,16,128]{4,3,1,2,0:T(8,128)S(1)}, u32[]{:S(2)}, u32[]{:S(2)}) %collective-permute-start.4) | collective-permute-done | bytes 131104 | tf_op jit(solution)/shard_map/ppermute | solution.py:17
  39.5 1.6 collective-permute-start.6
  41.8 2.1 collective-permute-done.6
  43.9 1.5 collective-permute-done.5
  46.1 1.4 collective-permute-done.7
  47.5 4.6 %collective-permute-done.8 = f32[8,18,1,128]{3,2,1,0:T(1,128)S(1)} collective-permute-done((f32[8,18,1,128]{3,2,1,0:T(1,128)S(1)}, f32[8,18,1,128]{3,2,1,0:T(1,128)S(1)}, u32[]{:S(2)}, u32[]{:S(2)}) %collective-permute-start.8) | collective-permute-done | bytes 73760 | tf_op jit(solution)/shard_map/ppermute | solution.py:27
  53.1 6.7 %collective-permute-done.9 = f32[2,6,1,16,128]{4,3,1,2,0:T(8,128)S(1)} collective-permute-done((f32[2,6,1,16,128]{4,3,1,2,0:T(8,128)S(1)}, f32[2,6,1,16,128]{4,3,1,2,0:T(8,128)S(1)}, u32[]{:S(2)}, u32[]{:S(2)}) %collective-permute-start.9) | collective-permute-done | bytes 98336 | tf_op jit(solution)/shard_map/ppermute | solution.py:17
  59.9 7.3 %collective-permute-done.10 = f32[2,6,1,16,128]{4,3,1,2,0:T(8,128)S(1)} collective-permute-done((f32[2,6,1,16,128]{4,3,1,2,0:T(8,128)S(1)}, f32[2,6,1,16,128]{4,3,1,2,0:T(8,128)S(1)}, u32[]{:S(2)}, u32[]{:S(2)}) %collective-permute-start.10) | collective-permute-done | bytes 98336 | tf_op jit(solution)/shard_map/ppermute | solution.py:17
  67.3 6.4 %collective-permute-done.11 = f32[2,6,1,16,128]{4,3,1,2,0:T(8,128)S(1)} collective-permute-done((f32[2,6,1,16,128]{4,3,1,2,0:T(8,128)S(1)}, f32[2,6,1,16,128]{4,3,1,2,0:T(8,128)S(1)}, u32[]{:S(2)}, u32[]{:S(2)}) %collective-permute-start.11) | collective-permute-done | bytes 98336 | tf_op jit(solution)/shard_map/ppermute | solution.py:17
  73.9 5.5 %collective-permute-done.12 = f32[2,6,1,16,128]{4,3,1,2,0:T(8,128)S(1)} collective-permute-done((f32[2,6,1,16,128]{4,3,1,2,0:T(8,128)S(1)}, f32[2,6,1,16,128]{4,3,1,2,0:T(8,128)S(1)}, u32[]{:S(2)}, u32[]{:S(2)}) %collective-permute-start.12) | collective-permute-done | bytes 98336 | tf_op jit(solution)/shard_map/ppermute | solution.py:17
  79.8 6.4 %collective-permute-done.13 = f32[2,6,1,16,128]{4,3,1,2,0:T(8,128)S(1)} collective-permute-done((f32[2,6,1,16,128]{4,3,1,2,0:T(8,128)S(1)}, f32[2,6,1,16,128]{4,3,1,2,0:T(8,128)S(1)}, u32[]{:S(2)}, u32[]{:S(2)}) %collective-permute-start.13) | collective-permute-done | bytes 98336 | tf_op jit(solution)/shard_map/ppermute | solution.py:17
  86.7 0.8 collective-permute-start.15
  87.4 1.3 collective-permute-start.14
  88.8 2.0 collective-permute-done.15
  90.8 0.7 collective-permute-done.14
  92.2 0.7 fusion.13
  93.5 4.5 %collective-permute-done.17 = f32[6,18,1,128]{3,2,1,0:T(1,128)S(1)} collective-permute-done((f32[6,18,1,128]{3,2,1,0:T(1,128)S(1)}, f32[6,18,1,128]{3,2,1,0:T(1,128)S(1)}, u32[]{:S(2)}, u32[]{:S(2)}) %collective-permute-start.17) | collective-permute-done | bytes 55328 | tf_op jit(solution)/shard_map/ppermute | solution.py:27
  98.9 16.5 %collective-permute-done.18 = f32[8,16,16,128]{3,2,1,0:T(8,128)S(1)} collective-permute-done((f32[8,16,16,128]{3,2,1,0:T(8,128)S(1)}, f32[8,16,16,128]{3,2,1,0:T(8,128)S(1)}, u32[]{:S(2)}, u32[]{:S(2)}) %collective-permute-start.18) | collective-permute-done | bytes 1048608 | tf_op jit(solution)/shard_map/ppermute | solution.py:17
  115.6 25.3 %collective-permute-done.19 = f32[8,16,16,128]{3,2,1,0:T(8,128)S(1)} collective-permute-done((f32[8,16,16,128]{3,2,1,0:T(8,128)S(1)}, f32[8,16,16,128]{3,2,1,0:T(8,128)S(1)}, u32[]{:S(2)}, u32[]{:S(2)}) %collective-permute-start.19) | collective-permute-done | bytes 1048608 | tf_op jit(solution)/shard_map/ppermute | solution.py:17
  141.2 19.2 %collective-permute-done.20 = f32[8,16,16,128]{3,2,1,0:T(8,128)S(1)} collective-permute-done((f32[8,16,16,128]{3,2,1,0:T(8,128)S(1)}, f32[8,16,16,128]{3,2,1,0:T(8,128)S(1)}, u32[]{:S(2)}, u32[]{:S(2)}) %collective-permute-start.20) | collective-permute-done | bytes 1048608 | tf_op jit(solution)/shard_map/ppermute | solution.py:17
  160.6 44.4 %collective-permute-done.21 = f32[8,16,16,128]{3,2,1,0:T(8,128)S(1)} collective-permute-done((f32[8,16,16,128]{3,2,1,0:T(8,128)S(1)}, f32[8,16,16,128]{3,2,1,0:T(8,128)S(1)}, u32[]{:S(2)}, u32[]{:S(2)}) %collective-permute-start.21) | collective-permute-done | bytes 1048608 | tf_op jit(solution)/shard_map/ppermute | solution.py:17
  205.3 16.8 %collective-permute-done.22 = f32[8,16,16,128]{3,2,1,0:T(8,128)S(1)} collective-permute-done((f32[8,16,16,128]{3,2,1,0:T(8,128)S(1)}, f32[8,16,16,128]{3,2,1,0:T(8,128)S(1)}, u32[]{:S(2)}, u32[]{:S(2)}) %collective-permute-start.22) | collective-permute-done | bytes 1048608 | tf_op jit(solution)/shard_map/ppermute | solution.py:17
  225.1 4.4 %collective-permute-start.24 = (f32[8,16,2,128]{3,2,1,0:T(2,128)S(1)}, f32[8,16,2,128]{3,2,1,0:T(2,128)S(1)}, u32[]{:S(2)}, u32[]{:S(2)}) collective-permute-start(f32[8,16,2,128]{3,2,1,0:T(2,128)S(1)} %get-tuple-element.15), channel_id=1, source_target_pairs={{1,0},{2,1},{3,2},{4,3},{5,4},{6,5},{7,6},{8,7},{9,8},{10,9},{11,1... | collective-permute-start | bytes 393224 | tf_op jit(solution)/shard_map/ppermute | solution.py:29
  229.7 2.5 %collective-permute-done.23 = f32[8,16,2,128]{3,2,1,0:T(2,128)S(1)} collective-permute-done((f32[8,16,2,128]{3,2,1,0:T(2,128)S(1)}, f32[8,16,2,128]{3,2,1,0:T(2,128)S(1)}, u32[]{:S(2)}, u32[]{:S(2)}) %collective-permute-start.23) | collective-permute-done | bytes 131104 | tf_op jit(solution)/shard_map/ppermute | solution.py:27
  232.2 0.7 fusion.9
  232.9 1.0 slice.520
  233.9 0.7 slice_bitcast_fusion
  (110 shorter events, 11.6 us)
Async XLA Ops:
  1.5 8.2 %collective-permute-start = (f32[2,8,1,16,128]{4,3,1,2,0:T(8,128)S(1)}, f32[2,8,1,16,128]{4,3,1,2,0:T(8,128)S(1)}, u32[]{:S(2)}, u32[]{:S(2)}) collective-permute-start(f32[2,8,1,16,128]{4,3,1,2,0:T(8,128)S(1)} %pad_maximum_fusion.31), channel_id=1, source_target_pairs={{0,1},{1,2},{2,3},{3,4},{4,5},{5,6},{6,7},{7,8},{8,9},{9,10},{10,1... | collective-permute-start | bytes 393224 | tf_op jit(solution)/shard_map/ppermute | solution.py:17
  9.8 9.1 %collective-permute-start.1 = (f32[2,8,1,16,128]{4,3,1,2,0:T(8,128)S(1)}, f32[2,8,1,16,128]{4,3,1,2,0:T(8,128)S(1)}, u32[]{:S(2)}, u32[]{:S(2)}) collective-permute-start(f32[2,8,1,16,128]{4,3,1,2,0:T(8,128)S(1)} %broadcast_select_fusion.4), channel_id=1, source_target_pairs={{0,2},{1,3},{2,4},{3,5},{4,6},{5,7},{6,8},{7,9},{8,10},{9,11},{10,... | collective-permute-start | bytes 393224 | tf_op jit(solution)/shard_map/ppermute | solution.py:17
  18.9 6.8 %collective-permute-start.2 = (f32[2,8,1,16,128]{4,3,1,2,0:T(8,128)S(1)}, f32[2,8,1,16,128]{4,3,1,2,0:T(8,128)S(1)}, u32[]{:S(2)}, u32[]{:S(2)}) collective-permute-start(f32[2,8,1,16,128]{4,3,1,2,0:T(8,128)S(1)} %broadcast_select_fusion.5), channel_id=1, source_target_pairs={{0,4},{1,5},{2,6},{3,7},{4,8},{5,9},{6,10},{7,11},{8,12},{9,13},{1... | collective-permute-start | bytes 393224 | tf_op jit(solution)/shard_map/ppermute | solution.py:17
  25.8 5.9 %collective-permute-start.3 = (f32[2,8,1,16,128]{4,3,1,2,0:T(8,128)S(1)}, f32[2,8,1,16,128]{4,3,1,2,0:T(8,128)S(1)}, u32[]{:S(2)}, u32[]{:S(2)}) collective-permute-start(f32[2,8,1,16,128]{4,3,1,2,0:T(8,128)S(1)} %broadcast_select_fusion.6), channel_id=1, source_target_pairs={{0,8},{1,9},{2,10},{3,11},{4,12},{5,13},{6,14},{7,15},{8,0},{9,1},... | collective-permute-start | bytes 393224 | tf_op jit(solution)/shard_map/ppermute | solution.py:17
  31.9 7.1 %collective-permute-start.4 = (f32[2,8,1,16,128]{4,3,1,2,0:T(8,128)S(1)}, f32[2,8,1,16,128]{4,3,1,2,0:T(8,128)S(1)}, u32[]{:S(2)}, u32[]{:S(2)}) collective-permute-start(f32[2,8,1,16,128]{4,3,1,2,0:T(8,128)S(1)} %broadcast_select_fusion.7), channel_id=1, source_target_pairs={{0,1},{1,2},{2,3},{3,4},{4,5},{5,6},{6,7},{7,8},{8,9},{9,10},{10,1... | collective-permute-start | bytes 393224 | tf_op jit(solution)/shard_map/ppermute | solution.py:17
  32.0 9.6 %copy-start = (f32[7,16,16,128]{3,2,1,0:T(8,128)S(1)}, f32[7,16,16,128]{3,2,1,0:T(8,128)}, u32[]{:S(2)}) copy-start(f32[7,16,16,128]{3,2,1,0:T(8,128)} %param.5) | copy-start | bytes 2752516
  39.1 6.2 %copy-start.1 = (f32[16,16,128]{2,1,0:T(8,128)S(1)}, f32[16,16,128]{2,1,0:T(8,128)}, u32[]{:S(2)}) copy-start(f32[16,16,128]{2,1,0:T(8,128)} %param.6) | copy-start | bytes 393220
  39.5 4.3 %collective-permute-start.6 = (f32[8,1,16,128]{3,2,0,1:T(8,128)S(1)}, f32[8,1,16,128]{3,2,0,1:T(8,128)S(1)}, u32[]{:S(2)}, u32[]{:S(2)}) collective-permute-start(f32[8,1,16,128]{3,2,0,1:T(8,128)S(1)} %get-tuple-element.36), channel_id=1, source_target_pairs={{0,16},{16,0},{1,17},{17,1},{2,18},{18,2},{3,19},{19,3},{4,20},{20... | collective-permute-start | bytes 196616 | tf_op jit(solution)/shard_map/ppermute | solution.py:27
  41.1 4.3 %collective-permute-start.5 = (f32[8,1,16,128]{3,2,1,0:T(8,128)S(1)}, f32[8,1,16,128]{3,2,1,0:T(8,128)S(1)}, u32[]{:S(2)}, u32[]{:S(2)}) collective-permute-start(f32[8,1,16,128]{3,2,1,0:T(8,128)S(1)} %get-tuple-element.37), channel_id=1, source_target_pairs={{16,0},{0,16},{17,1},{1,17},{18,2},{2,18},{19,3},{3,19},{20,4},{4,... | collective-permute-start | bytes 196616 | tf_op jit(solution)/shard_map/ppermute | solution.py:29
  45.5 2.0 collective-permute-start.7
  45.5 6.5 %collective-permute-start.8 = (f32[8,18,1,128]{3,2,1,0:T(1,128)S(1)}, f32[8,18,1,128]{3,2,1,0:T(1,128)S(1)}, u32[]{:S(2)}, u32[]{:S(2)}) collective-permute-start(f32[8,18,1,128]{3,2,1,0:T(1,128)S(1)} %get-tuple-element.19), channel_id=1, source_target_pairs={{0,1},{1,2},{2,3},{3,4},{4,5},{5,6},{6,7},{7,8},{8,9},{9,10},{10,1... | collective-permute-start | bytes 221192 | tf_op jit(solution)/shard_map/ppermute | solution.py:27
  53.0 6.8 %collective-permute-start.9 = (f32[2,6,1,16,128]{4,3,1,2,0:T(8,128)S(1)}, f32[2,6,1,16,128]{4,3,1,2,0:T(8,128)S(1)}, u32[]{:S(2)}, u32[]{:S(2)}) collective-permute-start(f32[2,6,1,16,128]{4,3,1,2,0:T(8,128)S(1)} %pad_maximum_fusion.32), channel_id=1, source_target_pairs={{0,1},{1,2},{2,3},{3,4},{4,5},{5,6},{6,7},{7,8},{8,9},{9,10},{10,1... | collective-permute-start | bytes 294920 | tf_op jit(solution)/shard_map/ppermute | solution.py:17
  59.9 7.3 %collective-permute-start.10 = (f32[2,6,1,16,128]{4,3,1,2,0:T(8,128)S(1)}, f32[2,6,1,16,128]{4,3,1,2,0:T(8,128)S(1)}, u32[]{:S(2)}, u32[]{:S(2)}) collective-permute-start(f32[2,6,1,16,128]{4,3,1,2,0:T(8,128)S(1)} %broadcast_select_fusion.8), channel_id=1, source_target_pairs={{0,2},{1,3},{2,4},{3,5},{4,6},{5,7},{6,8},{7,9},{8,10},{9,11},{10,... | collective-permute-start | bytes 294920 | tf_op jit(solution)/shard_map/ppermute | solution.py:17
  67.3 6.5 %collective-permute-start.11 = (f32[2,6,1,16,128]{4,3,1,2,0:T(8,128)S(1)}, f32[2,6,1,16,128]{4,3,1,2,0:T(8,128)S(1)}, u32[]{:S(2)}, u32[]{:S(2)}) collective-permute-start(f32[2,6,1,16,128]{4,3,1,2,0:T(8,128)S(1)} %broadcast_select_fusion.9), channel_id=1, source_target_pairs={{0,4},{1,5},{2,6},{3,7},{4,8},{5,9},{6,10},{7,11},{8,12},{9,13},{1... | collective-permute-start | bytes 294920 | tf_op jit(solution)/shard_map/ppermute | solution.py:17
  73.8 5.5 %collective-permute-start.12 = (f32[2,6,1,16,128]{4,3,1,2,0:T(8,128)S(1)}, f32[2,6,1,16,128]{4,3,1,2,0:T(8,128)S(1)}, u32[]{:S(2)}, u32[]{:S(2)}) collective-permute-start(f32[2,6,1,16,128]{4,3,1,2,0:T(8,128)S(1)} %broadcast_select_fusion.10), channel_id=1, source_target_pairs={{0,8},{1,9},{2,10},{3,11},{4,12},{5,13},{6,14},{7,15},{8,0},{9,1},... | collective-permute-start | bytes 294920 | tf_op jit(solution)/shard_map/ppermute | solution.py:17
  79.4 6.7 %collective-permute-start.13 = (f32[2,6,1,16,128]{4,3,1,2,0:T(8,128)S(1)}, f32[2,6,1,16,128]{4,3,1,2,0:T(8,128)S(1)}, u32[]{:S(2)}, u32[]{:S(2)}) collective-permute-start(f32[2,6,1,16,128]{4,3,1,2,0:T(8,128)S(1)} %broadcast_select_fusion.11), channel_id=1, source_target_pairs={{0,1},{1,2},{2,3},{3,4},{4,5},{5,6},{6,7},{7,8},{8,9},{9,10},{10,1... | collective-permute-start | bytes 294920 | tf_op jit(solution)/shard_map/ppermute | solution.py:17
  86.7 4.2 %collective-permute-start.15 = (f32[6,1,16,128]{3,2,0,1:T(8,128)S(1)}, f32[6,1,16,128]{3,2,0,1:T(8,128)S(1)}, u32[]{:S(2)}, u32[]{:S(2)}) collective-permute-start(f32[6,1,16,128]{3,2,0,1:T(8,128)S(1)} %get-tuple-element.34), channel_id=1, source_target_pairs={{0,16},{16,0},{1,17},{17,1},{2,18},{18,2},{3,19},{19,3},{4,20},{20... | collective-permute-start | bytes 147464 | tf_op jit(solution)/shard_map/ppermute | solution.py:27
  87.4 4.1 %collective-permute-start.14 = (f32[6,1,16,128]{3,2,1,0:T(8,128)S(1)}, f32[6,1,16,128]{3,2,1,0:T(8,128)S(1)}, u32[]{:S(2)}, u32[]{:S(2)}) collective-permute-start(f32[6,1,16,128]{3,2,1,0:T(8,128)S(1)} %get-tuple-element.35), channel_id=1, source_target_pairs={{16,0},{0,16},{17,1},{1,17},{18,2},{2,18},{19,3},{3,19},{20,4},{4,... | collective-permute-start | bytes 147464 | tf_op jit(solution)/shard_map/ppermute | solution.py:29
  91.6 1.9 collective-permute-start.16
  91.7 6.3 %collective-permute-start.17 = (f32[6,18,1,128]{3,2,1,0:T(1,128)S(1)}, f32[6,18,1,128]{3,2,1,0:T(1,128)S(1)}, u32[]{:S(2)}, u32[]{:S(2)}) collective-permute-start(f32[6,18,1,128]{3,2,1,0:T(1,128)S(1)} %get-tuple-element.29), channel_id=1, source_target_pairs={{0,1},{1,2},{2,3},{3,4},{4,5},{5,6},{6,7},{7,8},{8,9},{9,10},{10,1... | collective-permute-start | bytes 165896 | tf_op jit(solution)/shard_map/ppermute | solution.py:27
  98.2 0.7 copy-start.2
  98.4 17.0 %collective-permute-start.18 = (f32[8,16,16,128]{3,2,1,0:T(8,128)S(1)}, f32[8,16,16,128]{3,2,1,0:T(8,128)S(1)}, u32[]{:S(2)}, u32[]{:S(2)}) collective-permute-start(f32[8,16,16,128]{3,2,1,0:T(8,128)S(1)} %fusion.3), channel_id=1, source_target_pairs={{0,1},{1,2},{2,3},{3,4},{4,5},{5,6},{6,7},{7,8},{8,9},{9,10},{10,1... | collective-permute-start | bytes 3145736 | tf_op jit(solution)/shard_map/ppermute | solution.py:17
  115.6 25.3 %collective-permute-start.19 = (f32[8,16,16,128]{3,2,1,0:T(8,128)S(1)}, f32[8,16,16,128]{3,2,1,0:T(8,128)S(1)}, u32[]{:S(2)}, u32[]{:S(2)}) collective-permute-start(f32[8,16,16,128]{3,2,1,0:T(8,128)S(1)} %broadcast_select_fusion), channel_id=1, source_target_pairs={{0,2},{1,3},{2,4},{3,5},{4,6},{5,7},{6,8},{7,9},{8,10},{9,11},{10,... | collective-permute-start | bytes 3145736 | tf_op jit(solution)/shard_map/ppermute | solution.py:17
  141.1 19.2 %collective-permute-start.20 = (f32[8,16,16,128]{3,2,1,0:T(8,128)S(1)}, f32[8,16,16,128]{3,2,1,0:T(8,128)S(1)}, u32[]{:S(2)}, u32[]{:S(2)}) collective-permute-start(f32[8,16,16,128]{3,2,1,0:T(8,128)S(1)} %broadcast_select_fusion.1), channel_id=1, source_target_pairs={{0,4},{1,5},{2,6},{3,7},{4,8},{5,9},{6,10},{7,11},{8,12},{9,13},{1... | collective-permute-start | bytes 3145736 | tf_op jit(solution)/shard_map/ppermute | solution.py:17
  160.5 44.4 %collective-permute-start.21 = (f32[8,16,16,128]{3,2,1,0:T(8,128)S(1)}, f32[8,16,16,128]{3,2,1,0:T(8,128)S(1)}, u32[]{:S(2)}, u32[]{:S(2)}) collective-permute-start(f32[8,16,16,128]{3,2,1,0:T(8,128)S(1)} %broadcast_select_fusion.2), channel_id=1, source_target_pairs={{0,8},{1,9},{2,10},{3,11},{4,12},{5,13},{6,14},{7,15},{8,0},{9,1},... | collective-permute-start | bytes 3145736 | tf_op jit(solution)/shard_map/ppermute | solution.py:17
  205.1 17.0 %collective-permute-start.22 = (f32[8,16,16,128]{3,2,1,0:T(8,128)S(1)}, f32[8,16,16,128]{3,2,1,0:T(8,128)S(1)}, u32[]{:S(2)}, u32[]{:S(2)}) collective-permute-start(f32[8,16,16,128]{3,2,1,0:T(8,128)S(1)} %broadcast_select_fusion.3), channel_id=1, source_target_pairs={{0,1},{1,2},{2,3},{3,4},{4,5},{5,6},{6,7},{7,8},{8,9},{9,10},{10,1... | collective-permute-start | bytes 3145736 | tf_op jit(solution)/shard_map/ppermute | solution.py:17
  224.5 5.1 %copy-start.3 = (s32[16]{0:T(128)S(1)}, s32[16]{0:T(128)}, u32[]{:S(2)}) copy-start(s32[16]{0:T(128)} %param.8) | copy-start | bytes 196
  225.1 7.1 %collective-permute-start.23 = (f32[8,16,2,128]{3,2,1,0:T(2,128)S(1)}, f32[8,16,2,128]{3,2,1,0:T(2,128)S(1)}, u32[]{:S(2)}, u32[]{:S(2)}) collective-permute-start(f32[8,16,2,128]{3,2,1,0:T(2,128)S(1)} %get-tuple-element.14), channel_id=1, source_target_pairs={{0,1},{1,2},{2,3},{3,4},{4,5},{5,6},{6,7},{7,8},{8,9},{9,10},{10,1... | collective-permute-start | bytes 393224 | tf_op jit(solution)/shard_map/ppermute | solution.py:27
  225.1 7.1 %collective-permute-start.24 = (f32[8,16,2,128]{3,2,1,0:T(2,128)S(1)}, f32[8,16,2,128]{3,2,1,0:T(2,128)S(1)}, u32[]{:S(2)}, u32[]{:S(2)}) collective-permute-start(f32[8,16,2,128]{3,2,1,0:T(2,128)S(1)} %get-tuple-element.15), channel_id=1, source_target_pairs={{1,0},{2,1},{3,2},{4,3},{5,4},{6,5},{7,6},{8,7},{9,8},{10,9},{11,1... | collective-permute-start | bytes 393224 | tf_op jit(solution)/shard_map/ppermute | solution.py:29
where the time goes:
time: 235 us
  waiting for transfers between devices  210 us (89%)
  starting transfers between devices  11 us (5%)
  other arithmetic  8.66 us (4%)
  local copies, waits for them, and re-layouts  3.31 us (1%)
    ppermute x15, waiting for transfers between devices, passed_along(): return lax.ppermute(value, axis, pairs)  190 us
    ppermute x5, waiting for transfers between devices, extended(): lax.ppermute(tail, axis, [(i, (i + 1) % count) for i in range(count)])  15.7 us
    ppermute x5, starting transfers between devices, extended(): lax.ppermute(head, axis, [((i + 1) % count, i) for i in range(count)])  6.4 us
  transfers between devices with their start and end apart: 25, of which 24 were waited for; matrix products, arithmetic and copies ran while one was open for 1% of the time, Pallas kernels for 0%

commit v1 on v0

v1 whole, which is shorter than its diff:
```python
import jax
import jax.numpy as jnp
from jax import lax
from jax.sharding import PartitionSpec as P

FRAC_DEN = 64

shear_jump = 1.5
visc_step = 0.05
field_floor = 0.25


def vertical_slope(values):
    padded = jnp.concatenate([values[..., :1], values, values[..., -1:]], axis=-1)
    return (padded[..., 2:] - padded[..., :-2]) * 0.5


def field_stress(padded):
    velocity = padded[1:4]
    grad_x = (velocity[:, 2:, 1:-1] - velocity[:, :-2, 1:-1]) * 0.5
    grad_y = (velocity[:, 1:-1, 2:] - velocity[:, 1:-1, :-2]) * 0.5
    interior = padded[:, 1:-1, 1:-1]
    grad_z = vertical_slope(interior[1:4])
    magnet = interior[4:7]
    mag_square = magnet[0] * magnet[0] + magnet[1] * magnet[1] + magnet[2] * magnet[2]
    unit_field = magnet / jnp.sqrt(jnp.maximum(mag_square, field_floor))
    slopes = (grad_x, grad_y, grad_z)
    aligned = jnp.zeros_like(mag_square)
    for first_axis in range(3):
        for second_axis in range(3):
            aligned = (
                aligned
                + unit_field[first_axis] * unit_field[second_axis] * slopes[second_axis][first_axis]
            )
    velocity_div = grad_x[0] + grad_y[1] + grad_z[2]
    anisotropy = aligned - velocity_div / 3.0
    pressure_gap = 3.0 * visc_step * interior[0] * anisotropy
    tensor = jnp.stack(
        [
            pressure_gap * (unit_field[0] * unit_field[0] - 1.0 / 3.0),
            pressure_gap * (unit_field[1] * unit_field[1] - 1.0 / 3.0),
            pressure_gap * (unit_field[2] * unit_field[2] - 1.0 / 3.0),
            pressure_gap * unit_field[0] * unit_field[1],
            pressure_gap * unit_field[0] * unit_field[2],
            pressure_gap * unit_field[1] * unit_field[2],
        ]
    )
    return (tensor, pressure_gap * anisotropy)


def divergence(padded):
    interior = padded[:, 1:-1, 1:-1]

    def along_x(component):
        return (padded[component, 2:, 1:-1] - padded[component, :-2, 1:-1]) * 0.5

    def along_y(component):
        return (padded[component, 1:-1, 2:] - padded[component, 1:-1, :-2]) * 0.5

    vertical = vertical_slope(interior)
    force_x = along_x(0) + along_y(3) + vertical[4]
    force_y = along_x(3) + along_y(1) + vertical[5]
    force_z = along_x(4) + along_y(5) + vertical[2]
    return jnp.stack([force_x, force_y, force_z])


def fromm_blend(back_two, back_one, centre, ahead_one, fraction):
    slope_here = (ahead_one - back_one) * 0.5
    slope_back = (centre - back_two) * 0.5
    return (
        centre
        + fraction * (back_one - centre)
        + fraction * (1.0 - fraction) * 0.5 * (slope_back - slope_here)
    )


def radial_ghosts(density, velocity, magnet, shear_cells):
    az_cells = density.shape[1]
    radials = lax.axis_size("rad")
    azimuths = lax.axis_size("az")
    me = lax.axis_index("rad")

    def strip(near, far):
        return jnp.concatenate(
            [velocity[:, near], density[None, near], magnet[:, near], velocity[:, far]], axis=0
        )

    low = strip(0, 1)
    high = strip(-1, -2)
    blocks = shear_cells // az_cells
    remainder = shear_cells % az_cells

    def flat(rad, az):
        return rad * azimuths + az % azimuths

    last = radials - 1

    def wrap(data, steps):
        pairs = [(flat(last, az), flat(0, az + steps)) for az in range(azimuths)]
        pairs += [(flat(0, az), flat(last, az - steps)) for az in range(azimuths)]
        return lax.ppermute(data, ("rad", "az"), pairs)

    def branch(steps):
        def run(data):
            return wrap(data, steps), wrap(data, steps + 1)

        return run

    edge = jnp.where(me == 0, low, high)
    if radials == 2:
        other = jnp.where(me == 0, high, low)
        straight = lax.ppermute(other, "rad", [(0, 1), (1, 0)])
        from_below = from_above = straight
    else:
        from_below = lax.ppermute(high, "rad", [(i, i + 1) for i in range(last)])
        from_above = lax.ppermute(low, "rad", [(i + 1, i) for i in range(last)])
    whole, next_one = lax.switch(blocks, [branch(k) for k in range(azimuths)], edge)
    joined = jnp.concatenate(
        [jnp.where(me == 0, next_one, whole), jnp.where(me == 0, whole, next_one)], axis=1
    )
    start = jnp.where(me == 0, az_cells - remainder, remainder)
    sheared = lax.dynamic_slice_in_dim(joined, start, az_cells, axis=1)
    marker = jnp.zeros((10, 1, 1), jnp.float32).at[jnp.array([1, 8])].set(shear_jump)
    below = jnp.where(me == 0, sheared + marker, from_below)
    above = jnp.where(me == last, sheared - marker, from_above)
    return below, above


def widen(fields, density, shear_cells):
    velocity, magnet = fields[0:3], fields[3:6]
    below, above = radial_ghosts(density, velocity, magnet, shear_cells)
    stacked = jnp.concatenate([density[None], fields[:6]], axis=0)

    def nearest(strip):
        return jnp.concatenate([strip[3:4], strip[0:3], strip[4:7]], axis=0)[:, None]

    def second(strip):
        return jnp.concatenate([strip[0:1] * 0, strip[7:10], strip[4:7] * 0], axis=0)[:, None]

    tall = jnp.concatenate(
        [second(below), nearest(below), stacked, nearest(above), second(above)], axis=1
    )
    azimuths = lax.axis_size("az")
    head, tail = tall[:, :, :2], tall[:, :, -2:]
    before = lax.ppermute(tail, "az", [(i, (i + 1) % azimuths) for i in range(azimuths)])
    after = lax.ppermute(head, "az", [((i + 1) % azimuths, i) for i in range(azimuths)])
    return jnp.concatenate([before, tall, after], axis=2)


def remap(updated, shift_int, frac_num):
    quantities, columns, az_cells, depth = updated.shape
    azimuths = lax.axis_size("az")
    share = quantities * columns // azimuths
    pieces = updated.transpose(1, 0, 2, 3).reshape(azimuths * share, az_cells, depth)
    gathered = lax.all_to_all(pieces, "az", 0, 0, tiled=True)
    total = azimuths * az_cells
    whole = gathered.reshape(azimuths, share, az_cells, depth).transpose(1, 0, 2, 3)
    whole = whole.reshape(share, total, depth)
    mine = (lax.axis_index("az") * share + jnp.arange(share)) // quantities
    amounts = jnp.take(shift_int, mine)
    fractions = jnp.take(frac_num, mine).astype(jnp.float32) / FRAC_DEN
    doubled = jnp.concatenate([whole[:, -2:], whole, whole, whole[:, :1]], axis=1)

    def move(rows, amount):
        return lax.dynamic_slice_in_dim(rows, (total - amount) % total, total + 3, axis=0)

    if quantities % share == 0:
        around = lax.dynamic_slice_in_dim(
            doubled, (total - amounts[0]) % total, total + 3, axis=1
        )
    else:
        around = jax.vmap(move)(doubled, amounts)
    moved = fromm_blend(
        around[:, 0:total],
        around[:, 1 : total + 1],
        around[:, 2 : total + 2],
        around[:, 3 : total + 3],
        fractions[:, None, None],
    )
    back = moved.reshape(share, azimuths, az_cells, depth).transpose(1, 0, 2, 3)
    back = back.reshape(azimuths * share, az_cells, depth)
    result = lax.all_to_all(back, "az", 0, 0, tiled=True)
    return result.reshape(columns, quantities, az_cells, depth).transpose(1, 0, 2, 3)


def local(fields, density, shift_int, frac_num, boundary_shift):
    padded = widen(fields, density, boundary_shift[0])
    tensor, heating = field_stress(padded)
    force_terms = divergence(tensor)
    updated = jnp.concatenate(
        [
            density[None],
            fields[0:3] + force_terms / density,
            fields[3:6],
            (fields[6] + heating[1:-1, 1:-1])[None],
        ],
        axis=0,
    )
    result = remap(updated, shift_int, frac_num)
    return (result[1:], result[0])


def solution(mesh):
    in_specs = (P(None, "rad", "az", None), P("rad", "az", None), P("rad"), P("rad"), P())
    out_specs = (P(None, "rad", "az", None), P("rad", "az", None))
    return jax.shard_map(local, mesh=mesh, in_specs=in_specs, out_specs=out_specs, check_vma=False)
```

time: 235 us -> 97.2 us (0.41)
  waiting for transfers between devices: 210 us -> 30.9 us
  blocking collectives: 0 us -> 31.5 us
  starting transfers between devices: 11 us -> 18.7 us
  local copies, waits for them, and re-layouts: 3.31 us -> 7.6 us
  other arithmetic: 8.66 us -> 6.29 us
    ppermute x25 -> x5, waiting for transfers between devices: 210 us -> 9.43 us  [the longest x2 6.65 us: wrap(): return lax.ppermute(data, ('rad', 'az'), pairs)]
    all_to_all x0 -> x1, blocking collectives: none -> 31.5 us  [remap(): result = lax.all_to_all(back, 'az', 0, 0, tiled=True)]
    all_to_all x0 -> x1, waiting for transfers between devices: none -> 21.5 us  [remap(): gathered = lax.all_to_all(pieces, 'az', 0, 0, tiled=True)]
    all_to_all x0 -> x1, starting transfers between devices: none -> 5.95 us  [remap(): gathered = lax.all_to_all(pieces, 'az', 0, 0, tiled=True)]
    select_n x23 -> x5, other arithmetic: 4.1 us -> 1.08 us  [the longest x1 0.94 us: radial_ghosts(): jnp.where(me == 0, next_one, whole)]
    ppermute x25 -> x5, starting transfers between devices: 11 us -> 12.7 us  [the longest x2 5.24 us: wrap(): return lax.ppermute(data, ('rad', 'az'), pairs)]
  transfers between devices with their start and end apart: 25 -> 6, of which waited for: 24 -> 4; matrix products, arithmetic and copies ran while one was open for 1% -> 2% of each run, Pallas kernels for 0% -> 0%
where the time goes in v1:
time: 97.2 us; the launch traced here: 96.8 us
  blocking collectives  31.5 us (32%)
  waiting for transfers between devices  30.9 us (32%)
  starting transfers between devices  18.7 us (19%)
  local copies, waits for them, and re-layouts  7.6 us (8%)
  other arithmetic  6.29 us (6%)
  between operations  1.73 us (2%)
    all_to_all x1, blocking collectives, remap(): result = lax.all_to_all(back, 'az', 0, 0, tiled=True)  31.5 us
    all_to_all x1, waiting for transfers between devices, remap(): gathered = lax.all_to_all(pieces, 'az', 0, 0, tiled=True)  21.5 us
    ppermute x2, waiting for transfers between devices, wrap(): return lax.ppermute(data, ('rad', 'az'), pairs)  6.65 us
    all_to_all x1, starting transfers between devices, remap(): gathered = lax.all_to_all(pieces, 'az', 0, 0, tiled=True)  5.95 us
    ppermute x2, starting transfers between devices, wrap(): return lax.ppermute(data, ('rad', 'az'), pairs)  5.24 us
    ppermute x1, starting transfers between devices, widen(): lax.ppermute(head, 'az', [((i + 1) % azimuths, i) for i in range(azimuths)])  4.43 us
    ppermute x1, starting transfers between devices, radial_ghosts(): straight = lax.ppermute(other, 'rad', [(0, 1), (1, 0)])  3 us
    ppermute x1, waiting for transfers between devices, widen(): lax.ppermute(tail, 'az', [(i, (i + 1) % azimuths) for i in range(azimuths)])  2.78 us
  transfers between devices with their start and end apart: 6, of which 4 were waited for; matrix products, arithmetic and copies ran while one was open for 2% of the time, Pallas kernels for 0%

profile of v1, /device:TPU:0, one launch (start us, length us, event | category | flops | bytes accessed | tf_op | source)
XLA Modules:
  0.0 96.8 jit_solution(2357840080527693668)
XLA Ops:
  0.7 0.8 slice_bitcast_fusion.6
  1.5 0.7 fusion.55
  2.3 3.0 %collective-permute-start.32 = (f32[10,16,128]{2,1,0:T(8,128)S(1)}, f32[10,16,128]{2,1,0:T(8,128)S(1)}, u32[]{:S(2)}, u32[]{:S(2)}) collective-permute-start(f32[10,16,128]{2,1,0:T(8,128)S(1)} %get-tuple-element.66), channel_id=1, source_target_pairs={{0,16},{16,0},{1,17},{17,1},{2,18},{18,2},{3,19},{19,3},{4,20},{20... | collective-permute-start | bytes 245768 | tf_op jit(solution)/shard_map/ppermute | solution.py:112
  5.9 11.9 %conditional.1 = (f32[10,16,128]{2,1,0:T(8,128)}, f32[10,16,128]{2,1,0:T(8,128)}) conditional(s32[]{:T(128)} %clamp.3, f32[10,16,128]{2,1,0:T(8,128)S(1)} %get-tuple-element.65, f32[10,16,128]{2,1,0:T(8,128)S(1)} %get-tuple-element.65, f32[10,16,128]{2,1,0:T(8,128)S(1)} %get-tuple-element.65, ...), branch_computations={%region_0.1_spmd, %region_1.2_spmd, %region_2.3_spmd, %region_3.4_... | conditional | bytes 655456 | solution.py:117
  6.0 3.8 %collective-permute-start.2 = (f32[10,16,128]{2,1,0:T(8,128)S(1)}, f32[10,16,128]{2,1,0:T(8,128)}, u32[]{:S(2)}, u32[]{:S(2)}) collective-permute-start(f32[10,16,128]{2,1,0:T(8,128)S(1)} %param.1), channel_id=1, source_target_pairs={{16,1},{17,2},{18,3},{19,4},{20,5},{21,6},{22,7},{23,8},{24,9},{25... | collective-permute-start | bytes 245768 | tf_op jit(solution)/shard_map/cond/branch_1_fun/ppermute | solution.py:101
  9.7 1.5 %collective-permute-start.3 = (f32[10,16,128]{2,1,0:T(8,128)S(1)}, f32[10,16,128]{2,1,0:T(8,128)}, u32[]{:S(2)}, u32[]{:S(2)}) collective-permute-start(f32[10,16,128]{2,1,0:T(8,128)S(1)} %param.1), channel_id=1, source_target_pairs={{16,2},{17,3},{18,4},{19,5},{20,6},{21,7},{22,8},{23,9},{24,10},{2... | collective-permute-start | bytes 245768 | tf_op jit(solution)/shard_map/cond/branch_1_fun/ppermute | solution.py:101
  11.2 2.4 %collective-permute-done.2 = f32[10,16,128]{2,1,0:T(8,128)} collective-permute-done((f32[10,16,128]{2,1,0:T(8,128)S(1)}, f32[10,16,128]{2,1,0:T(8,128)}, u32[]{:S(2)}, u32[]{:S(2)}) %collective-permute-start.2) | collective-permute-done | bytes 81952 | tf_op jit(solution)/shard_map/cond/branch_1_fun/ppermute | solution.py:101
  13.6 4.3 %collective-permute-done.3 = f32[10,16,128]{2,1,0:T(8,128)} collective-permute-done((f32[10,16,128]{2,1,0:T(8,128)S(1)}, f32[10,16,128]{2,1,0:T(8,128)}, u32[]{:S(2)}, u32[]{:S(2)}) %collective-permute-start.3) | collective-permute-done | bytes 81952 | tf_op jit(solution)/shard_map/cond/branch_1_fun/ppermute | solution.py:101
  17.9 0.9 broadcast_select_fusion.1
  19.0 1.0 slice-done
  20.3 4.4 %collective-permute-start.34 = (f32[7,20,2,128]{3,2,1,0:T(2,128)S(1)}, f32[7,20,2,128]{3,2,1,0:T(2,128)S(1)}, u32[]{:S(2)}, u32[]{:S(2)}) collective-permute-start(f32[7,20,2,128]{3,2,1,0:T(2,128)S(1)} %get-tuple-element.49), channel_id=1, source_target_pairs={{1,0},{2,1},{3,2},{4,3},{5,4},{6,5},{7,6},{8,7},{9,8},{10,9},{11,1... | collective-permute-start | bytes 430088 | tf_op jit(solution)/shard_map/ppermute | solution.py:146
  24.7 2.8 %collective-permute-done.33 = f32[7,20,2,128]{3,2,1,0:T(2,128)S(1)} collective-permute-done((f32[7,20,2,128]{3,2,1,0:T(2,128)S(1)}, f32[7,20,2,128]{3,2,1,0:T(2,128)S(1)}, u32[]{:S(2)}, u32[]{:S(2)}) %collective-permute-start.33) | collective-permute-done | bytes 143392 | tf_op jit(solution)/shard_map/ppermute | solution.py:145
  27.5 0.3 pad_maximum_fusion
  27.8 0.2 fusion.30
  28.0 0.2 fusion.52
  28.2 0.2 fusion.14
  28.4 0.6 fusion.11
  29.1 0.3 constant_dynamic-update-slice_fusion.4
  29.7 0.3 fusion.53
  30.1 1.1 %copy-done.2 = f32[7,16,16,128]{3,2,1,0:T(8,128)S(1)} copy-done((f32[7,16,16,128]{3,2,1,0:T(8,128)S(1)}, f32[7,16,16,128]{3,2,1,0:T(8,128)}, u32[]{:S(2)}) %copy-start.2) | copy-done | bytes 917528
  31.2 0.7 fusion.9
  31.9 0.2 slice_add_fusion.2
  32.2 1.1 %pad_maximum_fusion.1 = f32[8,16,16,128]{3,2,0,1:T(8,128)} fusion(f32[1,16,16,128]{3,2,0,1:T(8,128)S(1)} %fusion.33, f32[1,16,16,128]{3,2,0,1:T(8,128)S(1)} %bitcast.90, f32[3,16,16,128]{3,2,1,0:T(8,128)S(1)} %get-tuple-element.52, f32[3,16,16,128]{3,2,1,0:T(8,128)S(1)} %get-tuple-element.53), kind=kLoop, calls=%fused_computation.17 | loop fusion | flops 786432 | bytes 2097152 | tf_op jit(solution)/shard_map/concatenate | solution.py:190
  33.3 6.0 %all-to-all-start = ((f32[128,16,128]{2,1,0:T(8,128)}), f32[128,16,128]{2,1,0:T(8,128)S(1)}, u32[]{:S(2)}, u32[]{:S(2)}) async-start(f32[128,16,128]{2,1,0:T(8,128)} %bitcast.22), calls=%async_computation | async-start | bytes 2097152 | tf_op jit(solution)/shard_map/all_to_all | solution.py:155
  39.3 0.6 gather_fusion
  40.0 0.6 gather_fusion.1
  40.7 21.5 %all-to-all-done = f32[128,16,128]{2,1,0:T(8,128)S(1)} async-done(((f32[128,16,128]{2,1,0:T(8,128)}), f32[128,16,128]{2,1,0:T(8,128)S(1)}, u32[]{:S(2)}, u32[]{:S(2)}) %all-to-all-start) | async-done | bytes 1048608 | tf_op jit(solution)/shard_map/all_to_all | solution.py:155
  62.3 0.5 fusion.2
  62.8 0.6 fusion.6
  63.5 31.5 %all_to_all.10 = f32[128,16,128]{2,1,0:T(8,128)S(1)} all-to-all(f32[128,16,128]{2,1,0:T(8,128)S(1)} %bitcast.87), channel_id=1, replica_groups=mesh['rad'=2,'az'=16] {'az'}, dimensions={0} | all-to-all | bytes 2097152 | tf_op jit(solution)/shard_map/all_to_all | solution.py:182
  95.1 0.7 slice_bitcast_fusion
  95.8 1.0 %copy.32 = f32[7,16,16,128]{3,2,1,0:T(8,128)} copy(f32[7,16,16,128]{3,2,0,1:T(8,128)S(1)} %slice.449) | data formatting | bytes 1835008
  (43 shorter events, 1.4 us)
Async XLA Ops:
  0.6 38.7 %copy-start = (s32[16]{0:T(128)S(1)}, s32[16]{0:T(128)}, u32[]{:S(2)}) copy-start(s32[16]{0:T(128)} %param.26) | copy-start | bytes 196
  0.6 18.2 %copy-start.4 = (f32[10]{0:T(128)S(1)}, f32[10]{0:T(128)}, u32[]{:S(2)}) copy-start(f32[10]{0:T(128)} %constant.118) | copy-start | bytes 124
  0.7 18.2 %copy-start.5 = (f32[10]{0:T(128)S(1)}, f32[10]{0:T(128)}, u32[]{:S(2)}) copy-start(f32[10]{0:T(128)} %constant.119) | copy-start | bytes 124
  2.3 16.6 %collective-permute-start.32 = (f32[10,16,128]{2,1,0:T(8,128)S(1)}, f32[10,16,128]{2,1,0:T(8,128)S(1)}, u32[]{:S(2)}, u32[]{:S(2)}) collective-permute-start(f32[10,16,128]{2,1,0:T(8,128)S(1)} %get-tuple-element.66), channel_id=1, source_target_pairs={{0,16},{16,0},{1,17},{17,1},{2,18},{18,2},{3,19},{19,3},{4,20},{20... | collective-permute-start | bytes 245768 | tf_op jit(solution)/shard_map/ppermute | solution.py:112
  6.0 7.6 %collective-permute-start.2 = (f32[10,16,128]{2,1,0:T(8,128)S(1)}, f32[10,16,128]{2,1,0:T(8,128)}, u32[]{:S(2)}, u32[]{:S(2)}) collective-permute-start(f32[10,16,128]{2,1,0:T(8,128)S(1)} %param.1), channel_id=1, source_target_pairs={{16,1},{17,2},{18,3},{19,4},{20,5},{21,6},{22,7},{23,8},{24,9},{25... | collective-permute-start | bytes 245768 | tf_op jit(solution)/shard_map/cond/branch_1_fun/ppermute | solution.py:101
  9.7 8.1 %collective-permute-start.3 = (f32[10,16,128]{2,1,0:T(8,128)S(1)}, f32[10,16,128]{2,1,0:T(8,128)}, u32[]{:S(2)}, u32[]{:S(2)}) collective-permute-start(f32[10,16,128]{2,1,0:T(8,128)S(1)} %param.1), channel_id=1, source_target_pairs={{16,2},{17,3},{18,4},{19,5},{20,6},{21,7},{22,8},{23,9},{24,10},{2... | collective-permute-start | bytes 245768 | tf_op jit(solution)/shard_map/cond/branch_1_fun/ppermute | solution.py:101
  18.8 1.2 %slice-start = ((f32[7,16,16,128]{3,2,1,0:T(8,128)}), f32[6,16,16,128]{3,2,1,0:T(8,128)S(1)}, s32[]{:S(2)}) async-start(f32[7,16,16,128]{3,2,1,0:T(8,128)} %param.24), calls=%async_computation.2 | async-start | bytes 1572864 | tf_op jit(solution)/shard_map/slice | solution.py:132
  18.8 1.2 %copy-start.3 = (f32[16,16,128]{2,1,0:T(8,128)S(1)}, f32[16,16,128]{2,1,0:T(8,128)}, u32[]{:S(2)}) copy-start(f32[16,16,128]{2,1,0:T(8,128)} %param.25) | copy-start | bytes 393220
  20.2 7.3 %collective-permute-start.33 = (f32[7,20,2,128]{3,2,1,0:T(2,128)S(1)}, f32[7,20,2,128]{3,2,1,0:T(2,128)S(1)}, u32[]{:S(2)}, u32[]{:S(2)}) collective-permute-start(f32[7,20,2,128]{3,2,1,0:T(2,128)S(1)} %get-tuple-element.48), channel_id=1, source_target_pairs={{0,1},{1,2},{2,3},{3,4},{4,5},{5,6},{6,7},{7,8},{8,9},{9,10},{10,1... | collective-permute-start | bytes 430088 | tf_op jit(solution)/shard_map/ppermute | solution.py:145
  20.3 7.2 %collective-permute-start.34 = (f32[7,20,2,128]{3,2,1,0:T(2,128)S(1)}, f32[7,20,2,128]{3,2,1,0:T(2,128)S(1)}, u32[]{:S(2)}, u32[]{:S(2)}) collective-permute-start(f32[7,20,2,128]{3,2,1,0:T(2,128)S(1)} %get-tuple-element.49), channel_id=1, source_target_pairs={{1,0},{2,1},{3,2},{4,3},{5,4},{6,5},{7,6},{8,7},{9,8},{10,9},{11,1... | collective-permute-start | bytes 430088 | tf_op jit(solution)/shard_map/ppermute | solution.py:146
  30.0 1.2 %copy-start.2 = (f32[7,16,16,128]{3,2,1,0:T(8,128)S(1)}, f32[7,16,16,128]{3,2,1,0:T(8,128)}, u32[]{:S(2)}) copy-start(f32[7,16,16,128]{3,2,1,0:T(8,128)} %param.24) | copy-start | bytes 2752516
  33.3 6.7 %copy-start.1 = (s32[16]{0:T(128)S(1)}, s32[16]{0:T(128)}, u32[]{:S(2)}) copy-start(s32[16]{0:T(128)} %param.27) | copy-start | bytes 196
  33.3 28.9 %all-to-all-start = ((f32[128,16,128]{2,1,0:T(8,128)}), f32[128,16,128]{2,1,0:T(8,128)S(1)}, u32[]{:S(2)}, u32[]{:S(2)}) async-start(f32[128,16,128]{2,1,0:T(8,128)} %bitcast.22), calls=%async_computation | async-start | bytes 2097152 | tf_op jit(solution)/shard_map/all_to_all | solution.py:155

commit v2 on v1

--- a/solution.py
+++ b/solution.py
@@ -147,15 +147,18 @@
     return jnp.concatenate([before, tall, after], axis=2)
 
 
-def remap(updated, shift_int, frac_num):
-    quantities, columns, az_cells, depth = updated.shape
+def gather_columns(block):
+    quantities, columns, az_cells, depth = block.shape
     azimuths = lax.axis_size("az")
     share = quantities * columns // azimuths
-    pieces = updated.transpose(1, 0, 2, 3).reshape(azimuths * share, az_cells, depth)
+    pieces = block.transpose(1, 0, 2, 3).reshape(azimuths * share, az_cells, depth)
     gathered = lax.all_to_all(pieces, "az", 0, 0, tiled=True)
-    total = azimuths * az_cells
     whole = gathered.reshape(azimuths, share, az_cells, depth).transpose(1, 0, 2, 3)
-    whole = whole.reshape(share, total, depth)
+    return whole.reshape(share, azimuths * az_cells, depth)
+
+
+def move_columns(whole, quantities, shift_int, frac_num):
+    share, total, _ = whole.shape
     mine = (lax.axis_index("az") * share + jnp.arange(share)) // quantities
     amounts = jnp.take(shift_int, mine)
     fractions = jnp.take(frac_num, mine).astype(jnp.float32) / FRAC_DEN
@@ -170,34 +173,45 @@
         )
     else:
         around = jax.vmap(move)(doubled, amounts)
-    moved = fromm_blend(
+    return fromm_blend(
         around[:, 0:total],
         around[:, 1 : total + 1],
         around[:, 2 : total + 2],
         around[:, 3 : total + 3],
         fractions[:, None, None],
     )
+
+
+def return_columns(moved, quantities, columns):
+    share, total, depth = moved.shape
+    azimuths = lax.axis_size("az")
+    az_cells = total // azimuths
     back = moved.reshape(share, azimuths, az_cells, depth).transpose(1, 0, 2, 3)
     back = back.reshape(azimuths * share, az_cells, depth)
     result = lax.all_to_all(back, "az", 0, 0, tiled=True)
     return result.reshape(columns, quantities, az_cells, depth).transpose(1, 0, 2, 3)
 
 
+def remap(block, shift_int, frac_num):
+    whole = gather_columns(block)
+    moved = move_columns(whole, block.shape[0], shift_int, frac_num)
+    return return_columns(moved, block.shape[0], block.shape[1])
+
+
 def local(fields, density, shift_int, frac_num, boundary_shift):
+    still = remap(jnp.concatenate([density[None], fields[3:6]], axis=0), shift_int, frac_num)
     padded = widen(fields, density, boundary_shift[0])
     tensor, heating = field_stress(padded)
     force_terms = divergence(tensor)
     updated = jnp.concatenate(
         [
-            density[None],
             fields[0:3] + force_terms / density,
-            fields[3:6],
             (fields[6] + heating[1:-1, 1:-1])[None],
         ],
         axis=0,
     )
     result = remap(updated, shift_int, frac_num)
-    return (result[1:], result[0])
+    return (jnp.concatenate([result[0:3], still[1:4], result[3:4]], axis=0), still[0])
 
 
 def solution(mesh):

time: 97.2 us -> 111 us (1.14)
  blocking collectives: 31.5 us -> 0 us
  waiting for transfers between devices: 30.9 us -> 62.3 us
  starting transfers between devices: 18.7 us -> 30.8 us
  local copies, waits for them, and re-layouts: 7.6 us -> 9.18 us
    all_to_all x1 -> x4, waiting for transfers between devices: 21.5 us -> 54.6 us  [the longest x2 28 us: return_columns(): result = lax.all_to_all(back, 'az', 0, 0, tiled=True)]
    all_to_all x1 -> x0, blocking collectives: 31.5 us -> none  [remap(): result = lax.all_to_all(back, 'az', 0, 0, tiled=True)]
    all_to_all x1 -> x4, starting transfers between devices: 5.95 us -> 18 us  [the longest x2 9.81 us: gather_columns(): gathered = lax.all_to_all(pieces, 'az', 0, 0, tiled=True)]
    ppermute x2, waiting for transfers between devices: 6.65 us -> 4.79 us  [wrap(): return lax.ppermute(data, ('rad', 'az'), pairs)]
    reshape x2 -> x3, local copies, waits for them, and re-layouts: 0.19 us -> 1.76 us  [the longest x2 1.72 us: return_columns(): back = moved.reshape(share, azimuths, az_cells, depth).transpose(1, 0, 2, 3)]
    concatenate x2 -> x4, other arithmetic: 1.62 us -> 2.27 us  [the longest x1 0.87 us: local(): jnp.concatenate([fields[0:3] + force_terms / density, (fields[6] + heatin...]
  transfers between devices with their start and end apart: 6 -> 9, of which waited for: 4 -> 7; matrix products, arithmetic and copies ran while one was open for 2% -> 4% of each run, Pallas kernels for 0% -> 0%
where the time goes in v2:
time: 111 us
  waiting for transfers between devices  62.3 us (56%)
  starting transfers between devices  30.8 us (28%)
  local copies, waits for them, and re-layouts  9.18 us (8%)
  other arithmetic  6.94 us (6%)
  between operations  1.8 us (2%)
    all_to_all x2, waiting for transfers between devices, return_columns(): result = lax.all_to_all(back, 'az', 0, 0, tiled=True)  28 us
    all_to_all x2, waiting for transfers between devices, gather_columns(): gathered = lax.all_to_all(pieces, 'az', 0, 0, tiled=True)  26.6 us
    all_to_all x2, starting transfers between devices, gather_columns(): gathered = lax.all_to_all(pieces, 'az', 0, 0, tiled=True)  9.81 us
    all_to_all x2, starting transfers between devices, return_columns(): result = lax.all_to_all(back, 'az', 0, 0, tiled=True)  8.2 us
    ppermute x2, starting transfers between devices, wrap(): return lax.ppermute(data, ('rad', 'az'), pairs)  5.24 us
    ppermute x2, waiting for transfers between devices, wrap(): return lax.ppermute(data, ('rad', 'az'), pairs)  4.79 us
    ppermute x1, starting transfers between devices, widen(): lax.ppermute(head, 'az', [((i + 1) % azimuths, i) for i in range(azimuths)])  3.68 us
    ppermute x1, starting transfers between devices, radial_ghosts(): straight = lax.ppermute(other, 'rad', [(0, 1), (1, 0)])  3 us
  transfers between devices with their start and end apart: 9, of which 7 were waited for; matrix products, arithmetic and copies ran while one was open for 4% of the time, Pallas kernels for 0%

profile of v2, /device:TPU:0, one launch (start us, length us, event | category | flops | bytes accessed | tf_op | source)
XLA Modules:
  0.0 110.9 jit_solution(15740946442912362908)
XLA Ops:
  0.7 0.8 slice_bitcast_fusion.6
  1.5 0.7 fusion.64
  2.3 3.0 %collective-permute-start.32 = (f32[10,16,128]{2,1,0:T(8,128)S(1)}, f32[10,16,128]{2,1,0:T(8,128)S(1)}, u32[]{:S(2)}, u32[]{:S(2)}) collective-permute-start(f32[10,16,128]{2,1,0:T(8,128)S(1)} %get-tuple-element.66), channel_id=1, source_target_pairs={{0,16},{16,0},{1,17},{17,1},{2,18},{18,2},{3,19},{19,3},{4,20},{20... | collective-permute-start | bytes 245768 | tf_op jit(solution)/shard_map/ppermute | solution.py:112
  5.9 10.1 %conditional.1 = (f32[10,16,128]{2,1,0:T(8,128)}, f32[10,16,128]{2,1,0:T(8,128)}) conditional(s32[]{:T(128)} %clamp.3, f32[10,16,128]{2,1,0:T(8,128)S(1)} %get-tuple-element.65, f32[10,16,128]{2,1,0:T(8,128)S(1)} %get-tuple-element.65, f32[10,16,128]{2,1,0:T(8,128)S(1)} %get-tuple-element.65, ...), branch_computations={%region_0.1_spmd, %region_1.2_spmd, %region_2.3_spmd, %region_3.4_... | conditional | bytes 655456 | solution.py:117
  6.0 2.8 %collective-permute-start.6 = (f32[10,16,128]{2,1,0:T(8,128)S(1)}, f32[10,16,128]{2,1,0:T(8,128)}, u32[]{:S(2)}, u32[]{:S(2)}) collective-permute-start(f32[10,16,128]{2,1,0:T(8,128)S(1)} %param.3), channel_id=1, source_target_pairs={{16,3},{17,4},{18,5},{19,6},{20,7},{21,8},{22,9},{23,10},{24,11},{... | collective-permute-start | bytes 245768 | tf_op jit(solution)/shard_map/cond/branch_3_fun/ppermute | solution.py:101
  8.8 2.4 %collective-permute-start.7 = (f32[10,16,128]{2,1,0:T(8,128)S(1)}, f32[10,16,128]{2,1,0:T(8,128)}, u32[]{:S(2)}, u32[]{:S(2)}) collective-permute-start(f32[10,16,128]{2,1,0:T(8,128)S(1)} %param.3), channel_id=1, source_target_pairs={{16,4},{17,5},{18,6},{19,7},{20,8},{21,9},{22,10},{23,11},{24,12},... | collective-permute-start | bytes 245768 | tf_op jit(solution)/shard_map/cond/branch_3_fun/ppermute | solution.py:101
  11.2 1.5 %collective-permute-done.6 = f32[10,16,128]{2,1,0:T(8,128)} collective-permute-done((f32[10,16,128]{2,1,0:T(8,128)S(1)}, f32[10,16,128]{2,1,0:T(8,128)}, u32[]{:S(2)}, u32[]{:S(2)}) %collective-permute-start.6) | collective-permute-done | bytes 81952 | tf_op jit(solution)/shard_map/cond/branch_3_fun/ppermute | solution.py:101
  12.7 3.3 %collective-permute-done.7 = f32[10,16,128]{2,1,0:T(8,128)} collective-permute-done((f32[10,16,128]{2,1,0:T(8,128)S(1)}, f32[10,16,128]{2,1,0:T(8,128)}, u32[]{:S(2)}, u32[]{:S(2)}) %collective-permute-start.7) | collective-permute-done | bytes 81952 | tf_op jit(solution)/shard_map/cond/branch_3_fun/ppermute | solution.py:101
  16.0 0.9 broadcast_select_fusion.1
  17.2 0.9 slice-done
  18.4 0.8 collective-permute-start.33
  19.2 3.7 %collective-permute-start.34 = (f32[7,20,2,128]{3,2,1,0:T(2,128)S(1)}, f32[7,20,2,128]{3,2,1,0:T(2,128)S(1)}, u32[]{:S(2)}, u32[]{:S(2)}) collective-permute-start(f32[7,20,2,128]{3,2,1,0:T(2,128)S(1)} %get-tuple-element.49), channel_id=1, source_target_pairs={{1,0},{2,1},{3,2},{4,3},{5,4},{6,5},{7,6},{8,7},{9,8},{10,9},{11,1... | collective-permute-start | bytes 430088 | tf_op jit(solution)/shard_map/ppermute | solution.py:146
  22.9 2.9 %collective-permute-done.33 = f32[7,20,2,128]{3,2,1,0:T(2,128)S(1)} collective-permute-done((f32[7,20,2,128]{3,2,1,0:T(2,128)S(1)}, f32[7,20,2,128]{3,2,1,0:T(2,128)S(1)}, u32[]{:S(2)}, u32[]{:S(2)}) %collective-permute-start.33) | collective-permute-done | bytes 143392 | tf_op jit(solution)/shard_map/ppermute | solution.py:145
  26.7 0.6 fusion.3
  28.3 1.1 copy-done.2
  29.5 0.7 fusion.1
  30.4 0.9 pad_maximum_fusion.8
  31.3 5.7 %all-to-all-start = ((f32[64,16,128]{2,1,0:T(8,128)}), f32[64,16,128]{2,1,0:T(8,128)S(1)}, u32[]{:S(2)}, u32[]{:S(2)}) async-start(f32[64,16,128]{2,1,0:T(8,128)} %bitcast.21), calls=%async_computation | async-start | bytes 1048576 | tf_op jit(solution)/shard_map/all_to_all | solution.py:155
  37.0 0.9 pad_maximum_fusion.9
  37.9 13.6 %all-to-all-done = f32[64,16,128]{2,1,0:T(8,128)S(1)} async-done(((f32[64,16,128]{2,1,0:T(8,128)}), f32[64,16,128]{2,1,0:T(8,128)S(1)}, u32[]{:S(2)}, u32[]{:S(2)}) %all-to-all-start) | async-done | bytes 524320 | tf_op jit(solution)/shard_map/all_to_all | solution.py:155
  51.5 4.1 %all-to-all-start.2 = ((f32[64,16,128]{2,1,0:T(8,128)}), f32[64,16,128]{2,1,0:T(8,128)S(1)}, u32[]{:S(2)}, u32[]{:S(2)}) async-start(f32[64,16,128]{2,1,0:T(8,128)} %bitcast.34), calls=%async_computation.2 | async-start | bytes 1048576 | tf_op jit(solution)/shard_map/all_to_all | solution.py:155
  55.6 0.6 gather_fusion
  56.4 0.6 gather_fusion.1
  57.1 13.0 %all-to-all-done.2 = f32[64,16,128]{2,1,0:T(8,128)S(1)} async-done(((f32[64,16,128]{2,1,0:T(8,128)}), f32[64,16,128]{2,1,0:T(8,128)S(1)}, u32[]{:S(2)}, u32[]{:S(2)}) %all-to-all-start.2) | async-done | bytes 524320 | tf_op jit(solution)/shard_map/all_to_all | solution.py:155
  71.2 0.8 copy.29
  72.0 4.1 %all-to-all-start.1 = ((f32[64,16,128]{2,1,0:T(8,128)}), f32[64,16,128]{2,1,0:T(8,128)S(1)}, u32[]{:S(2)}, u32[]{:S(2)}) async-start(f32[64,16,128]{2,1,0:T(8,128)} %bitcast.29), calls=%async_computation.1 | async-start | bytes 1048576 | tf_op jit(solution)/shard_map/all_to_all | solution.py:191
  76.1 0.9 copy.33
  77.0 13.6 %all-to-all-done.1 = f32[64,16,128]{2,1,0:T(8,128)S(1)} async-done(((f32[64,16,128]{2,1,0:T(8,128)}), f32[64,16,128]{2,1,0:T(8,128)S(1)}, u32[]{:S(2)}, u32[]{:S(2)}) %all-to-all-start.1) | async-done | bytes 524320 | tf_op jit(solution)/shard_map/all_to_all | solution.py:191
  90.6 4.1 %all-to-all-start.3 = ((f32[64,16,128]{2,1,0:T(8,128)}), f32[64,16,128]{2,1,0:T(8,128)S(1)}, u32[]{:S(2)}, u32[]{:S(2)}) async-start(f32[64,16,128]{2,1,0:T(8,128)} %bitcast.40), calls=%async_computation.3 | async-start | bytes 1048576 | tf_op jit(solution)/shard_map/all_to_all | solution.py:191
  94.8 14.4 %all-to-all-done.3 = f32[64,16,128]{2,1,0:T(8,128)S(1)} async-done(((f32[64,16,128]{2,1,0:T(8,128)}), f32[64,16,128]{2,1,0:T(8,128)S(1)}, u32[]{:S(2)}, u32[]{:S(2)}) %all-to-all-start.3) | async-done | bytes 524320 | tf_op jit(solution)/shard_map/all_to_all | solution.py:191
  109.2 0.7 slice_bitcast_fusion
  109.9 1.0 copy.34
  (58 shorter events, 3.9 us)
Async XLA Ops:
  0.6 55.0 %copy-start = (s32[16]{0:T(128)S(1)}, s32[16]{0:T(128)}, u32[]{:S(2)}) copy-start(s32[16]{0:T(128)} %param.26) | copy-start | bytes 196
  0.6 16.4 %copy-start.4 = (f32[10]{0:T(128)S(1)}, f32[10]{0:T(128)}, u32[]{:S(2)}) copy-start(f32[10]{0:T(128)} %constant.121) | copy-start | bytes 124
  0.7 16.4 %copy-start.5 = (f32[10]{0:T(128)S(1)}, f32[10]{0:T(128)}, u32[]{:S(2)}) copy-start(f32[10]{0:T(128)} %constant.122) | copy-start | bytes 124
  2.3 14.7 %collective-permute-start.32 = (f32[10,16,128]{2,1,0:T(8,128)S(1)}, f32[10,16,128]{2,1,0:T(8,128)S(1)}, u32[]{:S(2)}, u32[]{:S(2)}) collective-permute-start(f32[10,16,128]{2,1,0:T(8,128)S(1)} %get-tuple-element.66), channel_id=1, source_target_pairs={{0,16},{16,0},{1,17},{17,1},{2,18},{18,2},{3,19},{19,3},{4,20},{20... | collective-permute-start | bytes 245768 | tf_op jit(solution)/shard_map/ppermute | solution.py:112
  6.0 6.7 %collective-permute-start.6 = (f32[10,16,128]{2,1,0:T(8,128)S(1)}, f32[10,16,128]{2,1,0:T(8,128)}, u32[]{:S(2)}, u32[]{:S(2)}) collective-permute-start(f32[10,16,128]{2,1,0:T(8,128)S(1)} %param.3), channel_id=1, source_target_pairs={{16,3},{17,4},{18,5},{19,6},{20,7},{21,8},{22,9},{23,10},{24,11},{... | collective-permute-start | bytes 245768 | tf_op jit(solution)/shard_map/cond/branch_3_fun/ppermute | solution.py:101
  8.8 7.2 %collective-permute-start.7 = (f32[10,16,128]{2,1,0:T(8,128)S(1)}, f32[10,16,128]{2,1,0:T(8,128)}, u32[]{:S(2)}, u32[]{:S(2)}) collective-permute-start(f32[10,16,128]{2,1,0:T(8,128)S(1)} %param.3), channel_id=1, source_target_pairs={{16,4},{17,5},{18,6},{19,7},{20,8},{21,9},{22,10},{23,11},{24,12},... | collective-permute-start | bytes 245768 | tf_op jit(solution)/shard_map/cond/branch_3_fun/ppermute | solution.py:101
  17.0 1.2 %slice-start = ((f32[7,16,16,128]{3,2,1,0:T(8,128)}), f32[6,16,16,128]{3,2,1,0:T(8,128)S(1)}, s32[]{:S(2)}) async-start(f32[7,16,16,128]{3,2,1,0:T(8,128)} %param.24), calls=%async_computation.4 | async-start | bytes 1572864 | tf_op jit(solution)/shard_map/slice | solution.py:132
  17.0 1.2 %copy-start.3 = (f32[16,16,128]{2,1,0:T(8,128)S(1)}, f32[16,16,128]{2,1,0:T(8,128)}, u32[]{:S(2)}) copy-start(f32[16,16,128]{2,1,0:T(8,128)} %param.25) | copy-start | bytes 393220
  18.4 7.4 %collective-permute-start.33 = (f32[7,20,2,128]{3,2,1,0:T(2,128)S(1)}, f32[7,20,2,128]{3,2,1,0:T(2,128)S(1)}, u32[]{:S(2)}, u32[]{:S(2)}) collective-permute-start(f32[7,20,2,128]{3,2,1,0:T(2,128)S(1)} %get-tuple-element.48), channel_id=1, source_target_pairs={{0,1},{1,2},{2,3},{3,4},{4,5},{5,6},{6,7},{7,8},{8,9},{9,10},{10,1... | collective-permute-start | bytes 430088 | tf_op jit(solution)/shard_map/ppermute | solution.py:145
  19.2 6.6 %collective-permute-start.34 = (f32[7,20,2,128]{3,2,1,0:T(2,128)S(1)}, f32[7,20,2,128]{3,2,1,0:T(2,128)S(1)}, u32[]{:S(2)}, u32[]{:S(2)}) collective-permute-start(f32[7,20,2,128]{3,2,1,0:T(2,128)S(1)} %get-tuple-element.49), channel_id=1, source_target_pairs={{1,0},{2,1},{3,2},{4,3},{5,4},{6,5},{7,6},{8,7},{9,8},{10,9},{11,1... | collective-permute-start | bytes 430088 | tf_op jit(solution)/shard_map/ppermute | solution.py:146
  28.2 1.2 %copy-start.2 = (f32[7,16,16,128]{3,2,1,0:T(8,128)S(1)}, f32[7,16,16,128]{3,2,1,0:T(8,128)}, u32[]{:S(2)}) copy-start(f32[7,16,16,128]{3,2,1,0:T(8,128)} %param.24) | copy-start | bytes 2752516
  31.3 20.2 %all-to-all-start = ((f32[64,16,128]{2,1,0:T(8,128)}), f32[64,16,128]{2,1,0:T(8,128)S(1)}, u32[]{:S(2)}, u32[]{:S(2)}) async-start(f32[64,16,128]{2,1,0:T(8,128)} %bitcast.21), calls=%async_computation | async-start | bytes 1048576 | tf_op jit(solution)/shard_map/all_to_all | solution.py:155
  37.0 19.3 %copy-start.1 = (s32[16]{0:T(128)S(1)}, s32[16]{0:T(128)}, u32[]{:S(2)}) copy-start(s32[16]{0:T(128)} %param.27) | copy-start | bytes 196
  51.5 18.6 %all-to-all-start.2 = ((f32[64,16,128]{2,1,0:T(8,128)}), f32[64,16,128]{2,1,0:T(8,128)S(1)}, u32[]{:S(2)}, u32[]{:S(2)}) async-start(f32[64,16,128]{2,1,0:T(8,128)} %bitcast.34), calls=%async_computation.2 | async-start | bytes 1048576 | tf_op jit(solution)/shard_map/all_to_all | solution.py:155
  72.0 18.6 %all-to-all-start.1 = ((f32[64,16,128]{2,1,0:T(8,128)}), f32[64,16,128]{2,1,0:T(8,128)S(1)}, u32[]{:S(2)}, u32[]{:S(2)}) async-start(f32[64,16,128]{2,1,0:T(8,128)} %bitcast.29), calls=%async_computation.1 | async-start | bytes 1048576 | tf_op jit(solution)/shard_map/all_to_all | solution.py:191
  90.6 18.6 %all-to-all-start.3 = ((f32[64,16,128]{2,1,0:T(8,128)}), f32[64,16,128]{2,1,0:T(8,128)S(1)}, u32[]{:S(2)}, u32[]{:S(2)}) async-start(f32[64,16,128]{2,1,0:T(8,128)} %bitcast.40), calls=%async_computation.3 | async-start | bytes 1048576 | tf_op jit(solution)/shard_map/all_to_all | solution.py:191

commit v3 on v1

--- a/solution.py
+++ b/solution.py
@@ -74,7 +74,7 @@
     )
 
 
-def radial_ghosts(density, velocity, magnet, shear_cells):
+def radial_ghosts(density, velocity, magnet, shear_cells, pieces):
     az_cells = density.shape[1]
     radials = lax.axis_size("rad")
     azimuths = lax.axis_size("az")
@@ -101,20 +101,29 @@
         return lax.ppermute(data, ("rad", "az"), pairs)
 
     def branch(steps):
-        def run(data):
-            return wrap(data, steps), wrap(data, steps + 1)
+        def run(data, other, pieces):
+            return (
+                wrap(data, steps),
+                wrap(data, steps + 1),
+                straight_of(other),
+                lax.all_to_all(pieces, "az", 0, 0, tiled=True),
+            )
 
         return run
 
+    def straight_of(other):
+        if radials == 2:
+            return (lax.ppermute(other[0], "rad", [(0, 1), (1, 0)]),) * 2
+        return (
+            lax.ppermute(other[0], "rad", [(i, i + 1) for i in range(last)]),
+            lax.ppermute(other[1], "rad", [(i + 1, i) for i in range(last)]),
+        )
+
     edge = jnp.where(me == 0, low, high)
-    if radials == 2:
-        other = jnp.where(me == 0, high, low)
-        straight = lax.ppermute(other, "rad", [(0, 1), (1, 0)])
-        from_below = from_above = straight
-    else:
-        from_below = lax.ppermute(high, "rad", [(i, i + 1) for i in range(last)])
-        from_above = lax.ppermute(low, "rad", [(i + 1, i) for i in range(last)])
-    whole, next_one = lax.switch(blocks, [branch(k) for k in range(azimuths)], edge)
+    other = (jnp.where(me == 0, high, low),) if radials == 2 else (high, low)
+    whole, next_one, (from_below, from_above), gathered = lax.switch(
+        blocks, [branch(k) for k in range(azimuths)], edge, other, pieces
+    )
     joined = jnp.concatenate(
         [jnp.where(me == 0, next_one, whole), jnp.where(me == 0, whole, next_one)], axis=1
     )
@@ -123,12 +132,12 @@
     marker = jnp.zeros((10, 1, 1), jnp.float32).at[jnp.array([1, 8])].set(shear_jump)
     below = jnp.where(me == 0, sheared + marker, from_below)
     above = jnp.where(me == last, sheared - marker, from_above)
-    return below, above
-
-
-def widen(fields, density, shear_cells):
+    return below, above, gathered
+
+
+def widen(fields, density, shear_cells, pieces):
     velocity, magnet = fields[0:3], fields[3:6]
-    below, above = radial_ghosts(density, velocity, magnet, shear_cells)
+    below, above, gathered = radial_ghosts(density, velocity, magnet, shear_cells, pieces)
     stacked = jnp.concatenate([density[None], fields[:6]], axis=0)
 
     def nearest(strip):
@@ -144,18 +153,19 @@
     head, tail = tall[:, :, :2], tall[:, :, -2:]
     before = lax.ppermute(tail, "az", [(i, (i + 1) % azimuths) for i in range(azimuths)])
     after = lax.ppermute(head, "az", [((i + 1) % azimuths, i) for i in range(azimuths)])
-    return jnp.concatenate([before, tall, after], axis=2)
-
-
-def remap(updated, shift_int, frac_num):
-    quantities, columns, az_cells, depth = updated.shape
+    return jnp.concatenate([before, tall, after], axis=2), gathered
+
+
+def cut_columns(block):
+    quantities, columns, az_cells, depth = block.shape
     azimuths = lax.axis_size("az")
-    share = quantities * columns // azimuths
-    pieces = updated.transpose(1, 0, 2, 3).reshape(azimuths * share, az_cells, depth)
-    gathered = lax.all_to_all(pieces, "az", 0, 0, tiled=True)
+    return block.transpose(1, 0, 2, 3).reshape(azimuths, -1, az_cells, depth)
+
+
+def move_columns(gathered, quantities, shift_int, frac_num):
+    azimuths, share, az_cells, depth = gathered.shape
     total = azimuths * az_cells
-    whole = gathered.reshape(azimuths, share, az_cells, depth).transpose(1, 0, 2, 3)
-    whole = whole.reshape(share, total, depth)
+    whole = gathered.transpose(1, 0, 2, 3).reshape(share, total, depth)
     mine = (lax.axis_index("az") * share + jnp.arange(share)) // quantities
     amounts = jnp.take(shift_int, mine)
     fractions = jnp.take(frac_num, mine).astype(jnp.float32) / FRAC_DEN
@@ -177,27 +187,34 @@
         around[:, 3 : total + 3],
         fractions[:, None, None],
     )
-    back = moved.reshape(share, azimuths, az_cells, depth).transpose(1, 0, 2, 3)
-    back = back.reshape(azimuths * share, az_cells, depth)
-    result = lax.all_to_all(back, "az", 0, 0, tiled=True)
-    return result.reshape(columns, quantities, az_cells, depth).transpose(1, 0, 2, 3)
+    return moved.reshape(share, azimuths, az_cells, depth).transpose(1, 0, 2, 3)
+
+
+def join_columns(returned, quantities):
+    azimuths, share, az_cells, depth = returned.shape
+    return returned.reshape(-1, quantities, az_cells, depth).transpose(1, 0, 2, 3)
 
 
 def local(fields, density, shift_int, frac_num, boundary_shift):
-    padded = widen(fields, density, boundary_shift[0])
+    still = jnp.concatenate([density[None], fields[3:6]], axis=0)
+    padded, gathered = widen(fields, density, boundary_shift[0], cut_columns(still))
+    still_moved = move_columns(gathered, 4, shift_int, frac_num)
     tensor, heating = field_stress(padded)
     force_terms = divergence(tensor)
     updated = jnp.concatenate(
         [
-            density[None],
             fields[0:3] + force_terms / density,
-            fields[3:6],
             (fields[6] + heating[1:-1, 1:-1])[None],
         ],
         axis=0,
     )
-    result = remap(updated, shift_int, frac_num)
-    return (result[1:], result[0])
+    share = still_moved.shape[1]
+    both = jnp.concatenate([cut_columns(updated), still_moved], axis=1)
+    both = lax.all_to_all(both, "az", 0, 0, tiled=True)
+    still = join_columns(both[:, share:], 4)
+    updated_moved = move_columns(both[:, :share], 4, shift_int, frac_num)
+    result = join_columns(lax.all_to_all(updated_moved, "az", 0, 0, tiled=True), 4)
+    return (jnp.concatenate([result[0:3], still[1:4], result[3:4]], axis=0), still[0])
 
 
 def solution(mesh):

time: 97.2 us -> 100 us (1.029)
  starting transfers between devices: 18.7 us -> 29.6 us
  waiting for transfers between devices: 30.9 us -> 20.9 us
  local copies, waits for them, and re-layouts: 7.6 us -> 10.4 us
  blocking collectives: 31.5 us -> 30 us
  other arithmetic: 6.29 us -> 7.3 us
    all_to_all x1 -> x2, waiting for transfers between devices: 21.5 us -> 14.4 us  [the longest x1 13.8 us: local(): lax.all_to_all(updated_moved, 'az', 0, 0, tiled=True)]
    ppermute x1, starting transfers between devices: 0.06 us -> 6.88 us  [widen(): lax.ppermute(tail, 'az', [(i, (i + 1) % azimuths) for i in range(azimuths)])]
    all_to_all x1 -> x2, starting transfers between devices: 5.95 us -> 12.4 us  [the longest x1 7.45 us: run(): lax.all_to_all(pieces, 'az', 0, 0, tiled=True)]
    ppermute x1, waiting for transfers between devices: 2.78 us -> 0.01 us  [widen(): lax.ppermute(tail, 'az', [(i, (i + 1) % azimuths) for i in range(azimuths)])]
    transpose x0 -> x2, other arithmetic: none -> 2.05 us  [cut_columns(): return block.transpose(1, 0, 2, 3).reshape(azimuths, -1, az_cells, depth)]
    cond x0 -> x2, local copies, waits for them, and re-layouts: none -> 1.97 us  [the longest x1 1.08 us: radial_ghosts(): lax.switch(blocks, [branch(k) for k in range(azimuths)], edge, other, pie...]
    all_to_all x1, blocking collectives: 31.5 us -> 30 us  [local(): both = lax.all_to_all(both, 'az', 0, 0, tiled=True)]
    ppermute x1, starting transfers between devices: 3 us -> 1.56 us  [straight_of(): return (lax.ppermute(other[0], 'rad', [(0, 1), (1, 0)]),) * 2]
  transfers between devices with their start and end apart: 6 -> 7, of which waited for: 4 -> 4; matrix products, arithmetic and copies ran while one was open for 2% -> 5% of each run, Pallas kernels for 0% -> 0%
where the time goes in v3:
time: 100 us
  blocking collectives  30 us (30%)
  starting transfers between devices  29.6 us (30%)
  waiting for transfers between devices  20.9 us (21%)
  local copies, waits for them, and re-layouts  10.4 us (10%)
  other arithmetic  7.3 us (7%)
  between operations  1.81 us (2%)
    all_to_all x1, blocking collectives, local(): both = lax.all_to_all(both, 'az', 0, 0, tiled=True)  30 us
    all_to_all x1, waiting for transfers between devices, local(): lax.all_to_all(updated_moved, 'az', 0, 0, tiled=True)  13.8 us
    all_to_all x1, starting transfers between devices, run(): lax.all_to_all(pieces, 'az', 0, 0, tiled=True)  7.45 us
    ppermute x1, starting transfers between devices, widen(): lax.ppermute(tail, 'az', [(i, (i + 1) % azimuths) for i in range(azimuths)])  6.88 us
    ppermute x2, waiting for transfers between devices, wrap(): return lax.ppermute(data, ('rad', 'az'), pairs)  6.44 us
    ppermute x2, starting transfers between devices, wrap(): return lax.ppermute(data, ('rad', 'az'), pairs)  5.45 us
    all_to_all x1, starting transfers between devices, local(): lax.all_to_all(updated_moved, 'az', 0, 0, tiled=True)  4.99 us
    ppermute x1, starting transfers between devices, widen(): lax.ppermute(head, 'az', [((i + 1) % azimuths, i) for i in range(azimuths)])  3.33 us
  transfers between devices with their start and end apart: 7, of which 4 were waited for; matrix products, arithmetic and copies ran while one was open for 5% of the time, Pallas kernels for 0%

profile of v3, /device:TPU:0, one launch (start us, length us, event | category | flops | bytes accessed | tf_op | source)
XLA Modules:
  0.0 100.1 jit_solution(14081687305583499500)
XLA Ops:
  1.3 0.8 slice_bitcast_fusion.8
  2.2 0.7 fusion.63
  2.9 2.0 %maximum_bitcast_fusion = f32[16,4,16,128]{3,2,1,0:T(8,128)} fusion(f32[1,16,16,128]{3,2,0,1:T(8,128)} %bitcast.99, f32[7,16,16,128]{3,2,1,0:T(8,128)} %param.24), kind=kLoop, calls=%fused_computation.51 | loop fusion | flops 131072 | bytes 1048576 | tf_op jit(solution)/shard_map/transpose | solution.py:162
  4.9 22.5 %conditional.1 = (f32[10,16,128]{2,1,0:T(8,128)}, f32[10,16,128]{2,1,0:T(8,128)}, f32[10,16,128]{2,1,0:T(8,128)}, f32[10,16,128]{2,1,0:T(8,128)S(1)}, f32[16,4,16,128]{3,2,1,0:T(8,128)}) conditional(s32[]{:T(128)} %clamp.3, (f32[10,16,128]{2,1,0:T(8,128)S(1)}, f32[10,16,128]{2,1,0:T(8,128)S(1)}, ...), branch_computations={%region_0.1_spmd, %region_1.2_spmd, %region_2.3_spmd, %region_3.4_... | conditional | bytes 2719936 | solution.py:124
  5.0 7.4 %all-to-all-start.9 = ((f32[16,4,16,128]{3,2,1,0:T(8,128)}), f32[16,4,16,128]{3,2,1,0:T(8,128)}, u32[]{:S(2)}, u32[]{:S(2)}) async-start(f32[16,4,16,128]{3,2,1,0:T(8,128)} %get-tuple-element.126), calls=%async_computation.9 | async-start | bytes 1048576 | tf_op jit(solution)/shard_map/cond/branch_9_fun/all_to_all | solution.py:109
  12.4 1.6 %collective-permute-start.29 = (f32[10,16,128]{2,1,0:T(8,128)S(1)}, f32[10,16,128]{2,1,0:T(8,128)}, u32[]{:S(2)}, u32[]{:S(2)}) collective-permute-start(f32[10,16,128]{2,1,0:T(8,128)S(1)} %get-tuple-element.125), channel_id=1, source_target_pairs={{0,16},{16,0},{1,17},{17,1},{2,18},{18,2},{3,19},{19,3},{4,20},{20... | collective-permute-start | bytes 245768 | tf_op jit(solution)/shard_map/cond/branch_9_fun/ppermute | solution.py:116
  14.0 2.2 %collective-permute-start.27 = (f32[10,16,128]{2,1,0:T(8,128)S(1)}, f32[10,16,128]{2,1,0:T(8,128)}, u32[]{:S(2)}, u32[]{:S(2)}) collective-permute-start(f32[10,16,128]{2,1,0:T(8,128)S(1)} %get-tuple-element.124), channel_id=1, source_target_pairs={{16,9},{17,10},{18,11},{19,12},{20,13},{21,14},{22,15},{23,0},{24,... | collective-permute-start | bytes 245768 | tf_op jit(solution)/shard_map/cond/branch_9_fun/ppermute | solution.py:101
  16.1 3.3 %collective-permute-start.28 = (f32[10,16,128]{2,1,0:T(8,128)S(1)}, f32[10,16,128]{2,1,0:T(8,128)}, u32[]{:S(2)}, u32[]{:S(2)}) collective-permute-start(f32[10,16,128]{2,1,0:T(8,128)S(1)} %get-tuple-element.124), channel_id=1, source_target_pairs={{16,10},{17,11},{18,12},{19,13},{20,14},{21,15},{22,0},{23,1},{24,... | collective-permute-start | bytes 245768 | tf_op jit(solution)/shard_map/cond/branch_9_fun/ppermute | solution.py:101
  19.4 0.9 copy.111
  20.3 4.8 %collective-permute-done.27 = f32[10,16,128]{2,1,0:T(8,128)} collective-permute-done((f32[10,16,128]{2,1,0:T(8,128)S(1)}, f32[10,16,128]{2,1,0:T(8,128)}, u32[]{:S(2)}, u32[]{:S(2)}) %collective-permute-start.27) | collective-permute-done | bytes 81952 | tf_op jit(solution)/shard_map/cond/branch_9_fun/ppermute | solution.py:101
  25.2 1.6 %collective-permute-done.28 = f32[10,16,128]{2,1,0:T(8,128)} collective-permute-done((f32[10,16,128]{2,1,0:T(8,128)S(1)}, f32[10,16,128]{2,1,0:T(8,128)}, u32[]{:S(2)}, u32[]{:S(2)}) %collective-permute-start.28) | collective-permute-done | bytes 81952 | tf_op jit(solution)/shard_map/cond/branch_9_fun/ppermute | solution.py:101
  26.7 0.7 all-to-all-done.9
  27.4 0.9 broadcast_select_fusion.1
  28.6 1.0 slice-done
  29.8 6.9 %collective-permute-start.48 = (f32[7,20,2,128]{3,2,1,0:T(2,128)S(1)}, f32[7,20,2,128]{3,2,1,0:T(2,128)S(1)}, u32[]{:S(2)}, u32[]{:S(2)}) collective-permute-start(f32[7,20,2,128]{3,2,1,0:T(2,128)S(1)} %get-tuple-element.182), channel_id=1, source_target_pairs={{0,1},{1,2},{2,3},{3,4},{4,5},{5,6},{6,7},{7,8},{8,9},{9,10},{10,1... | collective-permute-start | bytes 430088 | tf_op jit(solution)/shard_map/ppermute | solution.py:154
  36.7 3.3 %collective-permute-start.49 = (f32[7,20,2,128]{3,2,1,0:T(2,128)S(1)}, f32[7,20,2,128]{3,2,1,0:T(2,128)S(1)}, u32[]{:S(2)}, u32[]{:S(2)}) collective-permute-start(f32[7,20,2,128]{3,2,1,0:T(2,128)S(1)} %get-tuple-element.183), channel_id=1, source_target_pairs={{1,0},{2,1},{3,2},{4,3},{5,4},{6,5},{7,6},{8,7},{9,8},{10,9},{11,1... | collective-permute-start | bytes 430088 | tf_op jit(solution)/shard_map/ppermute | solution.py:155
  40.1 0.6 gather_fusion
  40.8 1.1 %copy.43 = f32[16,4,16,128]{3,2,0,1:T(8,128)S(1)} copy(f32[16,4,16,128]{3,2,1,0:T(8,128)} %get-tuple-element.156) | data formatting | bytes 1048576 | tf_op jit(solution)/shard_map/cond | solution.py:124
  41.9 0.6 gather_fusion.1
  42.9 0.3 fusion.21
  44.1 0.6 fusion.3
  44.8 0.3 constant_dynamic-update-slice_fusion.4
  45.4 0.3 fusion.61
  45.8 1.1 %copy-done.2 = f32[7,16,16,128]{3,2,1,0:T(8,128)S(1)} copy-done((f32[7,16,16,128]{3,2,1,0:T(8,128)S(1)}, f32[7,16,16,128]{3,2,1,0:T(8,128)}, u32[]{:S(2)}) %copy-start.2) | copy-done | bytes 917528
  46.9 0.7 fusion.1
  47.9 30.0 %all_to_all.74 = f32[16,8,16,128]{3,2,1,0:T(8,128)S(1)} all-to-all(f32[16,8,16,128]{3,2,1,0:T(8,128)S(1)} %pad_maximum_fusion.1), channel_id=1, replica_groups=mesh['rad'=2,'az'=16] {'az'}, dimensions={0} | all-to-all | bytes 2097152 | tf_op jit(solution)/shard_map/all_to_all | solution.py:213
  78.4 0.3 fusion.16
  78.7 0.9 copy.61
  79.5 5.0 %all-to-all-start.17 = ((f32[16,4,16,128]{3,2,1,0:T(8,128)}), f32[16,4,16,128]{3,2,1,0:T(8,128)S(1)}, u32[]{:S(2)}, u32[]{:S(2)}) async-start(f32[16,4,16,128]{3,2,1,0:T(8,128)} %bitcast.81), calls=%async_computation.17 | async-start | bytes 1048576 | tf_op jit(solution)/shard_map/all_to_all | solution.py:216
  84.6 0.7 slice_bitcast_fusion.2
  85.2 13.8 %all-to-all-done.17 = f32[16,4,16,128]{3,2,1,0:T(8,128)S(1)} async-done(((f32[16,4,16,128]{3,2,1,0:T(8,128)}), f32[16,4,16,128]{3,2,1,0:T(8,128)S(1)}, u32[]{:S(2)}, u32[]{:S(2)}) %all-to-all-start.17) | async-done | bytes 524320 | tf_op jit(solution)/shard_map/all_to_all | solution.py:216
  99.1 1.0 %copy.47 = f32[7,16,16,128]{3,2,1,0:T(8,128)} copy(f32[7,16,16,128]{3,2,0,1:T(8,128)S(1)} %pad_maximum_fusion.2) | data formatting | bytes 1835008
  (57 shorter events, 3.0 us)
Async XLA Ops:
  0.6 39.4 %copy-start = (s32[16]{0:T(128)S(1)}, s32[16]{0:T(128)}, u32[]{:S(2)}) copy-start(s32[16]{0:T(128)} %param.26) | copy-start | bytes 196
  4.9 23.5 %copy-start.4 = (f32[10]{0:T(128)S(1)}, f32[10]{0:T(128)}, u32[]{:S(2)}) copy-start(f32[10]{0:T(128)} %constant.121) | copy-start | bytes 124
  4.9 23.5 %copy-start.5 = (f32[10]{0:T(128)S(1)}, f32[10]{0:T(128)}, u32[]{:S(2)}) copy-start(f32[10]{0:T(128)} %constant.122) | copy-start | bytes 124
  5.0 22.5 %all-to-all-start.9 = ((f32[16,4,16,128]{3,2,1,0:T(8,128)}), f32[16,4,16,128]{3,2,1,0:T(8,128)}, u32[]{:S(2)}, u32[]{:S(2)}) async-start(f32[16,4,16,128]{3,2,1,0:T(8,128)} %get-tuple-element.126), calls=%async_computation.9 | async-start | bytes 1048576 | tf_op jit(solution)/shard_map/cond/branch_9_fun/all_to_all | solution.py:109
  12.4 7.0 %collective-permute-start.29 = (f32[10,16,128]{2,1,0:T(8,128)S(1)}, f32[10,16,128]{2,1,0:T(8,128)}, u32[]{:S(2)}, u32[]{:S(2)}) collective-permute-start(f32[10,16,128]{2,1,0:T(8,128)S(1)} %get-tuple-element.125), channel_id=1, source_target_pairs={{0,16},{16,0},{1,17},{17,1},{2,18},{18,2},{3,19},{19,3},{4,20},{20... | collective-permute-start | bytes 245768 | tf_op jit(solution)/shard_map/cond/branch_9_fun/ppermute | solution.py:116
  14.0 11.2 %collective-permute-start.27 = (f32[10,16,128]{2,1,0:T(8,128)S(1)}, f32[10,16,128]{2,1,0:T(8,128)}, u32[]{:S(2)}, u32[]{:S(2)}) collective-permute-start(f32[10,16,128]{2,1,0:T(8,128)S(1)} %get-tuple-element.124), channel_id=1, source_target_pairs={{16,9},{17,10},{18,11},{19,12},{20,13},{21,14},{22,15},{23,0},{24,... | collective-permute-start | bytes 245768 | tf_op jit(solution)/shard_map/cond/branch_9_fun/ppermute | solution.py:101
  16.1 10.6 %collective-permute-start.28 = (f32[10,16,128]{2,1,0:T(8,128)S(1)}, f32[10,16,128]{2,1,0:T(8,128)}, u32[]{:S(2)}, u32[]{:S(2)}) collective-permute-start(f32[10,16,128]{2,1,0:T(8,128)S(1)} %get-tuple-element.124), channel_id=1, source_target_pairs={{16,10},{17,11},{18,12},{19,13},{20,14},{21,15},{22,0},{23,1},{24,... | collective-permute-start | bytes 245768 | tf_op jit(solution)/shard_map/cond/branch_9_fun/ppermute | solution.py:101
  28.4 1.2 %slice-start = ((f32[7,16,16,128]{3,2,1,0:T(8,128)}), f32[6,16,16,128]{3,2,1,0:T(8,128)S(1)}, s32[]{:S(2)}) async-start(f32[7,16,16,128]{3,2,1,0:T(8,128)} %param.24), calls=%async_computation.18 | async-start | bytes 1572864 | tf_op jit(solution)/shard_map/slice | solution.py:141
  28.4 1.2 %copy-start.3 = (f32[16,16,128]{2,1,0:T(8,128)S(1)}, f32[16,16,128]{2,1,0:T(8,128)}, u32[]{:S(2)}) copy-start(f32[16,16,128]{2,1,0:T(8,128)} %param.25) | copy-start | bytes 393220
  29.7 12.2 %copy-start.1 = (s32[16]{0:T(128)S(1)}, s32[16]{0:T(128)}, u32[]{:S(2)}) copy-start(s32[16]{0:T(128)} %param.27) | copy-start | bytes 196
  29.8 13.4 %collective-permute-start.48 = (f32[7,20,2,128]{3,2,1,0:T(2,128)S(1)}, f32[7,20,2,128]{3,2,1,0:T(2,128)S(1)}, u32[]{:S(2)}, u32[]{:S(2)}) collective-permute-start(f32[7,20,2,128]{3,2,1,0:T(2,128)S(1)} %get-tuple-element.182), channel_id=1, source_target_pairs={{0,1},{1,2},{2,3},{3,4},{4,5},{5,6},{6,7},{7,8},{8,9},{9,10},{10,1... | collective-permute-start | bytes 430088 | tf_op jit(solution)/shard_map/ppermute | solution.py:154
  36.7 6.5 %collective-permute-start.49 = (f32[7,20,2,128]{3,2,1,0:T(2,128)S(1)}, f32[7,20,2,128]{3,2,1,0:T(2,128)S(1)}, u32[]{:S(2)}, u32[]{:S(2)}) collective-permute-start(f32[7,20,2,128]{3,2,1,0:T(2,128)S(1)} %get-tuple-element.183), channel_id=1, source_target_pairs={{1,0},{2,1},{3,2},{4,3},{5,4},{6,5},{7,6},{8,7},{9,8},{10,9},{11,1... | collective-permute-start | bytes 430088 | tf_op jit(solution)/shard_map/ppermute | solution.py:155
  45.7 1.2 %copy-start.2 = (f32[7,16,16,128]{3,2,1,0:T(8,128)S(1)}, f32[7,16,16,128]{3,2,1,0:T(8,128)}, u32[]{:S(2)}) copy-start(f32[7,16,16,128]{3,2,1,0:T(8,128)} %param.24) | copy-start | bytes 2752516
  79.5 19.5 %all-to-all-start.17 = ((f32[16,4,16,128]{3,2,1,0:T(8,128)}), f32[16,4,16,128]{3,2,1,0:T(8,128)S(1)}, u32[]{:S(2)}, u32[]{:S(2)}) async-start(f32[16,4,16,128]{3,2,1,0:T(8,128)} %bitcast.81), calls=%async_computation.17 | async-start | bytes 1048576 | tf_op jit(solution)/shard_map/all_to_all | solution.py:216

commit v4 on v1

v4 whole, which is shorter than its diff:
```python
import functools

import jax
import jax.numpy as jnp
from jax import lax
from jax.experimental import pallas as pl
from jax.experimental.pallas import tpu as pltpu
from jax.sharding import PartitionSpec as P

FRAC_DEN = 64

shear_jump = 1.5
visc_step = 0.05
field_floor = 0.25

PACKED = 10
TOP = 8


def up_and_down(values):
    lane = lax.broadcasted_iota(jnp.int32, values.shape, values.ndim - 1)
    depth = values.shape[-1]
    up = pltpu.roll(values, depth - 1, values.ndim - 1)
    down = pltpu.roll(values, 1, values.ndim - 1)
    return jnp.where(lane == depth - 1, values, up), jnp.where(lane == 0, values, down)


def vertical_slope(values):
    up, down = up_and_down(values)
    return (up - down) * 0.5


def stress(density, magnet, grad_x, grad_y, grad_z):
    square = magnet[0] * magnet[0] + magnet[1] * magnet[1] + magnet[2] * magnet[2]
    inverse = lax.rsqrt(jnp.maximum(square, field_floor))
    unit = [component * inverse for component in magnet]
    slopes = (grad_x, grad_y, grad_z)
    aligned = None
    for direction in range(3):
        along = (
            unit[0] * slopes[direction][0]
            + unit[1] * slopes[direction][1]
            + unit[2] * slopes[direction][2]
        )
        term = unit[direction] * along
        aligned = term if aligned is None else aligned + term
    anisotropy = aligned - (grad_x[0] + grad_y[1] + grad_z[2]) * (1.0 / 3.0)
    gap = (3.0 * visc_step) * density * anisotropy
    return gap, anisotropy, unit


def stress_kernel(
    info,
    fields,
    density,
    head,
    tail,
    before,
    after,
    straight_below,
    straight_above,
    whole,
    next_one,
    out,
    joined,
    vel,
    mass,
    px,
    py,
    pzz,
    heat,
):
    columns, cells, depth = density.shape
    first, last, remainder = info[0], info[1], info[2]
    end = TOP + cells

    def place(far, near, ghost, start, jump):
        for component in range(3):
            added = jump if component == 1 else 0.0
            vel[component, near, TOP - 1 : end + 1] = (
                joined[component, pl.ds(start, cells + 2)] + added
            )
            vel[component, far, TOP:end] = joined[7 + component, pl.ds(start + 1, cells)] + added
        for row in range(4):
            mass[row, ghost] = joined[3 + row, pl.ds(start + 1, cells)]

    def lay(one, two):
        for row in range(PACKED):
            joined[row, 1 : cells + 1] = one[row]
            if two is not None:
                joined[row, cells + 1 : 2 * cells + 1] = two[row]
        final = one if two is None else two
        spot = (1 if two is None else 2) * cells + 1
        for component in range(3):
            joined[component, 0:1] = one[PACKED, 2 * component : 2 * component + 1]
            joined[component, spot : spot + 1] = final[PACKED, 2 * component + 1 : 2 * component + 2]

    below = (0, 1, 0)
    above = (columns + 3, columns + 2, columns + 1)

    @pl.when(first == 1)
    def _():
        lay(next_one, whole)
        place(*below, cells - remainder, shear_jump)

    @pl.when(first == 0)
    def _():
        lay(straight_below, None)
        place(*below, 0, 0.0)

    @pl.when(last == 1)
    def _():
        lay(whole, next_one)
        place(*above, remainder, -shear_jump)

    @pl.when(last == 0)
    def _():
        lay(straight_above, None)
        place(*above, 0, 0.0)

    vel[:, 2 : columns + 2, TOP:end] = fields[0:3]
    mass[0, 1 : columns + 1] = density[...]
    mass[1:4, 1 : columns + 1] = fields[3:6]
    for component in range(3):
        for column in range(columns):
            vel[component, 2 + column, TOP - 1 : TOP] = before[component, column : column + 1]
            vel[component, 2 + column, end : end + 1] = after[component, column : column + 1]

    for layer, spot, high, low in (
        (before, TOP - 1, (head, 0), (before, 7)),
        (after, end, (after, 7), (tail, 0)),
    ):
        grad_x, grad_y, grad_z = [], [], []
        for component in range(3):
            row = layer[component]
            left = jnp.concatenate(
                [vel[component, 1, spot : spot + 1], layer[component, 0 : columns - 1]], axis=0
            )
            right = jnp.concatenate(
                [layer[component, 1:columns], vel[component, columns + 2, spot : spot + 1]], axis=0
            )
            grad_x.append((right - left) * 0.5)
            grad_y.append((high[0][high[1] + component] - low[0][low[1] + component]) * 0.5)
            grad_z.append(vertical_slope(row))
        magnet = [layer[4], layer[5], layer[6]]
        gap, _, unit = stress(layer[3], magnet, grad_x, grad_y, grad_z)
        edge = gap * unit[1]
        parts = (edge * unit[0], edge * unit[1] - gap * (1.0 / 3.0), edge * unit[2])
        for row in range(3):
            for column in range(columns):
                py[row, 1 + column, spot : spot + 1] = parts[row][column : column + 1]

    def tensor_column(ghost, carry):
        here = ghost + 1
        grad_x = [
            (vel[i, here + 1, TOP:end] - vel[i, here - 1, TOP:end]) * 0.5 for i in range(3)
        ]
        grad_y = [
            (vel[i, here, TOP + 1 : end + 1] - vel[i, here, TOP - 1 : end - 1]) * 0.5
            for i in range(3)
        ]
        grad_z = [vertical_slope(vel[i, here, TOP:end]) for i in range(3)]
        magnet = [mass[1, ghost], mass[2, ghost], mass[3, ghost]]
        gap, anisotropy, unit = stress(mass[0, ghost], magnet, grad_x, grad_y, grad_z)
        third = gap * (1.0 / 3.0)
        along_x, along_y = gap * unit[0], gap * unit[1]
        px[0, ghost] = along_x * unit[0] - third
        cross = along_x * unit[1]
        px[1, ghost] = cross
        px[2, ghost] = along_x * unit[2]
        py[0, ghost, TOP:end] = cross
        py[1, ghost, TOP:end] = along_y * unit[1] - third
        py[2, ghost, TOP:end] = along_y * unit[2]
        pzz[ghost] = gap * unit[2] * unit[2] - third
        heat[ghost] = gap * anisotropy
        return carry

    lax.fori_loop(0, columns + 2, tensor_column, 0)

    def update_column(column, carry):
        ghost = column + 1
        inverse = 1.0 / mass[0, ghost]

        def slope(axis):
            return (px[axis, ghost + 1] - px[axis, ghost - 1]) * 0.5 + (
                py[axis, ghost, TOP + 1 : end + 1] - py[axis, ghost, TOP - 1 : end - 1]
            ) * 0.5

        vertical = (px[2, ghost], py[2, ghost, TOP:end], pzz[ghost])
        for axis in range(3):
            force = slope(axis) + vertical_slope(vertical[axis])
            out[column, axis] = fields[axis, column] + force * inverse
        out[column, 3] = fields[6, column] + heat[ghost]
        return carry

    lax.fori_loop(0, columns, update_column, 0)


def updated_columns(info, fields, density, *layers):
    columns, cells, depth = density.shape
    tall = cells + 2 * TOP
    smem = pl.BlockSpec(memory_space=pltpu.SMEM)
    vmem = pl.BlockSpec(memory_space=pltpu.VMEM)
    f32 = jnp.float32
    return pl.pallas_call(
        stress_kernel,
        out_shape=jax.ShapeDtypeStruct((columns, 4, cells, depth), f32),
        in_specs=[smem] + [vmem] * 10,
        out_specs=vmem,
        scratch_shapes=[
            pltpu.VMEM((PACKED, 2 * cells + TOP, depth), f32),
            pltpu.VMEM((3, columns + 4, tall, depth), f32),
            pltpu.VMEM((4, columns + 2, cells, depth), f32),
            pltpu.VMEM((3, columns + 2, cells, depth), f32),
            pltpu.VMEM((3, columns + 2, tall, depth), f32),
            pltpu.VMEM((columns + 2, cells, depth), f32),
            pltpu.VMEM((columns + 2, cells, depth), f32),
        ],
        compiler_params=pltpu.CompilerParams(vmem_limit_bytes=24 * 2**20),
        name="stress_update",
    )(info, fields, density, *layers)


def move_kernel(quantities, rank, shift, frac, gathered, out, twice):
    azimuths, share, cells, depth = gathered.shape
    total = azimuths * cells
    for pair in range(share):
        for block in range(azimuths):
            rows = gathered[block, pair]
            twice[pair, TOP + block * cells : TOP + (block + 1) * cells] = rows
            twice[pair, TOP + total + block * cells : TOP + total + (block + 1) * cells] = rows
        twice[pair, 0:TOP] = gathered[azimuths - 1, pair, cells - TOP : cells]
        column = (rank[0] * share + pair) // quantities
        amount = shift[column]
        fraction = frac[column].astype(jnp.float32) * (1.0 / FRAC_DEN)
        bend = fraction * (1.0 - fraction) * 0.25
        start = TOP + lax.rem(total - amount, total)

        def blend(block, carry):
            spot = start + block * cells
            back_two = twice[pair, pl.ds(spot - 2, cells)]
            back_one = twice[pair, pl.ds(spot - 1, cells)]
            centre = twice[pair, pl.ds(spot, cells)]
            ahead = twice[pair, pl.ds(spot + 1, cells)]
            out[block, pair] = (
                centre
                + fraction * (back_one - centre)
                + bend * ((centre - back_two) - (ahead - back_one))
            )
            return carry

        lax.fori_loop(0, azimuths, blend, 0)


def move_columns(gathered, quantities, rank, shift_int, frac_num):
    azimuths, share, cells, depth = gathered.shape
    smem = pl.BlockSpec(memory_space=pltpu.SMEM)
    vmem = pl.BlockSpec(memory_space=pltpu.VMEM)
    return pl.pallas_call(
        functools.partial(move_kernel, quantities),
        out_shape=jax.ShapeDtypeStruct(gathered.shape, jnp.float32),
        in_specs=[smem, smem, smem, vmem],
        out_specs=vmem,
        scratch_shapes=[pltpu.VMEM((share, 2 * azimuths * cells + TOP, depth), jnp.float32)],
        compiler_params=pltpu.CompilerParams(vmem_limit_bytes=16 * 2**20),
        name="move",
    )(rank, shift_int, frac_num, gathered)


def cut_columns(block):
    quantities, columns, cells, depth = block.shape
    azimuths = lax.axis_size("az")
    return block.transpose(1, 0, 2, 3).reshape(azimuths, -1, cells, depth)


def join_columns(returned, quantities):
    azimuths, share, cells, depth = returned.shape
    return returned.reshape(-1, quantities, cells, depth).transpose(1, 0, 2, 3)


def exchange(blocks, head, tail, low, high, pieces):
    radials = lax.axis_size("rad")
    azimuths = lax.axis_size("az")
    rad = lax.axis_index("rad")
    even = lax.axis_index("az") % 2 == 0
    last = radials - 1

    def flat(rad, az):
        return rad * azimuths + az % azimuths

    def wrap(data, steps):
        pairs = [(flat(last, az), flat(0, az + steps)) for az in range(azimuths)]
        pairs += [(flat(0, az), flat(last, az - steps)) for az in range(azimuths)]
        return lax.ppermute(data, ("rad", "az"), pairs)

    def layers(head, tail):
        inner = [(az, az ^ 1) for az in range(azimuths)]
        outer = [(az, (az - 1 if az % 2 == 0 else az + 1) % azimuths) for az in range(azimuths)]
        far = lax.ppermute(jnp.where(even, head, tail), "az", outer)
        near = lax.ppermute(jnp.where(even, tail, head), "az", inner)
        return jnp.where(even, far, near), jnp.where(even, near, far)

    def rim(main, before, after, column):
        ends = jnp.stack([before[0:3, column], after[0:3, column]], axis=1)
        ends = ends.reshape(1, 6, main.shape[-1])
        ends = jnp.pad(ends, ((0, 0), (0, main.shape[1] - 6), (0, 0)))
        return jnp.concatenate([main, ends], axis=0)

    def branch(steps):
        def run(head, tail, low, high, pieces):
            gathered = lax.all_to_all(pieces, "az", 0, 0, tiled=True)
            before, after = layers(head, tail)
            low = rim(low, before, after, 0)
            high = rim(high, before, after, -1)
            edge = jnp.where(rad == 0, low, high)
            whole = wrap(edge, steps)
            next_one = wrap(edge, steps + 1)
            if radials == 2:
                other = jnp.where(rad == 0, high, low)
                below = above = lax.ppermute(other, "rad", [(0, 1), (1, 0)])
            else:
                below = lax.ppermute(high, "rad", [(i, i + 1) for i in range(last)])
                above = lax.ppermute(low, "rad", [(i + 1, i) for i in range(last)])
            return before, after, below, above, whole, next_one, gathered

        return run

    return lax.switch(
        blocks, [branch(steps) for steps in range(azimuths)], head, tail, low, high, pieces
    )


def local(fields, density, shift_int, frac_num, boundary_shift):
    velocity, magnet = fields[0:3], fields[3:6]
    cells = density.shape[1]
    radials = lax.axis_size("rad")
    rad = lax.axis_index("rad")
    shear_cells = boundary_shift[0]

    def layer(near, far):
        return jnp.concatenate(
            [velocity[:, :, near], density[None, :, near], magnet[:, :, near], velocity[:, :, far]]
        )

    def strip(near, far):
        return jnp.concatenate(
            [velocity[:, near], density[None, near], magnet[:, near], velocity[:, far]]
        )

    head, tail = layer(0, 1), layer(-1, -2)
    low, high = strip(0, 1), strip(-1, -2)
    still = jnp.concatenate([density[None], magnet], axis=0)
    before, after, below, above, whole, next_one, gathered = exchange(
        shear_cells // cells, head, tail, low, high, cut_columns(still)
    )
    rank = lax.axis_index("az").reshape(1)
    still_moved = move_columns(gathered, 4, rank, shift_int, frac_num)
    info = jnp.stack(
        [
            (rad == 0).astype(jnp.int32),
            (rad == radials - 1).astype(jnp.int32),
            shear_cells % cells,
        ]
    )
    updated = updated_columns(
        info, fields, density, head, tail, before, after, below, above, whole, next_one
    )
    share = still_moved.shape[1]
    updated = updated.reshape(still_moved.shape)
    both = jnp.concatenate([updated, still_moved], axis=1)
    both = lax.all_to_all(both, "az", 0, 0, tiled=True)
    still = join_columns(both[:, share:], 4)
    updated_moved = move_columns(both[:, :share], 4, rank, shift_int, frac_num)
    result = join_columns(lax.all_to_all(updated_moved, "az", 0, 0, tiled=True), 4)
    return (jnp.concatenate([result[0:3], still[1:4], result[3:4]], axis=0), still[0])


def solution(mesh):
    in_specs = (P(None, "rad", "az", None), P("rad", "az", None), P("rad"), P("rad"), P())
    out_specs = (P(None, "rad", "az", None), P("rad", "az", None))
    return jax.shard_map(local, mesh=mesh, in_specs=in_specs, out_specs=out_specs, check_vma=False)
```

time: 97.2 us -> 100 us (1.029)
  Pallas kernels: 0 us -> 8.25 us
  other arithmetic: 6.29 us -> 2.2 us
  waiting for transfers between devices: 30.9 us -> 29.7 us
    ppermute x3, waiting for transfers between devices: 2.78 us -> 14.2 us  [the longest x1 10.9 us: layers(): far = lax.ppermute(jnp.where(even, head, tail), 'az', outer)]
    pallas_call x0 -> x3, Pallas kernels: none -> 8.25 us  [the longest x1 4.34 us: updated_columns(): pl.pallas_call(stress_kernel, out_shape=jax.ShapeDtypeStruct((columns, 4,...]
    all_to_all x1 -> x2, waiting for transfers between devices: 21.5 us -> 13.8 us  [the longest x1 13.8 us: local(): lax.all_to_all(updated_moved, 'az', 0, 0, tiled=True)]
    all_to_all x1 -> x2, starting transfers between devices: 5.95 us -> 12.4 us  [the longest x1 7.45 us: run(): gathered = lax.all_to_all(pieces, 'az', 0, 0, tiled=True)]
    ppermute x2, starting transfers between devices: 5.24 us -> 0.01 us  [wrap(): return lax.ppermute(data, ('rad', 'az'), pairs)]
    ppermute x2, waiting for transfers between devices: 6.65 us -> 1.83 us  [wrap(): return lax.ppermute(data, ('rad', 'az'), pairs)]
    transpose x0 -> x1, other arithmetic: none -> 1.89 us  [cut_columns(): return block.transpose(1, 0, 2, 3).reshape(azimuths, -1, cells, depth)]
    mul x7 -> x0, other arithmetic: 1.77 us -> none  [the longest x2 1.26 us: vertical_slope(): return (padded[..., 2:] - padded[..., :-2]) * 0.5]
  transfers between devices with their start and end apart: 6 -> 7, of which waited for: 4 -> 4; matrix products, arithmetic and copies ran while one was open for 2% -> 2% of each run, Pallas kernels for 0% -> 0%
where the time goes in v4:
time: 100 us; the launch traced here: 98.9 us
  blocking collectives  31.2 us (31%)
  waiting for transfers between devices  29.7 us (30%)
  starting transfers between devices  18.6 us (19%)
  Pallas kernels  8.25 us (8%)
  local copies, waits for them, and re-layouts  7.3 us (7%)
  other arithmetic  2.2 us (2%)
  between operations  1.48 us (1%)
    all_to_all x1, blocking collectives, local(): both = lax.all_to_all(both, 'az', 0, 0, tiled=True)  31.2 us
    all_to_all x1, waiting for transfers between devices, local(): lax.all_to_all(updated_moved, 'az', 0, 0, tiled=True)  13.8 us
    ppermute x1, waiting for transfers between devices, layers(): far = lax.ppermute(jnp.where(even, head, tail), 'az', outer)  10.9 us
    all_to_all x1, starting transfers between devices, run(): gathered = lax.all_to_all(pieces, 'az', 0, 0, tiled=True)  7.45 us
    all_to_all x1, starting transfers between devices, local(): lax.all_to_all(updated_moved, 'az', 0, 0, tiled=True)  4.99 us
    pallas_call x1, Pallas kernels, updated_columns(): pl.pallas_call(stress_kernel, out_shape=jax.ShapeDtypeStruct((columns, 4,...  4.34 us
    ppermute x1, starting transfers between devices, layers(): far = lax.ppermute(jnp.where(even, head, tail), 'az', outer)  4.33 us
    pallas_call x2, Pallas kernels, move_columns(): pl.pallas_call(functools.partial(move_kernel, quantities), out_shape=jax....  3.9 us
  transfers between devices with their start and end apart: 7, of which 4 were waited for; matrix products, arithmetic and copies ran while one was open for 2% of the time, Pallas kernels for 0%

profile of v4, /device:TPU:0, one launch (start us, length us, event | category | flops | bytes accessed | tf_op | source)
XLA Modules:
  0.0 98.9 jit_solution(1250622630367547253)
XLA Ops:
  1.3 0.7 fusion.65
  2.0 0.9 fusion.66
  2.9 1.5 %fusion.64 = (f32[3,16,1,128]{3,2,1,0:T(1,128)S(1)}, f32[3,16,1,128]{3,2,1,0:T(1,128)S(1)}, f32[3,16,1,128]{3,2,1,0:T(1,128)S(1)}, f32[3,16,1,128]{3,2,1,0:T(1,1...) fusion(f32[7,16,16,128]{3,2,1,0:T(8,128)} %fields.1), kind=kLoop, calls=%fused_computation.224 | loop fusion | bytes 294912 | tf_op jit(solution)/shard_map/slice | solution.py:342
  4.4 0.0 copy-start.1
  4.4 0.9 slice_bitcast_fusion.4
  5.3 0.1 copy-done.1
  5.4 1.9 %maximum_bitcast_fusion = f32[16,4,16,128]{3,2,1,0:T(8,128)} fusion(f32[1,16,16,128]{3,2,0,1:T(8,128)S(1)} %bitcast.65, f32[7,16,16,128]{3,2,1,0:T(8,128)} %fields.1), kind=kLoop, calls=%fused_computation.179 | loop fusion | flops 131072 | bytes 1048576 | tf_op jit(solution)/shard_map/transpose | solution.py:273
  7.3 0.0 copy-start.2
  7.3 0.0 copy-start.3
  7.3 31.2 %conditional.1 = (f32[10,16,128]{2,1,0:T(8,128)}, f32[10,16,128]{2,1,0:T(8,128)}, f32[11,16,128]{2,1,0:T(8,128)}, f32[11,16,128]{2,1,0:T(8,128)S(1)}, f32[11,16,...) conditional(s32[]{:T(128)} %clamp.3, (pred[]{:T(512)}, ...), branch_computations={%region_0.1_spmd, %region_1.2_spmd, %region_2.3_spmd, %region_3.4_... | conditional | flops 241153 | bytes 5187940 | solution.py:328
  7.4 7.4 %all-to-all-start.11 = ((f32[16,4,16,128]{3,2,1,0:T(8,128)}), f32[16,4,16,128]{3,2,1,0:T(8,128)}, u32[]{:S(2)}, u32[]{:S(2)}) async-start(f32[16,4,16,128]{3,2,1,0:T(8,128)} %get-tuple-element.307), calls=%async_computation.11 | async-start | bytes 1048576 | tf_op jit(solution)/shard_map/cond/branch_11_fun/all_to_all | solution.py:311
  14.9 0.4 collective-permute-start.56
  15.3 4.3 %collective-permute-start.55 = (f32[10,16,128]{2,1,0:T(8,128)S(1)}, f32[10,16,128]{2,1,0:T(8,128)S(1)}, u32[]{:S(2)}, u32[]{:S(2)}) collective-permute-start(f32[10,16,128]{2,1,0:T(8,128)S(1)} %get-tuple-element.493), channel_id=1, source_target_pairs={{0,15},{1,2},{2,1},{3,4},{4,3},{5,6},{6,5},{7,8},{8,7},{9,10},{10,... | collective-permute-start | bytes 245768 | tf_op jit(solution)/shard_map/cond/branch_11_fun/ppermute | solution.py:299
  19.6 10.9 %collective-permute-done.55 = f32[10,16,128]{2,1,0:T(8,128)S(1)} collective-permute-done((f32[10,16,128]{2,1,0:T(8,128)S(1)}, f32[10,16,128]{2,1,0:T(8,128)S(1)}, u32[]{:S(2)}, u32[]{:S(2)}) %collective-permute-start.55) | collective-permute-done | bytes 81952 | tf_op jit(solution)/shard_map/cond/branch_11_fun/ppermute | solution.py:299
  30.7 0.5 copy-done.15
  31.2 0.0 copy-done.32
  31.2 1.4 %collective-permute-start.57 = (f32[11,16,128]{2,1,0:T(8,128)S(1)}, f32[11,16,128]{2,1,0:T(8,128)}, u32[]{:S(2)}, u32[]{:S(2)}) collective-permute-start(f32[11,16,128]{2,1,0:T(8,128)S(1)} %get-tuple-element.489), channel_id=1, source_target_pairs={{0,16},{16,0},{1,17},{17,1},{2,18},{18,2},{3,19},{19,3},{4,20},{20... | collective-permute-start | bytes 270344 | tf_op jit(solution)/shard_map/cond/branch_11_fun/ppermute | solution.py:320
  32.6 3.2 %collective-permute-done.57 = f32[11,16,128]{2,1,0:T(8,128)} collective-permute-done((f32[11,16,128]{2,1,0:T(8,128)S(1)}, f32[11,16,128]{2,1,0:T(8,128)}, u32[]{:S(2)}, u32[]{:S(2)}) %collective-permute-start.57) | collective-permute-done | bytes 90144 | tf_op jit(solution)/shard_map/cond/branch_11_fun/ppermute | solution.py:320
  35.8 0.9 copy.136
  36.7 1.8 %collective-permute-done.59 = f32[11,16,128]{2,1,0:T(8,128)} collective-permute-done((f32[11,16,128]{2,1,0:T(8,128)S(1)}, f32[11,16,128]{2,1,0:T(8,128)}, u32[]{:S(2)}, u32[]{:S(2)}) %collective-permute-start.59) | collective-permute-done | bytes 90144 | tf_op jit(solution)/shard_map/cond/branch_11_fun/ppermute | solution.py:294
  38.6 0.1 pad_add_fusion.info
  38.7 1.8 %move.2 = f32[16,4,16,128]{3,2,1,0:T(8,128)S(1)} custom-call(s32[1]{0:T(128)} %bitcast.rank, s32[16]{0:T(128)S(1)} %copy-done.2, s32[16]{0:T(128)S(1)} %copy-done.3, f32[16,4,16,128]{3,2,1,0:T(8,128)} %get-tuple-element.351.gathered), custom_call_target="tpu_custom_call" | custom-call | tf_op jit(solution)/shard_map/move/pallas_call | solution.py:259
  40.5 4.3 %stress_update.1 = f32[16,4,16,128]{3,2,1,0:T(8,128)S(1)} custom-call(s32[3]{0:T(128)S(1)} %pad_add_fusion.info, f32[7,16,16,128]{3,2,1,0:T(8,128)S(1)} %copy-done, f32[16,16,128]{2,1,0:T(8,128)S(1)} %copy-done.1, f32[10,16,128]{2,1,0:T(8,128)S(1)} %get-tuple-element.568.head, f32[10,16,128]{2,1,0:T(8,128)S(1)} %get-tuple-element.569.tail, ...), custom_call_target="tpu_custom_call" | custom-call | tf_op jit(solution)/shard_map/stress_update/pallas_call | solution.py:205
  44.9 0.1 pad_maximum_fusion.32
  45.0 31.2 %all_to_all.74 = f32[16,8,16,128]{3,2,1,0:T(8,128)S(1)} all-to-all(f32[16,8,16,128]{3,2,1,0:T(8,128)S(1)} %pad_maximum_fusion.32), channel_id=1, replica_groups=mesh['rad'=2,'az'=16] {'az'}, dimensions={0} | all-to-all | bytes 2097152 | tf_op jit(solution)/shard_map/all_to_all | solution.py:371
  76.2 0.1 slice_bitcast_fusion
  76.2 2.1 %move.3 = f32[16,4,16,128]{3,2,1,0:T(8,128)} custom-call(s32[1]{0:T(128)} %bitcast.rank, s32[16]{0:T(128)S(1)} %copy-done.2, s32[16]{0:T(128)S(1)} %copy-done.3, f32[16,4,16,128]{3,2,1,0:T(8,128)S(1)} %get-tuple-element.549.gathered), custom_call_target="tpu_custom_call" | custom-call | tf_op jit(solution)/shard_map/move/pallas_call | solution.py:259
  78.3 5.0 %all-to-all-start.17 = ((f32[16,4,16,128]{3,2,1,0:T(8,128)}), f32[16,4,16,128]{3,2,1,0:T(8,128)S(1)}, u32[]{:S(2)}, u32[]{:S(2)}) async-start(f32[16,4,16,128]{3,2,1,0:T(8,128)} %move.3), calls=%async_computation.17 | async-start | bytes 1048576 | tf_op jit(solution)/shard_map/all_to_all | solution.py:374
  83.3 0.7 slice_bitcast_fusion.1
  84.0 13.8 %all-to-all-done.17 = f32[16,4,16,128]{3,2,1,0:T(8,128)S(1)} async-done(((f32[16,4,16,128]{3,2,1,0:T(8,128)}), f32[16,4,16,128]{3,2,1,0:T(8,128)S(1)}, u32[]{:S(2)}, u32[]{:S(2)}) %all-to-all-start.17) | async-done | bytes 524320 | tf_op jit(solution)/shard_map/all_to_all | solution.py:374
  97.8 0.1 pad_maximum_fusion.33
  97.9 1.0 %copy.38 = f32[7,16,16,128]{3,2,1,0:T(8,128)} copy(f32[7,16,16,128]{3,2,0,1:T(8,128)S(1)} %pad_maximum_fusion.33) | data formatting | bytes 1835008
  (26 shorter events, 0.2 us)
Async XLA Ops:
  4.4 1.0 %copy-start.1 = (f32[16,16,128]{2,1,0:T(8,128)S(1)}, f32[16,16,128]{2,1,0:T(8,128)}, u32[]{:S(2)}) copy-start(f32[16,16,128]{2,1,0:T(8,128)} %density.1) | copy-start | bytes 393220
  7.3 31.4 %copy-start.2 = (s32[16]{0:T(128)S(1)}, s32[16]{0:T(128)}, u32[]{:S(2)}) copy-start(s32[16]{0:T(128)} %shift.3) | copy-start | bytes 196
  7.3 31.3 %copy-start.3 = (s32[16]{0:T(128)S(1)}, s32[16]{0:T(128)}, u32[]{:S(2)}) copy-start(s32[16]{0:T(128)} %frac.3) | copy-start | bytes 196
  7.4 31.2 %all-to-all-start.11 = ((f32[16,4,16,128]{3,2,1,0:T(8,128)}), f32[16,4,16,128]{3,2,1,0:T(8,128)}, u32[]{:S(2)}, u32[]{:S(2)}) async-start(f32[16,4,16,128]{3,2,1,0:T(8,128)} %get-tuple-element.307), calls=%async_computation.11 | async-start | bytes 1048576 | tf_op jit(solution)/shard_map/cond/branch_11_fun/all_to_all | solution.py:311
  14.9 4.8 %collective-permute-start.56 = (f32[10,16,128]{2,1,0:T(8,128)S(1)}, f32[10,16,128]{2,1,0:T(8,128)S(1)}, u32[]{:S(2)}, u32[]{:S(2)}) collective-permute-start(f32[10,16,128]{2,1,0:T(8,128)S(1)} %get-tuple-element.492), channel_id=1, source_target_pairs={{0,1},{1,0},{2,3},{3,2},{4,5},{5,4},{6,7},{7,6},{8,9},{9,8},{10,11... | collective-permute-start | bytes 245768 | tf_op jit(solution)/shard_map/cond/branch_11_fun/ppermute | solution.py:300
  15.3 15.3 %collective-permute-start.55 = (f32[10,16,128]{2,1,0:T(8,128)S(1)}, f32[10,16,128]{2,1,0:T(8,128)S(1)}, u32[]{:S(2)}, u32[]{:S(2)}) collective-permute-start(f32[10,16,128]{2,1,0:T(8,128)S(1)} %get-tuple-element.493), channel_id=1, source_target_pairs={{0,15},{1,2},{2,1},{3,4},{4,3},{5,6},{6,5},{7,8},{8,7},{9,10},{10,... | collective-permute-start | bytes 245768 | tf_op jit(solution)/shard_map/cond/branch_11_fun/ppermute | solution.py:299
  30.5 0.6 copy-start.15
  30.6 0.7 copy-start.32
  31.2 4.6 %collective-permute-start.57 = (f32[11,16,128]{2,1,0:T(8,128)S(1)}, f32[11,16,128]{2,1,0:T(8,128)}, u32[]{:S(2)}, u32[]{:S(2)}) collective-permute-start(f32[11,16,128]{2,1,0:T(8,128)S(1)} %get-tuple-element.489), channel_id=1, source_target_pairs={{0,16},{16,0},{1,17},{17,1},{2,18},{18,2},{3,19},{19,3},{4,20},{20... | collective-permute-start | bytes 270344 | tf_op jit(solution)/shard_map/cond/branch_11_fun/ppermute | solution.py:320
  32.6 6.0 %collective-permute-start.59 = (f32[11,16,128]{2,1,0:T(8,128)S(1)}, f32[11,16,128]{2,1,0:T(8,128)}, u32[]{:S(2)}, u32[]{:S(2)}) collective-permute-start(f32[11,16,128]{2,1,0:T(8,128)S(1)} %get-tuple-element.488), channel_id=1, source_target_pairs={{16,12},{17,13},{18,14},{19,15},{20,0},{21,1},{22,2},{23,3},{24,4}... | collective-permute-start | bytes 270344 | tf_op jit(solution)/shard_map/cond/branch_11_fun/ppermute | solution.py:294
  32.6 6.0 %collective-permute-start.58 = (f32[11,16,128]{2,1,0:T(8,128)S(1)}, f32[11,16,128]{2,1,0:T(8,128)}, u32[]{:S(2)}, u32[]{:S(2)}) collective-permute-start(f32[11,16,128]{2,1,0:T(8,128)S(1)} %get-tuple-element.488), channel_id=1, source_target_pairs={{16,11},{17,12},{18,13},{19,14},{20,15},{21,0},{22,1},{23,2},{24,3... | collective-permute-start | bytes 270344 | tf_op jit(solution)/shard_map/cond/branch_11_fun/ppermute | solution.py:294
  38.6 1.9 %copy-start = (f32[7,16,16,128]{3,2,1,0:T(8,128)S(1)}, f32[7,16,16,128]{3,2,1,0:T(8,128)}, u32[]{:S(2)}) copy-start(f32[7,16,16,128]{3,2,1,0:T(8,128)} %fields.1) | copy-start | bytes 2752516
  38.7 1.9 %copy-start.20 = (f32[10,16,128]{2,1,0:T(8,128)S(1)}, f32[10,16,128]{2,1,0:T(8,128)}, u32[]{:S(2)}) copy-start(f32[10,16,128]{2,1,0:T(8,128)} %get-tuple-element.346.after) | copy-start | bytes 245764
  78.3 19.5 %all-to-all-start.17 = ((f32[16,4,16,128]{3,2,1,0:T(8,128)}), f32[16,4,16,128]{3,2,1,0:T(8,128)S(1)}, u32[]{:S(2)}, u32[]{:S(2)}) async-start(f32[16,4,16,128]{3,2,1,0:T(8,128)} %move.3), calls=%async_computation.17 | async-start | bytes 1048576 | tf_op jit(solution)/shard_map/all_to_all | solution.py:374

commit v5 on v4

--- a/solution.py
+++ b/solution.py
@@ -47,6 +47,120 @@
     anisotropy = aligned - (grad_x[0] + grad_y[1] + grad_z[2]) * (1.0 / 3.0)
     gap = (3.0 * visc_step) * density * anisotropy
     return gap, anisotropy, unit
+
+
+def pack_kernel(quantities, rank, fields, density, head, tail, low, high, still):
+    columns, cells, depth = density.shape
+    slots, share = still.shape[0], still.shape[1]
+
+    def source(row):
+        if row == 3:
+            return density
+        return fields.at[row if row < 3 else row - 1 if row < 7 else row - 7]
+
+    for row in range(PACKED):
+        second = 1 if row >= 7 else 0
+        origin = source(row)
+        low[row] = origin[second]
+        high[row] = origin[columns - 1 - second]
+        for column in range(columns):
+            head[row, column : column + 1] = origin[column, second : second + 1]
+            tail[row, column : column + 1] = origin[column, cells - 1 - second : cells - second]
+    for slot in range(slots):
+        for item in range(share):
+            column, row = pair_of(lax.bitwise_xor(rank[0], slot), item, share, quantities)
+            if isinstance(row, int):
+                still[slot, item] = density[column] if row == 0 else fields[2 + row, column]
+            else:
+                still[slot, item] = jnp.where(
+                    row == 0, density[column], fields[jnp.maximum(row, 1) + 2, column]
+                )
+
+
+def pair_of(rank, item, share, quantities):
+    if share % quantities == 0:
+        return rank * (share // quantities) + item // quantities, item % quantities
+    flat = rank * share + item
+    return flat // quantities, flat % quantities
+
+
+def pack(rank, fields, density):
+    columns, cells, depth = density.shape
+    slots = lax.axis_size("az")
+    share = 4 * columns // slots
+    f32 = jnp.float32
+    layer = jax.ShapeDtypeStruct((PACKED, columns, depth), f32)
+    rim = jax.ShapeDtypeStruct((PACKED, cells, depth), f32)
+    vmem = pl.BlockSpec(memory_space=pltpu.VMEM)
+    return pl.pallas_call(
+        functools.partial(pack_kernel, 4),
+        out_shape=(
+            layer,
+            layer,
+            rim,
+            rim,
+            jax.ShapeDtypeStruct((slots, share, cells, depth), f32),
+        ),
+        in_specs=[pl.BlockSpec(memory_space=pltpu.SMEM), vmem, vmem],
+        out_specs=[vmem] * 5,
+        compiler_params=pltpu.CompilerParams(vmem_limit_bytes=16 * 2**20),
+        name="pack",
+    )(rank, fields, density)
+
+
+def join_kernel(quantities, rank, moving, still, new_fields, new_density):
+    slots, share = still.shape[0], still.shape[1]
+    for slot in range(slots):
+        for item in range(share):
+            column, row = pair_of(lax.bitwise_xor(rank[0], slot), item, share, quantities)
+            if isinstance(row, int):
+                new_fields[6 if row == 3 else row, column] = moving[slot, item]
+                if row == 0:
+                    new_density[column] = still[slot, item]
+                else:
+                    new_fields[2 + row, column] = still[slot, item]
+            else:
+                new_fields[jnp.where(row == 3, 6, row), column] = moving[slot, item]
+
+                @pl.when(row == 0)
+                def _():
+                    new_density[column] = still[slot, item]
+
+                @pl.when(row > 0)
+                def _():
+                    new_fields[2 + row, column] = still[slot, item]
+
+
+def join(rank, moving, still, columns):
+    _, _, cells, depth = still.shape
+    f32 = jnp.float32
+    vmem = pl.BlockSpec(memory_space=pltpu.VMEM)
+    return pl.pallas_call(
+        functools.partial(join_kernel, 4),
+        out_shape=(
+            jax.ShapeDtypeStruct((7, columns, cells, depth), f32),
+            jax.ShapeDtypeStruct((columns, cells, depth), f32),
+        ),
+        in_specs=[pl.BlockSpec(memory_space=pltpu.SMEM), vmem, vmem],
+        out_specs=[vmem] * 2,
+        compiler_params=pltpu.CompilerParams(vmem_limit_bytes=16 * 2**20),
+        name="join",
+    )(rank, moving, still)
+
+
+def swap(slots):
+    count = slots.shape[0]
+    stride = count
+    while stride > 1:
+        radix = 4 if stride % 4 == 0 else 2
+        stride //= radix
+        cut = slots.reshape(count // (radix * stride), radix, stride, *slots.shape[1:])
+        parts = [cut[:, 0]]
+        for step in range(1, radix):
+            pairs = [(rank, rank ^ (step * stride)) for rank in range(count)]
+            parts.append(lax.ppermute(cut[:, step], "az", pairs))
+        slots = jnp.stack(parts, axis=1).reshape(slots.shape)
+    return slots
 
 
 def stress_kernel(
@@ -71,6 +185,7 @@
     heat,
 ):
     columns, cells, depth = density.shape
+    share = out.shape[1]
     first, last, remainder = info[0], info[1], info[2]
     end = TOP + cells
 
@@ -187,10 +302,14 @@
             ) * 0.5
 
         vertical = (px[2, ghost], py[2, ghost, TOP:end], pzz[ghost])
-        for axis in range(3):
-            force = slope(axis) + vertical_slope(vertical[axis])
-            out[column, axis] = fields[axis, column] + force * inverse
-        out[column, 3] = fields[6, column] + heat[ghost]
+        for axis in range(4):
+            flat = column * 4 + axis
+            slot = lax.bitwise_xor(info[3], flat // share)
+            if axis < 3:
+                force = slope(axis) + vertical_slope(vertical[axis])
+                out[slot, flat % share] = fields[axis, column] + force * inverse
+            else:
+                out[slot, flat % share] = fields[6, column] + heat[ghost]
         return carry
 
     lax.fori_loop(0, columns, update_column, 0)
@@ -199,12 +318,13 @@
 def updated_columns(info, fields, density, *layers):
     columns, cells, depth = density.shape
     tall = cells + 2 * TOP
+    slots = lax.axis_size("az")
     smem = pl.BlockSpec(memory_space=pltpu.SMEM)
     vmem = pl.BlockSpec(memory_space=pltpu.VMEM)
     f32 = jnp.float32
     return pl.pallas_call(
         stress_kernel,
-        out_shape=jax.ShapeDtypeStruct((columns, 4, cells, depth), f32),
+        out_shape=jax.ShapeDtypeStruct((slots, 4 * columns // slots, cells, depth), f32),
         in_specs=[smem] + [vmem] * 10,
         out_specs=vmem,
         scratch_shapes=[
@@ -222,34 +342,39 @@
 
 
 def move_kernel(quantities, rank, shift, frac, gathered, out, twice):
-    azimuths, share, cells, depth = gathered.shape
-    total = azimuths * cells
-    for pair in range(share):
-        for block in range(azimuths):
-            rows = gathered[block, pair]
-            twice[pair, TOP + block * cells : TOP + (block + 1) * cells] = rows
-            twice[pair, TOP + total + block * cells : TOP + total + (block + 1) * cells] = rows
-        twice[pair, 0:TOP] = gathered[azimuths - 1, pair, cells - TOP : cells]
-        column = (rank[0] * share + pair) // quantities
-        amount = shift[column]
+    slots, share, cells, depth = gathered.shape
+    total = slots * cells
+    me = rank[0]
+    for item in range(share):
+        column, _ = pair_of(me, item, share, quantities)
         fraction = frac[column].astype(jnp.float32) * (1.0 / FRAC_DEN)
         bend = fraction * (1.0 - fraction) * 0.25
-        start = TOP + lax.rem(total - amount, total)
-
-        def blend(block, carry):
-            spot = start + block * cells
-            back_two = twice[pair, pl.ds(spot - 2, cells)]
-            back_one = twice[pair, pl.ds(spot - 1, cells)]
-            centre = twice[pair, pl.ds(spot, cells)]
-            ahead = twice[pair, pl.ds(spot + 1, cells)]
-            out[block, pair] = (
+        start = TOP + lax.rem(total - shift[column], total)
+
+        def lay(slot, carry):
+            rows = gathered[slot, item]
+            spot = pl.multiple_of(TOP + lax.bitwise_xor(me, slot) * cells, TOP)
+            twice[item, pl.ds(spot, cells)] = rows
+            twice[item, pl.ds(pl.multiple_of(spot + total, TOP), cells)] = rows
+            return carry
+
+        lax.fori_loop(0, slots, lay, 0, unroll=4)
+        twice[item, 0:TOP] = twice[item, total : total + TOP]
+
+        def blend(slot, carry):
+            spot = start + lax.bitwise_xor(me, slot) * cells
+            back_two = twice[item, pl.ds(spot - 2, cells)]
+            back_one = twice[item, pl.ds(spot - 1, cells)]
+            centre = twice[item, pl.ds(spot, cells)]
+            ahead = twice[item, pl.ds(spot + 1, cells)]
+            out[slot, item] = (
                 centre
                 + fraction * (back_one - centre)
                 + bend * ((centre - back_two) - (ahead - back_one))
             )
             return carry
 
-        lax.fori_loop(0, azimuths, blend, 0)
+        lax.fori_loop(0, slots, blend, 0, unroll=4)
 
 
 def move_columns(gathered, quantities, rank, shift_int, frac_num):
@@ -267,22 +392,20 @@
     )(rank, shift_int, frac_num, gathered)
 
 
-def cut_columns(block):
-    quantities, columns, cells, depth = block.shape
+def azimuthal_layers(head, tail):
     azimuths = lax.axis_size("az")
-    return block.transpose(1, 0, 2, 3).reshape(azimuths, -1, cells, depth)
-
-
-def join_columns(returned, quantities):
-    azimuths, share, cells, depth = returned.shape
-    return returned.reshape(-1, quantities, cells, depth).transpose(1, 0, 2, 3)
-
-
-def exchange(blocks, head, tail, low, high, pieces):
+    even = lax.axis_index("az") % 2 == 0
+    inner = [(az, az ^ 1) for az in range(azimuths)]
+    outer = [(az, (az - 1 if az % 2 == 0 else az + 1) % azimuths) for az in range(azimuths)]
+    far = lax.ppermute(jnp.where(even, head, tail), "az", outer)
+    near = lax.ppermute(jnp.where(even, tail, head), "az", inner)
+    return jnp.where(even, far, near), jnp.where(even, near, far)
+
+
+def rims(blocks, low, high, before, after):
     radials = lax.axis_size("rad")
     azimuths = lax.axis_size("az")
     rad = lax.axis_index("rad")
-    even = lax.axis_index("az") % 2 == 0
     last = radials - 1
 
     def flat(rad, az):
@@ -293,86 +416,53 @@
         pairs += [(flat(0, az), flat(last, az - steps)) for az in range(azimuths)]
         return lax.ppermute(data, ("rad", "az"), pairs)
 
-    def layers(head, tail):
-        inner = [(az, az ^ 1) for az in range(azimuths)]
-        outer = [(az, (az - 1 if az % 2 == 0 else az + 1) % azimuths) for az in range(azimuths)]
-        far = lax.ppermute(jnp.where(even, head, tail), "az", outer)
-        near = lax.ppermute(jnp.where(even, tail, head), "az", inner)
-        return jnp.where(even, far, near), jnp.where(even, near, far)
-
-    def rim(main, before, after, column):
+    def with_ends(main, column):
         ends = jnp.stack([before[0:3, column], after[0:3, column]], axis=1)
         ends = ends.reshape(1, 6, main.shape[-1])
         ends = jnp.pad(ends, ((0, 0), (0, main.shape[1] - 6), (0, 0)))
         return jnp.concatenate([main, ends], axis=0)
 
+    low, high = with_ends(low, 0), with_ends(high, -1)
+    edge = jnp.where(rad == 0, low, high)
+    if radials == 2:
+        other = jnp.where(rad == 0, high, low)
+        below = above = lax.ppermute(other, "rad", [(0, 1), (1, 0)])
+    else:
+        below = lax.ppermute(high, "rad", [(i, i + 1) for i in range(last)])
+        above = lax.ppermute(low, "rad", [(i + 1, i) for i in range(last)])
+
     def branch(steps):
-        def run(head, tail, low, high, pieces):
-            gathered = lax.all_to_all(pieces, "az", 0, 0, tiled=True)
-            before, after = layers(head, tail)
-            low = rim(low, before, after, 0)
-            high = rim(high, before, after, -1)
-            edge = jnp.where(rad == 0, low, high)
-            whole = wrap(edge, steps)
-            next_one = wrap(edge, steps + 1)
-            if radials == 2:
-                other = jnp.where(rad == 0, high, low)
-                below = above = lax.ppermute(other, "rad", [(0, 1), (1, 0)])
-            else:
-                below = lax.ppermute(high, "rad", [(i, i + 1) for i in range(last)])
-                above = lax.ppermute(low, "rad", [(i + 1, i) for i in range(last)])
-            return before, after, below, above, whole, next_one, gathered
-
-        return run
-
-    return lax.switch(
-        blocks, [branch(steps) for steps in range(azimuths)], head, tail, low, high, pieces
-    )
+        return lambda data: (wrap(data, steps), wrap(data, steps + 1))
+
+    whole, next_one = lax.switch(blocks, [branch(steps) for steps in range(azimuths)], edge)
+    return below, above, whole, next_one
 
 
 def local(fields, density, shift_int, frac_num, boundary_shift):
-    velocity, magnet = fields[0:3], fields[3:6]
-    cells = density.shape[1]
+    columns, cells, _ = density.shape
     radials = lax.axis_size("rad")
     rad = lax.axis_index("rad")
     shear_cells = boundary_shift[0]
-
-    def layer(near, far):
-        return jnp.concatenate(
-            [velocity[:, :, near], density[None, :, near], magnet[:, :, near], velocity[:, :, far]]
-        )
-
-    def strip(near, far):
-        return jnp.concatenate(
-            [velocity[:, near], density[None, near], magnet[:, near], velocity[:, far]]
-        )
-
-    head, tail = layer(0, 1), layer(-1, -2)
-    low, high = strip(0, 1), strip(-1, -2)
-    still = jnp.concatenate([density[None], magnet], axis=0)
-    before, after, below, above, whole, next_one, gathered = exchange(
-        shear_cells // cells, head, tail, low, high, cut_columns(still)
-    )
-    rank = lax.axis_index("az").reshape(1)
-    still_moved = move_columns(gathered, 4, rank, shift_int, frac_num)
+    az = lax.axis_index("az")
+    rank = az.reshape(1)
+    head, tail, low, high, still = pack(rank, fields, density)
+    before, after = azimuthal_layers(head, tail)
+    before, after, still = lax.optimization_barrier((before, after, still))
+    still = swap(still)
+    layers = rims(shear_cells // cells, low, high, before, after)
     info = jnp.stack(
         [
             (rad == 0).astype(jnp.int32),
             (rad == radials - 1).astype(jnp.int32),
             shear_cells % cells,
+            az,
         ]
     )
-    updated = updated_columns(
-        info, fields, density, head, tail, before, after, below, above, whole, next_one
-    )
-    share = still_moved.shape[1]
-    updated = updated.reshape(still_moved.shape)
-    both = jnp.concatenate([updated, still_moved], axis=1)
-    both = lax.all_to_all(both, "az", 0, 0, tiled=True)
-    still = join_columns(both[:, share:], 4)
-    updated_moved = move_columns(both[:, :share], 4, rank, shift_int, frac_num)
-    result = join_columns(lax.all_to_all(updated_moved, "az", 0, 0, tiled=True), 4)
-    return (jnp.concatenate([result[0:3], still[1:4], result[3:4]], axis=0), still[0])
+    moving = updated_columns(info, fields, density, head, tail, before, after, *layers)
+    moving = swap(moving)
+    still = swap(move_columns(still, 4, rank, shift_int, frac_num))
+    moving = swap(move_columns(moving, 4, rank, shift_int, frac_num))
+    return join(rank, moving, still, columns)
 
 
 def solution(mesh):

time: 100 us -> 86.9 us (0.87)
  blocking collectives: 31.2 us -> 0 us
  starting transfers between devices: 18.6 us -> 36.7 us
  waiting for transfers between devices: 29.7 us -> 37.5 us
  local copies, waits for them, and re-layouts: 7.3 us -> 3.07 us
  other arithmetic: 2.2 us -> 0.43 us
    all_to_all x1 -> x0, blocking collectives: 31.2 us -> none  [local(): both = lax.all_to_all(both, 'az', 0, 0, tiled=True)]
    ppermute x3 -> x27, starting transfers between devices: 6.14 us -> 34.1 us  [the longest x24 26.4 us: swap(): parts.append(lax.ppermute(cut[:, step], 'az', pairs))]
    ppermute x3 -> x27, waiting for transfers between devices: 14.2 us -> 30.5 us  [the longest x24 29.1 us: swap(): parts.append(lax.ppermute(cut[:, step], 'az', pairs))]
    all_to_all x2 -> x0, waiting for transfers between devices: 13.8 us -> none  [the longest x1 13.8 us: local(): lax.all_to_all(updated_moved, 'az', 0, 0, tiled=True)]
    all_to_all x2 -> x0, starting transfers between devices: 12.4 us -> none  [the longest x1 7.45 us: run(): gathered = lax.all_to_all(pieces, 'az', 0, 0, tiled=True)]
    ppermute x2, waiting for transfers between devices: 1.83 us -> 7.08 us  [wrap(): return lax.ppermute(data, ('rad', 'az'), pairs)]
    slice x7 -> x9, local copies, waits for them, and re-layouts: 3.13 us -> 0.3 us  [the longest x8 0.3 us: swap(): parts = [cut[:, 0]]]
    ppermute x2, starting transfers between devices: 0.01 us -> 2.6 us  [wrap(): return lax.ppermute(data, ('rad', 'az'), pairs)]
  transfers between devices with their start and end apart: 7 -> 29, of which waited for: 4 -> 13; matrix products, arithmetic and copies ran while one was open for 2% -> 1% of each run, Pallas kernels for 0% -> 7%
where the time goes in v5:
time: 86.9 us; the launch traced here: 86.8 us
  waiting for transfers between devices  37.5 us (43%)
  starting transfers between devices  36.7 us (42%)
  Pallas kernels  7.45 us (9%)
  local copies, waits for them, and re-layouts  3.07 us (4%)
  between operations  1.57 us (2%)
    ppermute x24, waiting for transfers between devices, swap(): parts.append(lax.ppermute(cut[:, step], 'az', pairs))  29.1 us
    ppermute x24, starting transfers between devices, swap(): parts.append(lax.ppermute(cut[:, step], 'az', pairs))  26.4 us
    ppermute x2, waiting for transfers between devices, wrap(): return lax.ppermute(data, ('rad', 'az'), pairs)  7.08 us
    ppermute x1, starting transfers between devices, azimuthal_layers(): far = lax.ppermute(jnp.where(even, head, tail), 'az', outer)  5.67 us
    pallas_call x1, Pallas kernels, updated_columns(): pl.pallas_call(stress_kernel, out_shape=jax.ShapeDtypeStruct((slots, 4 *...  4.27 us
    unnamed x12, local copies, waits for them, and re-layouts  2.75 us
    ppermute x2, starting transfers between devices, wrap(): return lax.ppermute(data, ('rad', 'az'), pairs)  2.6 us
    pallas_call x2, Pallas kernels, move_columns(): pl.pallas_call(functools.partial(move_kernel, quantities), out_shape=jax....  1.99 us
  transfers between devices with their start and end apart: 29, of which 13 were waited for; matrix products, arithmetic and copies ran while one was open for 1% of the time, Pallas kernels for 7%

profile of v5, /device:TPU:0, one launch (start us, length us, event | category | flops | bytes accessed | tf_op | source)
XLA Modules:
  0.0 86.8 jit_solution(13036183873232684256)
XLA Ops:
  0.7 1.2 %copy-done = f32[7,16,16,128]{3,2,1,0:T(8,128)S(1)} copy-done((f32[7,16,16,128]{3,2,1,0:T(8,128)S(1)}, f32[7,16,16,128]{3,2,1,0:T(8,128)}, u32[]{:S(2)}) %copy-start) | copy-done | bytes 917528
  3.4 5.7 %collective-permute-start.32 = (f32[10,16,128]{2,1,0:T(8,128)S(1)}, f32[10,16,128]{2,1,0:T(8,128)S(1)}, u32[]{:S(2)}, u32[]{:S(2)}) collective-permute-start(f32[10,16,128]{2,1,0:T(8,128)S(1)} %get-tuple-element.75), channel_id=1, source_target_pairs={{0,15},{1,2},{2,1},{3,4},{4,3},{5,6},{6,5},{7,8},{8,7},{9,10},{10,... | collective-permute-start | bytes 245768 | tf_op jit(solution)/shard_map/ppermute | solution.py:400
  9.9 1.3 %collective-permute-done.32 = f32[10,16,128]{2,1,0:T(8,128)S(1)} collective-permute-done((f32[10,16,128]{2,1,0:T(8,128)S(1)}, f32[10,16,128]{2,1,0:T(8,128)S(1)}, u32[]{:S(2)}, u32[]{:S(2)}) %collective-permute-start.32) | collective-permute-done | bytes 81952 | tf_op jit(solution)/shard_map/ppermute | solution.py:400
  11.3 1.6 %collective-permute-start.34 = (f32[11,16,128]{2,1,0:T(8,128)S(1)}, f32[11,16,128]{2,1,0:T(8,128)S(1)}, u32[]{:S(2)}, u32[]{:S(2)}) collective-permute-start(f32[11,16,128]{2,1,0:T(8,128)S(1)} %get-tuple-element.71), channel_id=1, source_target_pairs={{0,16},{16,0},{1,17},{17,1},{2,18},{18,2},{3,19},{19,3},{4,20},{20... | collective-permute-start | bytes 270344 | tf_op jit(solution)/shard_map/ppermute | solution.py:429
  12.9 1.8 %collective-permute-start.49 = (f32[1,4,4,16,128]{4,3,2,1,0:T(8,128)S(1)}, f32[1,4,4,16,128]{4,3,2,1,0:T(8,128)S(1)}, u32[]{:S(2)}, u32[]{:S(2)}) collective-permute-start(f32[1,4,4,16,128]{4,3,2,1,0:T(8,128)S(1)} %get-tuple-element.51), channel_id=1, source_target_pairs={{0,12},{1,13},{2,14},{3,15},{4,8},{5,9},{6,10},{7,11},{8,4},{9,5},... | collective-permute-start | bytes 393224 | tf_op jit(solution)/shard_map/ppermute | solution.py:161
  14.8 9.7 %conditional.1 = (f32[11,16,128]{2,1,0:T(8,128)}, f32[11,16,128]{2,1,0:T(8,128)}) conditional(s32[]{:T(128)} %clamp.3, f32[11,16,128]{2,1,0:T(8,128)S(1)} %get-tuple-element.70, f32[11,16,128]{2,1,0:T(8,128)S(1)} %get-tuple-element.70, f32[11,16,128]{2,1,0:T(8,128)S(1)} %get-tuple-element.70, ...), branch_computations={%region_0.1_spmd, %region_1.2_spmd, %region_2.3_spmd, %region_3.4_... | conditional | bytes 720992 | solution.py:437
  14.8 2.6 %collective-permute-start.23 = (f32[11,16,128]{2,1,0:T(8,128)S(1)}, f32[11,16,128]{2,1,0:T(8,128)}, u32[]{:S(2)}, u32[]{:S(2)}) collective-permute-start(f32[11,16,128]{2,1,0:T(8,128)S(1)} %param.11), channel_id=1, source_target_pairs={{16,12},{17,13},{18,14},{19,15},{20,0},{21,1},{22,2},{23,3},{24,4}... | collective-permute-start | bytes 270344 | tf_op jit(solution)/shard_map/cond/branch_11_fun/ppermute | solution.py:417
  17.4 6.1 %collective-permute-done.23 = f32[11,16,128]{2,1,0:T(8,128)} collective-permute-done((f32[11,16,128]{2,1,0:T(8,128)S(1)}, f32[11,16,128]{2,1,0:T(8,128)}, u32[]{:S(2)}, u32[]{:S(2)}) %collective-permute-start.23) | collective-permute-done | bytes 90144 | tf_op jit(solution)/shard_map/cond/branch_11_fun/ppermute | solution.py:417
  23.4 1.0 %collective-permute-done.22 = f32[11,16,128]{2,1,0:T(8,128)} collective-permute-done((f32[11,16,128]{2,1,0:T(8,128)S(1)}, f32[11,16,128]{2,1,0:T(8,128)}, u32[]{:S(2)}, u32[]{:S(2)}) %collective-permute-start.22) | collective-permute-done | bytes 90144 | tf_op jit(solution)/shard_map/cond/branch_11_fun/ppermute | solution.py:417
  24.4 6.1 %collective-permute-start.47 = (f32[1,4,4,16,128]{4,3,2,1,0:T(8,128)S(1)}, f32[1,4,4,16,128]{4,3,2,1,0:T(8,128)S(1)}, u32[]{:S(2)}, u32[]{:S(2)}) collective-permute-start(f32[1,4,4,16,128]{4,3,2,1,0:T(8,128)S(1)} %get-tuple-element.53), channel_id=1, source_target_pairs={{0,4},{1,5},{2,6},{3,7},{4,0},{5,1},{6,2},{7,3},{8,12},{9,13},{10,... | collective-permute-start | bytes 393224 | tf_op jit(solution)/shard_map/ppermute | solution.py:161
  30.6 4.3 %stress_update.1 = f32[16,4,16,128]{3,2,1,0:T(8,128)S(1)} custom-call(s32[4]{0:T(128)S(1)} %pad_add_fusion.info, f32[7,16,16,128]{3,2,1,0:T(8,128)S(1)} %copy-done.1, f32[16,16,128]{2,1,0:T(8,128)S(1)} %copy-done.3, f32[10,16,128]{2,1,0:T(8,128)S(1)} %get-tuple-element.28.head, f32[10,16,128]{2,1,0:T(8,128)S(1)} %get-tuple-element.29.tail, ...), custom_call_target="tpu_custom_call" | custom-call | tf_op jit(solution)/shard_map/stress_update/pallas_call | solution.py:325
  35.0 1.5 %collective-permute-start.36 = (f32[1,4,4,16,128]{4,3,2,1,0:T(8,128)S(1)}, f32[1,4,4,16,128]{4,3,2,1,0:T(8,128)S(1)}, u32[]{:S(2)}, u32[]{:S(2)}) collective-permute-start(f32[1,4,4,16,128]{4,3,2,1,0:T(8,128)S(1)} %get-tuple-element.68), channel_id=1, source_target_pairs={{0,8},{1,9},{2,10},{3,11},{4,12},{5,13},{6,14},{7,15},{8,0},{9,1},... | collective-permute-start | bytes 393224 | tf_op jit(solution)/shard_map/ppermute | solution.py:161
  36.4 2.9 %collective-permute-start.35 = (f32[1,4,4,16,128]{4,3,2,1,0:T(8,128)S(1)}, f32[1,4,4,16,128]{4,3,2,1,0:T(8,128)S(1)}, u32[]{:S(2)}, u32[]{:S(2)}) collective-permute-start(f32[1,4,4,16,128]{4,3,2,1,0:T(8,128)S(1)} %get-tuple-element.69), channel_id=1, source_target_pairs={{0,4},{1,5},{2,6},{3,7},{4,0},{5,1},{6,2},{7,3},{8,12},{9,13},{10,... | collective-permute-start | bytes 393224 | tf_op jit(solution)/shard_map/ppermute | solution.py:161
  40.0 1.0 %collective-permute-start.51 = (f32[4,1,4,16,128]{4,3,2,0,1:T(8,128)S(1)}, f32[4,1,4,16,128]{4,3,2,0,1:T(8,128)S(1)}, u32[]{:S(2)}, u32[]{:S(2)}) collective-permute-start(f32[4,1,4,16,128]{4,3,2,0,1:T(8,128)S(1)} %get-tuple-element.48), channel_id=1, source_target_pairs={{0,2},{1,3},{2,0},{3,1},{4,6},{5,7},{6,4},{7,5},{8,10},{9,11},{10,... | collective-permute-start | bytes 393224 | tf_op jit(solution)/shard_map/ppermute | solution.py:161
  41.0 2.2 %collective-permute-done.37 = f32[1,4,4,16,128]{4,3,2,1,0:T(8,128)S(1)} collective-permute-done((f32[1,4,4,16,128]{4,3,2,1,0:T(8,128)S(1)}, f32[1,4,4,16,128]{4,3,2,1,0:T(8,128)S(1)}, u32[]{:S(2)}, u32[]{:S(2)}) %collective-permute-start.37) | collective-permute-done | bytes 131104 | tf_op jit(solution)/shard_map/ppermute | solution.py:161
  43.2 5.6 %collective-permute-done.36 = f32[1,4,4,16,128]{4,3,2,1,0:T(8,128)S(1)} collective-permute-done((f32[1,4,4,16,128]{4,3,2,1,0:T(8,128)S(1)}, f32[1,4,4,16,128]{4,3,2,1,0:T(8,128)S(1)}, u32[]{:S(2)}, u32[]{:S(2)}) %collective-permute-start.36) | collective-permute-done | bytes 131104 | tf_op jit(solution)/shard_map/ppermute | solution.py:161
  48.9 1.3 %collective-permute-start.40 = (f32[4,1,4,16,128]{4,3,2,0,1:T(8,128)S(1)}, f32[4,1,4,16,128]{4,3,2,0,1:T(8,128)S(1)}, u32[]{:S(2)}, u32[]{:S(2)}) collective-permute-start(f32[4,1,4,16,128]{4,3,2,0,1:T(8,128)S(1)} %get-tuple-element.63), channel_id=1, source_target_pairs={{0,3},{1,2},{2,1},{3,0},{4,7},{5,6},{6,5},{7,4},{8,11},{9,10},{10,... | collective-permute-start | bytes 393224 | tf_op jit(solution)/shard_map/ppermute | solution.py:161
  51.6 1.0 %move.3 = f32[16,4,16,128]{3,2,1,0:T(8,128)S(1)} custom-call(s32[1]{0:T(128)} %bitcast.rank, s32[16]{0:T(128)S(1)} %copy-done.4, s32[16]{0:T(128)S(1)} %copy-done.5, f32[16,4,16,128]{3,2,1,0:T(8,128)S(1)} %bitcast.150), custom_call_target="tpu_custom_call" | custom-call | tf_op jit(solution)/shard_map/move/pallas_call | solution.py:384
  52.6 1.3 %collective-permute-start.55 = (f32[1,4,4,16,128]{4,3,2,1,0:T(8,128)S(1)}, f32[1,4,4,16,128]{4,3,2,1,0:T(8,128)S(1)}, u32[]{:S(2)}, u32[]{:S(2)}) collective-permute-start(f32[1,4,4,16,128]{4,3,2,1,0:T(8,128)S(1)} %get-tuple-element.43), channel_id=1, source_target_pairs={{0,12},{1,13},{2,14},{3,15},{4,8},{5,9},{6,10},{7,11},{8,4},{9,5},... | collective-permute-start | bytes 393224 | tf_op jit(solution)/shard_map/ppermute | solution.py:161
  54.8 2.3 %collective-permute-start.53 = (f32[1,4,4,16,128]{4,3,2,1,0:T(8,128)S(1)}, f32[1,4,4,16,128]{4,3,2,1,0:T(8,128)S(1)}, u32[]{:S(2)}, u32[]{:S(2)}) collective-permute-start(f32[1,4,4,16,128]{4,3,2,1,0:T(8,128)S(1)} %get-tuple-element.45), channel_id=1, source_target_pairs={{0,4},{1,5},{2,6},{3,7},{4,0},{5,1},{6,2},{7,3},{8,12},{9,13},{10,... | collective-permute-start | bytes 393224 | tf_op jit(solution)/shard_map/ppermute | solution.py:161
  57.6 1.0 %move.2 = f32[16,4,16,128]{3,2,1,0:T(8,128)S(1)} custom-call(s32[1]{0:T(128)} %bitcast.rank, s32[16]{0:T(128)S(1)} %copy-done.4, s32[16]{0:T(128)S(1)} %copy-done.5, f32[16,4,16,128]{3,2,1,0:T(8,128)S(1)} %bitcast.151), custom_call_target="tpu_custom_call" | custom-call | tf_op jit(solution)/shard_map/move/pallas_call | solution.py:384
  58.7 1.3 %collective-permute-start.43 = (f32[1,4,4,16,128]{4,3,2,1,0:T(8,128)S(1)}, f32[1,4,4,16,128]{4,3,2,1,0:T(8,128)S(1)}, u32[]{:S(2)}, u32[]{:S(2)}) collective-permute-start(f32[1,4,4,16,128]{4,3,2,1,0:T(8,128)S(1)} %get-tuple-element.59), channel_id=1, source_target_pairs={{0,12},{1,13},{2,14},{3,15},{4,8},{5,9},{6,10},{7,11},{8,4},{9,5},... | collective-permute-start | bytes 393224 | tf_op jit(solution)/shard_map/ppermute | solution.py:161
  59.9 1.0 %collective-permute-done.55 = f32[1,4,4,16,128]{4,3,2,1,0:T(8,128)S(1)} collective-permute-done((f32[1,4,4,16,128]{4,3,2,1,0:T(8,128)S(1)}, f32[1,4,4,16,128]{4,3,2,1,0:T(8,128)S(1)}, u32[]{:S(2)}, u32[]{:S(2)}) %collective-permute-start.55) | collective-permute-done | bytes 131104 | tf_op jit(solution)/shard_map/ppermute | solution.py:161
  60.9 2.2 %collective-permute-start.41 = (f32[1,4,4,16,128]{4,3,2,1,0:T(8,128)S(1)}, f32[1,4,4,16,128]{4,3,2,1,0:T(8,128)S(1)}, u32[]{:S(2)}, u32[]{:S(2)}) collective-permute-start(f32[1,4,4,16,128]{4,3,2,1,0:T(8,128)S(1)} %get-tuple-element.61), channel_id=1, source_target_pairs={{0,4},{1,5},{2,6},{3,7},{4,0},{5,1},{6,2},{7,3},{8,12},{9,13},{10,... | collective-permute-start | bytes 393224 | tf_op jit(solution)/shard_map/ppermute | solution.py:161
  63.1 3.5 %collective-permute-done.54 = f32[1,4,4,16,128]{4,3,2,1,0:T(8,128)S(1)} collective-permute-done((f32[1,4,4,16,128]{4,3,2,1,0:T(8,128)S(1)}, f32[1,4,4,16,128]{4,3,2,1,0:T(8,128)S(1)}, u32[]{:S(2)}, u32[]{:S(2)}) %collective-permute-start.54) | collective-permute-done | bytes 131104 | tf_op jit(solution)/shard_map/ppermute | solution.py:161
  66.8 1.4 %collective-permute-start.57 = (f32[4,1,4,16,128]{4,3,2,0,1:T(8,128)S(1)}, f32[4,1,4,16,128]{4,3,2,0,1:T(8,128)S(1)}, u32[]{:S(2)}, u32[]{:S(2)}) collective-permute-start(f32[4,1,4,16,128]{4,3,2,0,1:T(8,128)S(1)} %get-tuple-element.40), channel_id=1, source_target_pairs={{0,2},{1,3},{2,0},{3,1},{4,6},{5,7},{6,4},{7,5},{8,10},{9,11},{10,... | collective-permute-start | bytes 393224 | tf_op jit(solution)/shard_map/ppermute | solution.py:161
  68.2 1.2 %collective-permute-done.43 = f32[1,4,4,16,128]{4,3,2,1,0:T(8,128)S(1)} collective-permute-done((f32[1,4,4,16,128]{4,3,2,1,0:T(8,128)S(1)}, f32[1,4,4,16,128]{4,3,2,1,0:T(8,128)S(1)}, u32[]{:S(2)}, u32[]{:S(2)}) %collective-permute-start.43) | collective-permute-done | bytes 131104 | tf_op jit(solution)/shard_map/ppermute | solution.py:161
  69.4 7.5 %collective-permute-done.42 = f32[1,4,4,16,128]{4,3,2,1,0:T(8,128)S(1)} collective-permute-done((f32[1,4,4,16,128]{4,3,2,1,0:T(8,128)S(1)}, f32[1,4,4,16,128]{4,3,2,1,0:T(8,128)S(1)}, u32[]{:S(2)}, u32[]{:S(2)}) %collective-permute-start.42) | collective-permute-done | bytes 131104 | tf_op jit(solution)/shard_map/ppermute | solution.py:161
  77.0 1.0 %collective-permute-start.46 = (f32[4,1,4,16,128]{4,3,2,0,1:T(8,128)S(1)}, f32[4,1,4,16,128]{4,3,2,0,1:T(8,128)S(1)}, u32[]{:S(2)}, u32[]{:S(2)}) collective-permute-start(f32[4,1,4,16,128]{4,3,2,0,1:T(8,128)S(1)} %get-tuple-element.55), channel_id=1, source_target_pairs={{0,3},{1,2},{2,1},{3,0},{4,7},{5,6},{6,5},{7,4},{8,11},{9,10},{10,... | collective-permute-start | bytes 393224 | tf_op jit(solution)/shard_map/ppermute | solution.py:161
  79.0 3.7 %collective-permute-done.46 = f32[4,1,4,16,128]{4,3,2,0,1:T(8,128)S(1)} collective-permute-done((f32[4,1,4,16,128]{4,3,2,0,1:T(8,128)S(1)}, f32[4,1,4,16,128]{4,3,2,0,1:T(8,128)S(1)}, u32[]{:S(2)}, u32[]{:S(2)}) %collective-permute-start.46) | collective-permute-done | bytes 131104 | tf_op jit(solution)/shard_map/ppermute | solution.py:161
  82.7 3.0 %collective-permute-done.45 = f32[4,1,4,16,128]{4,3,2,0,1:T(8,128)S(1)} collective-permute-done((f32[4,1,4,16,128]{4,3,2,0,1:T(8,128)S(1)}, f32[4,1,4,16,128]{4,3,2,0,1:T(8,128)S(1)}, u32[]{:S(2)}, u32[]{:S(2)}) %collective-permute-start.45) | collective-permute-done | bytes 131104 | tf_op jit(solution)/shard_map/ppermute | solution.py:161
  85.7 1.0 %join.1 = (f32[7,16,16,128]{3,2,1,0:T(8,128)}, f32[16,16,128]{2,1,0:T(8,128)}) custom-call(s32[1]{0:T(128)} %bitcast.rank, f32[16,4,16,128]{3,2,1,0:T(8,128)S(1)} %bitcast.147, f32[16,4,16,128]{3,2,1,0:T(8,128)S(1)} %bitcast.146), custom_call_target="tpu_custom_call" | custom-call | tf_op jit(solution)/shard_map/join/pallas_call | solution.py:138
  (69 shorter events, 6.8 us)
Async XLA Ops:
  0.6 1.2 %copy-start = (f32[7,16,16,128]{3,2,1,0:T(8,128)S(1)}, f32[7,16,16,128]{3,2,1,0:T(8,128)}, u32[]{:S(2)}) copy-start(f32[7,16,16,128]{3,2,1,0:T(8,128)} %fields.3) | copy-start | bytes 2752516
  2.9 7.0 %collective-permute-start.33 = (f32[10,16,128]{2,1,0:T(8,128)S(1)}, f32[10,16,128]{2,1,0:T(8,128)S(1)}, u32[]{:S(2)}, u32[]{:S(2)}) collective-permute-start(f32[10,16,128]{2,1,0:T(8,128)S(1)} %get-tuple-element.74), channel_id=1, source_target_pairs={{0,1},{1,0},{2,3},{3,2},{4,5},{5,4},{6,7},{7,6},{8,9},{9,8},{10,11... | collective-permute-start | bytes 245768 | tf_op jit(solution)/shard_map/ppermute | solution.py:401
  3.4 7.8 %collective-permute-start.32 = (f32[10,16,128]{2,1,0:T(8,128)S(1)}, f32[10,16,128]{2,1,0:T(8,128)S(1)}, u32[]{:S(2)}, u32[]{:S(2)}) collective-permute-start(f32[10,16,128]{2,1,0:T(8,128)S(1)} %get-tuple-element.75), channel_id=1, source_target_pairs={{0,15},{1,2},{2,1},{3,4},{4,3},{5,6},{6,5},{7,8},{8,7},{9,10},{10,... | collective-permute-start | bytes 245768 | tf_op jit(solution)/shard_map/ppermute | solution.py:400
  9.8 20.8 %copy-start.1 = (f32[7,16,16,128]{3,2,1,0:T(8,128)S(1)}, f32[7,16,16,128]{3,2,1,0:T(8,128)}, u32[]{:S(2)}) copy-start(f32[7,16,16,128]{3,2,1,0:T(8,128)} %fields.3) | copy-start | bytes 2752516
  11.3 19.2 %collective-permute-start.34 = (f32[11,16,128]{2,1,0:T(8,128)S(1)}, f32[11,16,128]{2,1,0:T(8,128)S(1)}, u32[]{:S(2)}, u32[]{:S(2)}) collective-permute-start(f32[11,16,128]{2,1,0:T(8,128)S(1)} %get-tuple-element.71), channel_id=1, source_target_pairs={{0,16},{16,0},{1,17},{17,1},{2,18},{18,2},{3,19},{19,3},{4,20},{20... | collective-permute-start | bytes 270344 | tf_op jit(solution)/shard_map/ppermute | solution.py:429
  12.9 17.7 %copy-start.3 = (f32[16,16,128]{2,1,0:T(8,128)S(1)}, f32[16,16,128]{2,1,0:T(8,128)}, u32[]{:S(2)}) copy-start(f32[16,16,128]{2,1,0:T(8,128)} %density.3) | copy-start | bytes 393220
  12.9 23.5 %collective-permute-start.49 = (f32[1,4,4,16,128]{4,3,2,1,0:T(8,128)S(1)}, f32[1,4,4,16,128]{4,3,2,1,0:T(8,128)S(1)}, u32[]{:S(2)}, u32[]{:S(2)}) collective-permute-start(f32[1,4,4,16,128]{4,3,2,1,0:T(8,128)S(1)} %get-tuple-element.51), channel_id=1, source_target_pairs={{0,12},{1,13},{2,14},{3,15},{4,8},{5,9},{6,10},{7,11},{8,4},{9,5},... | collective-permute-start | bytes 393224 | tf_op jit(solution)/shard_map/ppermute | solution.py:161
  14.8 24.6 %collective-permute-start.48 = (f32[1,4,4,16,128]{4,3,2,1,0:T(8,128)S(1)}, f32[1,4,4,16,128]{4,3,2,1,0:T(8,128)S(1)}, u32[]{:S(2)}, u32[]{:S(2)}) collective-permute-start(f32[1,4,4,16,128]{4,3,2,1,0:T(8,128)S(1)} %get-tuple-element.52), channel_id=1, source_target_pairs={{0,8},{1,9},{2,10},{3,11},{4,12},{5,13},{6,14},{7,15},{8,0},{9,1},... | collective-permute-start | bytes 393224 | tf_op jit(solution)/shard_map/ppermute | solution.py:161
  14.8 8.7 %collective-permute-start.23 = (f32[11,16,128]{2,1,0:T(8,128)S(1)}, f32[11,16,128]{2,1,0:T(8,128)}, u32[]{:S(2)}, u32[]{:S(2)}) collective-permute-start(f32[11,16,128]{2,1,0:T(8,128)S(1)} %param.11), channel_id=1, source_target_pairs={{16,12},{17,13},{18,14},{19,15},{20,0},{21,1},{22,2},{23,3},{24,4}... | collective-permute-start | bytes 270344 | tf_op jit(solution)/shard_map/cond/branch_11_fun/ppermute | solution.py:417
  17.4 7.1 %collective-permute-start.22 = (f32[11,16,128]{2,1,0:T(8,128)S(1)}, f32[11,16,128]{2,1,0:T(8,128)}, u32[]{:S(2)}, u32[]{:S(2)}) collective-permute-start(f32[11,16,128]{2,1,0:T(8,128)S(1)} %param.11), channel_id=1, source_target_pairs={{16,11},{17,12},{18,13},{19,14},{20,15},{21,0},{22,1},{23,2},{24,3... | collective-permute-start | bytes 270344 | tf_op jit(solution)/shard_map/cond/branch_11_fun/ppermute | solution.py:417
  24.4 14.9 %collective-permute-start.47 = (f32[1,4,4,16,128]{4,3,2,1,0:T(8,128)S(1)}, f32[1,4,4,16,128]{4,3,2,1,0:T(8,128)S(1)}, u32[]{:S(2)}, u32[]{:S(2)}) collective-permute-start(f32[1,4,4,16,128]{4,3,2,1,0:T(8,128)S(1)} %get-tuple-element.53), channel_id=1, source_target_pairs={{0,4},{1,5},{2,6},{3,7},{4,0},{5,1},{6,2},{7,3},{8,12},{9,13},{10,... | collective-permute-start | bytes 393224 | tf_op jit(solution)/shard_map/ppermute | solution.py:161
  34.9 8.3 %collective-permute-start.37 = (f32[1,4,4,16,128]{4,3,2,1,0:T(8,128)S(1)}, f32[1,4,4,16,128]{4,3,2,1,0:T(8,128)S(1)}, u32[]{:S(2)}, u32[]{:S(2)}) collective-permute-start(f32[1,4,4,16,128]{4,3,2,1,0:T(8,128)S(1)} %get-tuple-element.67), channel_id=1, source_target_pairs={{0,12},{1,13},{2,14},{3,15},{4,8},{5,9},{6,10},{7,11},{8,4},{9,5},... | collective-permute-start | bytes 393224 | tf_op jit(solution)/shard_map/ppermute | solution.py:161
  35.0 13.9 %collective-permute-start.36 = (f32[1,4,4,16,128]{4,3,2,1,0:T(8,128)S(1)}, f32[1,4,4,16,128]{4,3,2,1,0:T(8,128)S(1)}, u32[]{:S(2)}, u32[]{:S(2)}) collective-permute-start(f32[1,4,4,16,128]{4,3,2,1,0:T(8,128)S(1)} %get-tuple-element.68), channel_id=1, source_target_pairs={{0,8},{1,9},{2,10},{3,11},{4,12},{5,13},{6,14},{7,15},{8,0},{9,1},... | collective-permute-start | bytes 393224 | tf_op jit(solution)/shard_map/ppermute | solution.py:161
  36.4 12.4 %collective-permute-start.35 = (f32[1,4,4,16,128]{4,3,2,1,0:T(8,128)S(1)}, f32[1,4,4,16,128]{4,3,2,1,0:T(8,128)S(1)}, u32[]{:S(2)}, u32[]{:S(2)}) collective-permute-start(f32[1,4,4,16,128]{4,3,2,1,0:T(8,128)S(1)} %get-tuple-element.69), channel_id=1, source_target_pairs={{0,4},{1,5},{2,6},{3,7},{4,0},{5,1},{6,2},{7,3},{8,12},{9,13},{10,... | collective-permute-start | bytes 393224 | tf_op jit(solution)/shard_map/ppermute | solution.py:161
  39.4 11.0 %collective-permute-start.52 = (f32[4,1,4,16,128]{4,3,2,0,1:T(8,128)S(1)}, f32[4,1,4,16,128]{4,3,2,0,1:T(8,128)S(1)}, u32[]{:S(2)}, u32[]{:S(2)}) collective-permute-start(f32[4,1,4,16,128]{4,3,2,0,1:T(8,128)S(1)} %get-tuple-element.47), channel_id=1, source_target_pairs={{0,3},{1,2},{2,1},{3,0},{4,7},{5,6},{6,5},{7,4},{8,11},{9,10},{10,... | collective-permute-start | bytes 393224 | tf_op jit(solution)/shard_map/ppermute | solution.py:161
  40.0 10.8 %collective-permute-start.51 = (f32[4,1,4,16,128]{4,3,2,0,1:T(8,128)S(1)}, f32[4,1,4,16,128]{4,3,2,0,1:T(8,128)S(1)}, u32[]{:S(2)}, u32[]{:S(2)}) collective-permute-start(f32[4,1,4,16,128]{4,3,2,0,1:T(8,128)S(1)} %get-tuple-element.48), channel_id=1, source_target_pairs={{0,2},{1,3},{2,0},{3,1},{4,6},{5,7},{6,4},{7,5},{8,10},{9,11},{10,... | collective-permute-start | bytes 393224 | tf_op jit(solution)/shard_map/ppermute | solution.py:161
  43.2 7.6 %collective-permute-start.50 = (f32[4,1,4,16,128]{4,3,2,0,1:T(8,128)S(1)}, f32[4,1,4,16,128]{4,3,2,0,1:T(8,128)S(1)}, u32[]{:S(2)}, u32[]{:S(2)}) collective-permute-start(f32[4,1,4,16,128]{4,3,2,0,1:T(8,128)S(1)} %get-tuple-element.49), channel_id=1, source_target_pairs={{0,1},{1,0},{2,3},{3,2},{4,5},{5,4},{6,7},{7,6},{8,9},{9,8},{10,11... | collective-permute-start | bytes 393224 | tf_op jit(solution)/shard_map/ppermute | solution.py:161
  48.9 5.9 %collective-permute-start.40 = (f32[4,1,4,16,128]{4,3,2,0,1:T(8,128)S(1)}, f32[4,1,4,16,128]{4,3,2,0,1:T(8,128)S(1)}, u32[]{:S(2)}, u32[]{:S(2)}) collective-permute-start(f32[4,1,4,16,128]{4,3,2,0,1:T(8,128)S(1)} %get-tuple-element.63), channel_id=1, source_target_pairs={{0,3},{1,2},{2,1},{3,0},{4,7},{5,6},{6,5},{7,4},{8,11},{9,10},{10,... | collective-permute-start | bytes 393224 | tf_op jit(solution)/shard_map/ppermute | solution.py:161
  50.2 7.4 %collective-permute-start.39 = (f32[4,1,4,16,128]{4,3,2,0,1:T(8,128)S(1)}, f32[4,1,4,16,128]{4,3,2,0,1:T(8,128)S(1)}, u32[]{:S(2)}, u32[]{:S(2)}) collective-permute-start(f32[4,1,4,16,128]{4,3,2,0,1:T(8,128)S(1)} %get-tuple-element.64), channel_id=1, source_target_pairs={{0,2},{1,3},{2,0},{3,1},{4,6},{5,7},{6,4},{7,5},{8,10},{9,11},{10,... | collective-permute-start | bytes 393224 | tf_op jit(solution)/shard_map/ppermute | solution.py:161
  50.4 7.2 %collective-permute-start.38 = (f32[4,1,4,16,128]{4,3,2,0,1:T(8,128)S(1)}, f32[4,1,4,16,128]{4,3,2,0,1:T(8,128)S(1)}, u32[]{:S(2)}, u32[]{:S(2)}) collective-permute-start(f32[4,1,4,16,128]{4,3,2,0,1:T(8,128)S(1)} %get-tuple-element.65), channel_id=1, source_target_pairs={{0,1},{1,0},{2,3},{3,2},{4,5},{5,4},{6,7},{7,6},{8,9},{9,8},{10,11... | collective-permute-start | bytes 393224 | tf_op jit(solution)/shard_map/ppermute | solution.py:161
  52.6 8.3 %collective-permute-start.55 = (f32[1,4,4,16,128]{4,3,2,1,0:T(8,128)S(1)}, f32[1,4,4,16,128]{4,3,2,1,0:T(8,128)S(1)}, u32[]{:S(2)}, u32[]{:S(2)}) collective-permute-start(f32[1,4,4,16,128]{4,3,2,1,0:T(8,128)S(1)} %get-tuple-element.43), channel_id=1, source_target_pairs={{0,12},{1,13},{2,14},{3,15},{4,8},{5,9},{6,10},{7,11},{8,4},{9,5},... | collective-permute-start | bytes 393224 | tf_op jit(solution)/shard_map/ppermute | solution.py:161
  53.9 12.7 %collective-permute-start.54 = (f32[1,4,4,16,128]{4,3,2,1,0:T(8,128)S(1)}, f32[1,4,4,16,128]{4,3,2,1,0:T(8,128)S(1)}, u32[]{:S(2)}, u32[]{:S(2)}) collective-permute-start(f32[1,4,4,16,128]{4,3,2,1,0:T(8,128)S(1)} %get-tuple-element.44), channel_id=1, source_target_pairs={{0,8},{1,9},{2,10},{3,11},{4,12},{5,13},{6,14},{7,15},{8,0},{9,1},... | collective-permute-start | bytes 393224 | tf_op jit(solution)/shard_map/ppermute | solution.py:161
  54.8 11.8 %collective-permute-start.53 = (f32[1,4,4,16,128]{4,3,2,1,0:T(8,128)S(1)}, f32[1,4,4,16,128]{4,3,2,1,0:T(8,128)S(1)}, u32[]{:S(2)}, u32[]{:S(2)}) collective-permute-start(f32[1,4,4,16,128]{4,3,2,1,0:T(8,128)S(1)} %get-tuple-element.45), channel_id=1, source_target_pairs={{0,4},{1,5},{2,6},{3,7},{4,0},{5,1},{6,2},{7,3},{8,12},{9,13},{10,... | collective-permute-start | bytes 393224 | tf_op jit(solution)/shard_map/ppermute | solution.py:161
  58.7 10.7 %collective-permute-start.43 = (f32[1,4,4,16,128]{4,3,2,1,0:T(8,128)S(1)}, f32[1,4,4,16,128]{4,3,2,1,0:T(8,128)S(1)}, u32[]{:S(2)}, u32[]{:S(2)}) collective-permute-start(f32[1,4,4,16,128]{4,3,2,1,0:T(8,128)S(1)} %get-tuple-element.59), channel_id=1, source_target_pairs={{0,12},{1,13},{2,14},{3,15},{4,8},{5,9},{6,10},{7,11},{8,4},{9,5},... | collective-permute-start | bytes 393224 | tf_op jit(solution)/shard_map/ppermute | solution.py:161
  59.9 17.0 %collective-permute-start.42 = (f32[1,4,4,16,128]{4,3,2,1,0:T(8,128)S(1)}, f32[1,4,4,16,128]{4,3,2,1,0:T(8,128)S(1)}, u32[]{:S(2)}, u32[]{:S(2)}) collective-permute-start(f32[1,4,4,16,128]{4,3,2,1,0:T(8,128)S(1)} %get-tuple-element.60), channel_id=1, source_target_pairs={{0,8},{1,9},{2,10},{3,11},{4,12},{5,13},{6,14},{7,15},{8,0},{9,1},... | collective-permute-start | bytes 393224 | tf_op jit(solution)/shard_map/ppermute | solution.py:161
  60.9 16.0 %collective-permute-start.41 = (f32[1,4,4,16,128]{4,3,2,1,0:T(8,128)S(1)}, f32[1,4,4,16,128]{4,3,2,1,0:T(8,128)S(1)}, u32[]{:S(2)}, u32[]{:S(2)}) collective-permute-start(f32[1,4,4,16,128]{4,3,2,1,0:T(8,128)S(1)} %get-tuple-element.61), channel_id=1, source_target_pairs={{0,4},{1,5},{2,6},{3,7},{4,0},{5,1},{6,2},{7,3},{8,12},{9,13},{10,... | collective-permute-start | bytes 393224 | tf_op jit(solution)/shard_map/ppermute | solution.py:161
  66.7 12.0 %collective-permute-start.58 = (f32[4,1,4,16,128]{4,3,2,0,1:T(8,128)S(1)}, f32[4,1,4,16,128]{4,3,2,0,1:T(8,128)S(1)}, u32[]{:S(2)}, u32[]{:S(2)}) collective-permute-start(f32[4,1,4,16,128]{4,3,2,0,1:T(8,128)S(1)} %get-tuple-element.39), channel_id=1, source_target_pairs={{0,3},{1,2},{2,1},{3,0},{4,7},{5,6},{6,5},{7,4},{8,11},{9,10},{10,... | collective-permute-start | bytes 393224 | tf_op jit(solution)/shard_map/ppermute | solution.py:161
  66.8 12.1 %collective-permute-start.57 = (f32[4,1,4,16,128]{4,3,2,0,1:T(8,128)S(1)}, f32[4,1,4,16,128]{4,3,2,0,1:T(8,128)S(1)}, u32[]{:S(2)}, u32[]{:S(2)}) collective-permute-start(f32[4,1,4,16,128]{4,3,2,0,1:T(8,128)S(1)} %get-tuple-element.40), channel_id=1, source_target_pairs={{0,2},{1,3},{2,0},{3,1},{4,6},{5,7},{6,4},{7,5},{8,10},{9,11},{10,... | collective-permute-start | bytes 393224 | tf_op jit(solution)/shard_map/ppermute | solution.py:161
  69.4 9.5 %collective-permute-start.56 = (f32[4,1,4,16,128]{4,3,2,0,1:T(8,128)S(1)}, f32[4,1,4,16,128]{4,3,2,0,1:T(8,128)S(1)}, u32[]{:S(2)}, u32[]{:S(2)}) collective-permute-start(f32[4,1,4,16,128]{4,3,2,0,1:T(8,128)S(1)} %get-tuple-element.41), channel_id=1, source_target_pairs={{0,1},{1,0},{2,3},{3,2},{4,5},{5,4},{6,7},{7,6},{8,9},{9,8},{10,11... | collective-permute-start | bytes 393224 | tf_op jit(solution)/shard_map/ppermute | solution.py:161
  77.0 5.7 %collective-permute-start.46 = (f32[4,1,4,16,128]{4,3,2,0,1:T(8,128)S(1)}, f32[4,1,4,16,128]{4,3,2,0,1:T(8,128)S(1)}, u32[]{:S(2)}, u32[]{:S(2)}) collective-permute-start(f32[4,1,4,16,128]{4,3,2,0,1:T(8,128)S(1)} %get-tuple-element.55), channel_id=1, source_target_pairs={{0,3},{1,2},{2,1},{3,0},{4,7},{5,6},{6,5},{7,4},{8,11},{9,10},{10,... | collective-permute-start | bytes 393224 | tf_op jit(solution)/shard_map/ppermute | solution.py:161
  78.0 7.6 %collective-permute-start.45 = (f32[4,1,4,16,128]{4,3,2,0,1:T(8,128)S(1)}, f32[4,1,4,16,128]{4,3,2,0,1:T(8,128)S(1)}, u32[]{:S(2)}, u32[]{:S(2)}) collective-permute-start(f32[4,1,4,16,128]{4,3,2,0,1:T(8,128)S(1)} %get-tuple-element.56), channel_id=1, source_target_pairs={{0,2},{1,3},{2,0},{3,1},{4,6},{5,7},{6,4},{7,5},{8,10},{9,11},{10,... | collective-permute-start | bytes 393224 | tf_op jit(solution)/shard_map/ppermute | solution.py:161
  78.7 6.9 %collective-permute-start.44 = (f32[4,1,4,16,128]{4,3,2,0,1:T(8,128)S(1)}, f32[4,1,4,16,128]{4,3,2,0,1:T(8,128)S(1)}, u32[]{:S(2)}, u32[]{:S(2)}) collective-permute-start(f32[4,1,4,16,128]{4,3,2,0,1:T(8,128)S(1)} %get-tuple-element.57), channel_id=1, source_target_pairs={{0,1},{1,0},{2,3},{3,2},{4,5},{5,4},{6,7},{7,6},{8,9},{9,8},{10,11... | collective-permute-start | bytes 393224 | tf_op jit(solution)/shard_map/ppermute | solution.py:161
  (3 other events, 2.2 us)

commit v6 on v5

--- a/solution.py
+++ b/solution.py
@@ -112,15 +112,10 @@
     slots, share = still.shape[0], still.shape[1]
     for slot in range(slots):
         for item in range(share):
+            column, row = pair_of(slot, item, share, quantities)
+            new_fields[6 if row == 3 else row, column] = moving[slot, item]
             column, row = pair_of(lax.bitwise_xor(rank[0], slot), item, share, quantities)
-            if isinstance(row, int):
-                new_fields[6 if row == 3 else row, column] = moving[slot, item]
-                if row == 0:
-                    new_density[column] = still[slot, item]
-                else:
-                    new_fields[2 + row, column] = still[slot, item]
-            else:
-                new_fields[jnp.where(row == 3, 6, row), column] = moving[slot, item]
+            if not isinstance(row, int):
 
                 @pl.when(row == 0)
                 def _():
@@ -129,6 +124,11 @@
                 @pl.when(row > 0)
                 def _():
                     new_fields[2 + row, column] = still[slot, item]
+
+            elif row == 0:
+                new_density[column] = still[slot, item]
+            else:
+                new_fields[2 + row, column] = still[slot, item]
 
 
 def join(rank, moving, still, columns):
@@ -304,7 +304,7 @@
         vertical = (px[2, ghost], py[2, ghost, TOP:end], pzz[ghost])
         for axis in range(4):
             flat = column * 4 + axis
-            slot = lax.bitwise_xor(info[3], flat // share)
+            slot = flat // share
             if axis < 3:
                 force = slope(axis) + vertical_slope(vertical[axis])
                 out[slot, flat % share] = fields[axis, column] + force * inverse
@@ -341,7 +341,7 @@
     )(info, fields, density, *layers)
 
 
-def move_kernel(quantities, rank, shift, frac, gathered, out, twice):
+def move_kernel(quantities, mixed, rank, shift, frac, gathered, out, twice):
     slots, share, cells, depth = gathered.shape
     total = slots * cells
     me = rank[0]
@@ -353,7 +353,7 @@
 
         def lay(slot, carry):
             rows = gathered[slot, item]
-            spot = pl.multiple_of(TOP + lax.bitwise_xor(me, slot) * cells, TOP)
+            spot = pl.multiple_of(TOP + (lax.bitwise_xor(me, slot) if mixed else slot) * cells, TOP)
             twice[item, pl.ds(spot, cells)] = rows
             twice[item, pl.ds(pl.multiple_of(spot + total, TOP), cells)] = rows
             return carry
@@ -362,7 +362,7 @@
         twice[item, 0:TOP] = twice[item, total : total + TOP]
 
         def blend(slot, carry):
-            spot = start + lax.bitwise_xor(me, slot) * cells
+            spot = start + (lax.bitwise_xor(me, slot) if mixed else slot) * cells
             back_two = twice[item, pl.ds(spot - 2, cells)]
             back_one = twice[item, pl.ds(spot - 1, cells)]
             centre = twice[item, pl.ds(spot, cells)]
@@ -377,12 +377,12 @@
         lax.fori_loop(0, slots, blend, 0, unroll=4)
 
 
-def move_columns(gathered, quantities, rank, shift_int, frac_num):
+def move_columns(gathered, quantities, mixed, rank, shift_int, frac_num):
     azimuths, share, cells, depth = gathered.shape
     smem = pl.BlockSpec(memory_space=pltpu.SMEM)
     vmem = pl.BlockSpec(memory_space=pltpu.VMEM)
     return pl.pallas_call(
-        functools.partial(move_kernel, quantities),
+        functools.partial(move_kernel, quantities, mixed),
         out_shape=jax.ShapeDtypeStruct(gathered.shape, jnp.float32),
         in_specs=[smem, smem, smem, vmem],
         out_specs=vmem,
@@ -459,9 +459,10 @@
         ]
     )
     moving = updated_columns(info, fields, density, head, tail, before, after, *layers)
-    moving = swap(moving)
-    still = swap(move_columns(still, 4, rank, shift_int, frac_num))
-    moving = swap(move_columns(moving, 4, rank, shift_int, frac_num))
+    moving = lax.all_to_all(moving, "az", 0, 0, tiled=True)
+    still = swap(move_columns(still, 4, True, rank, shift_int, frac_num))
+    moving = move_columns(moving, 4, False, rank, shift_int, frac_num)
+    moving = lax.all_to_all(moving, "az", 0, 0, tiled=True)
     return join(rank, moving, still, columns)
 
 

time: 86.9 us -> 106 us (1.22)
  waiting for transfers between devices: 37.5 us -> 58.6 us
  starting transfers between devices: 36.7 us -> 33.9 us
  Pallas kernels: 7.45 us -> 8.99 us
    ppermute x24 -> x12, waiting for transfers between devices: 29.1 us -> 49.8 us  [swap(): parts.append(lax.ppermute(cut[:, step], 'az', pairs))]
    ppermute x24 -> x12, starting transfers between devices: 26.4 us -> 12.8 us  [swap(): parts.append(lax.ppermute(cut[:, step], 'az', pairs))]
    all_to_all x0 -> x2, starting transfers between devices: none -> 12.9 us  [local(): moving = lax.all_to_all(moving, 'az', 0, 0, tiled=True)]
    ppermute x2, starting transfers between devices: 2.6 us -> 0.47 us  [wrap(): return lax.ppermute(data, ('rad', 'az'), pairs)]
  transfers between devices with their start and end apart: 29 -> 19, of which waited for: 13 -> 9; matrix products, arithmetic and copies ran while one was open for 1% -> 0% of each run, Pallas kernels for 7% -> 3%
where the time goes in v6:
time: 106 us
  waiting for transfers between devices  58.6 us (55%)
  starting transfers between devices  33.9 us (32%)
  Pallas kernels  8.99 us (8%)
  local copies, waits for them, and re-layouts  2.27 us (2%)
  between operations  1.52 us (1%)
    ppermute x12, waiting for transfers between devices, swap(): parts.append(lax.ppermute(cut[:, step], 'az', pairs))  49.8 us
    all_to_all x2, starting transfers between devices, local(): moving = lax.all_to_all(moving, 'az', 0, 0, tiled=True)  12.9 us
    ppermute x12, starting transfers between devices, swap(): parts.append(lax.ppermute(cut[:, step], 'az', pairs))  12.8 us
    ppermute x2, waiting for transfers between devices, wrap(): return lax.ppermute(data, ('rad', 'az'), pairs)  7.42 us
    ppermute x1, starting transfers between devices, azimuthal_layers(): far = lax.ppermute(jnp.where(even, head, tail), 'az', outer)  5.67 us
    pallas_call x1, Pallas kernels, updated_columns(): pl.pallas_call(stress_kernel, out_shape=jax.ShapeDtypeStruct((slots, 4 *...  5.05 us
    pallas_call x2, Pallas kernels, move_columns(): pl.pallas_call(functools.partial(move_kernel, quantities, mixed), out_sha...  2.75 us
  transfers between devices with their start and end apart: 19, of which 9 were waited for; matrix products, arithmetic and copies ran while one was open for 0% of the time, Pallas kernels for 3%

profile of v6, /device:TPU:0, one launch (start us, length us, event | category | flops | bytes accessed | tf_op | source)
XLA Modules:
  0.0 105.6 jit_solution(427812552383841205)
XLA Ops:
  0.7 1.2 %copy-done = f32[7,16,16,128]{3,2,1,0:T(8,128)S(1)} copy-done((f32[7,16,16,128]{3,2,1,0:T(8,128)S(1)}, f32[7,16,16,128]{3,2,1,0:T(8,128)}, u32[]{:S(2)}) %copy-start) | copy-done | bytes 917528
  1.8 0.9 copy-done.2
  2.9 0.5 collective-permute-start.33
  3.4 5.7 %collective-permute-start.32 = (f32[10,16,128]{2,1,0:T(8,128)S(1)}, f32[10,16,128]{2,1,0:T(8,128)S(1)}, u32[]{:S(2)}, u32[]{:S(2)}) collective-permute-start(f32[10,16,128]{2,1,0:T(8,128)S(1)} %get-tuple-element.59), channel_id=1, source_target_pairs={{0,15},{1,2},{2,1},{3,4},{4,3},{5,6},{6,5},{7,8},{8,7},{9,10},{10,... | collective-permute-start | bytes 245768 | tf_op jit(solution)/shard_map/ppermute | solution.py:400
  9.8 1.4 %collective-permute-done.32 = f32[10,16,128]{2,1,0:T(8,128)S(1)} collective-permute-done((f32[10,16,128]{2,1,0:T(8,128)S(1)}, f32[10,16,128]{2,1,0:T(8,128)S(1)}, u32[]{:S(2)}, u32[]{:S(2)}) %collective-permute-start.32) | collective-permute-done | bytes 81952 | tf_op jit(solution)/shard_map/ppermute | solution.py:400
  11.3 1.6 %collective-permute-start.34 = (f32[11,16,128]{2,1,0:T(8,128)S(1)}, f32[11,16,128]{2,1,0:T(8,128)S(1)}, u32[]{:S(2)}, u32[]{:S(2)}) collective-permute-start(f32[11,16,128]{2,1,0:T(8,128)S(1)} %get-tuple-element.55), channel_id=1, source_target_pairs={{0,16},{16,0},{1,17},{17,1},{2,18},{18,2},{3,19},{19,3},{4,20},{20... | collective-permute-start | bytes 270344 | tf_op jit(solution)/shard_map/ppermute | solution.py:429
  13.0 7.9 %conditional.1 = (f32[11,16,128]{2,1,0:T(8,128)}, f32[11,16,128]{2,1,0:T(8,128)}) conditional(s32[]{:T(128)} %clamp.3, f32[11,16,128]{2,1,0:T(8,128)S(1)} %get-tuple-element.54, f32[11,16,128]{2,1,0:T(8,128)S(1)} %get-tuple-element.54, f32[11,16,128]{2,1,0:T(8,128)S(1)} %get-tuple-element.54, ...), branch_computations={%region_0.1_spmd, %region_1.2_spmd, %region_2.3_spmd, %region_3.4_... | conditional | bytes 720992 | solution.py:437
  13.0 0.4 collective-permute-start.18
  13.5 7.4 %collective-permute-done.19 = f32[11,16,128]{2,1,0:T(8,128)} collective-permute-done((f32[11,16,128]{2,1,0:T(8,128)S(1)}, f32[11,16,128]{2,1,0:T(8,128)}, u32[]{:S(2)}, u32[]{:S(2)}) %collective-permute-start.19) | collective-permute-done | bytes 90144 | tf_op jit(solution)/shard_map/cond/branch_9_fun/ppermute | solution.py:417
  20.9 5.1 %stress_update.1 = f32[16,4,16,128]{3,2,1,0:T(8,128)} custom-call(s32[4]{0:T(128)S(1)} %pad_add_fusion.info, f32[7,16,16,128]{3,2,1,0:T(8,128)S(1)} %copy-done.1, f32[16,16,128]{2,1,0:T(8,128)S(1)} %copy-done.3, f32[10,16,128]{2,1,0:T(8,128)S(1)} %get-tuple-element.28.head, f32[10,16,128]{2,1,0:T(8,128)S(1)} %get-tuple-element.29.tail, ...), custom_call_target="tpu_custom_call" | custom-call | tf_op jit(solution)/shard_map/stress_update/pallas_call | solution.py:325
  26.0 9.2 %all-to-all-start = ((f32[16,4,16,128]{3,2,1,0:T(8,128)}), f32[16,4,16,128]{3,2,1,0:T(8,128)S(1)}, u32[]{:S(2)}, u32[]{:S(2)}) async-start(f32[16,4,16,128]{3,2,1,0:T(8,128)} %stress_update.1), calls=%async_computation | async-start | bytes 1048576 | tf_op jit(solution)/shard_map/all_to_all | solution.py:462
  35.2 3.8 %collective-permute-start.37 = (f32[1,4,4,16,128]{4,3,2,1,0:T(8,128)S(1)}, f32[1,4,4,16,128]{4,3,2,1,0:T(8,128)S(1)}, u32[]{:S(2)}, u32[]{:S(2)}) collective-permute-start(f32[1,4,4,16,128]{4,3,2,1,0:T(8,128)S(1)} %get-tuple-element.51), channel_id=1, source_target_pairs={{0,12},{1,13},{2,14},{3,15},{4,8},{5,9},{6,10},{7,11},{8,4},{9,5},... | collective-permute-start | bytes 393224 | tf_op jit(solution)/shard_map/ppermute | solution.py:161
  39.0 0.7 collective-permute-start.35
  39.6 12.4 %collective-permute-done.37 = f32[1,4,4,16,128]{4,3,2,1,0:T(8,128)S(1)} collective-permute-done((f32[1,4,4,16,128]{4,3,2,1,0:T(8,128)S(1)}, f32[1,4,4,16,128]{4,3,2,1,0:T(8,128)S(1)}, u32[]{:S(2)}, u32[]{:S(2)}) %collective-permute-start.37) | collective-permute-done | bytes 131104 | tf_op jit(solution)/shard_map/ppermute | solution.py:161
  52.0 9.7 %collective-permute-done.36 = f32[1,4,4,16,128]{4,3,2,1,0:T(8,128)S(1)} collective-permute-done((f32[1,4,4,16,128]{4,3,2,1,0:T(8,128)S(1)}, f32[1,4,4,16,128]{4,3,2,1,0:T(8,128)S(1)}, u32[]{:S(2)}, u32[]{:S(2)}) %collective-permute-start.36) | collective-permute-done | bytes 131104 | tf_op jit(solution)/shard_map/ppermute | solution.py:161
  61.8 0.8 collective-permute-start.40
  62.5 0.9 collective-permute-start.39
  63.4 0.3 collective-permute-start.38
  63.7 1.8 %move.2 = f32[16,4,16,128]{3,2,1,0:T(8,128)} custom-call(s32[1]{0:T(128)} %bitcast.rank, s32[16]{0:T(128)S(1)} %copy-done.4, s32[16]{0:T(128)S(1)} %copy-done.5, f32[16,4,16,128]{3,2,1,0:T(8,128)S(1)} %all-to-all-done.gathered), custom_call_target="tpu_custom_call" | custom-call | tf_op jit(solution)/shard_map/move/pallas_call | solution.py:384
  65.5 3.7 %all-to-all-start.1 = ((f32[16,4,16,128]{3,2,1,0:T(8,128)}), f32[16,4,16,128]{3,2,1,0:T(8,128)S(1)}, u32[]{:S(2)}, u32[]{:S(2)}) async-start(f32[16,4,16,128]{3,2,1,0:T(8,128)} %move.2), calls=%async_computation.1 | async-start | bytes 1048576 | tf_op jit(solution)/shard_map/all_to_all | solution.py:465
  69.2 1.3 %collective-permute-done.39 = f32[4,1,4,16,128]{4,3,2,0,1:T(8,128)S(1)} collective-permute-done((f32[4,1,4,16,128]{4,3,2,0,1:T(8,128)S(1)}, f32[4,1,4,16,128]{4,3,2,0,1:T(8,128)S(1)}, u32[]{:S(2)}, u32[]{:S(2)}) %collective-permute-start.39) | collective-permute-done | bytes 131104 | tf_op jit(solution)/shard_map/ppermute | solution.py:161
  70.5 1.0 move.3
  71.5 2.6 %collective-permute-start.43 = (f32[1,4,4,16,128]{4,3,2,1,0:T(8,128)S(1)}, f32[1,4,4,16,128]{4,3,2,1,0:T(8,128)S(1)}, u32[]{:S(2)}, u32[]{:S(2)}) collective-permute-start(f32[1,4,4,16,128]{4,3,2,1,0:T(8,128)S(1)} %get-tuple-element.43), channel_id=1, source_target_pairs={{0,12},{1,13},{2,14},{3,15},{4,8},{5,9},{6,10},{7,11},{8,4},{9,5},... | collective-permute-start | bytes 393224 | tf_op jit(solution)/shard_map/ppermute | solution.py:161
  74.1 1.9 %collective-permute-start.41 = (f32[1,4,4,16,128]{4,3,2,1,0:T(8,128)S(1)}, f32[1,4,4,16,128]{4,3,2,1,0:T(8,128)S(1)}, u32[]{:S(2)}, u32[]{:S(2)}) collective-permute-start(f32[1,4,4,16,128]{4,3,2,1,0:T(8,128)S(1)} %get-tuple-element.45), channel_id=1, source_target_pairs={{0,4},{1,5},{2,6},{3,7},{4,0},{5,1},{6,2},{7,3},{8,12},{9,13},{10,... | collective-permute-start | bytes 393224 | tf_op jit(solution)/shard_map/ppermute | solution.py:161
  76.0 10.1 %collective-permute-done.43 = f32[1,4,4,16,128]{4,3,2,1,0:T(8,128)S(1)} collective-permute-done((f32[1,4,4,16,128]{4,3,2,1,0:T(8,128)S(1)}, f32[1,4,4,16,128]{4,3,2,1,0:T(8,128)S(1)}, u32[]{:S(2)}, u32[]{:S(2)}) %collective-permute-start.43) | collective-permute-done | bytes 131104 | tf_op jit(solution)/shard_map/ppermute | solution.py:161
  86.0 9.7 %collective-permute-done.42 = f32[1,4,4,16,128]{4,3,2,1,0:T(8,128)S(1)} collective-permute-done((f32[1,4,4,16,128]{4,3,2,1,0:T(8,128)S(1)}, f32[1,4,4,16,128]{4,3,2,1,0:T(8,128)S(1)}, u32[]{:S(2)}, u32[]{:S(2)}) %collective-permute-start.42) | collective-permute-done | bytes 131104 | tf_op jit(solution)/shard_map/ppermute | solution.py:161
  95.8 0.8 collective-permute-start.46
  96.6 0.8 collective-permute-start.45
  97.4 0.3 collective-permute-start.44
  97.7 3.9 %collective-permute-done.46 = f32[4,1,4,16,128]{4,3,2,0,1:T(8,128)S(1)} collective-permute-done((f32[4,1,4,16,128]{4,3,2,0,1:T(8,128)S(1)}, f32[4,1,4,16,128]{4,3,2,0,1:T(8,128)S(1)}, u32[]{:S(2)}, u32[]{:S(2)}) %collective-permute-start.46) | collective-permute-done | bytes 131104 | tf_op jit(solution)/shard_map/ppermute | solution.py:161
  101.7 2.8 %collective-permute-done.45 = f32[4,1,4,16,128]{4,3,2,0,1:T(8,128)S(1)} collective-permute-done((f32[4,1,4,16,128]{4,3,2,0,1:T(8,128)S(1)}, f32[4,1,4,16,128]{4,3,2,0,1:T(8,128)S(1)}, u32[]{:S(2)}, u32[]{:S(2)}) %collective-permute-start.45) | collective-permute-done | bytes 131104 | tf_op jit(solution)/shard_map/ppermute | solution.py:161
  104.5 1.0 join.1
  (41 shorter events, 0.7 us)
Async XLA Ops:
  0.6 1.2 %copy-start = (f32[7,16,16,128]{3,2,1,0:T(8,128)S(1)}, f32[7,16,16,128]{3,2,1,0:T(8,128)}, u32[]{:S(2)}) copy-start(f32[7,16,16,128]{3,2,1,0:T(8,128)} %fields.3) | copy-start | bytes 2752516
  1.8 0.9 copy-start.2
  2.7 18.2 %copy-start.1 = (f32[7,16,16,128]{3,2,1,0:T(8,128)S(1)}, f32[7,16,16,128]{3,2,1,0:T(8,128)}, u32[]{:S(2)}) copy-start(f32[7,16,16,128]{3,2,1,0:T(8,128)} %fields.3) | copy-start | bytes 2752516
  2.9 6.9 %collective-permute-start.33 = (f32[10,16,128]{2,1,0:T(8,128)S(1)}, f32[10,16,128]{2,1,0:T(8,128)S(1)}, u32[]{:S(2)}, u32[]{:S(2)}) collective-permute-start(f32[10,16,128]{2,1,0:T(8,128)S(1)} %get-tuple-element.58), channel_id=1, source_target_pairs={{0,1},{1,0},{2,3},{3,2},{4,5},{5,4},{6,7},{7,6},{8,9},{9,8},{10,11... | collective-permute-start | bytes 245768 | tf_op jit(solution)/shard_map/ppermute | solution.py:401
  3.4 7.8 %collective-permute-start.32 = (f32[10,16,128]{2,1,0:T(8,128)S(1)}, f32[10,16,128]{2,1,0:T(8,128)S(1)}, u32[]{:S(2)}, u32[]{:S(2)}) collective-permute-start(f32[10,16,128]{2,1,0:T(8,128)S(1)} %get-tuple-element.59), channel_id=1, source_target_pairs={{0,15},{1,2},{2,1},{3,4},{4,3},{5,6},{6,5},{7,8},{8,7},{9,10},{10,... | collective-permute-start | bytes 245768 | tf_op jit(solution)/shard_map/ppermute | solution.py:400
  11.3 9.6 %copy-start.3 = (f32[16,16,128]{2,1,0:T(8,128)S(1)}, f32[16,16,128]{2,1,0:T(8,128)}, u32[]{:S(2)}) copy-start(f32[16,16,128]{2,1,0:T(8,128)} %density.3) | copy-start | bytes 393220
  11.3 9.5 %collective-permute-start.34 = (f32[11,16,128]{2,1,0:T(8,128)S(1)}, f32[11,16,128]{2,1,0:T(8,128)S(1)}, u32[]{:S(2)}, u32[]{:S(2)}) collective-permute-start(f32[11,16,128]{2,1,0:T(8,128)S(1)} %get-tuple-element.55), channel_id=1, source_target_pairs={{0,16},{16,0},{1,17},{17,1},{2,18},{18,2},{3,19},{19,3},{4,20},{20... | collective-permute-start | bytes 270344 | tf_op jit(solution)/shard_map/ppermute | solution.py:429
  13.0 7.9 %collective-permute-start.19 = (f32[11,16,128]{2,1,0:T(8,128)S(1)}, f32[11,16,128]{2,1,0:T(8,128)}, u32[]{:S(2)}, u32[]{:S(2)}) collective-permute-start(f32[11,16,128]{2,1,0:T(8,128)S(1)} %param.9), channel_id=1, source_target_pairs={{16,10},{17,11},{18,12},{19,13},{20,14},{21,15},{22,0},{23,1},{24,... | collective-permute-start | bytes 270344 | tf_op jit(solution)/shard_map/cond/branch_9_fun/ppermute | solution.py:417
  13.0 7.9 %collective-permute-start.18 = (f32[11,16,128]{2,1,0:T(8,128)S(1)}, f32[11,16,128]{2,1,0:T(8,128)}, u32[]{:S(2)}, u32[]{:S(2)}) collective-permute-start(f32[11,16,128]{2,1,0:T(8,128)S(1)} %param.9), channel_id=1, source_target_pairs={{16,9},{17,10},{18,11},{19,12},{20,13},{21,14},{22,15},{23,0},{24,... | collective-permute-start | bytes 270344 | tf_op jit(solution)/shard_map/cond/branch_9_fun/ppermute | solution.py:417
  26.0 37.8 %all-to-all-start = ((f32[16,4,16,128]{3,2,1,0:T(8,128)}), f32[16,4,16,128]{3,2,1,0:T(8,128)S(1)}, u32[]{:S(2)}, u32[]{:S(2)}) async-start(f32[16,4,16,128]{3,2,1,0:T(8,128)} %stress_update.1), calls=%async_computation | async-start | bytes 1048576 | tf_op jit(solution)/shard_map/all_to_all | solution.py:462
  35.2 16.8 %collective-permute-start.37 = (f32[1,4,4,16,128]{4,3,2,1,0:T(8,128)S(1)}, f32[1,4,4,16,128]{4,3,2,1,0:T(8,128)S(1)}, u32[]{:S(2)}, u32[]{:S(2)}) collective-permute-start(f32[1,4,4,16,128]{4,3,2,1,0:T(8,128)S(1)} %get-tuple-element.51), channel_id=1, source_target_pairs={{0,12},{1,13},{2,14},{3,15},{4,8},{5,9},{6,10},{7,11},{8,4},{9,5},... | collective-permute-start | bytes 393224 | tf_op jit(solution)/shard_map/ppermute | solution.py:161
  39.0 22.7 %collective-permute-start.36 = (f32[1,4,4,16,128]{4,3,2,1,0:T(8,128)S(1)}, f32[1,4,4,16,128]{4,3,2,1,0:T(8,128)S(1)}, u32[]{:S(2)}, u32[]{:S(2)}) collective-permute-start(f32[1,4,4,16,128]{4,3,2,1,0:T(8,128)S(1)} %get-tuple-element.52), channel_id=1, source_target_pairs={{0,8},{1,9},{2,10},{3,11},{4,12},{5,13},{6,14},{7,15},{8,0},{9,1},... | collective-permute-start | bytes 393224 | tf_op jit(solution)/shard_map/ppermute | solution.py:161
  39.0 22.7 %collective-permute-start.35 = (f32[1,4,4,16,128]{4,3,2,1,0:T(8,128)S(1)}, f32[1,4,4,16,128]{4,3,2,1,0:T(8,128)S(1)}, u32[]{:S(2)}, u32[]{:S(2)}) collective-permute-start(f32[1,4,4,16,128]{4,3,2,1,0:T(8,128)S(1)} %get-tuple-element.53), channel_id=1, source_target_pairs={{0,4},{1,5},{2,6},{3,7},{4,0},{5,1},{6,2},{7,3},{8,12},{9,13},{10,... | collective-permute-start | bytes 393224 | tf_op jit(solution)/shard_map/ppermute | solution.py:161
  61.8 7.4 %collective-permute-start.40 = (f32[4,1,4,16,128]{4,3,2,0,1:T(8,128)S(1)}, f32[4,1,4,16,128]{4,3,2,0,1:T(8,128)S(1)}, u32[]{:S(2)}, u32[]{:S(2)}) collective-permute-start(f32[4,1,4,16,128]{4,3,2,0,1:T(8,128)S(1)} %get-tuple-element.47), channel_id=1, source_target_pairs={{0,3},{1,2},{2,1},{3,0},{4,7},{5,6},{6,5},{7,4},{8,11},{9,10},{10,... | collective-permute-start | bytes 393224 | tf_op jit(solution)/shard_map/ppermute | solution.py:161
  62.5 1.2 %copy-start.4 = (s32[16]{0:T(128)S(1)}, s32[16]{0:T(128)}, u32[]{:S(2)}) copy-start(s32[16]{0:T(128)} %shift.3) | copy-start | bytes 196
  62.5 1.2 %copy-start.5 = (s32[16]{0:T(128)S(1)}, s32[16]{0:T(128)}, u32[]{:S(2)}) copy-start(s32[16]{0:T(128)} %frac.3) | copy-start | bytes 196
  62.5 7.9 %collective-permute-start.39 = (f32[4,1,4,16,128]{4,3,2,0,1:T(8,128)S(1)}, f32[4,1,4,16,128]{4,3,2,0,1:T(8,128)S(1)}, u32[]{:S(2)}, u32[]{:S(2)}) collective-permute-start(f32[4,1,4,16,128]{4,3,2,0,1:T(8,128)S(1)} %get-tuple-element.48), channel_id=1, source_target_pairs={{0,2},{1,3},{2,0},{3,1},{4,6},{5,7},{6,4},{7,5},{8,10},{9,11},{10,... | collective-permute-start | bytes 393224 | tf_op jit(solution)/shard_map/ppermute | solution.py:161
  63.4 7.0 %collective-permute-start.38 = (f32[4,1,4,16,128]{4,3,2,0,1:T(8,128)S(1)}, f32[4,1,4,16,128]{4,3,2,0,1:T(8,128)S(1)}, u32[]{:S(2)}, u32[]{:S(2)}) collective-permute-start(f32[4,1,4,16,128]{4,3,2,0,1:T(8,128)S(1)} %get-tuple-element.49), channel_id=1, source_target_pairs={{0,1},{1,0},{2,3},{3,2},{4,5},{5,4},{6,7},{7,6},{8,9},{9,8},{10,11... | collective-permute-start | bytes 393224 | tf_op jit(solution)/shard_map/ppermute | solution.py:161
  65.5 39.1 %all-to-all-start.1 = ((f32[16,4,16,128]{3,2,1,0:T(8,128)}), f32[16,4,16,128]{3,2,1,0:T(8,128)S(1)}, u32[]{:S(2)}, u32[]{:S(2)}) async-start(f32[16,4,16,128]{3,2,1,0:T(8,128)} %move.2), calls=%async_computation.1 | async-start | bytes 1048576 | tf_op jit(solution)/shard_map/all_to_all | solution.py:465
  71.5 14.5 %collective-permute-start.43 = (f32[1,4,4,16,128]{4,3,2,1,0:T(8,128)S(1)}, f32[1,4,4,16,128]{4,3,2,1,0:T(8,128)S(1)}, u32[]{:S(2)}, u32[]{:S(2)}) collective-permute-start(f32[1,4,4,16,128]{4,3,2,1,0:T(8,128)S(1)} %get-tuple-element.43), channel_id=1, source_target_pairs={{0,12},{1,13},{2,14},{3,15},{4,8},{5,9},{6,10},{7,11},{8,4},{9,5},... | collective-permute-start | bytes 393224 | tf_op jit(solution)/shard_map/ppermute | solution.py:161
  74.1 21.6 %collective-permute-start.42 = (f32[1,4,4,16,128]{4,3,2,1,0:T(8,128)S(1)}, f32[1,4,4,16,128]{4,3,2,1,0:T(8,128)S(1)}, u32[]{:S(2)}, u32[]{:S(2)}) collective-permute-start(f32[1,4,4,16,128]{4,3,2,1,0:T(8,128)S(1)} %get-tuple-element.44), channel_id=1, source_target_pairs={{0,8},{1,9},{2,10},{3,11},{4,12},{5,13},{6,14},{7,15},{8,0},{9,1},... | collective-permute-start | bytes 393224 | tf_op jit(solution)/shard_map/ppermute | solution.py:161
  74.1 21.6 %collective-permute-start.41 = (f32[1,4,4,16,128]{4,3,2,1,0:T(8,128)S(1)}, f32[1,4,4,16,128]{4,3,2,1,0:T(8,128)S(1)}, u32[]{:S(2)}, u32[]{:S(2)}) collective-permute-start(f32[1,4,4,16,128]{4,3,2,1,0:T(8,128)S(1)} %get-tuple-element.45), channel_id=1, source_target_pairs={{0,4},{1,5},{2,6},{3,7},{4,0},{5,1},{6,2},{7,3},{8,12},{9,13},{10,... | collective-permute-start | bytes 393224 | tf_op jit(solution)/shard_map/ppermute | solution.py:161
  95.8 5.8 %collective-permute-start.46 = (f32[4,1,4,16,128]{4,3,2,0,1:T(8,128)S(1)}, f32[4,1,4,16,128]{4,3,2,0,1:T(8,128)S(1)}, u32[]{:S(2)}, u32[]{:S(2)}) collective-permute-start(f32[4,1,4,16,128]{4,3,2,0,1:T(8,128)S(1)} %get-tuple-element.39), channel_id=1, source_target_pairs={{0,3},{1,2},{2,1},{3,0},{4,7},{5,6},{6,5},{7,4},{8,11},{9,10},{10,... | collective-permute-start | bytes 393224 | tf_op jit(solution)/shard_map/ppermute | solution.py:161
  96.6 7.9 %collective-permute-start.45 = (f32[4,1,4,16,128]{4,3,2,0,1:T(8,128)S(1)}, f32[4,1,4,16,128]{4,3,2,0,1:T(8,128)S(1)}, u32[]{:S(2)}, u32[]{:S(2)}) collective-permute-start(f32[4,1,4,16,128]{4,3,2,0,1:T(8,128)S(1)} %get-tuple-element.40), channel_id=1, source_target_pairs={{0,2},{1,3},{2,0},{3,1},{4,6},{5,7},{6,4},{7,5},{8,10},{9,11},{10,... | collective-permute-start | bytes 393224 | tf_op jit(solution)/shard_map/ppermute | solution.py:161
  97.4 7.1 %collective-permute-start.44 = (f32[4,1,4,16,128]{4,3,2,0,1:T(8,128)S(1)}, f32[4,1,4,16,128]{4,3,2,0,1:T(8,128)S(1)}, u32[]{:S(2)}, u32[]{:S(2)}) collective-permute-start(f32[4,1,4,16,128]{4,3,2,0,1:T(8,128)S(1)} %get-tuple-element.41), channel_id=1, source_target_pairs={{0,1},{1,0},{2,3},{3,2},{4,5},{5,4},{6,7},{7,6},{8,9},{9,8},{10,11... | collective-permute-start | bytes 393224 | tf_op jit(solution)/shard_map/ppermute | solution.py:161

commit v7 on v5

--- a/solution.py
+++ b/solution.py
@@ -49,9 +49,19 @@
     return gap, anisotropy, unit
 
 
-def pack_kernel(quantities, rank, fields, density, head, tail, low, high, still):
+def pack_kernel(
+    quantities, rank, fields_in, density_in, head, tail, low, high, still, fields, density, sems
+):
     columns, cells, depth = density.shape
     slots, share = still.shape[0], still.shape[1]
+    copies = [
+        pltpu.make_async_copy(density_in, density, sems.at[0]),
+        pltpu.make_async_copy(fields_in.at[0:6], fields, sems.at[1]),
+    ]
+    for copy in copies:
+        copy.start()
+    for copy in copies:
+        copy.wait()
 
     def source(row):
         if row == 3:
@@ -101,8 +111,13 @@
             rim,
             jax.ShapeDtypeStruct((slots, share, cells, depth), f32),
         ),
-        in_specs=[pl.BlockSpec(memory_space=pltpu.SMEM), vmem, vmem],
+        in_specs=[pl.BlockSpec(memory_space=pltpu.SMEM)] + [pl.BlockSpec(memory_space=pl.ANY)] * 2,
         out_specs=[vmem] * 5,
+        scratch_shapes=[
+            pltpu.VMEM((6, columns, cells, depth), f32),
+            pltpu.VMEM((columns, cells, depth), f32),
+            pltpu.SemaphoreType.DMA((2,)),
+        ],
         compiler_params=pltpu.CompilerParams(vmem_limit_bytes=16 * 2**20),
         name="pack",
     )(rank, fields, density)
@@ -163,6 +178,58 @@
     return slots
 
 
+def window_kernel(info, straight_below, straight_above, whole, next_one, head, tail, below, above, start, stop, joined):
+    cells = below.shape[1]
+    first, last, remainder = info[0], info[1], info[2]
+
+    def shear(one, two, spot, out, jump):
+        joined[:, 0:cells] = one[...]
+        joined[:, cells : 2 * cells] = two[...]
+        for row in range(PACKED):
+            out[row] = joined[row, pl.ds(spot, cells)] + (jump if row in (1, 8) else 0.0)
+
+    @pl.when(first == 1)
+    def _():
+        shear(next_one, whole, cells - remainder, below, shear_jump)
+
+    @pl.when(first == 0)
+    def _():
+        below[...] = straight_below[...]
+
+    @pl.when(last == 1)
+    def _():
+        shear(whole, next_one, remainder, above, -shear_jump)
+
+    @pl.when(last == 0)
+    def _():
+        above[...] = straight_above[...]
+
+    for layer, out, row in ((head, start, 0), (tail, stop, cells - 1)):
+        out[0:PACKED] = layer[...]
+        for component in range(3):
+            for side, strip in ((0, below), (1, above)):
+                spot = 2 * component + side
+                out[PACKED, spot : spot + 1] = strip[component, row : row + 1]
+        out[PACKED, 6 : out.shape[1]] = jnp.zeros((out.shape[1] - 6, out.shape[2]), jnp.float32)
+
+
+def window(info, straight_below, straight_above, whole, next_one, head, tail):
+    _, cells, depth = whole.shape
+    columns = head.shape[1]
+    f32 = jnp.float32
+    vmem = pl.BlockSpec(memory_space=pltpu.VMEM)
+    rim = jax.ShapeDtypeStruct((PACKED, cells, depth), f32)
+    layer = jax.ShapeDtypeStruct((PACKED + 1, columns, depth), f32)
+    return pl.pallas_call(
+        window_kernel,
+        out_shape=(rim, rim, layer, layer),
+        in_specs=[pl.BlockSpec(memory_space=pltpu.SMEM)] + [vmem] * 6,
+        out_specs=[vmem] * 4,
+        scratch_shapes=[pltpu.VMEM((PACKED, 2 * cells, depth), f32)],
+        name="window",
+    )(info, straight_below, straight_above, whole, next_one, head, tail)
+
+
 def stress_kernel(
     info,
     fields,
@@ -171,12 +238,9 @@
     tail,
     before,
     after,
-    straight_below,
-    straight_above,
-    whole,
-    next_one,
+    below,
+    above,
     out,
-    joined,
     vel,
     mass,
     px,
@@ -186,53 +250,20 @@
 ):
     columns, cells, depth = density.shape
     share = out.shape[1]
-    first, last, remainder = info[0], info[1], info[2]
     end = TOP + cells
 
-    def place(far, near, ghost, start, jump):
+    for strip, far, near, ghost, corner in (
+        (below, 0, 1, 0, 0),
+        (above, columns + 3, columns + 2, columns + 1, 1),
+    ):
         for component in range(3):
-            added = jump if component == 1 else 0.0
-            vel[component, near, TOP - 1 : end + 1] = (
-                joined[component, pl.ds(start, cells + 2)] + added
-            )
-            vel[component, far, TOP:end] = joined[7 + component, pl.ds(start + 1, cells)] + added
+            spot = 2 * component + corner
+            vel[component, near, TOP:end] = strip[component]
+            vel[component, near, TOP - 1 : TOP] = before[PACKED, spot : spot + 1]
+            vel[component, near, end : end + 1] = after[PACKED, spot : spot + 1]
+            vel[component, far, TOP:end] = strip[7 + component]
         for row in range(4):
-            mass[row, ghost] = joined[3 + row, pl.ds(start + 1, cells)]
-
-    def lay(one, two):
-        for row in range(PACKED):
-            joined[row, 1 : cells + 1] = one[row]
-            if two is not None:
-                joined[row, cells + 1 : 2 * cells + 1] = two[row]
-        final = one if two is None else two
-        spot = (1 if two is None else 2) * cells + 1
-        for component in range(3):
-            joined[component, 0:1] = one[PACKED, 2 * component : 2 * component + 1]
-            joined[component, spot : spot + 1] = final[PACKED, 2 * component + 1 : 2 * component + 2]
-
-    below = (0, 1, 0)
-    above = (columns + 3, columns + 2, columns + 1)
-
-    @pl.when(first == 1)
-    def _():
-        lay(next_one, whole)
-        place(*below, cells - remainder, shear_jump)
-
-    @pl.when(first == 0)
-    def _():
-        lay(straight_below, None)
-        place(*below, 0, 0.0)
-
-    @pl.when(last == 1)
-    def _():
-        lay(whole, next_one)
-        place(*above, remainder, -shear_jump)
-
-    @pl.when(last == 0)
-    def _():
-        lay(straight_above, None)
-        place(*above, 0, 0.0)
-
+            mass[row, ghost] = strip[3 + row]
     vel[:, 2 : columns + 2, TOP:end] = fields[0:3]
     mass[0, 1 : columns + 1] = density[...]
     mass[1:4, 1 : columns + 1] = fields[3:6]
@@ -290,7 +321,7 @@
         heat[ghost] = gap * anisotropy
         return carry
 
-    lax.fori_loop(0, columns + 2, tensor_column, 0)
+    lax.fori_loop(0, columns + 2, tensor_column, 0, unroll=3)
 
     def update_column(column, carry):
         ghost = column + 1
@@ -304,7 +335,7 @@
         vertical = (px[2, ghost], py[2, ghost, TOP:end], pzz[ghost])
         for axis in range(4):
             flat = column * 4 + axis
-            slot = lax.bitwise_xor(info[3], flat // share)
+            slot = lax.bitwise_xor(info[0], flat // share)
             if axis < 3:
                 force = slope(axis) + vertical_slope(vertical[axis])
                 out[slot, flat % share] = fields[axis, column] + force * inverse
@@ -312,7 +343,7 @@
                 out[slot, flat % share] = fields[6, column] + heat[ghost]
         return carry
 
-    lax.fori_loop(0, columns, update_column, 0)
+    lax.fori_loop(0, columns, update_column, 0, unroll=4)
 
 
 def updated_columns(info, fields, density, *layers):
@@ -325,10 +356,9 @@
     return pl.pallas_call(
         stress_kernel,
         out_shape=jax.ShapeDtypeStruct((slots, 4 * columns // slots, cells, depth), f32),
-        in_specs=[smem] + [vmem] * 10,
+        in_specs=[smem] + [vmem] * 8,
         out_specs=vmem,
         scratch_shapes=[
-            pltpu.VMEM((PACKED, 2 * cells + TOP, depth), f32),
             pltpu.VMEM((3, columns + 4, tall, depth), f32),
             pltpu.VMEM((4, columns + 2, cells, depth), f32),
             pltpu.VMEM((3, columns + 2, cells, depth), f32),
@@ -402,7 +432,7 @@
     return jnp.where(even, far, near), jnp.where(even, near, far)
 
 
-def rims(blocks, low, high, before, after):
+def rims(blocks, low, high):
     radials = lax.axis_size("rad")
     azimuths = lax.axis_size("az")
     rad = lax.axis_index("rad")
@@ -416,13 +446,6 @@
         pairs += [(flat(0, az), flat(last, az - steps)) for az in range(azimuths)]
         return lax.ppermute(data, ("rad", "az"), pairs)
 
-    def with_ends(main, column):
-        ends = jnp.stack([before[0:3, column], after[0:3, column]], axis=1)
-        ends = ends.reshape(1, 6, main.shape[-1])
-        ends = jnp.pad(ends, ((0, 0), (0, main.shape[1] - 6), (0, 0)))
-        return jnp.concatenate([main, ends], axis=0)
-
-    low, high = with_ends(low, 0), with_ends(high, -1)
     edge = jnp.where(rad == 0, low, high)
     if radials == 2:
         other = jnp.where(rad == 0, high, low)
@@ -443,22 +466,20 @@
     radials = lax.axis_size("rad")
     rad = lax.axis_index("rad")
     shear_cells = boundary_shift[0]
-    az = lax.axis_index("az")
-    rank = az.reshape(1)
+    rank = lax.axis_index("az").reshape(1)
     head, tail, low, high, still = pack(rank, fields, density)
-    before, after = azimuthal_layers(head, tail)
-    before, after, still = lax.optimization_barrier((before, after, still))
-    still = swap(still)
-    layers = rims(shear_cells // cells, low, high, before, after)
     info = jnp.stack(
         [
             (rad == 0).astype(jnp.int32),
             (rad == radials - 1).astype(jnp.int32),
             shear_cells % cells,
-            az,
         ]
     )
-    moving = updated_columns(info, fields, density, head, tail, before, after, *layers)
+    below, above, start, stop = window(info, *rims(shear_cells // cells, low, high), head, tail)
+    still, start, stop = lax.optimization_barrier((still, start, stop))
+    before, after = azimuthal_layers(start, stop)
+    still = swap(still)
+    moving = updated_columns(rank, fields, density, head, tail, before, after, below, above)
     moving = swap(moving)
     still = swap(move_columns(still, 4, rank, shift_int, frac_num))
     moving = swap(move_columns(moving, 4, rank, shift_int, frac_num))

time: 86.9 us -> 85.7 us (0.986)
  waiting for transfers between devices: 37.5 us -> 29.5 us
  starting transfers between devices: 36.7 us -> 41.2 us
  other arithmetic: 0.43 us -> 1.97 us
  local copies, waits for them, and re-layouts: 3.07 us -> 4.32 us
    ppermute x24, starting transfers between devices: 26.4 us -> 31.7 us  [swap(): parts.append(lax.ppermute(cut[:, step], 'az', pairs))]
    ppermute x24, waiting for transfers between devices: 29.1 us -> 24.9 us  [swap(): parts.append(lax.ppermute(cut[:, step], 'az', pairs))]
    ppermute x1, starting transfers between devices: 5.67 us -> 2.76 us  [azimuthal_layers(): far = lax.ppermute(jnp.where(even, head, tail), 'az', outer)]
    pallas_call x1, Pallas kernels: 4.27 us -> 1.5 us  [updated_columns(): pl.pallas_call(stress_kernel, out_shape=jax.ShapeDtypeStruct((slots, 4 *...]
    ppermute x2, waiting for transfers between devices: 7.08 us -> 4.54 us  [wrap(): return lax.ppermute(data, ('rad', 'az'), pairs)]
    pallas_call x0 -> x1, Pallas kernels: none -> 1.85 us  [window(): pl.pallas_call(window_kernel, out_shape=(rim, rim, layer, layer), in_spec...]
    ppermute x1, starting transfers between devices: 1.56 us -> 2.94 us  [rims(): below = above = lax.ppermute(other, 'rad', [(0, 1), (1, 0)])]
    ppermute x1, waiting for transfers between devices: 1.35 us -> 0.01 us  [azimuthal_layers(): far = lax.ppermute(jnp.where(even, head, tail), 'az', outer)]
  transfers between devices with their start and end apart: 29 -> 29, of which waited for: 13 -> 10; matrix products, arithmetic and copies ran while one was open for 1% -> 1% of each run, Pallas kernels for 7% -> 4%
where the time goes in v7:
time: 85.7 us; the launch traced here: 85.3 us
  starting transfers between devices  41.2 us (48%)
  waiting for transfers between devices  29.5 us (34%)
  Pallas kernels  6.75 us (8%)
  local copies, waits for them, and re-layouts  4.32 us (5%)
  other arithmetic  1.97 us (2%)
  between operations  1.62 us (2%)
    ppermute x24, starting transfers between devices, swap(): parts.append(lax.ppermute(cut[:, step], 'az', pairs))  31.7 us
    ppermute x24, waiting for transfers between devices, swap(): parts.append(lax.ppermute(cut[:, step], 'az', pairs))  24.9 us
    ppermute x2, waiting for transfers between devices, wrap(): return lax.ppermute(data, ('rad', 'az'), pairs)  4.54 us
    unnamed x26, local copies, waits for them, and re-layouts  4.01 us
    ppermute x2, starting transfers between devices, wrap(): return lax.ppermute(data, ('rad', 'az'), pairs)  3.76 us
    ppermute x1, starting transfers between devices, rims(): below = above = lax.ppermute(other, 'rad', [(0, 1), (1, 0)])  2.94 us
    ppermute x1, starting transfers between devices, azimuthal_layers(): far = lax.ppermute(jnp.where(even, head, tail), 'az', outer)  2.76 us
    pallas_call x2, Pallas kernels, move_columns(): pl.pallas_call(functools.partial(move_kernel, quantities), out_shape=jax....  1.99 us
  transfers between devices with their start and end apart: 29, of which 10 were waited for; matrix products, arithmetic and copies ran while one was open for 1% of the time, Pallas kernels for 4%

profile of v7, /device:TPU:0, one launch (start us, length us, event | category | flops | bytes accessed | tf_op | source)
XLA Modules:
  0.0 85.3 jit_solution(17831991163120234276)
XLA Ops:
  0.6 1.2 %copy-done = f32[7,16,16,128]{3,2,1,0:T(8,128)S(1)} copy-done((f32[7,16,16,128]{3,2,1,0:T(8,128)S(1)}, f32[7,16,16,128]{3,2,1,0:T(8,128)}, u32[]{:S(2)}) %copy-start) | copy-done | bytes 917528
  1.8 0.9 %copy-done.2 = f32[16,16,128]{2,1,0:T(8,128)S(1)} copy-done((f32[16,16,128]{2,1,0:T(8,128)S(1)}, f32[16,16,128]{2,1,0:T(8,128)}, u32[]{:S(2)}) %copy-start.2) | copy-done | bytes 131096
  3.8 2.9 %collective-permute-start.32 = (f32[10,16,128]{2,1,0:T(8,128)S(1)}, f32[10,16,128]{2,1,0:T(8,128)S(1)}, u32[]{:S(2)}, u32[]{:S(2)}) collective-permute-start(f32[10,16,128]{2,1,0:T(8,128)S(1)} %get-tuple-element.83), channel_id=1, source_target_pairs={{0,16},{16,0},{1,17},{17,1},{2,18},{18,2},{3,19},{19,3},{4,20},{20... | collective-permute-start | bytes 245768 | tf_op jit(solution)/shard_map/ppermute | solution.py:452
  7.4 8.3 %conditional.1 = (f32[10,16,128]{2,1,0:T(8,128)}, f32[10,16,128]{2,1,0:T(8,128)}) conditional(s32[]{:T(128)} %clamp.3, f32[10,16,128]{2,1,0:T(8,128)S(1)} %get-tuple-element.82, f32[10,16,128]{2,1,0:T(8,128)S(1)} %get-tuple-element.82, f32[10,16,128]{2,1,0:T(8,128)S(1)} %get-tuple-element.82, ...), branch_computations={%region_0.1_spmd, %region_1.2_spmd, %region_2.3_spmd, %region_3.4_... | conditional | bytes 655456 | solution.py:460
  7.4 3.8 %collective-permute-start.1 = (f32[10,16,128]{2,1,0:T(8,128)S(1)}, f32[10,16,128]{2,1,0:T(8,128)}, u32[]{:S(2)}, u32[]{:S(2)}) collective-permute-start(f32[10,16,128]{2,1,0:T(8,128)S(1)} %param), channel_id=1, source_target_pairs={{16,1},{17,2},{18,3},{19,4},{20,5},{21,6},{22,7},{23,8},{24,9},{25... | collective-permute-start | bytes 245768 | tf_op jit(solution)/shard_map/cond/branch_0_fun/ppermute | solution.py:447
  11.2 3.9 %collective-permute-done.1 = f32[10,16,128]{2,1,0:T(8,128)} collective-permute-done((f32[10,16,128]{2,1,0:T(8,128)S(1)}, f32[10,16,128]{2,1,0:T(8,128)}, u32[]{:S(2)}, u32[]{:S(2)}) %collective-permute-start.1) | collective-permute-done | bytes 81952 | tf_op jit(solution)/shard_map/cond/branch_0_fun/ppermute | solution.py:447
  17.0 1.9 %window.1 = (f32[10,16,128]{2,1,0:T(8,128)}, f32[10,16,128]{2,1,0:T(8,128)}, f32[11,16,128]{2,1,0:T(8,128)}, f32[11,16,128]{2,1,0:T(8,128)}) custom-call(s32[3]{0:T(128)} %pad_add_fusion.info, f32[10,16,128]{2,1,0:T(8,128)} %copy-done.12, f32[10,16,128]{2,1,0:T(8,128)} %copy-done.12, f32[10,16,128]{2,1,0:T(8,128)} %get-tuple-element.37.whole, ...), custom_call_target="tpu_custom_call" | custom-call | tf_op jit(solution)/shard_map/window/pallas_call | solution.py:223
  18.8 1.0 %broadcast_select_fusion.2 = (f32[11,16,128]{2,1,0:T(8,128)S(1)}, f32[11,16,128]{2,1,0:T(8,128)S(1)}) fusion(f32[11,16,128]{2,1,0:T(8,128)} %get-tuple-element.42, f32[11,16,128]{2,1,0:T(8,128)} %get-tuple-element.41, pred[]{:T(512)S(6)} %eq.14), kind=kLoop, calls=%fused_computation.42 | loop fusion | flops 45056 | bytes 360449 | tf_op jit(solution)/shard_map/jit(_where)/select_n | solution.py:431
  19.9 2.8 %collective-permute-start.33 = (f32[11,16,128]{2,1,0:T(8,128)S(1)}, f32[11,16,128]{2,1,0:T(8,128)S(1)}, u32[]{:S(2)}, u32[]{:S(2)}) collective-permute-start(f32[11,16,128]{2,1,0:T(8,128)S(1)} %get-tuple-element.81), channel_id=1, source_target_pairs={{0,15},{1,2},{2,1},{3,4},{4,3},{5,6},{6,5},{7,8},{8,7},{9,10},{10,... | collective-permute-start | bytes 270344 | tf_op jit(solution)/shard_map/ppermute | solution.py:430
  23.0 4.2 %collective-permute-start.47 = (f32[1,4,4,16,128]{4,3,2,1,0:T(8,128)S(1)}, f32[1,4,4,16,128]{4,3,2,1,0:T(8,128)S(1)}, u32[]{:S(2)}, u32[]{:S(2)}) collective-permute-start(f32[1,4,4,16,128]{4,3,2,1,0:T(8,128)S(1)} %get-tuple-element.61), channel_id=1, source_target_pairs={{0,4},{1,5},{2,6},{3,7},{4,0},{5,1},{6,2},{7,3},{8,12},{9,13},{10,... | collective-permute-start | bytes 393224 | tf_op jit(solution)/shard_map/ppermute | solution.py:176
  27.3 1.5 %stress_update.1 = f32[16,4,16,128]{3,2,1,0:T(8,128)S(1)} custom-call(s32[1]{0:T(128)} %bitcast.rank.info, f32[7,16,16,128]{3,2,1,0:T(8,128)S(1)} %copy-done.1, f32[16,16,128]{2,1,0:T(8,128)S(1)} %copy-done.3, f32[10,16,128]{2,1,0:T(8,128)S(1)} %copy-done.5, f32[10,16,128]{2,1,0:T(8,128)S(1)} %copy-done.7, f32[11,16,128]{2,1,0:T(8,128)S(1)} %get-tuple-element.79.before, ...), custom_call_target="tpu_custom_call" | custom-call | tf_op jit(solution)/shard_map/stress_update/pallas_call | solution.py:356
  29.2 2.0 %collective-permute-start.36 = (f32[1,4,4,16,128]{4,3,2,1,0:T(8,128)S(1)}, f32[1,4,4,16,128]{4,3,2,1,0:T(8,128)S(1)}, u32[]{:S(2)}, u32[]{:S(2)}) collective-permute-start(f32[1,4,4,16,128]{4,3,2,1,0:T(8,128)S(1)} %get-tuple-element.76), channel_id=1, source_target_pairs={{0,8},{1,9},{2,10},{3,11},{4,12},{5,13},{6,14},{7,15},{8,0},{9,1},... | collective-permute-start | bytes 393224 | tf_op jit(solution)/shard_map/ppermute | solution.py:176
  31.3 5.9 %collective-permute-start.35 = (f32[1,4,4,16,128]{4,3,2,1,0:T(8,128)S(1)}, f32[1,4,4,16,128]{4,3,2,1,0:T(8,128)S(1)}, u32[]{:S(2)}, u32[]{:S(2)}) collective-permute-start(f32[1,4,4,16,128]{4,3,2,1,0:T(8,128)S(1)} %get-tuple-element.77), channel_id=1, source_target_pairs={{0,4},{1,5},{2,6},{3,7},{4,0},{5,1},{6,2},{7,3},{8,12},{9,13},{10,... | collective-permute-start | bytes 393224 | tf_op jit(solution)/shard_map/ppermute | solution.py:176
  37.1 5.1 %collective-permute-done.48 = f32[1,4,4,16,128]{4,3,2,1,0:T(8,128)S(1)} collective-permute-done((f32[1,4,4,16,128]{4,3,2,1,0:T(8,128)S(1)}, f32[1,4,4,16,128]{4,3,2,1,0:T(8,128)S(1)}, u32[]{:S(2)}, u32[]{:S(2)}) %collective-permute-start.48) | collective-permute-done | bytes 131104 | tf_op jit(solution)/shard_map/ppermute | solution.py:176
  42.5 1.8 %collective-permute-start.50 = (f32[4,1,4,16,128]{4,3,2,0,1:T(8,128)S(1)}, f32[4,1,4,16,128]{4,3,2,0,1:T(8,128)S(1)}, u32[]{:S(2)}, u32[]{:S(2)}) collective-permute-start(f32[4,1,4,16,128]{4,3,2,0,1:T(8,128)S(1)} %get-tuple-element.57), channel_id=1, source_target_pairs={{0,1},{1,0},{2,3},{3,2},{4,5},{5,4},{6,7},{7,6},{8,9},{9,8},{10,11... | collective-permute-start | bytes 393224 | tf_op jit(solution)/shard_map/ppermute | solution.py:176
  44.2 2.4 %collective-permute-done.36 = f32[1,4,4,16,128]{4,3,2,1,0:T(8,128)S(1)} collective-permute-done((f32[1,4,4,16,128]{4,3,2,1,0:T(8,128)S(1)}, f32[1,4,4,16,128]{4,3,2,1,0:T(8,128)S(1)}, u32[]{:S(2)}, u32[]{:S(2)}) %collective-permute-start.36) | collective-permute-done | bytes 131104 | tf_op jit(solution)/shard_map/ppermute | solution.py:176
  46.8 0.9 %collective-permute-start.40 = (f32[4,1,4,16,128]{4,3,2,0,1:T(8,128)S(1)}, f32[4,1,4,16,128]{4,3,2,0,1:T(8,128)S(1)}, u32[]{:S(2)}, u32[]{:S(2)}) collective-permute-start(f32[4,1,4,16,128]{4,3,2,0,1:T(8,128)S(1)} %get-tuple-element.71), channel_id=1, source_target_pairs={{0,3},{1,2},{2,1},{3,0},{4,7},{5,6},{6,5},{7,4},{8,11},{9,10},{10,... | collective-permute-start | bytes 393224 | tf_op jit(solution)/shard_map/ppermute | solution.py:176
  47.9 0.8 collective-permute-start.38
  49.5 1.0 %move.3 = f32[16,4,16,128]{3,2,1,0:T(8,128)S(1)} custom-call(s32[1]{0:T(128)} %bitcast.rank.info, s32[16]{0:T(128)S(1)} %copy-done.10, s32[16]{0:T(128)S(1)} %copy-done.11, f32[16,4,16,128]{3,2,1,0:T(8,128)S(1)} %bitcast.150), custom_call_target="tpu_custom_call" | custom-call | tf_op jit(solution)/shard_map/move/pallas_call | solution.py:414
  50.5 2.6 %collective-permute-start.55 = (f32[1,4,4,16,128]{4,3,2,1,0:T(8,128)S(1)}, f32[1,4,4,16,128]{4,3,2,1,0:T(8,128)S(1)}, u32[]{:S(2)}, u32[]{:S(2)}) collective-permute-start(f32[1,4,4,16,128]{4,3,2,1,0:T(8,128)S(1)} %get-tuple-element.51), channel_id=1, source_target_pairs={{0,12},{1,13},{2,14},{3,15},{4,8},{5,9},{6,10},{7,11},{8,4},{9,5},... | collective-permute-start | bytes 393224 | tf_op jit(solution)/shard_map/ppermute | solution.py:176
  53.1 1.9 %collective-permute-start.53 = (f32[1,4,4,16,128]{4,3,2,1,0:T(8,128)S(1)}, f32[1,4,4,16,128]{4,3,2,1,0:T(8,128)S(1)}, u32[]{:S(2)}, u32[]{:S(2)}) collective-permute-start(f32[1,4,4,16,128]{4,3,2,1,0:T(8,128)S(1)} %get-tuple-element.53), channel_id=1, source_target_pairs={{0,4},{1,5},{2,6},{3,7},{4,0},{5,1},{6,2},{7,3},{8,12},{9,13},{10,... | collective-permute-start | bytes 393224 | tf_op jit(solution)/shard_map/ppermute | solution.py:176
  55.0 1.0 %move.2 = f32[16,4,16,128]{3,2,1,0:T(8,128)S(1)} custom-call(s32[1]{0:T(128)} %bitcast.rank.info, s32[16]{0:T(128)S(1)} %copy-done.10, s32[16]{0:T(128)S(1)} %copy-done.11, f32[16,4,16,128]{3,2,1,0:T(8,128)S(1)} %bitcast.151), custom_call_target="tpu_custom_call" | custom-call | tf_op jit(solution)/shard_map/move/pallas_call | solution.py:414
  56.1 2.5 %collective-permute-start.43 = (f32[1,4,4,16,128]{4,3,2,1,0:T(8,128)S(1)}, f32[1,4,4,16,128]{4,3,2,1,0:T(8,128)S(1)}, u32[]{:S(2)}, u32[]{:S(2)}) collective-permute-start(f32[1,4,4,16,128]{4,3,2,1,0:T(8,128)S(1)} %get-tuple-element.67), channel_id=1, source_target_pairs={{0,12},{1,13},{2,14},{3,15},{4,8},{5,9},{6,10},{7,11},{8,4},{9,5},... | collective-permute-start | bytes 393224 | tf_op jit(solution)/shard_map/ppermute | solution.py:176
  58.9 1.6 %collective-permute-start.41 = (f32[1,4,4,16,128]{4,3,2,1,0:T(8,128)S(1)}, f32[1,4,4,16,128]{4,3,2,1,0:T(8,128)S(1)}, u32[]{:S(2)}, u32[]{:S(2)}) collective-permute-start(f32[1,4,4,16,128]{4,3,2,1,0:T(8,128)S(1)} %get-tuple-element.69), channel_id=1, source_target_pairs={{0,4},{1,5},{2,6},{3,7},{4,0},{5,1},{6,2},{7,3},{8,12},{9,13},{10,... | collective-permute-start | bytes 393224 | tf_op jit(solution)/shard_map/ppermute | solution.py:176
  60.5 4.0 %collective-permute-done.54 = f32[1,4,4,16,128]{4,3,2,1,0:T(8,128)S(1)} collective-permute-done((f32[1,4,4,16,128]{4,3,2,1,0:T(8,128)S(1)}, f32[1,4,4,16,128]{4,3,2,1,0:T(8,128)S(1)}, u32[]{:S(2)}, u32[]{:S(2)}) %collective-permute-start.54) | collective-permute-done | bytes 131104 | tf_op jit(solution)/shard_map/ppermute | solution.py:176
  64.7 1.5 %collective-permute-start.58 = (f32[4,1,4,16,128]{4,3,2,0,1:T(8,128)S(1)}, f32[4,1,4,16,128]{4,3,2,0,1:T(8,128)S(1)}, u32[]{:S(2)}, u32[]{:S(2)}) collective-permute-start(f32[4,1,4,16,128]{4,3,2,0,1:T(8,128)S(1)} %get-tuple-element.47), channel_id=1, source_target_pairs={{0,3},{1,2},{2,1},{3,0},{4,7},{5,6},{6,5},{7,4},{8,11},{9,10},{10,... | collective-permute-start | bytes 393224 | tf_op jit(solution)/shard_map/ppermute | solution.py:176
  66.1 3.0 %collective-permute-start.57 = (f32[4,1,4,16,128]{4,3,2,0,1:T(8,128)S(1)}, f32[4,1,4,16,128]{4,3,2,0,1:T(8,128)S(1)}, u32[]{:S(2)}, u32[]{:S(2)}) collective-permute-start(f32[4,1,4,16,128]{4,3,2,0,1:T(8,128)S(1)} %get-tuple-element.48), channel_id=1, source_target_pairs={{0,2},{1,3},{2,0},{3,1},{4,6},{5,7},{6,4},{7,5},{8,10},{9,11},{10,... | collective-permute-start | bytes 393224 | tf_op jit(solution)/shard_map/ppermute | solution.py:176
  69.2 6.3 %collective-permute-done.42 = f32[1,4,4,16,128]{4,3,2,1,0:T(8,128)S(1)} collective-permute-done((f32[1,4,4,16,128]{4,3,2,1,0:T(8,128)S(1)}, f32[1,4,4,16,128]{4,3,2,1,0:T(8,128)S(1)}, u32[]{:S(2)}, u32[]{:S(2)}) %collective-permute-start.42) | collective-permute-done | bytes 131104 | tf_op jit(solution)/shard_map/ppermute | solution.py:176
  75.8 1.5 %collective-permute-start.45 = (f32[4,1,4,16,128]{4,3,2,0,1:T(8,128)S(1)}, f32[4,1,4,16,128]{4,3,2,0,1:T(8,128)S(1)}, u32[]{:S(2)}, u32[]{:S(2)}) collective-permute-start(f32[4,1,4,16,128]{4,3,2,0,1:T(8,128)S(1)} %get-tuple-element.64), channel_id=1, source_target_pairs={{0,2},{1,3},{2,0},{3,1},{4,6},{5,7},{6,4},{7,5},{8,10},{9,11},{10,... | collective-permute-start | bytes 393224 | tf_op jit(solution)/shard_map/ppermute | solution.py:176
  77.6 3.7 %collective-permute-done.46 = f32[4,1,4,16,128]{4,3,2,0,1:T(8,128)S(1)} collective-permute-done((f32[4,1,4,16,128]{4,3,2,0,1:T(8,128)S(1)}, f32[4,1,4,16,128]{4,3,2,0,1:T(8,128)S(1)}, u32[]{:S(2)}, u32[]{:S(2)}) %collective-permute-start.46) | collective-permute-done | bytes 131104 | tf_op jit(solution)/shard_map/ppermute | solution.py:176
  81.3 3.0 %collective-permute-done.45 = f32[4,1,4,16,128]{4,3,2,0,1:T(8,128)S(1)} collective-permute-done((f32[4,1,4,16,128]{4,3,2,0,1:T(8,128)S(1)}, f32[4,1,4,16,128]{4,3,2,0,1:T(8,128)S(1)}, u32[]{:S(2)}, u32[]{:S(2)}) %collective-permute-start.45) | collective-permute-done | bytes 131104 | tf_op jit(solution)/shard_map/ppermute | solution.py:176
  84.3 1.0 %join.1 = (f32[7,16,16,128]{3,2,1,0:T(8,128)}, f32[16,16,128]{2,1,0:T(8,128)}) custom-call(s32[1]{0:T(128)} %bitcast.rank.info, f32[16,4,16,128]{3,2,1,0:T(8,128)S(1)} %bitcast.147, f32[16,4,16,128]{3,2,1,0:T(8,128)S(1)} %bitcast.146), custom_call_target="tpu_custom_call" | custom-call | tf_op jit(solution)/shard_map/join/pallas_call | solution.py:153
  (79 shorter events, 6.3 us)
Async XLA Ops:
  3.8 12.6 %collective-permute-start.32 = (f32[10,16,128]{2,1,0:T(8,128)S(1)}, f32[10,16,128]{2,1,0:T(8,128)S(1)}, u32[]{:S(2)}, u32[]{:S(2)}) collective-permute-start(f32[10,16,128]{2,1,0:T(8,128)S(1)} %get-tuple-element.83), channel_id=1, source_target_pairs={{0,16},{16,0},{1,17},{17,1},{2,18},{18,2},{3,19},{19,3},{4,20},{20... | collective-permute-start | bytes 245768 | tf_op jit(solution)/shard_map/ppermute | solution.py:452
  7.4 7.6 %collective-permute-start.1 = (f32[10,16,128]{2,1,0:T(8,128)S(1)}, f32[10,16,128]{2,1,0:T(8,128)}, u32[]{:S(2)}, u32[]{:S(2)}) collective-permute-start(f32[10,16,128]{2,1,0:T(8,128)S(1)} %param), channel_id=1, source_target_pairs={{16,1},{17,2},{18,3},{19,4},{20,5},{21,6},{22,7},{23,8},{24,9},{25... | collective-permute-start | bytes 245768 | tf_op jit(solution)/shard_map/cond/branch_0_fun/ppermute | solution.py:447
  11.2 4.5 %collective-permute-start = (f32[10,16,128]{2,1,0:T(8,128)S(1)}, f32[10,16,128]{2,1,0:T(8,128)}, u32[]{:S(2)}, u32[]{:S(2)}) collective-permute-start(f32[10,16,128]{2,1,0:T(8,128)S(1)} %param), channel_id=1, source_target_pairs={{16,0},{17,1},{18,2},{19,3},{20,4},{21,5},{22,6},{23,7},{24,8},{25... | collective-permute-start | bytes 245768 | tf_op jit(solution)/shard_map/cond/branch_0_fun/ppermute | solution.py:447
  18.8 8.4 %copy-start.1 = (f32[7,16,16,128]{3,2,1,0:T(8,128)S(1)}, f32[7,16,16,128]{3,2,1,0:T(8,128)}, u32[]{:S(2)}) copy-start(f32[7,16,16,128]{3,2,1,0:T(8,128)} %fields.1) | copy-start | bytes 2752516
  19.8 7.3 %collective-permute-start.34 = (f32[11,16,128]{2,1,0:T(8,128)S(1)}, f32[11,16,128]{2,1,0:T(8,128)S(1)}, u32[]{:S(2)}, u32[]{:S(2)}) collective-permute-start(f32[11,16,128]{2,1,0:T(8,128)S(1)} %get-tuple-element.80), channel_id=1, source_target_pairs={{0,1},{1,0},{2,3},{3,2},{4,5},{5,4},{6,7},{7,6},{8,9},{9,8},{10,11... | collective-permute-start | bytes 270344 | tf_op jit(solution)/shard_map/ppermute | solution.py:431
  19.9 7.3 %collective-permute-start.33 = (f32[11,16,128]{2,1,0:T(8,128)S(1)}, f32[11,16,128]{2,1,0:T(8,128)S(1)}, u32[]{:S(2)}, u32[]{:S(2)}) collective-permute-start(f32[11,16,128]{2,1,0:T(8,128)S(1)} %get-tuple-element.81), channel_id=1, source_target_pairs={{0,15},{1,2},{2,1},{3,4},{4,3},{5,6},{6,5},{7,8},{8,7},{9,10},{10,... | collective-permute-start | bytes 270344 | tf_op jit(solution)/shard_map/ppermute | solution.py:430
  22.7 4.5 %copy-start.8 = (f32[10,16,128]{2,1,0:T(8,128)S(1)}, f32[10,16,128]{2,1,0:T(8,128)}, u32[]{:S(2)}) copy-start(f32[10,16,128]{2,1,0:T(8,128)} %get-tuple-element.43.below) | copy-start | bytes 245764
  22.7 4.5 %copy-start.9 = (f32[10,16,128]{2,1,0:T(8,128)S(1)}, f32[10,16,128]{2,1,0:T(8,128)}, u32[]{:S(2)}) copy-start(f32[10,16,128]{2,1,0:T(8,128)} %get-tuple-element.44.above) | copy-start | bytes 245764
  22.7 8.5 %collective-permute-start.49 = (f32[1,4,4,16,128]{4,3,2,1,0:T(8,128)S(1)}, f32[1,4,4,16,128]{4,3,2,1,0:T(8,128)S(1)}, u32[]{:S(2)}, u32[]{:S(2)}) collective-permute-start(f32[1,4,4,16,128]{4,3,2,1,0:T(8,128)S(1)} %get-tuple-element.59), channel_id=1, source_target_pairs={{0,12},{1,13},{2,14},{3,15},{4,8},{5,9},{6,10},{7,11},{8,4},{9,5},... | collective-permute-start | bytes 393224 | tf_op jit(solution)/shard_map/ppermute | solution.py:176
  23.0 19.2 %collective-permute-start.48 = (f32[1,4,4,16,128]{4,3,2,1,0:T(8,128)S(1)}, f32[1,4,4,16,128]{4,3,2,1,0:T(8,128)S(1)}, u32[]{:S(2)}, u32[]{:S(2)}) collective-permute-start(f32[1,4,4,16,128]{4,3,2,1,0:T(8,128)S(1)} %get-tuple-element.60), channel_id=1, source_target_pairs={{0,8},{1,9},{2,10},{3,11},{4,12},{5,13},{6,14},{7,15},{8,0},{9,1},... | collective-permute-start | bytes 393224 | tf_op jit(solution)/shard_map/ppermute | solution.py:176
  23.0 19.2 %collective-permute-start.47 = (f32[1,4,4,16,128]{4,3,2,1,0:T(8,128)S(1)}, f32[1,4,4,16,128]{4,3,2,1,0:T(8,128)S(1)}, u32[]{:S(2)}, u32[]{:S(2)}) collective-permute-start(f32[1,4,4,16,128]{4,3,2,1,0:T(8,128)S(1)} %get-tuple-element.61), channel_id=1, source_target_pairs={{0,4},{1,5},{2,6},{3,7},{4,0},{5,1},{6,2},{7,3},{8,12},{9,13},{10,... | collective-permute-start | bytes 393224 | tf_op jit(solution)/shard_map/ppermute | solution.py:176
  28.8 13.6 %collective-permute-start.37 = (f32[1,4,4,16,128]{4,3,2,1,0:T(8,128)S(1)}, f32[1,4,4,16,128]{4,3,2,1,0:T(8,128)S(1)}, u32[]{:S(2)}, u32[]{:S(2)}) collective-permute-start(f32[1,4,4,16,128]{4,3,2,1,0:T(8,128)S(1)} %get-tuple-element.75), channel_id=1, source_target_pairs={{0,12},{1,13},{2,14},{3,15},{4,8},{5,9},{6,10},{7,11},{8,4},{9,5},... | collective-permute-start | bytes 393224 | tf_op jit(solution)/shard_map/ppermute | solution.py:176
  29.2 17.4 %collective-permute-start.36 = (f32[1,4,4,16,128]{4,3,2,1,0:T(8,128)S(1)}, f32[1,4,4,16,128]{4,3,2,1,0:T(8,128)S(1)}, u32[]{:S(2)}, u32[]{:S(2)}) collective-permute-start(f32[1,4,4,16,128]{4,3,2,1,0:T(8,128)S(1)} %get-tuple-element.76), channel_id=1, source_target_pairs={{0,8},{1,9},{2,10},{3,11},{4,12},{5,13},{6,14},{7,15},{8,0},{9,1},... | collective-permute-start | bytes 393224 | tf_op jit(solution)/shard_map/ppermute | solution.py:176
  31.3 15.4 %collective-permute-start.35 = (f32[1,4,4,16,128]{4,3,2,1,0:T(8,128)S(1)}, f32[1,4,4,16,128]{4,3,2,1,0:T(8,128)S(1)}, u32[]{:S(2)}, u32[]{:S(2)}) collective-permute-start(f32[1,4,4,16,128]{4,3,2,1,0:T(8,128)S(1)} %get-tuple-element.77), channel_id=1, source_target_pairs={{0,4},{1,5},{2,6},{3,7},{4,0},{5,1},{6,2},{7,3},{8,12},{9,13},{10,... | collective-permute-start | bytes 393224 | tf_op jit(solution)/shard_map/ppermute | solution.py:176
  42.3 5.6 %collective-permute-start.52 = (f32[4,1,4,16,128]{4,3,2,0,1:T(8,128)S(1)}, f32[4,1,4,16,128]{4,3,2,0,1:T(8,128)S(1)}, u32[]{:S(2)}, u32[]{:S(2)}) collective-permute-start(f32[4,1,4,16,128]{4,3,2,0,1:T(8,128)S(1)} %get-tuple-element.55), channel_id=1, source_target_pairs={{0,3},{1,2},{2,1},{3,0},{4,7},{5,6},{6,5},{7,4},{8,11},{9,10},{10,... | collective-permute-start | bytes 393224 | tf_op jit(solution)/shard_map/ppermute | solution.py:176
  42.4 6.3 %collective-permute-start.51 = (f32[4,1,4,16,128]{4,3,2,0,1:T(8,128)S(1)}, f32[4,1,4,16,128]{4,3,2,0,1:T(8,128)S(1)}, u32[]{:S(2)}, u32[]{:S(2)}) collective-permute-start(f32[4,1,4,16,128]{4,3,2,0,1:T(8,128)S(1)} %get-tuple-element.56), channel_id=1, source_target_pairs={{0,2},{1,3},{2,0},{3,1},{4,6},{5,7},{6,4},{7,5},{8,10},{9,11},{10,... | collective-permute-start | bytes 393224 | tf_op jit(solution)/shard_map/ppermute | solution.py:176
  42.5 6.3 %collective-permute-start.50 = (f32[4,1,4,16,128]{4,3,2,0,1:T(8,128)S(1)}, f32[4,1,4,16,128]{4,3,2,0,1:T(8,128)S(1)}, u32[]{:S(2)}, u32[]{:S(2)}) collective-permute-start(f32[4,1,4,16,128]{4,3,2,0,1:T(8,128)S(1)} %get-tuple-element.57), channel_id=1, source_target_pairs={{0,1},{1,0},{2,3},{3,2},{4,5},{5,4},{6,7},{7,6},{8,9},{9,8},{10,11... | collective-permute-start | bytes 393224 | tf_op jit(solution)/shard_map/ppermute | solution.py:176
  46.8 6.3 %collective-permute-start.40 = (f32[4,1,4,16,128]{4,3,2,0,1:T(8,128)S(1)}, f32[4,1,4,16,128]{4,3,2,0,1:T(8,128)S(1)}, u32[]{:S(2)}, u32[]{:S(2)}) collective-permute-start(f32[4,1,4,16,128]{4,3,2,0,1:T(8,128)S(1)} %get-tuple-element.71), channel_id=1, source_target_pairs={{0,3},{1,2},{2,1},{3,0},{4,7},{5,6},{6,5},{7,4},{8,11},{9,10},{10,... | collective-permute-start | bytes 393224 | tf_op jit(solution)/shard_map/ppermute | solution.py:176
  47.6 7.3 %collective-permute-start.39 = (f32[4,1,4,16,128]{4,3,2,0,1:T(8,128)S(1)}, f32[4,1,4,16,128]{4,3,2,0,1:T(8,128)S(1)}, u32[]{:S(2)}, u32[]{:S(2)}) collective-permute-start(f32[4,1,4,16,128]{4,3,2,0,1:T(8,128)S(1)} %get-tuple-element.72), channel_id=1, source_target_pairs={{0,2},{1,3},{2,0},{3,1},{4,6},{5,7},{6,4},{7,5},{8,10},{9,11},{10,... | collective-permute-start | bytes 393224 | tf_op jit(solution)/shard_map/ppermute | solution.py:176
  47.9 7.1 %collective-permute-start.38 = (f32[4,1,4,16,128]{4,3,2,0,1:T(8,128)S(1)}, f32[4,1,4,16,128]{4,3,2,0,1:T(8,128)S(1)}, u32[]{:S(2)}, u32[]{:S(2)}) collective-permute-start(f32[4,1,4,16,128]{4,3,2,0,1:T(8,128)S(1)} %get-tuple-element.73), channel_id=1, source_target_pairs={{0,1},{1,0},{2,3},{3,2},{4,5},{5,4},{6,7},{7,6},{8,9},{9,8},{10,11... | collective-permute-start | bytes 393224 | tf_op jit(solution)/shard_map/ppermute | solution.py:176
  50.5 8.4 %collective-permute-start.55 = (f32[1,4,4,16,128]{4,3,2,1,0:T(8,128)S(1)}, f32[1,4,4,16,128]{4,3,2,1,0:T(8,128)S(1)}, u32[]{:S(2)}, u32[]{:S(2)}) collective-permute-start(f32[1,4,4,16,128]{4,3,2,1,0:T(8,128)S(1)} %get-tuple-element.51), channel_id=1, source_target_pairs={{0,12},{1,13},{2,14},{3,15},{4,8},{5,9},{6,10},{7,11},{8,4},{9,5},... | collective-permute-start | bytes 393224 | tf_op jit(solution)/shard_map/ppermute | solution.py:176
  53.1 11.5 %collective-permute-start.54 = (f32[1,4,4,16,128]{4,3,2,1,0:T(8,128)S(1)}, f32[1,4,4,16,128]{4,3,2,1,0:T(8,128)S(1)}, u32[]{:S(2)}, u32[]{:S(2)}) collective-permute-start(f32[1,4,4,16,128]{4,3,2,1,0:T(8,128)S(1)} %get-tuple-element.52), channel_id=1, source_target_pairs={{0,8},{1,9},{2,10},{3,11},{4,12},{5,13},{6,14},{7,15},{8,0},{9,1},... | collective-permute-start | bytes 393224 | tf_op jit(solution)/shard_map/ppermute | solution.py:176
  53.1 11.5 %collective-permute-start.53 = (f32[1,4,4,16,128]{4,3,2,1,0:T(8,128)S(1)}, f32[1,4,4,16,128]{4,3,2,1,0:T(8,128)S(1)}, u32[]{:S(2)}, u32[]{:S(2)}) collective-permute-start(f32[1,4,4,16,128]{4,3,2,1,0:T(8,128)S(1)} %get-tuple-element.53), channel_id=1, source_target_pairs={{0,4},{1,5},{2,6},{3,7},{4,0},{5,1},{6,2},{7,3},{8,12},{9,13},{10,... | collective-permute-start | bytes 393224 | tf_op jit(solution)/shard_map/ppermute | solution.py:176
  56.1 13.1 %collective-permute-start.43 = (f32[1,4,4,16,128]{4,3,2,1,0:T(8,128)S(1)}, f32[1,4,4,16,128]{4,3,2,1,0:T(8,128)S(1)}, u32[]{:S(2)}, u32[]{:S(2)}) collective-permute-start(f32[1,4,4,16,128]{4,3,2,1,0:T(8,128)S(1)} %get-tuple-element.67), channel_id=1, source_target_pairs={{0,12},{1,13},{2,14},{3,15},{4,8},{5,9},{6,10},{7,11},{8,4},{9,5},... | collective-permute-start | bytes 393224 | tf_op jit(solution)/shard_map/ppermute | solution.py:176
  58.6 16.9 %collective-permute-start.42 = (f32[1,4,4,16,128]{4,3,2,1,0:T(8,128)S(1)}, f32[1,4,4,16,128]{4,3,2,1,0:T(8,128)S(1)}, u32[]{:S(2)}, u32[]{:S(2)}) collective-permute-start(f32[1,4,4,16,128]{4,3,2,1,0:T(8,128)S(1)} %get-tuple-element.68), channel_id=1, source_target_pairs={{0,8},{1,9},{2,10},{3,11},{4,12},{5,13},{6,14},{7,15},{8,0},{9,1},... | collective-permute-start | bytes 393224 | tf_op jit(solution)/shard_map/ppermute | solution.py:176
  58.9 16.6 %collective-permute-start.41 = (f32[1,4,4,16,128]{4,3,2,1,0:T(8,128)S(1)}, f32[1,4,4,16,128]{4,3,2,1,0:T(8,128)S(1)}, u32[]{:S(2)}, u32[]{:S(2)}) collective-permute-start(f32[1,4,4,16,128]{4,3,2,1,0:T(8,128)S(1)} %get-tuple-element.69), channel_id=1, source_target_pairs={{0,4},{1,5},{2,6},{3,7},{4,0},{5,1},{6,2},{7,3},{8,12},{9,13},{10,... | collective-permute-start | bytes 393224 | tf_op jit(solution)/shard_map/ppermute | solution.py:176
  64.7 12.7 %collective-permute-start.58 = (f32[4,1,4,16,128]{4,3,2,0,1:T(8,128)S(1)}, f32[4,1,4,16,128]{4,3,2,0,1:T(8,128)S(1)}, u32[]{:S(2)}, u32[]{:S(2)}) collective-permute-start(f32[4,1,4,16,128]{4,3,2,0,1:T(8,128)S(1)} %get-tuple-element.47), channel_id=1, source_target_pairs={{0,3},{1,2},{2,1},{3,0},{4,7},{5,6},{6,5},{7,4},{8,11},{9,10},{10,... | collective-permute-start | bytes 393224 | tf_op jit(solution)/shard_map/ppermute | solution.py:176
  66.1 11.4 %collective-permute-start.57 = (f32[4,1,4,16,128]{4,3,2,0,1:T(8,128)S(1)}, f32[4,1,4,16,128]{4,3,2,0,1:T(8,128)S(1)}, u32[]{:S(2)}, u32[]{:S(2)}) collective-permute-start(f32[4,1,4,16,128]{4,3,2,0,1:T(8,128)S(1)} %get-tuple-element.48), channel_id=1, source_target_pairs={{0,2},{1,3},{2,0},{3,1},{4,6},{5,7},{6,4},{7,5},{8,10},{9,11},{10,... | collective-permute-start | bytes 393224 | tf_op jit(solution)/shard_map/ppermute | solution.py:176
  69.2 8.4 %collective-permute-start.56 = (f32[4,1,4,16,128]{4,3,2,0,1:T(8,128)S(1)}, f32[4,1,4,16,128]{4,3,2,0,1:T(8,128)S(1)}, u32[]{:S(2)}, u32[]{:S(2)}) collective-permute-start(f32[4,1,4,16,128]{4,3,2,0,1:T(8,128)S(1)} %get-tuple-element.49), channel_id=1, source_target_pairs={{0,1},{1,0},{2,3},{3,2},{4,5},{5,4},{6,7},{7,6},{8,9},{9,8},{10,11... | collective-permute-start | bytes 393224 | tf_op jit(solution)/shard_map/ppermute | solution.py:176
  75.6 5.7 %collective-permute-start.46 = (f32[4,1,4,16,128]{4,3,2,0,1:T(8,128)S(1)}, f32[4,1,4,16,128]{4,3,2,0,1:T(8,128)S(1)}, u32[]{:S(2)}, u32[]{:S(2)}) collective-permute-start(f32[4,1,4,16,128]{4,3,2,0,1:T(8,128)S(1)} %get-tuple-element.63), channel_id=1, source_target_pairs={{0,3},{1,2},{2,1},{3,0},{4,7},{5,6},{6,5},{7,4},{8,11},{9,10},{10,... | collective-permute-start | bytes 393224 | tf_op jit(solution)/shard_map/ppermute | solution.py:176
  75.8 8.4 %collective-permute-start.45 = (f32[4,1,4,16,128]{4,3,2,0,1:T(8,128)S(1)}, f32[4,1,4,16,128]{4,3,2,0,1:T(8,128)S(1)}, u32[]{:S(2)}, u32[]{:S(2)}) collective-permute-start(f32[4,1,4,16,128]{4,3,2,0,1:T(8,128)S(1)} %get-tuple-element.64), channel_id=1, source_target_pairs={{0,2},{1,3},{2,0},{3,1},{4,6},{5,7},{6,4},{7,5},{8,10},{9,11},{10,... | collective-permute-start | bytes 393224 | tf_op jit(solution)/shard_map/ppermute | solution.py:176
  77.3 7.0 %collective-permute-start.44 = (f32[4,1,4,16,128]{4,3,2,0,1:T(8,128)S(1)}, f32[4,1,4,16,128]{4,3,2,0,1:T(8,128)S(1)}, u32[]{:S(2)}, u32[]{:S(2)}) collective-permute-start(f32[4,1,4,16,128]{4,3,2,0,1:T(8,128)S(1)} %get-tuple-element.65), channel_id=1, source_target_pairs={{0,1},{1,0},{2,3},{3,2},{4,5},{5,4},{6,7},{7,6},{8,9},{9,8},{10,11... | collective-permute-start | bytes 393224 | tf_op jit(solution)/shard_map/ppermute | solution.py:176
  (10 other events, 18.1 us)

commit v8 on v5

--- a/solution.py
+++ b/solution.py
@@ -49,9 +49,19 @@
     return gap, anisotropy, unit
 
 
-def pack_kernel(quantities, rank, fields, density, head, tail, low, high, still):
+def pack_kernel(
+    quantities, rank, fields_in, density_in, head, tail, low, high, still, fields, density, sems
+):
     columns, cells, depth = density.shape
     slots, share = still.shape[0], still.shape[1]
+    copies = [
+        pltpu.make_async_copy(density_in, density, sems.at[0]),
+        pltpu.make_async_copy(fields_in.at[0:6], fields, sems.at[1]),
+    ]
+    for copy in copies:
+        copy.start()
+    for copy in copies:
+        copy.wait()
 
     def source(row):
         if row == 3:
@@ -101,8 +111,13 @@
             rim,
             jax.ShapeDtypeStruct((slots, share, cells, depth), f32),
         ),
-        in_specs=[pl.BlockSpec(memory_space=pltpu.SMEM), vmem, vmem],
+        in_specs=[pl.BlockSpec(memory_space=pltpu.SMEM)] + [pl.BlockSpec(memory_space=pltpu.HBM)] * 2,
         out_specs=[vmem] * 5,
+        scratch_shapes=[
+            pltpu.VMEM((6, columns, cells, depth), f32),
+            pltpu.VMEM((columns, cells, depth), f32),
+            pltpu.SemaphoreType.DMA((2,)),
+        ],
         compiler_params=pltpu.CompilerParams(vmem_limit_bytes=16 * 2**20),
         name="pack",
     )(rank, fields, density)
@@ -148,17 +163,24 @@
     )(rank, moving, still)
 
 
-def swap(slots):
-    count = slots.shape[0]
-    stride = count
-    while stride > 1:
-        radix = 4 if stride % 4 == 0 else 2
-        stride //= radix
-        cut = slots.reshape(count // (radix * stride), radix, stride, *slots.shape[1:])
-        parts = [cut[:, 0]]
-        for step in range(1, radix):
-            pairs = [(rank, rank ^ (step * stride)) for rank in range(count)]
-            parts.append(lax.ppermute(cut[:, step], "az", pairs))
+def digit_radix(span):
+    return 4 if span % 4 == 0 else 2
+
+
+def send_step(cut, step):
+    radix, stride = cut.shape[1], cut.shape[2]
+    count = cut.shape[0] * radix * stride
+    pairs = [(rank, rank ^ (step * stride)) for rank in range(count)]
+    return lax.ppermute(cut[:, step], "az", pairs)
+
+
+def swap(slots, span=None):
+    span = slots.shape[0] if span is None else span
+    while span > 1:
+        radix = digit_radix(span)
+        span //= radix
+        cut = slots.reshape(-1, radix, span, *slots.shape[1:])
+        parts = [cut[:, 0]] + [send_step(cut, step) for step in range(1, radix)]
         slots = jnp.stack(parts, axis=1).reshape(slots.shape)
     return slots
 
@@ -290,7 +312,7 @@
         heat[ghost] = gap * anisotropy
         return carry
 
-    lax.fori_loop(0, columns + 2, tensor_column, 0)
+    lax.fori_loop(0, columns + 2, tensor_column, 0, unroll=3)
 
     def update_column(column, carry):
         ghost = column + 1
@@ -312,7 +334,7 @@
                 out[slot, flat % share] = fields[6, column] + heat[ghost]
         return carry
 
-    lax.fori_loop(0, columns, update_column, 0)
+    lax.fori_loop(0, columns, update_column, 0, unroll=4)
 
 
 def updated_columns(info, fields, density, *layers):
@@ -447,9 +469,16 @@
     rank = az.reshape(1)
     head, tail, low, high, still = pack(rank, fields, density)
     before, after = azimuthal_layers(head, tail)
-    before, after, still = lax.optimization_barrier((before, after, still))
-    still = swap(still)
+    count = still.shape[0]
+    radix = digit_radix(count)
+    span = count // radix
+    cut = still.reshape(1, radix, span, *still.shape[1:])
+    nearest = send_step(cut, 1)
+    before, after, nearest, cut = lax.optimization_barrier((before, after, nearest, cut))
+    parts = [cut[:, 0], nearest] + [send_step(cut, step) for step in range(2, radix)]
     layers = rims(shear_cells // cells, low, high, before, after)
+    parts, layers = lax.optimization_barrier((parts, layers))
+    still = swap(jnp.stack(parts, axis=1).reshape(still.shape), span)
     info = jnp.stack(
         [
             (rad == 0).astype(jnp.int32),

time: 86.9 us -> 82.6 us (0.951); the launches traced: 86.8 us -> 83.9 us
  waiting for transfers between devices: 37.5 us -> 33 us
  starting transfers between devices: 36.7 us -> 39.9 us
  Pallas kernels: 7.45 us -> 5.86 us
    ppermute x24, starting transfers between devices: 26.4 us -> 32 us  [send_step(): return lax.ppermute(cut[:, step], 'az', pairs)]
    ppermute x24, waiting for transfers between devices: 29.1 us -> 25.7 us  [send_step(): return lax.ppermute(cut[:, step], 'az', pairs)]
    ppermute x2, starting transfers between devices: 2.6 us -> 0.11 us  [wrap(): return lax.ppermute(data, ('rad', 'az'), pairs)]
    pallas_call x1, Pallas kernels: 4.27 us -> 2.47 us  [updated_columns(): pl.pallas_call(stress_kernel, out_shape=jax.ShapeDtypeStruct((slots, 4 *...]
    ppermute x2, waiting for transfers between devices: 7.08 us -> 5.91 us  [wrap(): return lax.ppermute(data, ('rad', 'az'), pairs)]
  transfers between devices with their start and end apart: 29 -> 29, of which waited for: 13 -> 11; matrix products, arithmetic and copies ran while one was open for 1% -> 1% of each run, Pallas kernels for 7% -> 2%
where the time goes in v8:
time: 82.6 us; the launch traced here: 83.9 us
  starting transfers between devices  39.9 us (48%)
  waiting for transfers between devices  33 us (40%)
  Pallas kernels  5.86 us (7%)
  local copies, waits for them, and re-layouts  3.07 us (4%)
  between operations  1.64 us (2%)
    ppermute x24, starting transfers between devices, send_step(): return lax.ppermute(cut[:, step], 'az', pairs)  32 us
    ppermute x24, waiting for transfers between devices, send_step(): return lax.ppermute(cut[:, step], 'az', pairs)  25.7 us
    ppermute x2, waiting for transfers between devices, wrap(): return lax.ppermute(data, ('rad', 'az'), pairs)  5.91 us
    ppermute x1, starting transfers between devices, azimuthal_layers(): far = lax.ppermute(jnp.where(even, head, tail), 'az', outer)  5.67 us
    unnamed x12, local copies, waits for them, and re-layouts  2.74 us
    pallas_call x1, Pallas kernels, updated_columns(): pl.pallas_call(stress_kernel, out_shape=jax.ShapeDtypeStruct((slots, 4 *...  2.47 us
    pallas_call x2, Pallas kernels, move_columns(): pl.pallas_call(functools.partial(move_kernel, quantities), out_shape=jax....  1.99 us
  transfers between devices with their start and end apart: 29, of which 11 were waited for; matrix products, arithmetic and copies ran while one was open for 1% of the time, Pallas kernels for 2%

profile of v8, /device:TPU:0, one launch (start us, length us, event | category | flops | bytes accessed | tf_op | source)
XLA Modules:
  0.0 83.9 jit_solution(12526402996515383414)
XLA Ops:
  0.7 1.2 %copy-done = f32[7,16,16,128]{3,2,1,0:T(8,128)S(1)} copy-done((f32[7,16,16,128]{3,2,1,0:T(8,128)S(1)}, f32[7,16,16,128]{3,2,1,0:T(8,128)}, u32[]{:S(2)}) %copy-start) | copy-done | bytes 917528
  1.8 0.9 %copy-done.2 = f32[16,16,128]{2,1,0:T(8,128)S(1)} copy-done((f32[16,16,128]{2,1,0:T(8,128)S(1)}, f32[16,16,128]{2,1,0:T(8,128)}, u32[]{:S(2)}) %copy-start.2) | copy-done | bytes 131096
  3.6 5.7 %collective-permute-start.32 = (f32[10,16,128]{2,1,0:T(8,128)S(1)}, f32[10,16,128]{2,1,0:T(8,128)S(1)}, u32[]{:S(2)}, u32[]{:S(2)}) collective-permute-start(f32[10,16,128]{2,1,0:T(8,128)S(1)} %get-tuple-element.92), channel_id=1, source_target_pairs={{0,15},{1,2},{2,1},{3,4},{4,3},{5,6},{6,5},{7,8},{8,7},{9,10},{10,... | collective-permute-start | bytes 245768 | tf_op jit(solution)/shard_map/ppermute | solution.py:422
  10.2 1.4 %collective-permute-done.32 = f32[10,16,128]{2,1,0:T(8,128)S(1)} collective-permute-done((f32[10,16,128]{2,1,0:T(8,128)S(1)}, f32[10,16,128]{2,1,0:T(8,128)S(1)}, u32[]{:S(2)}, u32[]{:S(2)}) %collective-permute-start.32) | collective-permute-done | bytes 81952 | tf_op jit(solution)/shard_map/ppermute | solution.py:422
  11.6 2.8 %collective-permute-done.34 = f32[1,4,4,16,128]{4,3,2,1,0:T(8,128)S(1)} collective-permute-done((f32[1,4,4,16,128]{4,3,2,1,0:T(8,128)S(1)}, f32[1,4,4,16,128]{4,3,2,1,0:T(8,128)S(1)}, u32[]{:S(2)}, u32[]{:S(2)}) %collective-permute-start.34) | collective-permute-done | bytes 131104 | tf_op jit(solution)/shard_map/ppermute | solution.py:174
  14.5 2.0 %collective-permute-start.36 = (f32[1,4,4,16,128]{4,3,2,1,0:T(8,128)S(1)}, f32[1,4,4,16,128]{4,3,2,1,0:T(8,128)S(1)}, u32[]{:S(2)}, u32[]{:S(2)}) collective-permute-start(f32[1,4,4,16,128]{4,3,2,1,0:T(8,128)S(1)} %get-tuple-element.84), channel_id=1, source_target_pairs={{0,12},{1,13},{2,14},{3,15},{4,8},{5,9},{6,10},{7,11},{8,4},{9,5},... | collective-permute-start | bytes 393224 | tf_op jit(solution)/shard_map/ppermute | solution.py:174
  16.8 1.6 %collective-permute-start.37 = (f32[11,16,128]{2,1,0:T(8,128)S(1)}, f32[11,16,128]{2,1,0:T(8,128)S(1)}, u32[]{:S(2)}, u32[]{:S(2)}) collective-permute-start(f32[11,16,128]{2,1,0:T(8,128)S(1)} %get-tuple-element.88), channel_id=1, source_target_pairs={{0,16},{16,0},{1,17},{17,1},{2,18},{18,2},{3,19},{19,3},{4,20},{20... | collective-permute-start | bytes 270344 | tf_op jit(solution)/shard_map/ppermute | solution.py:451
  18.4 6.0 %conditional.1 = (f32[11,16,128]{2,1,0:T(8,128)}, f32[11,16,128]{2,1,0:T(8,128)}) conditional(s32[]{:T(128)} %clamp.3, f32[11,16,128]{2,1,0:T(8,128)S(1)} %get-tuple-element.87, f32[11,16,128]{2,1,0:T(8,128)S(1)} %get-tuple-element.87, f32[11,16,128]{2,1,0:T(8,128)S(1)} %get-tuple-element.87, ...), branch_computations={%region_0.1_spmd, %region_1.2_spmd, %region_2.3_spmd, %region_3.4_... | conditional | bytes 720992 | solution.py:459
  18.6 5.9 %collective-permute-done.27 = f32[11,16,128]{2,1,0:T(8,128)} collective-permute-done((f32[11,16,128]{2,1,0:T(8,128)S(1)}, f32[11,16,128]{2,1,0:T(8,128)}, u32[]{:S(2)}, u32[]{:S(2)}) %collective-permute-start.27) | collective-permute-done | bytes 90144 | tf_op jit(solution)/shard_map/cond/branch_13_fun/ppermute | solution.py:439
  24.5 3.0 %collective-permute-done.35 = f32[1,4,4,16,128]{4,3,2,1,0:T(8,128)S(1)} collective-permute-done((f32[1,4,4,16,128]{4,3,2,1,0:T(8,128)S(1)}, f32[1,4,4,16,128]{4,3,2,1,0:T(8,128)S(1)}, u32[]{:S(2)}, u32[]{:S(2)}) %collective-permute-start.35) | collective-permute-done | bytes 131104 | tf_op jit(solution)/shard_map/ppermute | solution.py:174
  27.5 2.5 %stress_update.1 = f32[16,4,16,128]{3,2,1,0:T(8,128)S(1)} custom-call(s32[4]{0:T(128)S(1)} %pad_add_fusion.info, f32[7,16,16,128]{3,2,1,0:T(8,128)S(1)} %copy-done.1, f32[16,16,128]{2,1,0:T(8,128)S(1)} %copy-done.3, f32[10,16,128]{2,1,0:T(8,128)S(1)} %get-tuple-element.37.head, f32[10,16,128]{2,1,0:T(8,128)S(1)} %get-tuple-element.38.tail, ...), custom_call_target="tpu_custom_call" | custom-call | tf_op jit(solution)/shard_map/stress_update/pallas_call | solution.py:347
  30.0 2.7 %collective-permute-start.40 = (f32[1,4,4,16,128]{4,3,2,1,0:T(8,128)S(1)}, f32[1,4,4,16,128]{4,3,2,1,0:T(8,128)S(1)}, u32[]{:S(2)}, u32[]{:S(2)}) collective-permute-start(f32[1,4,4,16,128]{4,3,2,1,0:T(8,128)S(1)} %get-tuple-element.81), channel_id=1, source_target_pairs={{0,12},{1,13},{2,14},{3,15},{4,8},{5,9},{6,10},{7,11},{8,4},{9,5},... | collective-permute-start | bytes 393224 | tf_op jit(solution)/shard_map/ppermute | solution.py:174
  32.7 1.7 %collective-permute-start.38 = (f32[1,4,4,16,128]{4,3,2,1,0:T(8,128)S(1)}, f32[1,4,4,16,128]{4,3,2,1,0:T(8,128)S(1)}, u32[]{:S(2)}, u32[]{:S(2)}) collective-permute-start(f32[1,4,4,16,128]{4,3,2,1,0:T(8,128)S(1)} %get-tuple-element.83), channel_id=1, source_target_pairs={{0,4},{1,5},{2,6},{3,7},{4,0},{5,1},{6,2},{7,3},{8,12},{9,13},{10,... | collective-permute-start | bytes 393224 | tf_op jit(solution)/shard_map/ppermute | solution.py:174
  34.6 2.7 %collective-permute-start.52 = (f32[4,1,4,16,128]{4,3,2,0,1:T(8,128)S(1)}, f32[4,1,4,16,128]{4,3,2,0,1:T(8,128)S(1)}, u32[]{:S(2)}, u32[]{:S(2)}) collective-permute-start(f32[4,1,4,16,128]{4,3,2,0,1:T(8,128)S(1)} %get-tuple-element.65), channel_id=1, source_target_pairs={{0,3},{1,2},{2,1},{3,0},{4,7},{5,6},{6,5},{7,4},{8,11},{9,10},{10,... | collective-permute-start | bytes 393224 | tf_op jit(solution)/shard_map/ppermute | solution.py:174
  37.3 2.0 %collective-permute-start.51 = (f32[4,1,4,16,128]{4,3,2,0,1:T(8,128)S(1)}, f32[4,1,4,16,128]{4,3,2,0,1:T(8,128)S(1)}, u32[]{:S(2)}, u32[]{:S(2)}) collective-permute-start(f32[4,1,4,16,128]{4,3,2,0,1:T(8,128)S(1)} %get-tuple-element.66), channel_id=1, source_target_pairs={{0,2},{1,3},{2,0},{3,1},{4,6},{5,7},{6,4},{7,5},{8,10},{9,11},{10,... | collective-permute-start | bytes 393224 | tf_op jit(solution)/shard_map/ppermute | solution.py:174
  39.3 4.6 %collective-permute-done.39 = f32[1,4,4,16,128]{4,3,2,1,0:T(8,128)S(1)} collective-permute-done((f32[1,4,4,16,128]{4,3,2,1,0:T(8,128)S(1)}, f32[1,4,4,16,128]{4,3,2,1,0:T(8,128)S(1)}, u32[]{:S(2)}, u32[]{:S(2)}) %collective-permute-start.39) | collective-permute-done | bytes 131104 | tf_op jit(solution)/shard_map/ppermute | solution.py:174
  44.7 2.9 %collective-permute-start.42 = (f32[4,1,4,16,128]{4,3,2,0,1:T(8,128)S(1)}, f32[4,1,4,16,128]{4,3,2,0,1:T(8,128)S(1)}, u32[]{:S(2)}, u32[]{:S(2)}) collective-permute-start(f32[4,1,4,16,128]{4,3,2,0,1:T(8,128)S(1)} %get-tuple-element.78), channel_id=1, source_target_pairs={{0,2},{1,3},{2,0},{3,1},{4,6},{5,7},{6,4},{7,5},{8,10},{9,11},{10,... | collective-permute-start | bytes 393224 | tf_op jit(solution)/shard_map/ppermute | solution.py:174
  48.4 1.0 %move.3 = f32[16,4,16,128]{3,2,1,0:T(8,128)S(1)} custom-call(s32[1]{0:T(128)} %bitcast.rank, s32[16]{0:T(128)S(1)} %copy-done.4, s32[16]{0:T(128)S(1)} %copy-done.5, f32[16,4,16,128]{3,2,1,0:T(8,128)S(1)} %bitcast.153), custom_call_target="tpu_custom_call" | custom-call | tf_op jit(solution)/shard_map/move/pallas_call | solution.py:406
  49.4 1.2 %collective-permute-start.55 = (f32[1,4,4,16,128]{4,3,2,1,0:T(8,128)S(1)}, f32[1,4,4,16,128]{4,3,2,1,0:T(8,128)S(1)}, u32[]{:S(2)}, u32[]{:S(2)}) collective-permute-start(f32[1,4,4,16,128]{4,3,2,1,0:T(8,128)S(1)} %get-tuple-element.61), channel_id=1, source_target_pairs={{0,12},{1,13},{2,14},{3,15},{4,8},{5,9},{6,10},{7,11},{8,4},{9,5},... | collective-permute-start | bytes 393224 | tf_op jit(solution)/shard_map/ppermute | solution.py:174
  50.6 3.3 %collective-permute-start.53 = (f32[1,4,4,16,128]{4,3,2,1,0:T(8,128)S(1)}, f32[1,4,4,16,128]{4,3,2,1,0:T(8,128)S(1)}, u32[]{:S(2)}, u32[]{:S(2)}) collective-permute-start(f32[1,4,4,16,128]{4,3,2,1,0:T(8,128)S(1)} %get-tuple-element.63), channel_id=1, source_target_pairs={{0,4},{1,5},{2,6},{3,7},{4,0},{5,1},{6,2},{7,3},{8,12},{9,13},{10,... | collective-permute-start | bytes 393224 | tf_op jit(solution)/shard_map/ppermute | solution.py:174
  53.9 1.0 %move.2 = f32[16,4,16,128]{3,2,1,0:T(8,128)S(1)} custom-call(s32[1]{0:T(128)} %bitcast.rank, s32[16]{0:T(128)S(1)} %copy-done.4, s32[16]{0:T(128)S(1)} %copy-done.5, f32[16,4,16,128]{3,2,1,0:T(8,128)S(1)} %bitcast.154), custom_call_target="tpu_custom_call" | custom-call | tf_op jit(solution)/shard_map/move/pallas_call | solution.py:406
  55.0 1.2 %collective-permute-start.46 = (f32[1,4,4,16,128]{4,3,2,1,0:T(8,128)S(1)}, f32[1,4,4,16,128]{4,3,2,1,0:T(8,128)S(1)}, u32[]{:S(2)}, u32[]{:S(2)}) collective-permute-start(f32[1,4,4,16,128]{4,3,2,1,0:T(8,128)S(1)} %get-tuple-element.73), channel_id=1, source_target_pairs={{0,12},{1,13},{2,14},{3,15},{4,8},{5,9},{6,10},{7,11},{8,4},{9,5},... | collective-permute-start | bytes 393224 | tf_op jit(solution)/shard_map/ppermute | solution.py:174
  56.5 1.2 %collective-permute-done.55 = f32[1,4,4,16,128]{4,3,2,1,0:T(8,128)S(1)} collective-permute-done((f32[1,4,4,16,128]{4,3,2,1,0:T(8,128)S(1)}, f32[1,4,4,16,128]{4,3,2,1,0:T(8,128)S(1)}, u32[]{:S(2)}, u32[]{:S(2)}) %collective-permute-start.55) | collective-permute-done | bytes 131104 | tf_op jit(solution)/shard_map/ppermute | solution.py:174
  57.7 1.7 %collective-permute-start.44 = (f32[1,4,4,16,128]{4,3,2,1,0:T(8,128)S(1)}, f32[1,4,4,16,128]{4,3,2,1,0:T(8,128)S(1)}, u32[]{:S(2)}, u32[]{:S(2)}) collective-permute-start(f32[1,4,4,16,128]{4,3,2,1,0:T(8,128)S(1)} %get-tuple-element.75), channel_id=1, source_target_pairs={{0,4},{1,5},{2,6},{3,7},{4,0},{5,1},{6,2},{7,3},{8,12},{9,13},{10,... | collective-permute-start | bytes 393224 | tf_op jit(solution)/shard_map/ppermute | solution.py:174
  59.4 4.0 %collective-permute-done.54 = f32[1,4,4,16,128]{4,3,2,1,0:T(8,128)S(1)} collective-permute-done((f32[1,4,4,16,128]{4,3,2,1,0:T(8,128)S(1)}, f32[1,4,4,16,128]{4,3,2,1,0:T(8,128)S(1)}, u32[]{:S(2)}, u32[]{:S(2)}) %collective-permute-start.54) | collective-permute-done | bytes 131104 | tf_op jit(solution)/shard_map/ppermute | solution.py:174
  63.5 1.4 %collective-permute-start.58 = (f32[4,1,4,16,128]{4,3,2,0,1:T(8,128)S(1)}, f32[4,1,4,16,128]{4,3,2,0,1:T(8,128)S(1)}, u32[]{:S(2)}, u32[]{:S(2)}) collective-permute-start(f32[4,1,4,16,128]{4,3,2,0,1:T(8,128)S(1)} %get-tuple-element.57), channel_id=1, source_target_pairs={{0,3},{1,2},{2,1},{3,0},{4,7},{5,6},{6,5},{7,4},{8,11},{9,10},{10,... | collective-permute-start | bytes 393224 | tf_op jit(solution)/shard_map/ppermute | solution.py:174
  64.9 5.7 %collective-permute-start.57 = (f32[4,1,4,16,128]{4,3,2,0,1:T(8,128)S(1)}, f32[4,1,4,16,128]{4,3,2,0,1:T(8,128)S(1)}, u32[]{:S(2)}, u32[]{:S(2)}) collective-permute-start(f32[4,1,4,16,128]{4,3,2,0,1:T(8,128)S(1)} %get-tuple-element.58), channel_id=1, source_target_pairs={{0,2},{1,3},{2,0},{3,1},{4,6},{5,7},{6,4},{7,5},{8,10},{9,11},{10,... | collective-permute-start | bytes 393224 | tf_op jit(solution)/shard_map/ppermute | solution.py:174
  70.6 3.4 %collective-permute-done.45 = f32[1,4,4,16,128]{4,3,2,1,0:T(8,128)S(1)} collective-permute-done((f32[1,4,4,16,128]{4,3,2,1,0:T(8,128)S(1)}, f32[1,4,4,16,128]{4,3,2,1,0:T(8,128)S(1)}, u32[]{:S(2)}, u32[]{:S(2)}) %collective-permute-start.45) | collective-permute-done | bytes 131104 | tf_op jit(solution)/shard_map/ppermute | solution.py:174
  74.1 1.1 %collective-permute-start.49 = (f32[4,1,4,16,128]{4,3,2,0,1:T(8,128)S(1)}, f32[4,1,4,16,128]{4,3,2,0,1:T(8,128)S(1)}, u32[]{:S(2)}, u32[]{:S(2)}) collective-permute-start(f32[4,1,4,16,128]{4,3,2,0,1:T(8,128)S(1)} %get-tuple-element.69), channel_id=1, source_target_pairs={{0,3},{1,2},{2,1},{3,0},{4,7},{5,6},{6,5},{7,4},{8,11},{9,10},{10,... | collective-permute-start | bytes 393224 | tf_op jit(solution)/shard_map/ppermute | solution.py:174
  76.3 3.4 %collective-permute-done.49 = f32[4,1,4,16,128]{4,3,2,0,1:T(8,128)S(1)} collective-permute-done((f32[4,1,4,16,128]{4,3,2,0,1:T(8,128)S(1)}, f32[4,1,4,16,128]{4,3,2,0,1:T(8,128)S(1)}, u32[]{:S(2)}, u32[]{:S(2)}) %collective-permute-start.49) | collective-permute-done | bytes 131104 | tf_op jit(solution)/shard_map/ppermute | solution.py:174
  79.7 3.1 %collective-permute-done.48 = f32[4,1,4,16,128]{4,3,2,0,1:T(8,128)S(1)} collective-permute-done((f32[4,1,4,16,128]{4,3,2,0,1:T(8,128)S(1)}, f32[4,1,4,16,128]{4,3,2,0,1:T(8,128)S(1)}, u32[]{:S(2)}, u32[]{:S(2)}) %collective-permute-start.48) | collective-permute-done | bytes 131104 | tf_op jit(solution)/shard_map/ppermute | solution.py:174
  82.8 1.0 %join.1 = (f32[7,16,16,128]{3,2,1,0:T(8,128)}, f32[16,16,128]{2,1,0:T(8,128)}) custom-call(s32[1]{0:T(128)} %bitcast.rank, f32[16,4,16,128]{3,2,1,0:T(8,128)S(1)} %bitcast.150, f32[16,4,16,128]{3,2,1,0:T(8,128)S(1)} %bitcast.149), custom_call_target="tpu_custom_call" | custom-call | tf_op jit(solution)/shard_map/join/pallas_call | solution.py:153
  (70 shorter events, 5.0 us)
Async XLA Ops:
  0.6 1.2 %copy-start = (f32[7,16,16,128]{3,2,1,0:T(8,128)S(1)}, f32[7,16,16,128]{3,2,1,0:T(8,128)}, u32[]{:S(2)}) copy-start(f32[7,16,16,128]{3,2,1,0:T(8,128)} %fields.1) | copy-start | bytes 2752516
  3.1 7.0 %collective-permute-start.33 = (f32[10,16,128]{2,1,0:T(8,128)S(1)}, f32[10,16,128]{2,1,0:T(8,128)S(1)}, u32[]{:S(2)}, u32[]{:S(2)}) collective-permute-start(f32[10,16,128]{2,1,0:T(8,128)S(1)} %get-tuple-element.91), channel_id=1, source_target_pairs={{0,1},{1,0},{2,3},{3,2},{4,5},{5,4},{6,7},{7,6},{8,9},{9,8},{10,11... | collective-permute-start | bytes 245768 | tf_op jit(solution)/shard_map/ppermute | solution.py:423
  3.6 7.9 %collective-permute-start.32 = (f32[10,16,128]{2,1,0:T(8,128)S(1)}, f32[10,16,128]{2,1,0:T(8,128)S(1)}, u32[]{:S(2)}, u32[]{:S(2)}) collective-permute-start(f32[10,16,128]{2,1,0:T(8,128)S(1)} %get-tuple-element.92), channel_id=1, source_target_pairs={{0,15},{1,2},{2,1},{3,4},{4,3},{5,6},{6,5},{7,8},{8,7},{9,10},{10,... | collective-permute-start | bytes 245768 | tf_op jit(solution)/shard_map/ppermute | solution.py:422
  9.3 18.2 %copy-start.1 = (f32[7,16,16,128]{3,2,1,0:T(8,128)S(1)}, f32[7,16,16,128]{3,2,1,0:T(8,128)}, u32[]{:S(2)}) copy-start(f32[7,16,16,128]{3,2,1,0:T(8,128)} %fields.1) | copy-start | bytes 2752516
  9.3 5.0 %collective-permute-start.34 = (f32[1,4,4,16,128]{4,3,2,1,0:T(8,128)S(1)}, f32[1,4,4,16,128]{4,3,2,1,0:T(8,128)S(1)}, u32[]{:S(2)}, u32[]{:S(2)}) collective-permute-start(f32[1,4,4,16,128]{4,3,2,1,0:T(8,128)S(1)} %slice_bitcast_fusion.28), channel_id=1, source_target_pairs={{0,4},{1,5},{2,6},{3,7},{4,0},{5,1},{6,2},{7,3},{8,12},{9,13},{10,... | collective-permute-start | bytes 393224 | tf_op jit(solution)/shard_map/ppermute | solution.py:174
  14.5 10.0 %collective-permute-start.36 = (f32[1,4,4,16,128]{4,3,2,1,0:T(8,128)S(1)}, f32[1,4,4,16,128]{4,3,2,1,0:T(8,128)S(1)}, u32[]{:S(2)}, u32[]{:S(2)}) collective-permute-start(f32[1,4,4,16,128]{4,3,2,1,0:T(8,128)S(1)} %get-tuple-element.84), channel_id=1, source_target_pairs={{0,12},{1,13},{2,14},{3,15},{4,8},{5,9},{6,10},{7,11},{8,4},{9,5},... | collective-permute-start | bytes 393224 | tf_op jit(solution)/shard_map/ppermute | solution.py:174
  16.5 11.0 %collective-permute-start.35 = (f32[1,4,4,16,128]{4,3,2,1,0:T(8,128)S(1)}, f32[1,4,4,16,128]{4,3,2,1,0:T(8,128)S(1)}, u32[]{:S(2)}, u32[]{:S(2)}) collective-permute-start(f32[1,4,4,16,128]{4,3,2,1,0:T(8,128)S(1)} %get-tuple-element.85), channel_id=1, source_target_pairs={{0,8},{1,9},{2,10},{3,11},{4,12},{5,13},{6,14},{7,15},{8,0},{9,1},... | collective-permute-start | bytes 393224 | tf_op jit(solution)/shard_map/ppermute | solution.py:174
  16.8 10.7 %copy-start.3 = (f32[16,16,128]{2,1,0:T(8,128)S(1)}, f32[16,16,128]{2,1,0:T(8,128)}, u32[]{:S(2)}) copy-start(f32[16,16,128]{2,1,0:T(8,128)} %density.1) | copy-start | bytes 393220
  16.8 7.7 %collective-permute-start.37 = (f32[11,16,128]{2,1,0:T(8,128)S(1)}, f32[11,16,128]{2,1,0:T(8,128)S(1)}, u32[]{:S(2)}, u32[]{:S(2)}) collective-permute-start(f32[11,16,128]{2,1,0:T(8,128)S(1)} %get-tuple-element.88), channel_id=1, source_target_pairs={{0,16},{16,0},{1,17},{17,1},{2,18},{18,2},{3,19},{19,3},{4,20},{20... | collective-permute-start | bytes 270344 | tf_op jit(solution)/shard_map/ppermute | solution.py:451
  18.4 6.0 %collective-permute-start.27 = (f32[11,16,128]{2,1,0:T(8,128)S(1)}, f32[11,16,128]{2,1,0:T(8,128)}, u32[]{:S(2)}, u32[]{:S(2)}) collective-permute-start(f32[11,16,128]{2,1,0:T(8,128)S(1)} %param.13), channel_id=1, source_target_pairs={{16,14},{17,15},{18,0},{19,1},{20,2},{21,3},{22,4},{23,5},{24,6},{... | collective-permute-start | bytes 270344 | tf_op jit(solution)/shard_map/cond/branch_13_fun/ppermute | solution.py:439
  18.5 6.0 %collective-permute-start.26 = (f32[11,16,128]{2,1,0:T(8,128)S(1)}, f32[11,16,128]{2,1,0:T(8,128)}, u32[]{:S(2)}, u32[]{:S(2)}) collective-permute-start(f32[11,16,128]{2,1,0:T(8,128)S(1)} %param.13), channel_id=1, source_target_pairs={{16,13},{17,14},{18,15},{19,0},{20,1},{21,2},{22,3},{23,4},{24,5},... | collective-permute-start | bytes 270344 | tf_op jit(solution)/shard_map/cond/branch_13_fun/ppermute | solution.py:439
  30.0 9.3 %collective-permute-start.40 = (f32[1,4,4,16,128]{4,3,2,1,0:T(8,128)S(1)}, f32[1,4,4,16,128]{4,3,2,1,0:T(8,128)S(1)}, u32[]{:S(2)}, u32[]{:S(2)}) collective-permute-start(f32[1,4,4,16,128]{4,3,2,1,0:T(8,128)S(1)} %get-tuple-element.81), channel_id=1, source_target_pairs={{0,12},{1,13},{2,14},{3,15},{4,8},{5,9},{6,10},{7,11},{8,4},{9,5},... | collective-permute-start | bytes 393224 | tf_op jit(solution)/shard_map/ppermute | solution.py:174
  32.7 11.2 %collective-permute-start.39 = (f32[1,4,4,16,128]{4,3,2,1,0:T(8,128)S(1)}, f32[1,4,4,16,128]{4,3,2,1,0:T(8,128)S(1)}, u32[]{:S(2)}, u32[]{:S(2)}) collective-permute-start(f32[1,4,4,16,128]{4,3,2,1,0:T(8,128)S(1)} %get-tuple-element.82), channel_id=1, source_target_pairs={{0,8},{1,9},{2,10},{3,11},{4,12},{5,13},{6,14},{7,15},{8,0},{9,1},... | collective-permute-start | bytes 393224 | tf_op jit(solution)/shard_map/ppermute | solution.py:174
  32.7 11.2 %collective-permute-start.38 = (f32[1,4,4,16,128]{4,3,2,1,0:T(8,128)S(1)}, f32[1,4,4,16,128]{4,3,2,1,0:T(8,128)S(1)}, u32[]{:S(2)}, u32[]{:S(2)}) collective-permute-start(f32[1,4,4,16,128]{4,3,2,1,0:T(8,128)S(1)} %get-tuple-element.83), channel_id=1, source_target_pairs={{0,4},{1,5},{2,6},{3,7},{4,0},{5,1},{6,2},{7,3},{8,12},{9,13},{10,... | collective-permute-start | bytes 393224 | tf_op jit(solution)/shard_map/ppermute | solution.py:174
  34.6 13.0 %collective-permute-start.52 = (f32[4,1,4,16,128]{4,3,2,0,1:T(8,128)S(1)}, f32[4,1,4,16,128]{4,3,2,0,1:T(8,128)S(1)}, u32[]{:S(2)}, u32[]{:S(2)}) collective-permute-start(f32[4,1,4,16,128]{4,3,2,0,1:T(8,128)S(1)} %get-tuple-element.65), channel_id=1, source_target_pairs={{0,3},{1,2},{2,1},{3,0},{4,7},{5,6},{6,5},{7,4},{8,11},{9,10},{10,... | collective-permute-start | bytes 393224 | tf_op jit(solution)/shard_map/ppermute | solution.py:174
  37.3 10.4 %collective-permute-start.51 = (f32[4,1,4,16,128]{4,3,2,0,1:T(8,128)S(1)}, f32[4,1,4,16,128]{4,3,2,0,1:T(8,128)S(1)}, u32[]{:S(2)}, u32[]{:S(2)}) collective-permute-start(f32[4,1,4,16,128]{4,3,2,0,1:T(8,128)S(1)} %get-tuple-element.66), channel_id=1, source_target_pairs={{0,2},{1,3},{2,0},{3,1},{4,6},{5,7},{6,4},{7,5},{8,10},{9,11},{10,... | collective-permute-start | bytes 393224 | tf_op jit(solution)/shard_map/ppermute | solution.py:174
  39.3 8.3 %collective-permute-start.50 = (f32[4,1,4,16,128]{4,3,2,0,1:T(8,128)S(1)}, f32[4,1,4,16,128]{4,3,2,0,1:T(8,128)S(1)}, u32[]{:S(2)}, u32[]{:S(2)}) collective-permute-start(f32[4,1,4,16,128]{4,3,2,0,1:T(8,128)S(1)} %get-tuple-element.67), channel_id=1, source_target_pairs={{0,1},{1,0},{2,3},{3,2},{4,5},{5,4},{6,7},{7,6},{8,9},{9,8},{10,11... | collective-permute-start | bytes 393224 | tf_op jit(solution)/shard_map/ppermute | solution.py:174
  44.0 6.5 %collective-permute-start.43 = (f32[4,1,4,16,128]{4,3,2,0,1:T(8,128)S(1)}, f32[4,1,4,16,128]{4,3,2,0,1:T(8,128)S(1)}, u32[]{:S(2)}, u32[]{:S(2)}) collective-permute-start(f32[4,1,4,16,128]{4,3,2,0,1:T(8,128)S(1)} %get-tuple-element.77), channel_id=1, source_target_pairs={{0,3},{1,2},{2,1},{3,0},{4,7},{5,6},{6,5},{7,4},{8,11},{9,10},{10,... | collective-permute-start | bytes 393224 | tf_op jit(solution)/shard_map/ppermute | solution.py:174
  44.7 9.2 %collective-permute-start.42 = (f32[4,1,4,16,128]{4,3,2,0,1:T(8,128)S(1)}, f32[4,1,4,16,128]{4,3,2,0,1:T(8,128)S(1)}, u32[]{:S(2)}, u32[]{:S(2)}) collective-permute-start(f32[4,1,4,16,128]{4,3,2,0,1:T(8,128)S(1)} %get-tuple-element.78), channel_id=1, source_target_pairs={{0,2},{1,3},{2,0},{3,1},{4,6},{5,7},{6,4},{7,5},{8,10},{9,11},{10,... | collective-permute-start | bytes 393224 | tf_op jit(solution)/shard_map/ppermute | solution.py:174
  47.6 6.3 %collective-permute-start.41 = (f32[4,1,4,16,128]{4,3,2,0,1:T(8,128)S(1)}, f32[4,1,4,16,128]{4,3,2,0,1:T(8,128)S(1)}, u32[]{:S(2)}, u32[]{:S(2)}) collective-permute-start(f32[4,1,4,16,128]{4,3,2,0,1:T(8,128)S(1)} %get-tuple-element.79), channel_id=1, source_target_pairs={{0,1},{1,0},{2,3},{3,2},{4,5},{5,4},{6,7},{7,6},{8,9},{9,8},{10,11... | collective-permute-start | bytes 393224 | tf_op jit(solution)/shard_map/ppermute | solution.py:174
  49.4 8.3 %collective-permute-start.55 = (f32[1,4,4,16,128]{4,3,2,1,0:T(8,128)S(1)}, f32[1,4,4,16,128]{4,3,2,1,0:T(8,128)S(1)}, u32[]{:S(2)}, u32[]{:S(2)}) collective-permute-start(f32[1,4,4,16,128]{4,3,2,1,0:T(8,128)S(1)} %get-tuple-element.61), channel_id=1, source_target_pairs={{0,12},{1,13},{2,14},{3,15},{4,8},{5,9},{6,10},{7,11},{8,4},{9,5},... | collective-permute-start | bytes 393224 | tf_op jit(solution)/shard_map/ppermute | solution.py:174
  50.6 12.8 %collective-permute-start.54 = (f32[1,4,4,16,128]{4,3,2,1,0:T(8,128)S(1)}, f32[1,4,4,16,128]{4,3,2,1,0:T(8,128)S(1)}, u32[]{:S(2)}, u32[]{:S(2)}) collective-permute-start(f32[1,4,4,16,128]{4,3,2,1,0:T(8,128)S(1)} %get-tuple-element.62), channel_id=1, source_target_pairs={{0,8},{1,9},{2,10},{3,11},{4,12},{5,13},{6,14},{7,15},{8,0},{9,1},... | collective-permute-start | bytes 393224 | tf_op jit(solution)/shard_map/ppermute | solution.py:174
  50.6 12.8 %collective-permute-start.53 = (f32[1,4,4,16,128]{4,3,2,1,0:T(8,128)S(1)}, f32[1,4,4,16,128]{4,3,2,1,0:T(8,128)S(1)}, u32[]{:S(2)}, u32[]{:S(2)}) collective-permute-start(f32[1,4,4,16,128]{4,3,2,1,0:T(8,128)S(1)} %get-tuple-element.63), channel_id=1, source_target_pairs={{0,4},{1,5},{2,6},{3,7},{4,0},{5,1},{6,2},{7,3},{8,12},{9,13},{10,... | collective-permute-start | bytes 393224 | tf_op jit(solution)/shard_map/ppermute | solution.py:174
  55.0 15.6 %collective-permute-start.46 = (f32[1,4,4,16,128]{4,3,2,1,0:T(8,128)S(1)}, f32[1,4,4,16,128]{4,3,2,1,0:T(8,128)S(1)}, u32[]{:S(2)}, u32[]{:S(2)}) collective-permute-start(f32[1,4,4,16,128]{4,3,2,1,0:T(8,128)S(1)} %get-tuple-element.73), channel_id=1, source_target_pairs={{0,12},{1,13},{2,14},{3,15},{4,8},{5,9},{6,10},{7,11},{8,4},{9,5},... | collective-permute-start | bytes 393224 | tf_op jit(solution)/shard_map/ppermute | solution.py:174
  56.1 17.9 %collective-permute-start.45 = (f32[1,4,4,16,128]{4,3,2,1,0:T(8,128)S(1)}, f32[1,4,4,16,128]{4,3,2,1,0:T(8,128)S(1)}, u32[]{:S(2)}, u32[]{:S(2)}) collective-permute-start(f32[1,4,4,16,128]{4,3,2,1,0:T(8,128)S(1)} %get-tuple-element.74), channel_id=1, source_target_pairs={{0,8},{1,9},{2,10},{3,11},{4,12},{5,13},{6,14},{7,15},{8,0},{9,1},... | collective-permute-start | bytes 393224 | tf_op jit(solution)/shard_map/ppermute | solution.py:174
  57.7 16.3 %collective-permute-start.44 = (f32[1,4,4,16,128]{4,3,2,1,0:T(8,128)S(1)}, f32[1,4,4,16,128]{4,3,2,1,0:T(8,128)S(1)}, u32[]{:S(2)}, u32[]{:S(2)}) collective-permute-start(f32[1,4,4,16,128]{4,3,2,1,0:T(8,128)S(1)} %get-tuple-element.75), channel_id=1, source_target_pairs={{0,4},{1,5},{2,6},{3,7},{4,0},{5,1},{6,2},{7,3},{8,12},{9,13},{10,... | collective-permute-start | bytes 393224 | tf_op jit(solution)/shard_map/ppermute | solution.py:174
  63.5 12.5 %collective-permute-start.58 = (f32[4,1,4,16,128]{4,3,2,0,1:T(8,128)S(1)}, f32[4,1,4,16,128]{4,3,2,0,1:T(8,128)S(1)}, u32[]{:S(2)}, u32[]{:S(2)}) collective-permute-start(f32[4,1,4,16,128]{4,3,2,0,1:T(8,128)S(1)} %get-tuple-element.57), channel_id=1, source_target_pairs={{0,3},{1,2},{2,1},{3,0},{4,7},{5,6},{6,5},{7,4},{8,11},{9,10},{10,... | collective-permute-start | bytes 393224 | tf_op jit(solution)/shard_map/ppermute | solution.py:174
  64.9 11.4 %collective-permute-start.57 = (f32[4,1,4,16,128]{4,3,2,0,1:T(8,128)S(1)}, f32[4,1,4,16,128]{4,3,2,0,1:T(8,128)S(1)}, u32[]{:S(2)}, u32[]{:S(2)}) collective-permute-start(f32[4,1,4,16,128]{4,3,2,0,1:T(8,128)S(1)} %get-tuple-element.58), channel_id=1, source_target_pairs={{0,2},{1,3},{2,0},{3,1},{4,6},{5,7},{6,4},{7,5},{8,10},{9,11},{10,... | collective-permute-start | bytes 393224 | tf_op jit(solution)/shard_map/ppermute | solution.py:174
  70.6 5.7 %collective-permute-start.56 = (f32[4,1,4,16,128]{4,3,2,0,1:T(8,128)S(1)}, f32[4,1,4,16,128]{4,3,2,0,1:T(8,128)S(1)}, u32[]{:S(2)}, u32[]{:S(2)}) collective-permute-start(f32[4,1,4,16,128]{4,3,2,0,1:T(8,128)S(1)} %get-tuple-element.59), channel_id=1, source_target_pairs={{0,1},{1,0},{2,3},{3,2},{4,5},{5,4},{6,7},{7,6},{8,9},{9,8},{10,11... | collective-permute-start | bytes 393224 | tf_op jit(solution)/shard_map/ppermute | solution.py:174
  74.1 5.6 %collective-permute-start.49 = (f32[4,1,4,16,128]{4,3,2,0,1:T(8,128)S(1)}, f32[4,1,4,16,128]{4,3,2,0,1:T(8,128)S(1)}, u32[]{:S(2)}, u32[]{:S(2)}) collective-permute-start(f32[4,1,4,16,128]{4,3,2,0,1:T(8,128)S(1)} %get-tuple-element.69), channel_id=1, source_target_pairs={{0,3},{1,2},{2,1},{3,0},{4,7},{5,6},{6,5},{7,4},{8,11},{9,10},{10,... | collective-permute-start | bytes 393224 | tf_op jit(solution)/shard_map/ppermute | solution.py:174
  75.2 7.6 %collective-permute-start.48 = (f32[4,1,4,16,128]{4,3,2,0,1:T(8,128)S(1)}, f32[4,1,4,16,128]{4,3,2,0,1:T(8,128)S(1)}, u32[]{:S(2)}, u32[]{:S(2)}) collective-permute-start(f32[4,1,4,16,128]{4,3,2,0,1:T(8,128)S(1)} %get-tuple-element.70), channel_id=1, source_target_pairs={{0,2},{1,3},{2,0},{3,1},{4,6},{5,7},{6,4},{7,5},{8,10},{9,11},{10,... | collective-permute-start | bytes 393224 | tf_op jit(solution)/shard_map/ppermute | solution.py:174
  76.0 6.8 %collective-permute-start.47 = (f32[4,1,4,16,128]{4,3,2,0,1:T(8,128)S(1)}, f32[4,1,4,16,128]{4,3,2,0,1:T(8,128)S(1)}, u32[]{:S(2)}, u32[]{:S(2)}) collective-permute-start(f32[4,1,4,16,128]{4,3,2,0,1:T(8,128)S(1)} %get-tuple-element.71), channel_id=1, source_target_pairs={{0,1},{1,0},{2,3},{3,2},{4,5},{5,4},{6,7},{7,6},{8,9},{9,8},{10,11... | collective-permute-start | bytes 393224 | tf_op jit(solution)/shard_map/ppermute | solution.py:174
  (3 other events, 2.2 us)

commit v9 on v8

--- a/solution.py
+++ b/solution.py
@@ -56,7 +56,7 @@
     slots, share = still.shape[0], still.shape[1]
     copies = [
         pltpu.make_async_copy(density_in, density, sems.at[0]),
-        pltpu.make_async_copy(fields_in.at[0:6], fields, sems.at[1]),
+        pltpu.make_async_copy(fields_in, fields, sems.at[1]),
     ]
     for copy in copies:
         copy.start()
@@ -110,14 +110,12 @@
             rim,
             rim,
             jax.ShapeDtypeStruct((slots, share, cells, depth), f32),
+            jax.ShapeDtypeStruct(fields.shape, f32),
+            jax.ShapeDtypeStruct(density.shape, f32),
         ),
         in_specs=[pl.BlockSpec(memory_space=pltpu.SMEM)] + [pl.BlockSpec(memory_space=pltpu.HBM)] * 2,
-        out_specs=[vmem] * 5,
-        scratch_shapes=[
-            pltpu.VMEM((6, columns, cells, depth), f32),
-            pltpu.VMEM((columns, cells, depth), f32),
-            pltpu.SemaphoreType.DMA((2,)),
-        ],
+        out_specs=[vmem] * 7,
+        scratch_shapes=[pltpu.SemaphoreType.DMA((2,))],
         compiler_params=pltpu.CompilerParams(vmem_limit_bytes=16 * 2**20),
         name="pack",
     )(rank, fields, density)
@@ -467,14 +465,14 @@
     shear_cells = boundary_shift[0]
     az = lax.axis_index("az")
     rank = az.reshape(1)
-    head, tail, low, high, still = pack(rank, fields, density)
+    head, tail, low, high, still, fields, density = pack(rank, fields, density)
     before, after = azimuthal_layers(head, tail)
     count = still.shape[0]
     radix = digit_radix(count)
     span = count // radix
     cut = still.reshape(1, radix, span, *still.shape[1:])
     nearest = send_step(cut, 1)
-    before, after, nearest, cut = lax.optimization_barrier((before, after, nearest, cut))
+    before, after, cut = lax.optimization_barrier((before, after, cut))
     parts = [cut[:, 0], nearest] + [send_step(cut, step) for step in range(2, radix)]
     layers = rims(shear_cells // cells, low, high, before, after)
     parts, layers = lax.optimization_barrier((parts, layers))
@@ -488,6 +486,7 @@
         ]
     )
     moving = updated_columns(info, fields, density, head, tail, before, after, *layers)
+    moving, still = lax.optimization_barrier((moving, still))
     moving = swap(moving)
     still = swap(move_columns(still, 4, rank, shift_int, frac_num))
     moving = swap(move_columns(moving, 4, rank, shift_int, frac_num))

time: 82.6 us -> 90.7 us (1.098)
  waiting for transfers between devices: 33 us -> 42 us
  starting transfers between devices: 39.9 us -> 38.6 us
    ppermute x1, waiting for transfers between devices: 0.01 us -> 4.54 us  [rims(): below = above = lax.ppermute(other, 'rad', [(0, 1), (1, 0)])]
    ppermute x2, starting transfers between devices: 0.11 us -> 4.04 us  [wrap(): return lax.ppermute(data, ('rad', 'az'), pairs)]
    ppermute x24, waiting for transfers between devices: 25.7 us -> 29.4 us  [send_step(): return lax.ppermute(cut[:, step], 'az', pairs)]
    ppermute x24, starting transfers between devices: 32 us -> 28.3 us  [send_step(): return lax.ppermute(cut[:, step], 'az', pairs)]
    ppermute x1, starting transfers between devices: 1.56 us -> 0.02 us  [rims(): below = above = lax.ppermute(other, 'rad', [(0, 1), (1, 0)])]
    unnamed x12 -> x8, local copies, waits for them, and re-layouts: 2.74 us -> 2.08 us
  transfers between devices with their start and end apart: 29 -> 29, of which waited for: 11 -> 13; matrix products, arithmetic and copies ran while one was open for 1% -> 1% of each run, Pallas kernels for 2% -> 4%
where the time goes in v9:
time: 90.7 us; the launch traced here: 91.1 us
  waiting for transfers between devices  42 us (46%)
  starting transfers between devices  38.6 us (43%)
  Pallas kernels  6.03 us (7%)
  local copies, waits for them, and re-layouts  2.41 us (3%)
  between operations  1.58 us (2%)
    ppermute x24, waiting for transfers between devices, send_step(): return lax.ppermute(cut[:, step], 'az', pairs)  29.4 us
    ppermute x24, starting transfers between devices, send_step(): return lax.ppermute(cut[:, step], 'az', pairs)  28.3 us
    ppermute x2, waiting for transfers between devices, wrap(): return lax.ppermute(data, ('rad', 'az'), pairs)  6.63 us
    ppermute x1, starting transfers between devices, azimuthal_layers(): far = lax.ppermute(jnp.where(even, head, tail), 'az', outer)  5.67 us
    ppermute x1, waiting for transfers between devices, rims(): below = above = lax.ppermute(other, 'rad', [(0, 1), (1, 0)])  4.54 us
    ppermute x2, starting transfers between devices, wrap(): return lax.ppermute(data, ('rad', 'az'), pairs)  4.04 us
    pallas_call x1, Pallas kernels, updated_columns(): pl.pallas_call(stress_kernel, out_shape=jax.ShapeDtypeStruct((slots, 4 *...  2.47 us
    unnamed x8, local copies, waits for them, and re-layouts  2.08 us
  transfers between devices with their start and end apart: 29, of which 13 were waited for; matrix products, arithmetic and copies ran while one was open for 1% of the time, Pallas kernels for 4%

profile of v9, /device:TPU:0, one launch (start us, length us, event | category | flops | bytes accessed | tf_op | source)
XLA Modules:
  0.0 91.1 jit_solution(16874746197749090916)
XLA Ops:
  0.7 1.2 %copy-done = f32[7,16,16,128]{3,2,1,0:T(8,128)S(1)} copy-done((f32[7,16,16,128]{3,2,1,0:T(8,128)S(1)}, f32[7,16,16,128]{3,2,1,0:T(8,128)}, u32[]{:S(2)}) %copy-start) | copy-done | bytes 917528
  1.8 0.9 copy-done.1
  3.8 5.7 %collective-permute-start.32 = (f32[10,16,128]{2,1,0:T(8,128)S(1)}, f32[10,16,128]{2,1,0:T(8,128)S(1)}, u32[]{:S(2)}, u32[]{:S(2)}) collective-permute-start(f32[10,16,128]{2,1,0:T(8,128)S(1)} %get-tuple-element.98), channel_id=1, source_target_pairs={{0,15},{1,2},{2,1},{3,4},{4,3},{5,6},{6,5},{7,8},{8,7},{9,10},{10,... | collective-permute-start | bytes 245768 | tf_op jit(solution)/shard_map/ppermute | solution.py:420
  10.3 1.4 %collective-permute-done.32 = f32[10,16,128]{2,1,0:T(8,128)S(1)} collective-permute-done((f32[10,16,128]{2,1,0:T(8,128)S(1)}, f32[10,16,128]{2,1,0:T(8,128)S(1)}, u32[]{:S(2)}, u32[]{:S(2)}) %collective-permute-start.32) | collective-permute-done | bytes 81952 | tf_op jit(solution)/shard_map/ppermute | solution.py:420
  11.8 1.7 %collective-permute-start.36 = (f32[1,4,4,16,128]{4,3,2,1,0:T(8,128)S(1)}, f32[1,4,4,16,128]{4,3,2,1,0:T(8,128)S(1)}, u32[]{:S(2)}, u32[]{:S(2)}) collective-permute-start(f32[1,4,4,16,128]{4,3,2,1,0:T(8,128)S(1)} %get-tuple-element.90), channel_id=1, source_target_pairs={{0,12},{1,13},{2,14},{3,15},{4,8},{5,9},{6,10},{7,11},{8,4},{9,5},... | collective-permute-start | bytes 393224 | tf_op jit(solution)/shard_map/ppermute | solution.py:172
  14.0 10.7 %conditional.1 = (f32[11,16,128]{2,1,0:T(8,128)}, f32[11,16,128]{2,1,0:T(8,128)}) conditional(s32[]{:T(128)} %clamp.3, f32[11,16,128]{2,1,0:T(8,128)S(1)} %get-tuple-element.93, f32[11,16,128]{2,1,0:T(8,128)S(1)} %get-tuple-element.93, f32[11,16,128]{2,1,0:T(8,128)S(1)} %get-tuple-element.93, ...), branch_computations={%region_0.1_spmd, %region_1.2_spmd, %region_2.3_spmd, %region_3.4_... | conditional | bytes 720992 | solution.py:457
  14.0 2.8 %collective-permute-start.7 = (f32[11,16,128]{2,1,0:T(8,128)S(1)}, f32[11,16,128]{2,1,0:T(8,128)}, u32[]{:S(2)}, u32[]{:S(2)}) collective-permute-start(f32[11,16,128]{2,1,0:T(8,128)S(1)} %param.3), channel_id=1, source_target_pairs={{16,4},{17,5},{18,6},{19,7},{20,8},{21,9},{22,10},{23,11},{24,12},... | collective-permute-start | bytes 270344 | tf_op jit(solution)/shard_map/cond/branch_3_fun/ppermute | solution.py:437
  16.8 1.3 %collective-permute-start.6 = (f32[11,16,128]{2,1,0:T(8,128)S(1)}, f32[11,16,128]{2,1,0:T(8,128)}, u32[]{:S(2)}, u32[]{:S(2)}) collective-permute-start(f32[11,16,128]{2,1,0:T(8,128)S(1)} %param.3), channel_id=1, source_target_pairs={{16,3},{17,4},{18,5},{19,6},{20,7},{21,8},{22,9},{23,10},{24,11},{... | collective-permute-start | bytes 270344 | tf_op jit(solution)/shard_map/cond/branch_3_fun/ppermute | solution.py:437
  18.0 6.6 %collective-permute-done.7 = f32[11,16,128]{2,1,0:T(8,128)} collective-permute-done((f32[11,16,128]{2,1,0:T(8,128)S(1)}, f32[11,16,128]{2,1,0:T(8,128)}, u32[]{:S(2)}, u32[]{:S(2)}) %collective-permute-start.7) | collective-permute-done | bytes 90144 | tf_op jit(solution)/shard_map/cond/branch_3_fun/ppermute | solution.py:437
  24.7 4.5 %collective-permute-done.37.straight_below.straight_above = f32[11,16,128]{2,1,0:T(8,128)S(1)} collective-permute-done((f32[11,16,128]{2,1,0:T(8,128)S(1)}, f32[11,16,128]{2,1,0:T(8,128)S(1)}, u32[]{:S(2)}, u32[]{:S(2)}) %collective-permute-start.37) | collective-permute-done | bytes 90144 | tf_op jit(solution)/shard_map/ppermute | solution.py:449
  29.4 2.0 %collective-permute-start.39 = (f32[4,1,4,16,128]{4,3,2,0,1:T(8,128)S(1)}, f32[4,1,4,16,128]{4,3,2,0,1:T(8,128)S(1)}, u32[]{:S(2)}, u32[]{:S(2)}) collective-permute-start(f32[4,1,4,16,128]{4,3,2,0,1:T(8,128)S(1)} %get-tuple-element.88), channel_id=1, source_target_pairs={{0,2},{1,3},{2,0},{3,1},{4,6},{5,7},{6,4},{7,5},{8,10},{9,11},{10,... | collective-permute-start | bytes 393224 | tf_op jit(solution)/shard_map/ppermute | solution.py:172
  31.6 2.5 %stress_update.1 = f32[16,4,16,128]{3,2,1,0:T(8,128)S(1)} custom-call(s32[4]{0:T(128)S(1)} %pad_add_fusion.info, f32[7,16,16,128]{3,2,1,0:T(8,128)S(1)} %get-tuple-element.40.fields, f32[16,16,128]{2,1,0:T(8,128)S(1)} %get-tuple-element.41.density, f32[10,16,128]{2,1,0:T(8,128)S(1)} %get-tuple-element.42.head, f32[10,16,128]{2,1,0:T(8,128)S(1)} %get-tuple-element.43.tail, ...), custom_call_target="tpu_custom_call" | custom-call | tf_op jit(solution)/shard_map/stress_update/pallas_call | solution.py:345
  34.7 3.3 %collective-permute-done.39 = f32[4,1,4,16,128]{4,3,2,0,1:T(8,128)S(1)} collective-permute-done((f32[4,1,4,16,128]{4,3,2,0,1:T(8,128)S(1)}, f32[4,1,4,16,128]{4,3,2,0,1:T(8,128)S(1)}, u32[]{:S(2)}, u32[]{:S(2)}) %collective-permute-start.39) | collective-permute-done | bytes 131104 | tf_op jit(solution)/shard_map/ppermute | solution.py:172
  38.1 2.3 %collective-permute-start.43 = (f32[1,4,4,16,128]{4,3,2,1,0:T(8,128)S(1)}, f32[1,4,4,16,128]{4,3,2,1,0:T(8,128)S(1)}, u32[]{:S(2)}, u32[]{:S(2)}) collective-permute-start(f32[1,4,4,16,128]{4,3,2,1,0:T(8,128)S(1)} %get-tuple-element.83), channel_id=1, source_target_pairs={{0,12},{1,13},{2,14},{3,15},{4,8},{5,9},{6,10},{7,11},{8,4},{9,5},... | collective-permute-start | bytes 393224 | tf_op jit(solution)/shard_map/ppermute | solution.py:172
  40.3 3.9 %collective-permute-start.42 = (f32[1,4,4,16,128]{4,3,2,1,0:T(8,128)S(1)}, f32[1,4,4,16,128]{4,3,2,1,0:T(8,128)S(1)}, u32[]{:S(2)}, u32[]{:S(2)}) collective-permute-start(f32[1,4,4,16,128]{4,3,2,1,0:T(8,128)S(1)} %get-tuple-element.84), channel_id=1, source_target_pairs={{0,8},{1,9},{2,10},{3,11},{4,12},{5,13},{6,14},{7,15},{8,0},{9,1},... | collective-permute-start | bytes 393224 | tf_op jit(solution)/shard_map/ppermute | solution.py:172
  44.8 1.0 %move.3 = f32[16,4,16,128]{3,2,1,0:T(8,128)S(1)} custom-call(s32[1]{0:T(128)} %bitcast.rank, s32[16]{0:T(128)S(1)} %copy-done.2, s32[16]{0:T(128)S(1)} %copy-done.3, f32[16,4,16,128]{3,2,1,0:T(8,128)S(1)} %bitcast.150), custom_call_target="tpu_custom_call" | custom-call | tf_op jit(solution)/shard_map/move/pallas_call | solution.py:404
  45.8 2.4 %collective-permute-start.55 = (f32[1,4,4,16,128]{4,3,2,1,0:T(8,128)S(1)}, f32[1,4,4,16,128]{4,3,2,1,0:T(8,128)S(1)}, u32[]{:S(2)}, u32[]{:S(2)}) collective-permute-start(f32[1,4,4,16,128]{4,3,2,1,0:T(8,128)S(1)} %get-tuple-element.67), channel_id=1, source_target_pairs={{0,12},{1,13},{2,14},{3,15},{4,8},{5,9},{6,10},{7,11},{8,4},{9,5},... | collective-permute-start | bytes 393224 | tf_op jit(solution)/shard_map/ppermute | solution.py:172
  48.9 3.4 %collective-permute-start.53 = (f32[1,4,4,16,128]{4,3,2,1,0:T(8,128)S(1)}, f32[1,4,4,16,128]{4,3,2,1,0:T(8,128)S(1)}, u32[]{:S(2)}, u32[]{:S(2)}) collective-permute-start(f32[1,4,4,16,128]{4,3,2,1,0:T(8,128)S(1)} %get-tuple-element.69), channel_id=1, source_target_pairs={{0,4},{1,5},{2,6},{3,7},{4,0},{5,1},{6,2},{7,3},{8,12},{9,13},{10,... | collective-permute-start | bytes 393224 | tf_op jit(solution)/shard_map/ppermute | solution.py:172
  52.3 7.5 %collective-permute-done.42 = f32[1,4,4,16,128]{4,3,2,1,0:T(8,128)S(1)} collective-permute-done((f32[1,4,4,16,128]{4,3,2,1,0:T(8,128)S(1)}, f32[1,4,4,16,128]{4,3,2,1,0:T(8,128)S(1)}, u32[]{:S(2)}, u32[]{:S(2)}) %collective-permute-start.42) | collective-permute-done | bytes 131104 | tf_op jit(solution)/shard_map/ppermute | solution.py:172
  60.2 1.6 %collective-permute-start.44 = (f32[4,1,4,16,128]{4,3,2,0,1:T(8,128)S(1)}, f32[4,1,4,16,128]{4,3,2,0,1:T(8,128)S(1)}, u32[]{:S(2)}, u32[]{:S(2)}) collective-permute-start(f32[4,1,4,16,128]{4,3,2,0,1:T(8,128)S(1)} %get-tuple-element.81), channel_id=1, source_target_pairs={{0,1},{1,0},{2,3},{3,2},{4,5},{5,4},{6,7},{7,6},{8,9},{9,8},{10,11... | collective-permute-start | bytes 393224 | tf_op jit(solution)/shard_map/ppermute | solution.py:172
  61.8 2.9 %collective-permute-done.54 = f32[1,4,4,16,128]{4,3,2,1,0:T(8,128)S(1)} collective-permute-done((f32[1,4,4,16,128]{4,3,2,1,0:T(8,128)S(1)}, f32[1,4,4,16,128]{4,3,2,1,0:T(8,128)S(1)}, u32[]{:S(2)}, u32[]{:S(2)}) %collective-permute-start.54) | collective-permute-done | bytes 131104 | tf_op jit(solution)/shard_map/ppermute | solution.py:172
  66.4 1.0 %move.2 = f32[16,4,16,128]{3,2,1,0:T(8,128)S(1)} custom-call(s32[1]{0:T(128)} %bitcast.rank, s32[16]{0:T(128)S(1)} %copy-done.2, s32[16]{0:T(128)S(1)} %copy-done.3, f32[16,4,16,128]{3,2,1,0:T(8,128)S(1)} %bitcast.154), custom_call_target="tpu_custom_call" | custom-call | tf_op jit(solution)/shard_map/move/pallas_call | solution.py:404
  67.4 2.7 %collective-permute-start.49 = (f32[1,4,4,16,128]{4,3,2,1,0:T(8,128)S(1)}, f32[1,4,4,16,128]{4,3,2,1,0:T(8,128)S(1)}, u32[]{:S(2)}, u32[]{:S(2)}) collective-permute-start(f32[1,4,4,16,128]{4,3,2,1,0:T(8,128)S(1)} %get-tuple-element.75), channel_id=1, source_target_pairs={{0,12},{1,13},{2,14},{3,15},{4,8},{5,9},{6,10},{7,11},{8,4},{9,5},... | collective-permute-start | bytes 393224 | tf_op jit(solution)/shard_map/ppermute | solution.py:172
  70.2 1.7 %collective-permute-start.47 = (f32[1,4,4,16,128]{4,3,2,1,0:T(8,128)S(1)}, f32[1,4,4,16,128]{4,3,2,1,0:T(8,128)S(1)}, u32[]{:S(2)}, u32[]{:S(2)}) collective-permute-start(f32[1,4,4,16,128]{4,3,2,1,0:T(8,128)S(1)} %get-tuple-element.77), channel_id=1, source_target_pairs={{0,4},{1,5},{2,6},{3,7},{4,0},{5,1},{6,2},{7,3},{8,12},{9,13},{10,... | collective-permute-start | bytes 393224 | tf_op jit(solution)/shard_map/ppermute | solution.py:172
  71.9 1.1 %collective-permute-start.58 = (f32[4,1,4,16,128]{4,3,2,0,1:T(8,128)S(1)}, f32[4,1,4,16,128]{4,3,2,0,1:T(8,128)S(1)}, u32[]{:S(2)}, u32[]{:S(2)}) collective-permute-start(f32[4,1,4,16,128]{4,3,2,0,1:T(8,128)S(1)} %get-tuple-element.63), channel_id=1, source_target_pairs={{0,3},{1,2},{2,1},{3,0},{4,7},{5,6},{6,5},{7,4},{8,11},{9,10},{10,... | collective-permute-start | bytes 393224 | tf_op jit(solution)/shard_map/ppermute | solution.py:172
  73.0 1.5 %collective-permute-start.57 = (f32[4,1,4,16,128]{4,3,2,0,1:T(8,128)S(1)}, f32[4,1,4,16,128]{4,3,2,0,1:T(8,128)S(1)}, u32[]{:S(2)}, u32[]{:S(2)}) collective-permute-start(f32[4,1,4,16,128]{4,3,2,0,1:T(8,128)S(1)} %get-tuple-element.64), channel_id=1, source_target_pairs={{0,2},{1,3},{2,0},{3,1},{4,6},{5,7},{6,4},{7,5},{8,10},{9,11},{10,... | collective-permute-start | bytes 393224 | tf_op jit(solution)/shard_map/ppermute | solution.py:172
  74.5 1.3 %collective-permute-done.49 = f32[1,4,4,16,128]{4,3,2,1,0:T(8,128)S(1)} collective-permute-done((f32[1,4,4,16,128]{4,3,2,1,0:T(8,128)S(1)}, f32[1,4,4,16,128]{4,3,2,1,0:T(8,128)S(1)}, u32[]{:S(2)}, u32[]{:S(2)}) %collective-permute-start.49) | collective-permute-done | bytes 131104 | tf_op jit(solution)/shard_map/ppermute | solution.py:172
  75.8 5.4 %collective-permute-done.48 = f32[1,4,4,16,128]{4,3,2,1,0:T(8,128)S(1)} collective-permute-done((f32[1,4,4,16,128]{4,3,2,1,0:T(8,128)S(1)}, f32[1,4,4,16,128]{4,3,2,1,0:T(8,128)S(1)}, u32[]{:S(2)}, u32[]{:S(2)}) %collective-permute-start.48) | collective-permute-done | bytes 131104 | tf_op jit(solution)/shard_map/ppermute | solution.py:172
  81.3 1.0 %collective-permute-start.52 = (f32[4,1,4,16,128]{4,3,2,0,1:T(8,128)S(1)}, f32[4,1,4,16,128]{4,3,2,0,1:T(8,128)S(1)}, u32[]{:S(2)}, u32[]{:S(2)}) collective-permute-start(f32[4,1,4,16,128]{4,3,2,0,1:T(8,128)S(1)} %get-tuple-element.71), channel_id=1, source_target_pairs={{0,3},{1,2},{2,1},{3,0},{4,7},{5,6},{6,5},{7,4},{8,11},{9,10},{10,... | collective-permute-start | bytes 393224 | tf_op jit(solution)/shard_map/ppermute | solution.py:172
  83.3 3.6 %collective-permute-done.52 = f32[4,1,4,16,128]{4,3,2,0,1:T(8,128)S(1)} collective-permute-done((f32[4,1,4,16,128]{4,3,2,0,1:T(8,128)S(1)}, f32[4,1,4,16,128]{4,3,2,0,1:T(8,128)S(1)}, u32[]{:S(2)}, u32[]{:S(2)}) %collective-permute-start.52) | collective-permute-done | bytes 131104 | tf_op jit(solution)/shard_map/ppermute | solution.py:172
  86.9 3.1 %collective-permute-done.51 = f32[4,1,4,16,128]{4,3,2,0,1:T(8,128)S(1)} collective-permute-done((f32[4,1,4,16,128]{4,3,2,0,1:T(8,128)S(1)}, f32[4,1,4,16,128]{4,3,2,0,1:T(8,128)S(1)}, u32[]{:S(2)}, u32[]{:S(2)}) %collective-permute-start.51) | collective-permute-done | bytes 131104 | tf_op jit(solution)/shard_map/ppermute | solution.py:172
  90.0 1.0 %join.1 = (f32[7,16,16,128]{3,2,1,0:T(8,128)}, f32[16,16,128]{2,1,0:T(8,128)}) custom-call(s32[1]{0:T(128)} %bitcast.rank, f32[16,4,16,128]{3,2,1,0:T(8,128)S(1)} %bitcast.151, f32[16,4,16,128]{3,2,1,0:T(8,128)S(1)} %bitcast.149), custom_call_target="tpu_custom_call" | custom-call | tf_op jit(solution)/shard_map/join/pallas_call | solution.py:151
  (66 shorter events, 7.2 us)
Async XLA Ops:
  0.6 1.2 %copy-start = (f32[7,16,16,128]{3,2,1,0:T(8,128)S(1)}, f32[7,16,16,128]{3,2,1,0:T(8,128)}, u32[]{:S(2)}) copy-start(f32[7,16,16,128]{3,2,1,0:T(8,128)} %fields_in.1) | copy-start | bytes 2752516
  3.3 7.0 %collective-permute-start.33 = (f32[10,16,128]{2,1,0:T(8,128)S(1)}, f32[10,16,128]{2,1,0:T(8,128)S(1)}, u32[]{:S(2)}, u32[]{:S(2)}) collective-permute-start(f32[10,16,128]{2,1,0:T(8,128)S(1)} %get-tuple-element.97), channel_id=1, source_target_pairs={{0,1},{1,0},{2,3},{3,2},{4,5},{5,4},{6,7},{7,6},{8,9},{9,8},{10,11... | collective-permute-start | bytes 245768 | tf_op jit(solution)/shard_map/ppermute | solution.py:421
  3.8 7.9 %collective-permute-start.32 = (f32[10,16,128]{2,1,0:T(8,128)S(1)}, f32[10,16,128]{2,1,0:T(8,128)S(1)}, u32[]{:S(2)}, u32[]{:S(2)}) collective-permute-start(f32[10,16,128]{2,1,0:T(8,128)S(1)} %get-tuple-element.98), channel_id=1, source_target_pairs={{0,15},{1,2},{2,1},{3,4},{4,3},{5,6},{6,5},{7,8},{8,7},{9,10},{10,... | collective-permute-start | bytes 245768 | tf_op jit(solution)/shard_map/ppermute | solution.py:420
  9.5 15.2 %collective-permute-start.34 = (f32[1,4,4,16,128]{4,3,2,1,0:T(8,128)S(1)}, f32[1,4,4,16,128]{4,3,2,1,0:T(8,128)S(1)}, u32[]{:S(2)}, u32[]{:S(2)}) collective-permute-start(f32[1,4,4,16,128]{4,3,2,1,0:T(8,128)S(1)} %slice_bitcast_fusion.28), channel_id=1, source_target_pairs={{0,4},{1,5},{2,6},{3,7},{4,0},{5,1},{6,2},{7,3},{8,12},{9,13},{10,... | collective-permute-start | bytes 393224 | tf_op jit(solution)/shard_map/ppermute | solution.py:172
  11.8 17.4 %collective-permute-start.36 = (f32[1,4,4,16,128]{4,3,2,1,0:T(8,128)S(1)}, f32[1,4,4,16,128]{4,3,2,1,0:T(8,128)S(1)}, u32[]{:S(2)}, u32[]{:S(2)}) collective-permute-start(f32[1,4,4,16,128]{4,3,2,1,0:T(8,128)S(1)} %get-tuple-element.90), channel_id=1, source_target_pairs={{0,12},{1,13},{2,14},{3,15},{4,8},{5,9},{6,10},{7,11},{8,4},{9,5},... | collective-permute-start | bytes 393224 | tf_op jit(solution)/shard_map/ppermute | solution.py:172
  13.5 15.7 %collective-permute-start.35 = (f32[1,4,4,16,128]{4,3,2,1,0:T(8,128)S(1)}, f32[1,4,4,16,128]{4,3,2,1,0:T(8,128)S(1)}, u32[]{:S(2)}, u32[]{:S(2)}) collective-permute-start(f32[1,4,4,16,128]{4,3,2,1,0:T(8,128)S(1)} %get-tuple-element.91), channel_id=1, source_target_pairs={{0,8},{1,9},{2,10},{3,11},{4,12},{5,13},{6,14},{7,15},{8,0},{9,1},... | collective-permute-start | bytes 393224 | tf_op jit(solution)/shard_map/ppermute | solution.py:172
  14.0 10.7 %collective-permute-start.7 = (f32[11,16,128]{2,1,0:T(8,128)S(1)}, f32[11,16,128]{2,1,0:T(8,128)}, u32[]{:S(2)}, u32[]{:S(2)}) collective-permute-start(f32[11,16,128]{2,1,0:T(8,128)S(1)} %param.3), channel_id=1, source_target_pairs={{16,4},{17,5},{18,6},{19,7},{20,8},{21,9},{22,10},{23,11},{24,12},... | collective-permute-start | bytes 270344 | tf_op jit(solution)/shard_map/cond/branch_3_fun/ppermute | solution.py:437
  16.8 7.9 %collective-permute-start.6 = (f32[11,16,128]{2,1,0:T(8,128)S(1)}, f32[11,16,128]{2,1,0:T(8,128)}, u32[]{:S(2)}, u32[]{:S(2)}) collective-permute-start(f32[11,16,128]{2,1,0:T(8,128)S(1)} %param.3), channel_id=1, source_target_pairs={{16,3},{17,4},{18,5},{19,6},{20,7},{21,8},{22,9},{23,10},{24,11},{... | collective-permute-start | bytes 270344 | tf_op jit(solution)/shard_map/cond/branch_3_fun/ppermute | solution.py:437
  24.7 4.6 %collective-permute-start.37 = (f32[11,16,128]{2,1,0:T(8,128)S(1)}, f32[11,16,128]{2,1,0:T(8,128)S(1)}, u32[]{:S(2)}, u32[]{:S(2)}) collective-permute-start(f32[11,16,128]{2,1,0:T(8,128)S(1)} %get-tuple-element.94), channel_id=1, source_target_pairs={{0,16},{16,0},{1,17},{17,1},{2,18},{18,2},{3,19},{19,3},{4,20},{20... | collective-permute-start | bytes 270344 | tf_op jit(solution)/shard_map/ppermute | solution.py:449
  29.3 5.4 %collective-permute-start.40 = (f32[4,1,4,16,128]{4,3,2,0,1:T(8,128)S(1)}, f32[4,1,4,16,128]{4,3,2,0,1:T(8,128)S(1)}, u32[]{:S(2)}, u32[]{:S(2)}) collective-permute-start(f32[4,1,4,16,128]{4,3,2,0,1:T(8,128)S(1)} %get-tuple-element.87), channel_id=1, source_target_pairs={{0,3},{1,2},{2,1},{3,0},{4,7},{5,6},{6,5},{7,4},{8,11},{9,10},{10,... | collective-permute-start | bytes 393224 | tf_op jit(solution)/shard_map/ppermute | solution.py:172
  29.4 8.6 %collective-permute-start.39 = (f32[4,1,4,16,128]{4,3,2,0,1:T(8,128)S(1)}, f32[4,1,4,16,128]{4,3,2,0,1:T(8,128)S(1)}, u32[]{:S(2)}, u32[]{:S(2)}) collective-permute-start(f32[4,1,4,16,128]{4,3,2,0,1:T(8,128)S(1)} %get-tuple-element.88), channel_id=1, source_target_pairs={{0,2},{1,3},{2,0},{3,1},{4,6},{5,7},{6,4},{7,5},{8,10},{9,11},{10,... | collective-permute-start | bytes 393224 | tf_op jit(solution)/shard_map/ppermute | solution.py:172
  31.4 6.5 %collective-permute-start.38 = (f32[4,1,4,16,128]{4,3,2,0,1:T(8,128)S(1)}, f32[4,1,4,16,128]{4,3,2,0,1:T(8,128)S(1)}, u32[]{:S(2)}, u32[]{:S(2)}) collective-permute-start(f32[4,1,4,16,128]{4,3,2,0,1:T(8,128)S(1)} %get-tuple-element.89), channel_id=1, source_target_pairs={{0,1},{1,0},{2,3},{3,2},{4,5},{5,4},{6,7},{7,6},{8,9},{9,8},{10,11... | collective-permute-start | bytes 393224 | tf_op jit(solution)/shard_map/ppermute | solution.py:172
  38.1 10.8 %collective-permute-start.43 = (f32[1,4,4,16,128]{4,3,2,1,0:T(8,128)S(1)}, f32[1,4,4,16,128]{4,3,2,1,0:T(8,128)S(1)}, u32[]{:S(2)}, u32[]{:S(2)}) collective-permute-start(f32[1,4,4,16,128]{4,3,2,1,0:T(8,128)S(1)} %get-tuple-element.83), channel_id=1, source_target_pairs={{0,12},{1,13},{2,14},{3,15},{4,8},{5,9},{6,10},{7,11},{8,4},{9,5},... | collective-permute-start | bytes 393224 | tf_op jit(solution)/shard_map/ppermute | solution.py:172
  40.3 4.4 %copy-start.2 = (s32[16]{0:T(128)S(1)}, s32[16]{0:T(128)}, u32[]{:S(2)}) copy-start(s32[16]{0:T(128)} %shift.3) | copy-start | bytes 196
  40.3 4.4 %copy-start.3 = (s32[16]{0:T(128)S(1)}, s32[16]{0:T(128)}, u32[]{:S(2)}) copy-start(s32[16]{0:T(128)} %frac.3) | copy-start | bytes 196
  40.3 19.4 %collective-permute-start.42 = (f32[1,4,4,16,128]{4,3,2,1,0:T(8,128)S(1)}, f32[1,4,4,16,128]{4,3,2,1,0:T(8,128)S(1)}, u32[]{:S(2)}, u32[]{:S(2)}) collective-permute-start(f32[1,4,4,16,128]{4,3,2,1,0:T(8,128)S(1)} %get-tuple-element.84), channel_id=1, source_target_pairs={{0,8},{1,9},{2,10},{3,11},{4,12},{5,13},{6,14},{7,15},{8,0},{9,1},... | collective-permute-start | bytes 393224 | tf_op jit(solution)/shard_map/ppermute | solution.py:172
  44.3 15.5 %collective-permute-start.41 = (f32[1,4,4,16,128]{4,3,2,1,0:T(8,128)S(1)}, f32[1,4,4,16,128]{4,3,2,1,0:T(8,128)S(1)}, u32[]{:S(2)}, u32[]{:S(2)}) collective-permute-start(f32[1,4,4,16,128]{4,3,2,1,0:T(8,128)S(1)} %get-tuple-element.85), channel_id=1, source_target_pairs={{0,4},{1,5},{2,6},{3,7},{4,0},{5,1},{6,2},{7,3},{8,12},{9,13},{10,... | collective-permute-start | bytes 393224 | tf_op jit(solution)/shard_map/ppermute | solution.py:172
  45.8 14.4 %collective-permute-start.55 = (f32[1,4,4,16,128]{4,3,2,1,0:T(8,128)S(1)}, f32[1,4,4,16,128]{4,3,2,1,0:T(8,128)S(1)}, u32[]{:S(2)}, u32[]{:S(2)}) collective-permute-start(f32[1,4,4,16,128]{4,3,2,1,0:T(8,128)S(1)} %get-tuple-element.67), channel_id=1, source_target_pairs={{0,12},{1,13},{2,14},{3,15},{4,8},{5,9},{6,10},{7,11},{8,4},{9,5},... | collective-permute-start | bytes 393224 | tf_op jit(solution)/shard_map/ppermute | solution.py:172
  48.2 16.4 %collective-permute-start.54 = (f32[1,4,4,16,128]{4,3,2,1,0:T(8,128)S(1)}, f32[1,4,4,16,128]{4,3,2,1,0:T(8,128)S(1)}, u32[]{:S(2)}, u32[]{:S(2)}) collective-permute-start(f32[1,4,4,16,128]{4,3,2,1,0:T(8,128)S(1)} %get-tuple-element.68), channel_id=1, source_target_pairs={{0,8},{1,9},{2,10},{3,11},{4,12},{5,13},{6,14},{7,15},{8,0},{9,1},... | collective-permute-start | bytes 393224 | tf_op jit(solution)/shard_map/ppermute | solution.py:172
  48.9 15.8 %collective-permute-start.53 = (f32[1,4,4,16,128]{4,3,2,1,0:T(8,128)S(1)}, f32[1,4,4,16,128]{4,3,2,1,0:T(8,128)S(1)}, u32[]{:S(2)}, u32[]{:S(2)}) collective-permute-start(f32[1,4,4,16,128]{4,3,2,1,0:T(8,128)S(1)} %get-tuple-element.69), channel_id=1, source_target_pairs={{0,4},{1,5},{2,6},{3,7},{4,0},{5,1},{6,2},{7,3},{8,12},{9,13},{10,... | collective-permute-start | bytes 393224 | tf_op jit(solution)/shard_map/ppermute | solution.py:172
  59.9 5.6 %collective-permute-start.46 = (f32[4,1,4,16,128]{4,3,2,0,1:T(8,128)S(1)}, f32[4,1,4,16,128]{4,3,2,0,1:T(8,128)S(1)}, u32[]{:S(2)}, u32[]{:S(2)}) collective-permute-start(f32[4,1,4,16,128]{4,3,2,0,1:T(8,128)S(1)} %get-tuple-element.79), channel_id=1, source_target_pairs={{0,3},{1,2},{2,1},{3,0},{4,7},{5,6},{6,5},{7,4},{8,11},{9,10},{10,... | collective-permute-start | bytes 393224 | tf_op jit(solution)/shard_map/ppermute | solution.py:172
  59.9 6.4 %collective-permute-start.45 = (f32[4,1,4,16,128]{4,3,2,0,1:T(8,128)S(1)}, f32[4,1,4,16,128]{4,3,2,0,1:T(8,128)S(1)}, u32[]{:S(2)}, u32[]{:S(2)}) collective-permute-start(f32[4,1,4,16,128]{4,3,2,0,1:T(8,128)S(1)} %get-tuple-element.80), channel_id=1, source_target_pairs={{0,2},{1,3},{2,0},{3,1},{4,6},{5,7},{6,4},{7,5},{8,10},{9,11},{10,... | collective-permute-start | bytes 393224 | tf_op jit(solution)/shard_map/ppermute | solution.py:172
  60.2 6.1 %collective-permute-start.44 = (f32[4,1,4,16,128]{4,3,2,0,1:T(8,128)S(1)}, f32[4,1,4,16,128]{4,3,2,0,1:T(8,128)S(1)}, u32[]{:S(2)}, u32[]{:S(2)}) collective-permute-start(f32[4,1,4,16,128]{4,3,2,0,1:T(8,128)S(1)} %get-tuple-element.81), channel_id=1, source_target_pairs={{0,1},{1,0},{2,3},{3,2},{4,5},{5,4},{6,7},{7,6},{8,9},{9,8},{10,11... | collective-permute-start | bytes 393224 | tf_op jit(solution)/shard_map/ppermute | solution.py:172
  67.4 8.4 %collective-permute-start.49 = (f32[1,4,4,16,128]{4,3,2,1,0:T(8,128)S(1)}, f32[1,4,4,16,128]{4,3,2,1,0:T(8,128)S(1)}, u32[]{:S(2)}, u32[]{:S(2)}) collective-permute-start(f32[1,4,4,16,128]{4,3,2,1,0:T(8,128)S(1)} %get-tuple-element.75), channel_id=1, source_target_pairs={{0,12},{1,13},{2,14},{3,15},{4,8},{5,9},{6,10},{7,11},{8,4},{9,5},... | collective-permute-start | bytes 393224 | tf_op jit(solution)/shard_map/ppermute | solution.py:172
  70.2 11.0 %collective-permute-start.48 = (f32[1,4,4,16,128]{4,3,2,1,0:T(8,128)S(1)}, f32[1,4,4,16,128]{4,3,2,1,0:T(8,128)S(1)}, u32[]{:S(2)}, u32[]{:S(2)}) collective-permute-start(f32[1,4,4,16,128]{4,3,2,1,0:T(8,128)S(1)} %get-tuple-element.76), channel_id=1, source_target_pairs={{0,8},{1,9},{2,10},{3,11},{4,12},{5,13},{6,14},{7,15},{8,0},{9,1},... | collective-permute-start | bytes 393224 | tf_op jit(solution)/shard_map/ppermute | solution.py:172
  70.2 11.0 %collective-permute-start.47 = (f32[1,4,4,16,128]{4,3,2,1,0:T(8,128)S(1)}, f32[1,4,4,16,128]{4,3,2,1,0:T(8,128)S(1)}, u32[]{:S(2)}, u32[]{:S(2)}) collective-permute-start(f32[1,4,4,16,128]{4,3,2,1,0:T(8,128)S(1)} %get-tuple-element.77), channel_id=1, source_target_pairs={{0,4},{1,5},{2,6},{3,7},{4,0},{5,1},{6,2},{7,3},{8,12},{9,13},{10,... | collective-permute-start | bytes 393224 | tf_op jit(solution)/shard_map/ppermute | solution.py:172
  71.9 11.2 %collective-permute-start.58 = (f32[4,1,4,16,128]{4,3,2,0,1:T(8,128)S(1)}, f32[4,1,4,16,128]{4,3,2,0,1:T(8,128)S(1)}, u32[]{:S(2)}, u32[]{:S(2)}) collective-permute-start(f32[4,1,4,16,128]{4,3,2,0,1:T(8,128)S(1)} %get-tuple-element.63), channel_id=1, source_target_pairs={{0,3},{1,2},{2,1},{3,0},{4,7},{5,6},{6,5},{7,4},{8,11},{9,10},{10,... | collective-permute-start | bytes 393224 | tf_op jit(solution)/shard_map/ppermute | solution.py:172
  73.0 10.3 %collective-permute-start.57 = (f32[4,1,4,16,128]{4,3,2,0,1:T(8,128)S(1)}, f32[4,1,4,16,128]{4,3,2,0,1:T(8,128)S(1)}, u32[]{:S(2)}, u32[]{:S(2)}) collective-permute-start(f32[4,1,4,16,128]{4,3,2,0,1:T(8,128)S(1)} %get-tuple-element.64), channel_id=1, source_target_pairs={{0,2},{1,3},{2,0},{3,1},{4,6},{5,7},{6,4},{7,5},{8,10},{9,11},{10,... | collective-permute-start | bytes 393224 | tf_op jit(solution)/shard_map/ppermute | solution.py:172
  75.8 7.5 %collective-permute-start.56 = (f32[4,1,4,16,128]{4,3,2,0,1:T(8,128)S(1)}, f32[4,1,4,16,128]{4,3,2,0,1:T(8,128)S(1)}, u32[]{:S(2)}, u32[]{:S(2)}) collective-permute-start(f32[4,1,4,16,128]{4,3,2,0,1:T(8,128)S(1)} %get-tuple-element.65), channel_id=1, source_target_pairs={{0,1},{1,0},{2,3},{3,2},{4,5},{5,4},{6,7},{7,6},{8,9},{9,8},{10,11... | collective-permute-start | bytes 393224 | tf_op jit(solution)/shard_map/ppermute | solution.py:172
  81.3 5.6 %collective-permute-start.52 = (f32[4,1,4,16,128]{4,3,2,0,1:T(8,128)S(1)}, f32[4,1,4,16,128]{4,3,2,0,1:T(8,128)S(1)}, u32[]{:S(2)}, u32[]{:S(2)}) collective-permute-start(f32[4,1,4,16,128]{4,3,2,0,1:T(8,128)S(1)} %get-tuple-element.71), channel_id=1, source_target_pairs={{0,3},{1,2},{2,1},{3,0},{4,7},{5,6},{6,5},{7,4},{8,11},{9,10},{10,... | collective-permute-start | bytes 393224 | tf_op jit(solution)/shard_map/ppermute | solution.py:172
  82.4 7.7 %collective-permute-start.51 = (f32[4,1,4,16,128]{4,3,2,0,1:T(8,128)S(1)}, f32[4,1,4,16,128]{4,3,2,0,1:T(8,128)S(1)}, u32[]{:S(2)}, u32[]{:S(2)}) collective-permute-start(f32[4,1,4,16,128]{4,3,2,0,1:T(8,128)S(1)} %get-tuple-element.72), channel_id=1, source_target_pairs={{0,2},{1,3},{2,0},{3,1},{4,6},{5,7},{6,4},{7,5},{8,10},{9,11},{10,... | collective-permute-start | bytes 393224 | tf_op jit(solution)/shard_map/ppermute | solution.py:172
  83.1 6.9 %collective-permute-start.50 = (f32[4,1,4,16,128]{4,3,2,0,1:T(8,128)S(1)}, f32[4,1,4,16,128]{4,3,2,0,1:T(8,128)S(1)}, u32[]{:S(2)}, u32[]{:S(2)}) collective-permute-start(f32[4,1,4,16,128]{4,3,2,0,1:T(8,128)S(1)} %get-tuple-element.73), channel_id=1, source_target_pairs={{0,1},{1,0},{2,3},{3,2},{4,5},{5,4},{6,7},{7,6},{8,9},{9,8},{10,11... | collective-permute-start | bytes 393224 | tf_op jit(solution)/shard_map/ppermute | solution.py:172
  (1 other events, 0.9 us)

commit v10 on v8

--- a/solution.py
+++ b/solution.py
@@ -123,31 +123,20 @@
     )(rank, fields, density)
 
 
-def join_kernel(quantities, rank, moving, still, new_fields, new_density):
-    slots, share = still.shape[0], still.shape[1]
+def join_kernel(quantities, returned, new_fields, new_density):
+    slots, share = returned.shape[0], returned.shape[1] // 2
     for slot in range(slots):
         for item in range(share):
-            column, row = pair_of(lax.bitwise_xor(rank[0], slot), item, share, quantities)
-            if isinstance(row, int):
-                new_fields[6 if row == 3 else row, column] = moving[slot, item]
-                if row == 0:
-                    new_density[column] = still[slot, item]
-                else:
-                    new_fields[2 + row, column] = still[slot, item]
+            column, row = pair_of(slot, item, share, quantities)
+            new_fields[6 if row == 3 else row, column] = returned[slot, item]
+            if row == 0:
+                new_density[column] = returned[slot, share + item]
             else:
-                new_fields[jnp.where(row == 3, 6, row), column] = moving[slot, item]
-
-                @pl.when(row == 0)
-                def _():
-                    new_density[column] = still[slot, item]
-
-                @pl.when(row > 0)
-                def _():
-                    new_fields[2 + row, column] = still[slot, item]
-
-
-def join(rank, moving, still, columns):
-    _, _, cells, depth = still.shape
+                new_fields[2 + row, column] = returned[slot, share + item]
+
+
+def join(returned, columns):
+    _, _, cells, depth = returned.shape
     f32 = jnp.float32
     vmem = pl.BlockSpec(memory_space=pltpu.VMEM)
     return pl.pallas_call(
@@ -156,11 +145,11 @@
             jax.ShapeDtypeStruct((7, columns, cells, depth), f32),
             jax.ShapeDtypeStruct((columns, cells, depth), f32),
         ),
-        in_specs=[pl.BlockSpec(memory_space=pltpu.SMEM), vmem, vmem],
+        in_specs=[vmem],
         out_specs=[vmem] * 2,
         compiler_params=pltpu.CompilerParams(vmem_limit_bytes=16 * 2**20),
         name="join",
-    )(rank, moving, still)
+    )(returned)
 
 
 def digit_radix(span):
@@ -326,7 +315,7 @@
         vertical = (px[2, ghost], py[2, ghost, TOP:end], pzz[ghost])
         for axis in range(4):
             flat = column * 4 + axis
-            slot = lax.bitwise_xor(info[3], flat // share)
+            slot = flat // share
             if axis < 3:
                 force = slope(axis) + vertical_slope(vertical[axis])
                 out[slot, flat % share] = fields[axis, column] + force * inverse
@@ -363,7 +352,7 @@
     )(info, fields, density, *layers)
 
 
-def move_kernel(quantities, rank, shift, frac, gathered, out, twice):
+def move_kernel(quantities, mixed, rank, shift, frac, gathered, out, twice):
     slots, share, cells, depth = gathered.shape
     total = slots * cells
     me = rank[0]
@@ -375,7 +364,8 @@
 
         def lay(slot, carry):
             rows = gathered[slot, item]
-            spot = pl.multiple_of(TOP + lax.bitwise_xor(me, slot) * cells, TOP)
+            block = lax.bitwise_xor(me, slot) if mixed else slot
+            spot = pl.multiple_of(TOP + block * cells, TOP)
             twice[item, pl.ds(spot, cells)] = rows
             twice[item, pl.ds(pl.multiple_of(spot + total, TOP), cells)] = rows
             return carry
@@ -384,7 +374,7 @@
         twice[item, 0:TOP] = twice[item, total : total + TOP]
 
         def blend(slot, carry):
-            spot = start + lax.bitwise_xor(me, slot) * cells
+            spot = start + slot * cells
             back_two = twice[item, pl.ds(spot - 2, cells)]
             back_one = twice[item, pl.ds(spot - 1, cells)]
             centre = twice[item, pl.ds(spot, cells)]
@@ -399,12 +389,12 @@
         lax.fori_loop(0, slots, blend, 0, unroll=4)
 
 
-def move_columns(gathered, quantities, rank, shift_int, frac_num):
+def move_columns(gathered, quantities, mixed, rank, shift_int, frac_num):
     azimuths, share, cells, depth = gathered.shape
     smem = pl.BlockSpec(memory_space=pltpu.SMEM)
     vmem = pl.BlockSpec(memory_space=pltpu.VMEM)
     return pl.pallas_call(
-        functools.partial(move_kernel, quantities),
+        functools.partial(move_kernel, quantities, mixed),
         out_shape=jax.ShapeDtypeStruct(gathered.shape, jnp.float32),
         in_specs=[smem, smem, smem, vmem],
         out_specs=vmem,
@@ -488,10 +478,11 @@
         ]
     )
     moving = updated_columns(info, fields, density, head, tail, before, after, *layers)
-    moving = swap(moving)
-    still = swap(move_columns(still, 4, rank, shift_int, frac_num))
-    moving = swap(move_columns(moving, 4, rank, shift_int, frac_num))
-    return join(rank, moving, still, columns)
+    moving = lax.all_to_all(moving, "az", 0, 0, tiled=True)
+    still = move_columns(still, 4, True, rank, shift_int, frac_num)
+    moving = move_columns(moving, 4, False, rank, shift_int, frac_num)
+    both = jnp.concatenate([moving, still], axis=1)
+    return join(lax.all_to_all(both, "az", 0, 0, tiled=True), columns)
 
 
 def solution(mesh):

time: 82.6 us -> 86.5 us (1.047)
  blocking collectives: 0 us -> 29.9 us
  starting transfers between devices: 39.9 us -> 20.8 us
  waiting for transfers between devices: 33 us -> 25.5 us
    all_to_all x0 -> x1, blocking collectives: none -> 29.9 us  [local(): return join(lax.all_to_all(both, 'az', 0, 0, tiled=True), columns)]
    ppermute x24 -> x6, starting transfers between devices: 32 us -> 4.52 us  [send_step(): return lax.ppermute(cut[:, step], 'az', pairs)]
    ppermute x24 -> x6, waiting for transfers between devices: 25.7 us -> 17.9 us  [send_step(): return lax.ppermute(cut[:, step], 'az', pairs)]
    all_to_all x0 -> x1, starting transfers between devices: none -> 6.38 us  [local(): moving = lax.all_to_all(moving, 'az', 0, 0, tiled=True)]
    ppermute x2, starting transfers between devices: 0.11 us -> 2.14 us  [wrap(): return lax.ppermute(data, ('rad', 'az'), pairs)]
  transfers between devices with their start and end apart: 29 -> 12, of which waited for: 11 -> 7; matrix products, arithmetic and copies ran while one was open for 1% -> 0% of each run, Pallas kernels for 2% -> 1%
where the time goes in v10:
time: 86.5 us; the launch traced here: 87.5 us
  blocking collectives  29.9 us (35%)
  waiting for transfers between devices  25.5 us (29%)
  starting transfers between devices  20.8 us (24%)
  Pallas kernels  6.58 us (8%)
  local copies, waits for them, and re-layouts  2.85 us (3%)
  between operations  1.56 us (2%)
    all_to_all x1, blocking collectives, local(): return join(lax.all_to_all(both, 'az', 0, 0, tiled=True), columns)  29.9 us
    ppermute x6, waiting for transfers between devices, send_step(): return lax.ppermute(cut[:, step], 'az', pairs)  17.9 us
    all_to_all x1, starting transfers between devices, local(): moving = lax.all_to_all(moving, 'az', 0, 0, tiled=True)  6.38 us
    ppermute x2, waiting for transfers between devices, wrap(): return lax.ppermute(data, ('rad', 'az'), pairs)  6.3 us
    ppermute x1, starting transfers between devices, azimuthal_layers(): far = lax.ppermute(jnp.where(even, head, tail), 'az', outer)  5.67 us
    ppermute x6, starting transfers between devices, send_step(): return lax.ppermute(cut[:, step], 'az', pairs)  4.52 us
    pallas_call x1, Pallas kernels, updated_columns(): pl.pallas_call(stress_kernel, out_shape=jax.ShapeDtypeStruct((slots, 4 *...  3.23 us
    unnamed x12, local copies, waits for them, and re-layouts  2.74 us
  transfers between devices with their start and end apart: 12, of which 7 were waited for; matrix products, arithmetic and copies ran while one was open for 0% of the time, Pallas kernels for 1%

profile of v10, /device:TPU:0, one launch (start us, length us, event | category | flops | bytes accessed | tf_op | source)
XLA Modules:
  0.0 87.5 jit_solution(17342435845452632204)
XLA Ops:
  0.7 1.2 %copy-done = f32[7,16,16,128]{3,2,1,0:T(8,128)S(1)} copy-done((f32[7,16,16,128]{3,2,1,0:T(8,128)S(1)}, f32[7,16,16,128]{3,2,1,0:T(8,128)}, u32[]{:S(2)}) %copy-start) | copy-done | bytes 917528
  1.8 0.9 %copy-done.2 = f32[16,16,128]{2,1,0:T(8,128)S(1)} copy-done((f32[16,16,128]{2,1,0:T(8,128)S(1)}, f32[16,16,128]{2,1,0:T(8,128)}, u32[]{:S(2)}) %copy-start.2) | copy-done | bytes 131096
  2.7 0.4 pack.1
  3.1 0.5 collective-permute-start.33
  3.6 5.7 %collective-permute-start.32 = (f32[10,16,128]{2,1,0:T(8,128)S(1)}, f32[10,16,128]{2,1,0:T(8,128)S(1)}, u32[]{:S(2)}, u32[]{:S(2)}) collective-permute-start(f32[10,16,128]{2,1,0:T(8,128)S(1)} %get-tuple-element.68), channel_id=1, source_target_pairs={{0,15},{1,2},{2,1},{3,4},{4,3},{5,6},{6,5},{7,8},{8,7},{9,10},{10,... | collective-permute-start | bytes 245768 | tf_op jit(solution)/shard_map/ppermute | solution.py:412
  9.3 0.1 collective-permute-start.34
  10.2 1.4 %collective-permute-done.32 = f32[10,16,128]{2,1,0:T(8,128)S(1)} collective-permute-done((f32[10,16,128]{2,1,0:T(8,128)S(1)}, f32[10,16,128]{2,1,0:T(8,128)S(1)}, u32[]{:S(2)}, u32[]{:S(2)}) %collective-permute-start.32) | collective-permute-done | bytes 81952 | tf_op jit(solution)/shard_map/ppermute | solution.py:412
  11.6 2.8 %collective-permute-done.34 = f32[1,4,4,16,128]{4,3,2,1,0:T(8,128)S(1)} collective-permute-done((f32[1,4,4,16,128]{4,3,2,1,0:T(8,128)S(1)}, f32[1,4,4,16,128]{4,3,2,1,0:T(8,128)S(1)}, u32[]{:S(2)}, u32[]{:S(2)}) %collective-permute-start.34) | collective-permute-done | bytes 131104 | tf_op jit(solution)/shard_map/ppermute | solution.py:163
  14.5 2.0 %collective-permute-start.36 = (f32[1,4,4,16,128]{4,3,2,1,0:T(8,128)S(1)}, f32[1,4,4,16,128]{4,3,2,1,0:T(8,128)S(1)}, u32[]{:S(2)}, u32[]{:S(2)}) collective-permute-start(f32[1,4,4,16,128]{4,3,2,1,0:T(8,128)S(1)} %get-tuple-element.60), channel_id=1, source_target_pairs={{0,12},{1,13},{2,14},{3,15},{4,8},{5,9},{6,10},{7,11},{8,4},{9,5},... | collective-permute-start | bytes 393224 | tf_op jit(solution)/shard_map/ppermute | solution.py:163
  16.5 0.3 collective-permute-start.35
  16.8 1.6 %collective-permute-start.37 = (f32[11,16,128]{2,1,0:T(8,128)S(1)}, f32[11,16,128]{2,1,0:T(8,128)S(1)}, u32[]{:S(2)}, u32[]{:S(2)}) collective-permute-start(f32[11,16,128]{2,1,0:T(8,128)S(1)} %get-tuple-element.64), channel_id=1, source_target_pairs={{0,16},{16,0},{1,17},{17,1},{2,18},{18,2},{3,19},{19,3},{4,20},{20... | collective-permute-start | bytes 270344 | tf_op jit(solution)/shard_map/ppermute | solution.py:441
  18.4 0.1 pad_add_fusion.info
  18.4 8.4 %conditional.1 = (f32[11,16,128]{2,1,0:T(8,128)}, f32[11,16,128]{2,1,0:T(8,128)}) conditional(s32[]{:T(128)} %clamp.3, f32[11,16,128]{2,1,0:T(8,128)S(1)} %get-tuple-element.63, f32[11,16,128]{2,1,0:T(8,128)S(1)} %get-tuple-element.63, f32[11,16,128]{2,1,0:T(8,128)S(1)} %get-tuple-element.63, ...), branch_computations={%region_0.1_spmd, %region_1.2_spmd, %region_2.3_spmd, %region_3.4_... | conditional | bytes 720992 | solution.py:449
  18.4 2.1 %collective-permute-start.23 = (f32[11,16,128]{2,1,0:T(8,128)S(1)}, f32[11,16,128]{2,1,0:T(8,128)}, u32[]{:S(2)}, u32[]{:S(2)}) collective-permute-start(f32[11,16,128]{2,1,0:T(8,128)S(1)} %param.11), channel_id=1, source_target_pairs={{16,12},{17,13},{18,14},{19,15},{20,0},{21,1},{22,2},{23,3},{24,4}... | collective-permute-start | bytes 270344 | tf_op jit(solution)/shard_map/cond/branch_11_fun/ppermute | solution.py:429
  20.6 3.6 %collective-permute-done.23 = f32[11,16,128]{2,1,0:T(8,128)} collective-permute-done((f32[11,16,128]{2,1,0:T(8,128)S(1)}, f32[11,16,128]{2,1,0:T(8,128)}, u32[]{:S(2)}, u32[]{:S(2)}) %collective-permute-start.23) | collective-permute-done | bytes 90144 | tf_op jit(solution)/shard_map/cond/branch_11_fun/ppermute | solution.py:429
  24.2 2.7 %collective-permute-done.22 = f32[11,16,128]{2,1,0:T(8,128)} collective-permute-done((f32[11,16,128]{2,1,0:T(8,128)S(1)}, f32[11,16,128]{2,1,0:T(8,128)}, u32[]{:S(2)}, u32[]{:S(2)}) %collective-permute-start.22) | collective-permute-done | bytes 90144 | tf_op jit(solution)/shard_map/cond/branch_11_fun/ppermute | solution.py:429
  26.9 3.5 %collective-permute-done.35 = f32[1,4,4,16,128]{4,3,2,1,0:T(8,128)S(1)} collective-permute-done((f32[1,4,4,16,128]{4,3,2,1,0:T(8,128)S(1)}, f32[1,4,4,16,128]{4,3,2,1,0:T(8,128)S(1)}, u32[]{:S(2)}, u32[]{:S(2)}) %collective-permute-start.35) | collective-permute-done | bytes 131104 | tf_op jit(solution)/shard_map/ppermute | solution.py:163
  30.4 3.2 %stress_update.1 = f32[16,4,16,128]{3,2,1,0:T(8,128)} custom-call(s32[4]{0:T(128)S(1)} %pad_add_fusion.info, f32[7,16,16,128]{3,2,1,0:T(8,128)S(1)} %copy-done.1, f32[16,16,128]{2,1,0:T(8,128)S(1)} %copy-done.3, f32[10,16,128]{2,1,0:T(8,128)S(1)} %get-tuple-element.37.head, f32[10,16,128]{2,1,0:T(8,128)S(1)} %get-tuple-element.38.tail, ...), custom_call_target="tpu_custom_call" | custom-call | tf_op jit(solution)/shard_map/stress_update/pallas_call | solution.py:336
  33.6 6.4 %all-to-all-start = ((f32[16,4,16,128]{3,2,1,0:T(8,128)}), f32[16,4,16,128]{3,2,1,0:T(8,128)S(1)}, u32[]{:S(2)}, u32[]{:S(2)}) async-start(f32[16,4,16,128]{3,2,1,0:T(8,128)} %stress_update.1), calls=%async_computation | async-start | bytes 1048576 | tf_op jit(solution)/shard_map/all_to_all | solution.py:481
  40.1 1.7 %collective-permute-start.40 = (f32[4,1,4,16,128]{4,3,2,0,1:T(8,128)S(1)}, f32[4,1,4,16,128]{4,3,2,0,1:T(8,128)S(1)}, u32[]{:S(2)}, u32[]{:S(2)}) collective-permute-start(f32[4,1,4,16,128]{4,3,2,0,1:T(8,128)S(1)} %get-tuple-element.57), channel_id=1, source_target_pairs={{0,3},{1,2},{2,1},{3,0},{4,7},{5,6},{6,5},{7,4},{8,11},{9,10},{10,... | collective-permute-start | bytes 393224 | tf_op jit(solution)/shard_map/ppermute | solution.py:163
  41.9 0.4 collective-permute-start.39
  42.3 6.8 %collective-permute-done.40 = f32[4,1,4,16,128]{4,3,2,0,1:T(8,128)S(1)} collective-permute-done((f32[4,1,4,16,128]{4,3,2,0,1:T(8,128)S(1)}, f32[4,1,4,16,128]{4,3,2,0,1:T(8,128)S(1)}, u32[]{:S(2)}, u32[]{:S(2)}) %collective-permute-start.40) | collective-permute-done | bytes 131104 | tf_op jit(solution)/shard_map/ppermute | solution.py:163
  49.0 4.8 %collective-permute-done.39 = f32[4,1,4,16,128]{4,3,2,0,1:T(8,128)S(1)} collective-permute-done((f32[4,1,4,16,128]{4,3,2,0,1:T(8,128)S(1)}, f32[4,1,4,16,128]{4,3,2,0,1:T(8,128)S(1)}, u32[]{:S(2)}, u32[]{:S(2)}) %collective-permute-start.39) | collective-permute-done | bytes 131104 | tf_op jit(solution)/shard_map/ppermute | solution.py:163
  53.8 0.0 copy-start.4
  53.8 0.0 copy-start.5
  53.8 0.6 copy-done.4
  54.5 0.0 copy-done.5
  54.5 1.0 %move.3 = f32[16,4,16,128]{3,2,1,0:T(8,128)S(1)} custom-call(s32[1]{0:T(128)} %bitcast.rank, s32[16]{0:T(128)S(1)} %copy-done.4, s32[16]{0:T(128)S(1)} %copy-done.5, f32[16,4,16,128]{3,2,1,0:T(8,128)S(1)} %bitcast.46), custom_call_target="tpu_custom_call" | custom-call | tf_op jit(solution)/shard_map/move/pallas_call | solution.py:396
  55.5 1.0 %move.2 = f32[16,4,16,128]{3,2,1,0:T(8,128)S(1)} custom-call(s32[1]{0:T(128)} %bitcast.rank, s32[16]{0:T(128)S(1)} %copy-done.4, s32[16]{0:T(128)S(1)} %copy-done.5, f32[16,4,16,128]{3,2,1,0:T(8,128)S(1)} %all-to-all-done.gathered), custom_call_target="tpu_custom_call" | custom-call | tf_op jit(solution)/shard_map/move/pallas_call | solution.py:396
  56.5 0.1 pad_maximum_fusion
  56.6 29.9 %all_to_all.10.returned = f32[16,8,16,128]{3,2,1,0:T(8,128)S(1)} all-to-all(f32[16,8,16,128]{3,2,1,0:T(8,128)S(1)} %pad_maximum_fusion), channel_id=1, replica_groups=mesh['rad'=2,'az'=16] {'az'}, dimensions={0} | all-to-all | bytes 2097152 | tf_op jit(solution)/shard_map/all_to_all | solution.py:485
  86.5 1.0 %join.1 = (f32[7,16,16,128]{3,2,1,0:T(8,128)}, f32[16,16,128]{2,1,0:T(8,128)}) custom-call(f32[16,8,16,128]{3,2,1,0:T(8,128)S(1)} %all_to_all.10.returned), custom_call_target="tpu_custom_call" | custom-call | tf_op jit(solution)/shard_map/join/pallas_call | solution.py:142
  (26 shorter events, 0.3 us)
Async XLA Ops:
  0.6 1.2 %copy-start = (f32[7,16,16,128]{3,2,1,0:T(8,128)S(1)}, f32[7,16,16,128]{3,2,1,0:T(8,128)}, u32[]{:S(2)}) copy-start(f32[7,16,16,128]{3,2,1,0:T(8,128)} %fields.1) | copy-start | bytes 2752516
  1.8 0.9 %copy-start.2 = (f32[16,16,128]{2,1,0:T(8,128)S(1)}, f32[16,16,128]{2,1,0:T(8,128)}, u32[]{:S(2)}) copy-start(f32[16,16,128]{2,1,0:T(8,128)} %density.1) | copy-start | bytes 393220
  3.1 7.0 %collective-permute-start.33 = (f32[10,16,128]{2,1,0:T(8,128)S(1)}, f32[10,16,128]{2,1,0:T(8,128)S(1)}, u32[]{:S(2)}, u32[]{:S(2)}) collective-permute-start(f32[10,16,128]{2,1,0:T(8,128)S(1)} %get-tuple-element.67), channel_id=1, source_target_pairs={{0,1},{1,0},{2,3},{3,2},{4,5},{5,4},{6,7},{7,6},{8,9},{9,8},{10,11... | collective-permute-start | bytes 245768 | tf_op jit(solution)/shard_map/ppermute | solution.py:413
  3.6 7.9 %collective-permute-start.32 = (f32[10,16,128]{2,1,0:T(8,128)S(1)}, f32[10,16,128]{2,1,0:T(8,128)S(1)}, u32[]{:S(2)}, u32[]{:S(2)}) collective-permute-start(f32[10,16,128]{2,1,0:T(8,128)S(1)} %get-tuple-element.68), channel_id=1, source_target_pairs={{0,15},{1,2},{2,1},{3,4},{4,3},{5,6},{6,5},{7,8},{8,7},{9,10},{10,... | collective-permute-start | bytes 245768 | tf_op jit(solution)/shard_map/ppermute | solution.py:412
  9.3 21.1 %copy-start.1 = (f32[7,16,16,128]{3,2,1,0:T(8,128)S(1)}, f32[7,16,16,128]{3,2,1,0:T(8,128)}, u32[]{:S(2)}) copy-start(f32[7,16,16,128]{3,2,1,0:T(8,128)} %fields.1) | copy-start | bytes 2752516
  9.3 5.0 %collective-permute-start.34 = (f32[1,4,4,16,128]{4,3,2,1,0:T(8,128)S(1)}, f32[1,4,4,16,128]{4,3,2,1,0:T(8,128)S(1)}, u32[]{:S(2)}, u32[]{:S(2)}) collective-permute-start(f32[1,4,4,16,128]{4,3,2,1,0:T(8,128)S(1)} %slice_bitcast_fusion.4), channel_id=1, source_target_pairs={{0,4},{1,5},{2,6},{3,7},{4,0},{5,1},{6,2},{7,3},{8,12},{9,13},{10,... | collective-permute-start | bytes 393224 | tf_op jit(solution)/shard_map/ppermute | solution.py:163
  14.5 12.4 %collective-permute-start.36 = (f32[1,4,4,16,128]{4,3,2,1,0:T(8,128)S(1)}, f32[1,4,4,16,128]{4,3,2,1,0:T(8,128)S(1)}, u32[]{:S(2)}, u32[]{:S(2)}) collective-permute-start(f32[1,4,4,16,128]{4,3,2,1,0:T(8,128)S(1)} %get-tuple-element.60), channel_id=1, source_target_pairs={{0,12},{1,13},{2,14},{3,15},{4,8},{5,9},{6,10},{7,11},{8,4},{9,5},... | collective-permute-start | bytes 393224 | tf_op jit(solution)/shard_map/ppermute | solution.py:163
  16.5 13.9 %collective-permute-start.35 = (f32[1,4,4,16,128]{4,3,2,1,0:T(8,128)S(1)}, f32[1,4,4,16,128]{4,3,2,1,0:T(8,128)S(1)}, u32[]{:S(2)}, u32[]{:S(2)}) collective-permute-start(f32[1,4,4,16,128]{4,3,2,1,0:T(8,128)S(1)} %get-tuple-element.61), channel_id=1, source_target_pairs={{0,8},{1,9},{2,10},{3,11},{4,12},{5,13},{6,14},{7,15},{8,0},{9,1},... | collective-permute-start | bytes 393224 | tf_op jit(solution)/shard_map/ppermute | solution.py:163
  16.8 13.6 %copy-start.3 = (f32[16,16,128]{2,1,0:T(8,128)S(1)}, f32[16,16,128]{2,1,0:T(8,128)}, u32[]{:S(2)}) copy-start(f32[16,16,128]{2,1,0:T(8,128)} %density.1) | copy-start | bytes 393220
  16.8 10.1 %collective-permute-start.37 = (f32[11,16,128]{2,1,0:T(8,128)S(1)}, f32[11,16,128]{2,1,0:T(8,128)S(1)}, u32[]{:S(2)}, u32[]{:S(2)}) collective-permute-start(f32[11,16,128]{2,1,0:T(8,128)S(1)} %get-tuple-element.64), channel_id=1, source_target_pairs={{0,16},{16,0},{1,17},{17,1},{2,18},{18,2},{3,19},{19,3},{4,20},{20... | collective-permute-start | bytes 270344 | tf_op jit(solution)/shard_map/ppermute | solution.py:441
  18.4 5.7 %collective-permute-start.23 = (f32[11,16,128]{2,1,0:T(8,128)S(1)}, f32[11,16,128]{2,1,0:T(8,128)}, u32[]{:S(2)}, u32[]{:S(2)}) collective-permute-start(f32[11,16,128]{2,1,0:T(8,128)S(1)} %param.11), channel_id=1, source_target_pairs={{16,12},{17,13},{18,14},{19,15},{20,0},{21,1},{22,2},{23,3},{24,4}... | collective-permute-start | bytes 270344 | tf_op jit(solution)/shard_map/cond/branch_11_fun/ppermute | solution.py:429
  20.6 6.3 %collective-permute-start.22 = (f32[11,16,128]{2,1,0:T(8,128)S(1)}, f32[11,16,128]{2,1,0:T(8,128)}, u32[]{:S(2)}, u32[]{:S(2)}) collective-permute-start(f32[11,16,128]{2,1,0:T(8,128)S(1)} %param.11), channel_id=1, source_target_pairs={{16,11},{17,12},{18,13},{19,14},{20,15},{21,0},{22,1},{23,2},{24,3... | collective-permute-start | bytes 270344 | tf_op jit(solution)/shard_map/cond/branch_11_fun/ppermute | solution.py:429
  33.6 21.9 %all-to-all-start = ((f32[16,4,16,128]{3,2,1,0:T(8,128)}), f32[16,4,16,128]{3,2,1,0:T(8,128)S(1)}, u32[]{:S(2)}, u32[]{:S(2)}) async-start(f32[16,4,16,128]{3,2,1,0:T(8,128)} %stress_update.1), calls=%async_computation | async-start | bytes 1048576 | tf_op jit(solution)/shard_map/all_to_all | solution.py:481
  40.1 8.9 %collective-permute-start.40 = (f32[4,1,4,16,128]{4,3,2,0,1:T(8,128)S(1)}, f32[4,1,4,16,128]{4,3,2,0,1:T(8,128)S(1)}, u32[]{:S(2)}, u32[]{:S(2)}) collective-permute-start(f32[4,1,4,16,128]{4,3,2,0,1:T(8,128)S(1)} %get-tuple-element.57), channel_id=1, source_target_pairs={{0,3},{1,2},{2,1},{3,0},{4,7},{5,6},{6,5},{7,4},{8,11},{9,10},{10,... | collective-permute-start | bytes 393224 | tf_op jit(solution)/shard_map/ppermute | solution.py:163
  41.9 11.9 %collective-permute-start.39 = (f32[4,1,4,16,128]{4,3,2,0,1:T(8,128)S(1)}, f32[4,1,4,16,128]{4,3,2,0,1:T(8,128)S(1)}, u32[]{:S(2)}, u32[]{:S(2)}) collective-permute-start(f32[4,1,4,16,128]{4,3,2,0,1:T(8,128)S(1)} %get-tuple-element.58), channel_id=1, source_target_pairs={{0,2},{1,3},{2,0},{3,1},{4,6},{5,7},{6,4},{7,5},{8,10},{9,11},{10,... | collective-permute-start | bytes 393224 | tf_op jit(solution)/shard_map/ppermute | solution.py:163
  42.2 11.5 %collective-permute-start.38 = (f32[4,1,4,16,128]{4,3,2,0,1:T(8,128)S(1)}, f32[4,1,4,16,128]{4,3,2,0,1:T(8,128)S(1)}, u32[]{:S(2)}, u32[]{:S(2)}) collective-permute-start(f32[4,1,4,16,128]{4,3,2,0,1:T(8,128)S(1)} %get-tuple-element.59), channel_id=1, source_target_pairs={{0,1},{1,0},{2,3},{3,2},{4,5},{5,4},{6,7},{7,6},{8,9},{9,8},{10,11... | collective-permute-start | bytes 393224 | tf_op jit(solution)/shard_map/ppermute | solution.py:163
  53.8 0.7 copy-start.4
  53.8 0.7 copy-start.5

commit v11 on v9

--- a/solution.py
+++ b/solution.py
@@ -471,9 +471,9 @@
     radix = digit_radix(count)
     span = count // radix
     cut = still.reshape(1, radix, span, *still.shape[1:])
-    nearest = send_step(cut, 1)
-    before, after, cut = lax.optimization_barrier((before, after, cut))
-    parts = [cut[:, 0], nearest] + [send_step(cut, step) for step in range(2, radix)]
+    parts = [cut[:, 0]] + [send_step(cut, step) for step in (2, 3, 1) if step < radix]
+    before, after, parts = lax.optimization_barrier((before, after, parts))
+    parts = parts[:1] + parts[-1:] + parts[1:-1]
     layers = rims(shear_cells // cells, low, high, before, after)
     parts, layers = lax.optimization_barrier((parts, layers))
     still = swap(jnp.stack(parts, axis=1).reshape(still.shape), span)

time: 90.7 us -> 93.9 us (1.035); the launches traced: 91.1 us -> 95.6 us
  waiting for transfers between devices: 42 us -> 48.9 us
  starting transfers between devices: 38.6 us -> 36.2 us
    ppermute x24, waiting for transfers between devices: 29.4 us -> 41.7 us  [send_step(): return lax.ppermute(cut[:, step], 'az', pairs)]
    ppermute x1, waiting for transfers between devices: 4.54 us -> 0.01 us  [rims(): below = above = lax.ppermute(other, 'rad', [(0, 1), (1, 0)])]
    ppermute x2, starting transfers between devices: 4.04 us -> 0.75 us  [wrap(): return lax.ppermute(data, ('rad', 'az'), pairs)]
    ppermute x1, starting transfers between devices: 0.02 us -> 1.56 us  [rims(): below = above = lax.ppermute(other, 'rad', [(0, 1), (1, 0)])]
    ppermute x1, waiting for transfers between devices: 1.45 us -> 0.01 us  [azimuthal_layers(): far = lax.ppermute(jnp.where(even, head, tail), 'az', outer)]
  transfers between devices with their start and end apart: 29 -> 29, of which waited for: 13 -> 13; matrix products, arithmetic and copies ran while one was open for 1% -> 0% of each run, Pallas kernels for 4% -> 4%
where the time goes in v11:
time: 93.9 us; the launch traced here: 95.6 us
  waiting for transfers between devices  48.9 us (52%)
  starting transfers between devices  36.2 us (39%)
  Pallas kernels  6.04 us (6%)
  local copies, waits for them, and re-layouts  2.41 us (3%)
  between operations  1.56 us (2%)
    ppermute x24, waiting for transfers between devices, send_step(): return lax.ppermute(cut[:, step], 'az', pairs)  41.7 us
    ppermute x24, starting transfers between devices, send_step(): return lax.ppermute(cut[:, step], 'az', pairs)  27.7 us
    ppermute x2, waiting for transfers between devices, wrap(): return lax.ppermute(data, ('rad', 'az'), pairs)  7.18 us
    ppermute x1, starting transfers between devices, azimuthal_layers(): far = lax.ppermute(jnp.where(even, head, tail), 'az', outer)  5.67 us
    pallas_call x1, Pallas kernels, updated_columns(): pl.pallas_call(stress_kernel, out_shape=jax.ShapeDtypeStruct((slots, 4 *...  2.48 us
    unnamed x8, local copies, waits for them, and re-layouts  2.08 us
    pallas_call x2, Pallas kernels, move_columns(): pl.pallas_call(functools.partial(move_kernel, quantities), out_shape=jax....  1.99 us
  transfers between devices with their start and end apart: 29, of which 13 were waited for; matrix products, arithmetic and copies ran while one was open for 0% of the time, Pallas kernels for 4%

profile of v11, /device:TPU:0, one launch (start us, length us, event | category | flops | bytes accessed | tf_op | source)
XLA Modules:
  0.0 95.6 jit_solution(10755368307570157815)
XLA Ops:
  0.7 1.2 %copy-done = f32[7,16,16,128]{3,2,1,0:T(8,128)S(1)} copy-done((f32[7,16,16,128]{3,2,1,0:T(8,128)S(1)}, f32[7,16,16,128]{3,2,1,0:T(8,128)}, u32[]{:S(2)}) %copy-start) | copy-done | bytes 917528
  1.8 0.9 copy-done.1
  3.8 5.7 %collective-permute-start.32 = (f32[10,16,128]{2,1,0:T(8,128)S(1)}, f32[10,16,128]{2,1,0:T(8,128)S(1)}, u32[]{:S(2)}, u32[]{:S(2)}) collective-permute-start(f32[10,16,128]{2,1,0:T(8,128)S(1)} %get-tuple-element.105), channel_id=1, source_target_pairs={{0,15},{1,2},{2,1},{3,4},{4,3},{5,6},{6,5},{7,8},{8,7},{9,10},{10,... | collective-permute-start | bytes 245768 | tf_op jit(solution)/shard_map/ppermute | solution.py:420
  10.5 2.6 %collective-permute-start.34 = (f32[1,4,4,16,128]{4,3,2,1,0:T(8,128)S(1)}, f32[1,4,4,16,128]{4,3,2,1,0:T(8,128)S(1)}, u32[]{:S(2)}, u32[]{:S(2)}) collective-permute-start(f32[1,4,4,16,128]{4,3,2,1,0:T(8,128)S(1)} %get-tuple-element.98), channel_id=1, source_target_pairs={{0,8},{1,9},{2,10},{3,11},{4,12},{5,13},{6,14},{7,15},{8,0},{9,1},... | collective-permute-start | bytes 393224 | tf_op jit(solution)/shard_map/ppermute | solution.py:172
  13.1 4.7 %collective-permute-done.36 = f32[1,4,4,16,128]{4,3,2,1,0:T(8,128)S(1)} collective-permute-done((f32[1,4,4,16,128]{4,3,2,1,0:T(8,128)S(1)}, f32[1,4,4,16,128]{4,3,2,1,0:T(8,128)S(1)}, u32[]{:S(2)}, u32[]{:S(2)}) %collective-permute-start.36) | collective-permute-done | bytes 131104 | tf_op jit(solution)/shard_map/ppermute | solution.py:172
  17.7 1.1 %collective-permute-done.35 = f32[1,4,4,16,128]{4,3,2,1,0:T(8,128)S(1)} collective-permute-done((f32[1,4,4,16,128]{4,3,2,1,0:T(8,128)S(1)}, f32[1,4,4,16,128]{4,3,2,1,0:T(8,128)S(1)}, u32[]{:S(2)}, u32[]{:S(2)}) %collective-permute-start.35) | collective-permute-done | bytes 131104 | tf_op jit(solution)/shard_map/ppermute | solution.py:172
  18.8 4.6 %collective-permute-done.34 = f32[1,4,4,16,128]{4,3,2,1,0:T(8,128)S(1)} collective-permute-done((f32[1,4,4,16,128]{4,3,2,1,0:T(8,128)S(1)}, f32[1,4,4,16,128]{4,3,2,1,0:T(8,128)S(1)}, u32[]{:S(2)}, u32[]{:S(2)}) %collective-permute-start.34) | collective-permute-done | bytes 131104 | tf_op jit(solution)/shard_map/ppermute | solution.py:172
  23.6 1.6 %collective-permute-start.37 = (f32[11,16,128]{2,1,0:T(8,128)S(1)}, f32[11,16,128]{2,1,0:T(8,128)S(1)}, u32[]{:S(2)}, u32[]{:S(2)}) collective-permute-start(f32[11,16,128]{2,1,0:T(8,128)S(1)} %get-tuple-element.101), channel_id=1, source_target_pairs={{0,16},{16,0},{1,17},{17,1},{2,18},{18,2},{3,19},{19,3},{4,20},{20... | collective-permute-start | bytes 270344 | tf_op jit(solution)/shard_map/ppermute | solution.py:449
  25.8 8.0 %conditional.1 = (f32[11,16,128]{2,1,0:T(8,128)}, f32[11,16,128]{2,1,0:T(8,128)}) conditional(s32[]{:T(128)} %clamp.3, f32[11,16,128]{2,1,0:T(8,128)S(1)} %get-tuple-element.100, f32[11,16,128]{2,1,0:T(8,128)S(1)} %get-tuple-element.100, f32[11,16,128]{2,1,0:T(8,128)S(1)} %get-tuple-element.100, ...), branch_computations={%region_0.1_spmd, %region_1.2_spmd, %region_2.3_spmd, %region_3.4_... | conditional | bytes 720992 | solution.py:457
  26.6 7.2 %collective-permute-done.19 = f32[11,16,128]{2,1,0:T(8,128)} collective-permute-done((f32[11,16,128]{2,1,0:T(8,128)S(1)}, f32[11,16,128]{2,1,0:T(8,128)}, u32[]{:S(2)}, u32[]{:S(2)}) %collective-permute-start.19) | collective-permute-done | bytes 90144 | tf_op jit(solution)/shard_map/cond/branch_9_fun/ppermute | solution.py:437
  33.9 3.8 %collective-permute-start.39 = (f32[4,1,4,16,128]{4,3,2,0,1:T(8,128)S(1)}, f32[4,1,4,16,128]{4,3,2,0,1:T(8,128)S(1)}, u32[]{:S(2)}, u32[]{:S(2)}) collective-permute-start(f32[4,1,4,16,128]{4,3,2,0,1:T(8,128)S(1)} %get-tuple-element.94), channel_id=1, source_target_pairs={{0,2},{1,3},{2,0},{3,1},{4,6},{5,7},{6,4},{7,5},{8,10},{9,11},{10,... | collective-permute-start | bytes 393224 | tf_op jit(solution)/shard_map/ppermute | solution.py:172
  37.9 2.5 %stress_update.1 = f32[16,4,16,128]{3,2,1,0:T(8,128)S(1)} custom-call(s32[4]{0:T(128)S(1)} %pad_add_fusion.info, f32[7,16,16,128]{3,2,1,0:T(8,128)S(1)} %get-tuple-element.43.fields, f32[16,16,128]{2,1,0:T(8,128)S(1)} %get-tuple-element.44.density, f32[10,16,128]{2,1,0:T(8,128)S(1)} %get-tuple-element.45.head, f32[10,16,128]{2,1,0:T(8,128)S(1)} %get-tuple-element.46.tail, ...), custom_call_target="tpu_custom_call" | custom-call | tf_op jit(solution)/shard_map/stress_update/pallas_call | solution.py:345
  40.4 2.7 %collective-permute-done.39 = f32[4,1,4,16,128]{4,3,2,0,1:T(8,128)S(1)} collective-permute-done((f32[4,1,4,16,128]{4,3,2,0,1:T(8,128)S(1)}, f32[4,1,4,16,128]{4,3,2,0,1:T(8,128)S(1)}, u32[]{:S(2)}, u32[]{:S(2)}) %collective-permute-start.39) | collective-permute-done | bytes 131104 | tf_op jit(solution)/shard_map/ppermute | solution.py:172
  43.1 3.6 %collective-permute-start.43 = (f32[1,4,4,16,128]{4,3,2,1,0:T(8,128)S(1)}, f32[1,4,4,16,128]{4,3,2,1,0:T(8,128)S(1)}, u32[]{:S(2)}, u32[]{:S(2)}) collective-permute-start(f32[1,4,4,16,128]{4,3,2,1,0:T(8,128)S(1)} %get-tuple-element.89), channel_id=1, source_target_pairs={{0,12},{1,13},{2,14},{3,15},{4,8},{5,9},{6,10},{7,11},{8,4},{9,5},... | collective-permute-start | bytes 393224 | tf_op jit(solution)/shard_map/ppermute | solution.py:172
  47.6 1.0 %move.3 = f32[16,4,16,128]{3,2,1,0:T(8,128)S(1)} custom-call(s32[1]{0:T(128)} %bitcast.rank, s32[16]{0:T(128)S(1)} %copy-done.2, s32[16]{0:T(128)S(1)} %copy-done.3, f32[16,4,16,128]{3,2,1,0:T(8,128)S(1)} %bitcast.150), custom_call_target="tpu_custom_call" | custom-call | tf_op jit(solution)/shard_map/move/pallas_call | solution.py:404
  48.6 3.6 %collective-permute-start.55 = (f32[1,4,4,16,128]{4,3,2,1,0:T(8,128)S(1)}, f32[1,4,4,16,128]{4,3,2,1,0:T(8,128)S(1)}, u32[]{:S(2)}, u32[]{:S(2)}) collective-permute-start(f32[1,4,4,16,128]{4,3,2,1,0:T(8,128)S(1)} %get-tuple-element.73), channel_id=1, source_target_pairs={{0,12},{1,13},{2,14},{3,15},{4,8},{5,9},{6,10},{7,11},{8,4},{9,5},... | collective-permute-start | bytes 393224 | tf_op jit(solution)/shard_map/ppermute | solution.py:172
  52.2 3.0 %collective-permute-start.53 = (f32[1,4,4,16,128]{4,3,2,1,0:T(8,128)S(1)}, f32[1,4,4,16,128]{4,3,2,1,0:T(8,128)S(1)}, u32[]{:S(2)}, u32[]{:S(2)}) collective-permute-start(f32[1,4,4,16,128]{4,3,2,1,0:T(8,128)S(1)} %get-tuple-element.75), channel_id=1, source_target_pairs={{0,4},{1,5},{2,6},{3,7},{4,0},{5,1},{6,2},{7,3},{8,12},{9,13},{10,... | collective-permute-start | bytes 393224 | tf_op jit(solution)/shard_map/ppermute | solution.py:172
  55.2 7.9 %collective-permute-done.42 = f32[1,4,4,16,128]{4,3,2,1,0:T(8,128)S(1)} collective-permute-done((f32[1,4,4,16,128]{4,3,2,1,0:T(8,128)S(1)}, f32[1,4,4,16,128]{4,3,2,1,0:T(8,128)S(1)}, u32[]{:S(2)}, u32[]{:S(2)}) %collective-permute-start.42) | collective-permute-done | bytes 131104 | tf_op jit(solution)/shard_map/ppermute | solution.py:172
  63.3 1.4 %collective-permute-start.45 = (f32[4,1,4,16,128]{4,3,2,0,1:T(8,128)S(1)}, f32[4,1,4,16,128]{4,3,2,0,1:T(8,128)S(1)}, u32[]{:S(2)}, u32[]{:S(2)}) collective-permute-start(f32[4,1,4,16,128]{4,3,2,0,1:T(8,128)S(1)} %get-tuple-element.86), channel_id=1, source_target_pairs={{0,2},{1,3},{2,0},{3,1},{4,6},{5,7},{6,4},{7,5},{8,10},{9,11},{10,... | collective-permute-start | bytes 393224 | tf_op jit(solution)/shard_map/ppermute | solution.py:172
  65.1 2.9 %collective-permute-done.54 = f32[1,4,4,16,128]{4,3,2,1,0:T(8,128)S(1)} collective-permute-done((f32[1,4,4,16,128]{4,3,2,1,0:T(8,128)S(1)}, f32[1,4,4,16,128]{4,3,2,1,0:T(8,128)S(1)}, u32[]{:S(2)}, u32[]{:S(2)}) %collective-permute-start.54) | collective-permute-done | bytes 131104 | tf_op jit(solution)/shard_map/ppermute | solution.py:172
  68.0 1.0 %collective-permute-done.46 = f32[4,1,4,16,128]{4,3,2,0,1:T(8,128)S(1)} collective-permute-done((f32[4,1,4,16,128]{4,3,2,0,1:T(8,128)S(1)}, f32[4,1,4,16,128]{4,3,2,0,1:T(8,128)S(1)}, u32[]{:S(2)}, u32[]{:S(2)}) %collective-permute-start.46) | collective-permute-done | bytes 131104 | tf_op jit(solution)/shard_map/ppermute | solution.py:172
  69.1 2.6 %collective-permute-done.45 = f32[4,1,4,16,128]{4,3,2,0,1:T(8,128)S(1)} collective-permute-done((f32[4,1,4,16,128]{4,3,2,0,1:T(8,128)S(1)}, f32[4,1,4,16,128]{4,3,2,0,1:T(8,128)S(1)}, u32[]{:S(2)}, u32[]{:S(2)}) %collective-permute-start.45) | collective-permute-done | bytes 131104 | tf_op jit(solution)/shard_map/ppermute | solution.py:172
  71.7 1.0 %move.2 = f32[16,4,16,128]{3,2,1,0:T(8,128)S(1)} custom-call(s32[1]{0:T(128)} %bitcast.rank, s32[16]{0:T(128)S(1)} %copy-done.2, s32[16]{0:T(128)S(1)} %copy-done.3, f32[16,4,16,128]{3,2,1,0:T(8,128)S(1)} %bitcast.154), custom_call_target="tpu_custom_call" | custom-call | tf_op jit(solution)/shard_map/move/pallas_call | solution.py:404
  72.7 2.6 %collective-permute-start.49 = (f32[1,4,4,16,128]{4,3,2,1,0:T(8,128)S(1)}, f32[1,4,4,16,128]{4,3,2,1,0:T(8,128)S(1)}, u32[]{:S(2)}, u32[]{:S(2)}) collective-permute-start(f32[1,4,4,16,128]{4,3,2,1,0:T(8,128)S(1)} %get-tuple-element.81), channel_id=1, source_target_pairs={{0,12},{1,13},{2,14},{3,15},{4,8},{5,9},{6,10},{7,11},{8,4},{9,5},... | collective-permute-start | bytes 393224 | tf_op jit(solution)/shard_map/ppermute | solution.py:172
  75.3 1.9 %collective-permute-start.47 = (f32[1,4,4,16,128]{4,3,2,1,0:T(8,128)S(1)}, f32[1,4,4,16,128]{4,3,2,1,0:T(8,128)S(1)}, u32[]{:S(2)}, u32[]{:S(2)}) collective-permute-start(f32[1,4,4,16,128]{4,3,2,1,0:T(8,128)S(1)} %get-tuple-element.83), channel_id=1, source_target_pairs={{0,4},{1,5},{2,6},{3,7},{4,0},{5,1},{6,2},{7,3},{8,12},{9,13},{10,... | collective-permute-start | bytes 393224 | tf_op jit(solution)/shard_map/ppermute | solution.py:172
  77.3 0.9 collective-permute-start.57
  78.2 2.9 %collective-permute-done.49 = f32[1,4,4,16,128]{4,3,2,1,0:T(8,128)S(1)} collective-permute-done((f32[1,4,4,16,128]{4,3,2,1,0:T(8,128)S(1)}, f32[1,4,4,16,128]{4,3,2,1,0:T(8,128)S(1)}, u32[]{:S(2)}, u32[]{:S(2)}) %collective-permute-start.49) | collective-permute-done | bytes 131104 | tf_op jit(solution)/shard_map/ppermute | solution.py:172
  81.1 4.7 %collective-permute-done.48 = f32[1,4,4,16,128]{4,3,2,1,0:T(8,128)S(1)} collective-permute-done((f32[1,4,4,16,128]{4,3,2,1,0:T(8,128)S(1)}, f32[1,4,4,16,128]{4,3,2,1,0:T(8,128)S(1)}, u32[]{:S(2)}, u32[]{:S(2)}) %collective-permute-start.48) | collective-permute-done | bytes 131104 | tf_op jit(solution)/shard_map/ppermute | solution.py:172
  86.1 1.4 %collective-permute-start.51 = (f32[4,1,4,16,128]{4,3,2,0,1:T(8,128)S(1)}, f32[4,1,4,16,128]{4,3,2,0,1:T(8,128)S(1)}, u32[]{:S(2)}, u32[]{:S(2)}) collective-permute-start(f32[4,1,4,16,128]{4,3,2,0,1:T(8,128)S(1)} %get-tuple-element.78), channel_id=1, source_target_pairs={{0,2},{1,3},{2,0},{3,1},{4,6},{5,7},{6,4},{7,5},{8,10},{9,11},{10,... | collective-permute-start | bytes 393224 | tf_op jit(solution)/shard_map/ppermute | solution.py:172
  87.8 3.7 %collective-permute-done.52 = f32[4,1,4,16,128]{4,3,2,0,1:T(8,128)S(1)} collective-permute-done((f32[4,1,4,16,128]{4,3,2,0,1:T(8,128)S(1)}, f32[4,1,4,16,128]{4,3,2,0,1:T(8,128)S(1)}, u32[]{:S(2)}, u32[]{:S(2)}) %collective-permute-start.52) | collective-permute-done | bytes 131104 | tf_op jit(solution)/shard_map/ppermute | solution.py:172
  91.5 3.0 %collective-permute-done.51 = f32[4,1,4,16,128]{4,3,2,0,1:T(8,128)S(1)} collective-permute-done((f32[4,1,4,16,128]{4,3,2,0,1:T(8,128)S(1)}, f32[4,1,4,16,128]{4,3,2,0,1:T(8,128)S(1)}, u32[]{:S(2)}, u32[]{:S(2)}) %collective-permute-start.51) | collective-permute-done | bytes 131104 | tf_op jit(solution)/shard_map/ppermute | solution.py:172
  94.6 1.0 %join.1 = (f32[7,16,16,128]{3,2,1,0:T(8,128)}, f32[16,16,128]{2,1,0:T(8,128)}) custom-call(s32[1]{0:T(128)} %bitcast.rank, f32[16,4,16,128]{3,2,1,0:T(8,128)S(1)} %bitcast.151, f32[16,4,16,128]{3,2,1,0:T(8,128)S(1)} %bitcast.149), custom_call_target="tpu_custom_call" | custom-call | tf_op jit(solution)/shard_map/join/pallas_call | solution.py:151
  (65 shorter events, 5.6 us)
Async XLA Ops:
  0.6 1.2 %copy-start = (f32[7,16,16,128]{3,2,1,0:T(8,128)S(1)}, f32[7,16,16,128]{3,2,1,0:T(8,128)}, u32[]{:S(2)}) copy-start(f32[7,16,16,128]{3,2,1,0:T(8,128)} %fields_in.1) | copy-start | bytes 2752516
  1.8 0.9 copy-start.1
  3.3 9.8 %collective-permute-start.33 = (f32[10,16,128]{2,1,0:T(8,128)S(1)}, f32[10,16,128]{2,1,0:T(8,128)S(1)}, u32[]{:S(2)}, u32[]{:S(2)}) collective-permute-start(f32[10,16,128]{2,1,0:T(8,128)S(1)} %get-tuple-element.104), channel_id=1, source_target_pairs={{0,1},{1,0},{2,3},{3,2},{4,5},{5,4},{6,7},{7,6},{8,9},{9,8},{10,11... | collective-permute-start | bytes 245768 | tf_op jit(solution)/shard_map/ppermute | solution.py:421
  3.8 9.3 %collective-permute-start.32 = (f32[10,16,128]{2,1,0:T(8,128)S(1)}, f32[10,16,128]{2,1,0:T(8,128)S(1)}, u32[]{:S(2)}, u32[]{:S(2)}) collective-permute-start(f32[10,16,128]{2,1,0:T(8,128)S(1)} %get-tuple-element.105), channel_id=1, source_target_pairs={{0,15},{1,2},{2,1},{3,4},{4,3},{5,6},{6,5},{7,8},{8,7},{9,10},{10,... | collective-permute-start | bytes 245768 | tf_op jit(solution)/shard_map/ppermute | solution.py:420
  9.5 8.2 %collective-permute-start.36 = (f32[1,4,4,16,128]{4,3,2,1,0:T(8,128)S(1)}, f32[1,4,4,16,128]{4,3,2,1,0:T(8,128)S(1)}, u32[]{:S(2)}, u32[]{:S(2)}) collective-permute-start(f32[1,4,4,16,128]{4,3,2,1,0:T(8,128)S(1)} %get-tuple-element.96), channel_id=1, source_target_pairs={{0,4},{1,5},{2,6},{3,7},{4,0},{5,1},{6,2},{7,3},{8,12},{9,13},{10,... | collective-permute-start | bytes 393224 | tf_op jit(solution)/shard_map/ppermute | solution.py:172
  9.6 9.2 %collective-permute-start.35 = (f32[1,4,4,16,128]{4,3,2,1,0:T(8,128)S(1)}, f32[1,4,4,16,128]{4,3,2,1,0:T(8,128)S(1)}, u32[]{:S(2)}, u32[]{:S(2)}) collective-permute-start(f32[1,4,4,16,128]{4,3,2,1,0:T(8,128)S(1)} %get-tuple-element.97), channel_id=1, source_target_pairs={{0,12},{1,13},{2,14},{3,15},{4,8},{5,9},{6,10},{7,11},{8,4},{9,5},... | collective-permute-start | bytes 393224 | tf_op jit(solution)/shard_map/ppermute | solution.py:172
  10.5 13.0 %collective-permute-start.34 = (f32[1,4,4,16,128]{4,3,2,1,0:T(8,128)S(1)}, f32[1,4,4,16,128]{4,3,2,1,0:T(8,128)S(1)}, u32[]{:S(2)}, u32[]{:S(2)}) collective-permute-start(f32[1,4,4,16,128]{4,3,2,1,0:T(8,128)S(1)} %get-tuple-element.98), channel_id=1, source_target_pairs={{0,8},{1,9},{2,10},{3,11},{4,12},{5,13},{6,14},{7,15},{8,0},{9,1},... | collective-permute-start | bytes 393224 | tf_op jit(solution)/shard_map/ppermute | solution.py:172
  23.6 10.2 %collective-permute-start.37 = (f32[11,16,128]{2,1,0:T(8,128)S(1)}, f32[11,16,128]{2,1,0:T(8,128)S(1)}, u32[]{:S(2)}, u32[]{:S(2)}) collective-permute-start(f32[11,16,128]{2,1,0:T(8,128)S(1)} %get-tuple-element.101), channel_id=1, source_target_pairs={{0,16},{16,0},{1,17},{17,1},{2,18},{18,2},{3,19},{19,3},{4,20},{20... | collective-permute-start | bytes 270344 | tf_op jit(solution)/shard_map/ppermute | solution.py:449
  25.8 7.9 %collective-permute-start.19 = (f32[11,16,128]{2,1,0:T(8,128)S(1)}, f32[11,16,128]{2,1,0:T(8,128)}, u32[]{:S(2)}, u32[]{:S(2)}) collective-permute-start(f32[11,16,128]{2,1,0:T(8,128)S(1)} %param.9), channel_id=1, source_target_pairs={{16,10},{17,11},{18,12},{19,13},{20,14},{21,15},{22,0},{23,1},{24,... | collective-permute-start | bytes 270344 | tf_op jit(solution)/shard_map/cond/branch_9_fun/ppermute | solution.py:437
  25.9 7.9 %collective-permute-start.18 = (f32[11,16,128]{2,1,0:T(8,128)S(1)}, f32[11,16,128]{2,1,0:T(8,128)}, u32[]{:S(2)}, u32[]{:S(2)}) collective-permute-start(f32[11,16,128]{2,1,0:T(8,128)S(1)} %param.9), channel_id=1, source_target_pairs={{16,9},{17,10},{18,11},{19,12},{20,13},{21,14},{22,15},{23,0},{24,... | collective-permute-start | bytes 270344 | tf_op jit(solution)/shard_map/cond/branch_9_fun/ppermute | solution.py:437
  33.8 6.5 %collective-permute-start.40 = (f32[4,1,4,16,128]{4,3,2,0,1:T(8,128)S(1)}, f32[4,1,4,16,128]{4,3,2,0,1:T(8,128)S(1)}, u32[]{:S(2)}, u32[]{:S(2)}) collective-permute-start(f32[4,1,4,16,128]{4,3,2,0,1:T(8,128)S(1)} %get-tuple-element.93), channel_id=1, source_target_pairs={{0,3},{1,2},{2,1},{3,0},{4,7},{5,6},{6,5},{7,4},{8,11},{9,10},{10,... | collective-permute-start | bytes 393224 | tf_op jit(solution)/shard_map/ppermute | solution.py:172
  33.9 9.1 %collective-permute-start.39 = (f32[4,1,4,16,128]{4,3,2,0,1:T(8,128)S(1)}, f32[4,1,4,16,128]{4,3,2,0,1:T(8,128)S(1)}, u32[]{:S(2)}, u32[]{:S(2)}) collective-permute-start(f32[4,1,4,16,128]{4,3,2,0,1:T(8,128)S(1)} %get-tuple-element.94), channel_id=1, source_target_pairs={{0,2},{1,3},{2,0},{3,1},{4,6},{5,7},{6,4},{7,5},{8,10},{9,11},{10,... | collective-permute-start | bytes 393224 | tf_op jit(solution)/shard_map/ppermute | solution.py:172
  37.8 5.3 %collective-permute-start.38 = (f32[4,1,4,16,128]{4,3,2,0,1:T(8,128)S(1)}, f32[4,1,4,16,128]{4,3,2,0,1:T(8,128)S(1)}, u32[]{:S(2)}, u32[]{:S(2)}) collective-permute-start(f32[4,1,4,16,128]{4,3,2,0,1:T(8,128)S(1)} %get-tuple-element.95), channel_id=1, source_target_pairs={{0,1},{1,0},{2,3},{3,2},{4,5},{5,4},{6,7},{7,6},{8,9},{9,8},{10,11... | collective-permute-start | bytes 393224 | tf_op jit(solution)/shard_map/ppermute | solution.py:172
  43.1 9.1 %collective-permute-start.43 = (f32[1,4,4,16,128]{4,3,2,1,0:T(8,128)S(1)}, f32[1,4,4,16,128]{4,3,2,1,0:T(8,128)S(1)}, u32[]{:S(2)}, u32[]{:S(2)}) collective-permute-start(f32[1,4,4,16,128]{4,3,2,1,0:T(8,128)S(1)} %get-tuple-element.89), channel_id=1, source_target_pairs={{0,12},{1,13},{2,14},{3,15},{4,8},{5,9},{6,10},{7,11},{8,4},{9,5},... | collective-permute-start | bytes 393224 | tf_op jit(solution)/shard_map/ppermute | solution.py:172
  46.7 0.9 copy-start.3
  46.7 16.4 %collective-permute-start.42 = (f32[1,4,4,16,128]{4,3,2,1,0:T(8,128)S(1)}, f32[1,4,4,16,128]{4,3,2,1,0:T(8,128)S(1)}, u32[]{:S(2)}, u32[]{:S(2)}) collective-permute-start(f32[1,4,4,16,128]{4,3,2,1,0:T(8,128)S(1)} %get-tuple-element.90), channel_id=1, source_target_pairs={{0,8},{1,9},{2,10},{3,11},{4,12},{5,13},{6,14},{7,15},{8,0},{9,1},... | collective-permute-start | bytes 393224 | tf_op jit(solution)/shard_map/ppermute | solution.py:172
  46.7 16.4 %collective-permute-start.41 = (f32[1,4,4,16,128]{4,3,2,1,0:T(8,128)S(1)}, f32[1,4,4,16,128]{4,3,2,1,0:T(8,128)S(1)}, u32[]{:S(2)}, u32[]{:S(2)}) collective-permute-start(f32[1,4,4,16,128]{4,3,2,1,0:T(8,128)S(1)} %get-tuple-element.91), channel_id=1, source_target_pairs={{0,4},{1,5},{2,6},{3,7},{4,0},{5,1},{6,2},{7,3},{8,12},{9,13},{10,... | collective-permute-start | bytes 393224 | tf_op jit(solution)/shard_map/ppermute | solution.py:172
  48.6 16.0 %collective-permute-start.55 = (f32[1,4,4,16,128]{4,3,2,1,0:T(8,128)S(1)}, f32[1,4,4,16,128]{4,3,2,1,0:T(8,128)S(1)}, u32[]{:S(2)}, u32[]{:S(2)}) collective-permute-start(f32[1,4,4,16,128]{4,3,2,1,0:T(8,128)S(1)} %get-tuple-element.73), channel_id=1, source_target_pairs={{0,12},{1,13},{2,14},{3,15},{4,8},{5,9},{6,10},{7,11},{8,4},{9,5},... | collective-permute-start | bytes 393224 | tf_op jit(solution)/shard_map/ppermute | solution.py:172
  52.2 15.8 %collective-permute-start.54 = (f32[1,4,4,16,128]{4,3,2,1,0:T(8,128)S(1)}, f32[1,4,4,16,128]{4,3,2,1,0:T(8,128)S(1)}, u32[]{:S(2)}, u32[]{:S(2)}) collective-permute-start(f32[1,4,4,16,128]{4,3,2,1,0:T(8,128)S(1)} %get-tuple-element.74), channel_id=1, source_target_pairs={{0,8},{1,9},{2,10},{3,11},{4,12},{5,13},{6,14},{7,15},{8,0},{9,1},... | collective-permute-start | bytes 393224 | tf_op jit(solution)/shard_map/ppermute | solution.py:172
  52.2 15.8 %collective-permute-start.53 = (f32[1,4,4,16,128]{4,3,2,1,0:T(8,128)S(1)}, f32[1,4,4,16,128]{4,3,2,1,0:T(8,128)S(1)}, u32[]{:S(2)}, u32[]{:S(2)}) collective-permute-start(f32[1,4,4,16,128]{4,3,2,1,0:T(8,128)S(1)} %get-tuple-element.75), channel_id=1, source_target_pairs={{0,4},{1,5},{2,6},{3,7},{4,0},{5,1},{6,2},{7,3},{8,12},{9,13},{10,... | collective-permute-start | bytes 393224 | tf_op jit(solution)/shard_map/ppermute | solution.py:172
  63.2 5.9 %collective-permute-start.46 = (f32[4,1,4,16,128]{4,3,2,0,1:T(8,128)S(1)}, f32[4,1,4,16,128]{4,3,2,0,1:T(8,128)S(1)}, u32[]{:S(2)}, u32[]{:S(2)}) collective-permute-start(f32[4,1,4,16,128]{4,3,2,0,1:T(8,128)S(1)} %get-tuple-element.85), channel_id=1, source_target_pairs={{0,3},{1,2},{2,1},{3,0},{4,7},{5,6},{6,5},{7,4},{8,11},{9,10},{10,... | collective-permute-start | bytes 393224 | tf_op jit(solution)/shard_map/ppermute | solution.py:172
  63.3 8.4 %collective-permute-start.45 = (f32[4,1,4,16,128]{4,3,2,0,1:T(8,128)S(1)}, f32[4,1,4,16,128]{4,3,2,0,1:T(8,128)S(1)}, u32[]{:S(2)}, u32[]{:S(2)}) collective-permute-start(f32[4,1,4,16,128]{4,3,2,0,1:T(8,128)S(1)} %get-tuple-element.86), channel_id=1, source_target_pairs={{0,2},{1,3},{2,0},{3,1},{4,6},{5,7},{6,4},{7,5},{8,10},{9,11},{10,... | collective-permute-start | bytes 393224 | tf_op jit(solution)/shard_map/ppermute | solution.py:172
  64.7 7.0 %collective-permute-start.44 = (f32[4,1,4,16,128]{4,3,2,0,1:T(8,128)S(1)}, f32[4,1,4,16,128]{4,3,2,0,1:T(8,128)S(1)}, u32[]{:S(2)}, u32[]{:S(2)}) collective-permute-start(f32[4,1,4,16,128]{4,3,2,0,1:T(8,128)S(1)} %get-tuple-element.87), channel_id=1, source_target_pairs={{0,1},{1,0},{2,3},{3,2},{4,5},{5,4},{6,7},{7,6},{8,9},{9,8},{10,11... | collective-permute-start | bytes 393224 | tf_op jit(solution)/shard_map/ppermute | solution.py:172
  72.7 8.3 %collective-permute-start.49 = (f32[1,4,4,16,128]{4,3,2,1,0:T(8,128)S(1)}, f32[1,4,4,16,128]{4,3,2,1,0:T(8,128)S(1)}, u32[]{:S(2)}, u32[]{:S(2)}) collective-permute-start(f32[1,4,4,16,128]{4,3,2,1,0:T(8,128)S(1)} %get-tuple-element.81), channel_id=1, source_target_pairs={{0,12},{1,13},{2,14},{3,15},{4,8},{5,9},{6,10},{7,11},{8,4},{9,5},... | collective-permute-start | bytes 393224 | tf_op jit(solution)/shard_map/ppermute | solution.py:172
  75.3 10.4 %collective-permute-start.48 = (f32[1,4,4,16,128]{4,3,2,1,0:T(8,128)S(1)}, f32[1,4,4,16,128]{4,3,2,1,0:T(8,128)S(1)}, u32[]{:S(2)}, u32[]{:S(2)}) collective-permute-start(f32[1,4,4,16,128]{4,3,2,1,0:T(8,128)S(1)} %get-tuple-element.82), channel_id=1, source_target_pairs={{0,8},{1,9},{2,10},{3,11},{4,12},{5,13},{6,14},{7,15},{8,0},{9,1},... | collective-permute-start | bytes 393224 | tf_op jit(solution)/shard_map/ppermute | solution.py:172
  75.3 10.4 %collective-permute-start.47 = (f32[1,4,4,16,128]{4,3,2,1,0:T(8,128)S(1)}, f32[1,4,4,16,128]{4,3,2,1,0:T(8,128)S(1)}, u32[]{:S(2)}, u32[]{:S(2)}) collective-permute-start(f32[1,4,4,16,128]{4,3,2,1,0:T(8,128)S(1)} %get-tuple-element.83), channel_id=1, source_target_pairs={{0,4},{1,5},{2,6},{3,7},{4,0},{5,1},{6,2},{7,3},{8,12},{9,13},{10,... | collective-permute-start | bytes 393224 | tf_op jit(solution)/shard_map/ppermute | solution.py:172
  77.2 10.3 %collective-permute-start.58 = (f32[4,1,4,16,128]{4,3,2,0,1:T(8,128)S(1)}, f32[4,1,4,16,128]{4,3,2,0,1:T(8,128)S(1)}, u32[]{:S(2)}, u32[]{:S(2)}) collective-permute-start(f32[4,1,4,16,128]{4,3,2,0,1:T(8,128)S(1)} %get-tuple-element.69), channel_id=1, source_target_pairs={{0,3},{1,2},{2,1},{3,0},{4,7},{5,6},{6,5},{7,4},{8,11},{9,10},{10,... | collective-permute-start | bytes 393224 | tf_op jit(solution)/shard_map/ppermute | solution.py:172
  77.3 10.5 %collective-permute-start.57 = (f32[4,1,4,16,128]{4,3,2,0,1:T(8,128)S(1)}, f32[4,1,4,16,128]{4,3,2,0,1:T(8,128)S(1)}, u32[]{:S(2)}, u32[]{:S(2)}) collective-permute-start(f32[4,1,4,16,128]{4,3,2,0,1:T(8,128)S(1)} %get-tuple-element.70), channel_id=1, source_target_pairs={{0,2},{1,3},{2,0},{3,1},{4,6},{5,7},{6,4},{7,5},{8,10},{9,11},{10,... | collective-permute-start | bytes 393224 | tf_op jit(solution)/shard_map/ppermute | solution.py:172
  81.1 6.7 %collective-permute-start.56 = (f32[4,1,4,16,128]{4,3,2,0,1:T(8,128)S(1)}, f32[4,1,4,16,128]{4,3,2,0,1:T(8,128)S(1)}, u32[]{:S(2)}, u32[]{:S(2)}) collective-permute-start(f32[4,1,4,16,128]{4,3,2,0,1:T(8,128)S(1)} %get-tuple-element.71), channel_id=1, source_target_pairs={{0,1},{1,0},{2,3},{3,2},{4,5},{5,4},{6,7},{7,6},{8,9},{9,8},{10,11... | collective-permute-start | bytes 393224 | tf_op jit(solution)/shard_map/ppermute | solution.py:172
  85.8 5.7 %collective-permute-start.52 = (f32[4,1,4,16,128]{4,3,2,0,1:T(8,128)S(1)}, f32[4,1,4,16,128]{4,3,2,0,1:T(8,128)S(1)}, u32[]{:S(2)}, u32[]{:S(2)}) collective-permute-start(f32[4,1,4,16,128]{4,3,2,0,1:T(8,128)S(1)} %get-tuple-element.77), channel_id=1, source_target_pairs={{0,3},{1,2},{2,1},{3,0},{4,7},{5,6},{6,5},{7,4},{8,11},{9,10},{10,... | collective-permute-start | bytes 393224 | tf_op jit(solution)/shard_map/ppermute | solution.py:172
  86.1 8.4 %collective-permute-start.51 = (f32[4,1,4,16,128]{4,3,2,0,1:T(8,128)S(1)}, f32[4,1,4,16,128]{4,3,2,0,1:T(8,128)S(1)}, u32[]{:S(2)}, u32[]{:S(2)}) collective-permute-start(f32[4,1,4,16,128]{4,3,2,0,1:T(8,128)S(1)} %get-tuple-element.78), channel_id=1, source_target_pairs={{0,2},{1,3},{2,0},{3,1},{4,6},{5,7},{6,4},{7,5},{8,10},{9,11},{10,... | collective-permute-start | bytes 393224 | tf_op jit(solution)/shard_map/ppermute | solution.py:172
  87.6 7.0 %collective-permute-start.50 = (f32[4,1,4,16,128]{4,3,2,0,1:T(8,128)S(1)}, f32[4,1,4,16,128]{4,3,2,0,1:T(8,128)S(1)}, u32[]{:S(2)}, u32[]{:S(2)}) collective-permute-start(f32[4,1,4,16,128]{4,3,2,0,1:T(8,128)S(1)} %get-tuple-element.79), channel_id=1, source_target_pairs={{0,1},{1,0},{2,3},{3,2},{4,5},{5,4},{6,7},{7,6},{8,9},{9,8},{10,11... | collective-permute-start | bytes 393224 | tf_op jit(solution)/shard_map/ppermute | solution.py:172
  (1 other events, 0.9 us)

commit v12 on v5

--- a/solution.py
+++ b/solution.py
@@ -290,7 +290,7 @@
         heat[ghost] = gap * anisotropy
         return carry
 
-    lax.fori_loop(0, columns + 2, tensor_column, 0)
+    lax.fori_loop(0, columns + 2, tensor_column, 0, unroll=3)
 
     def update_column(column, carry):
         ghost = column + 1
@@ -312,7 +312,7 @@
                 out[slot, flat % share] = fields[6, column] + heat[ghost]
         return carry
 
-    lax.fori_loop(0, columns, update_column, 0)
+    lax.fori_loop(0, columns, update_column, 0, unroll=4)
 
 
 def updated_columns(info, fields, density, *layers):

time: 86.9 us -> 90.2 us (1.038)
  waiting for transfers between devices: 37.5 us -> 46.7 us
  starting transfers between devices: 36.7 us -> 32.3 us
  Pallas kernels: 7.45 us -> 5.67 us
    ppermute x2, waiting for transfers between devices: 7.08 us -> 15.2 us  [wrap(): return lax.ppermute(data, ('rad', 'az'), pairs)]
    ppermute x24, starting transfers between devices: 26.4 us -> 21.6 us  [swap(): parts.append(lax.ppermute(cut[:, step], 'az', pairs))]
    pallas_call x1, Pallas kernels: 4.27 us -> 2.48 us  [updated_columns(): pl.pallas_call(stress_kernel, out_shape=jax.ShapeDtypeStruct((slots, 4 *...]
    ppermute x24, waiting for transfers between devices: 29.1 us -> 30.2 us  [swap(): parts.append(lax.ppermute(cut[:, step], 'az', pairs))]
  transfers between devices with their start and end apart: 29 -> 29, of which waited for: 13 -> 12; matrix products, arithmetic and copies ran while one was open for 1% -> 1% of each run, Pallas kernels for 7% -> 5%
where the time goes in v12:
time: 90.2 us; the launch traced here: 89.7 us
  waiting for transfers between devices  46.7 us (52%)
  starting transfers between devices  32.3 us (36%)
  Pallas kernels  5.67 us (6%)
  local copies, waits for them, and re-layouts  3.07 us (3%)
  between operations  1.59 us (2%)
    ppermute x24, waiting for transfers between devices, swap(): parts.append(lax.ppermute(cut[:, step], 'az', pairs))  30.2 us
    ppermute x24, starting transfers between devices, swap(): parts.append(lax.ppermute(cut[:, step], 'az', pairs))  21.6 us
    ppermute x2, waiting for transfers between devices, wrap(): return lax.ppermute(data, ('rad', 'az'), pairs)  15.2 us
    ppermute x1, starting transfers between devices, azimuthal_layers(): far = lax.ppermute(jnp.where(even, head, tail), 'az', outer)  5.67 us
    ppermute x2, starting transfers between devices, wrap(): return lax.ppermute(data, ('rad', 'az'), pairs)  2.93 us
    unnamed x12, local copies, waits for them, and re-layouts  2.75 us
    pallas_call x1, Pallas kernels, updated_columns(): pl.pallas_call(stress_kernel, out_shape=jax.ShapeDtypeStruct((slots, 4 *...  2.48 us
    pallas_call x2, Pallas kernels, move_columns(): pl.pallas_call(functools.partial(move_kernel, quantities), out_shape=jax....  1.99 us
  transfers between devices with their start and end apart: 29, of which 12 were waited for; matrix products, arithmetic and copies ran while one was open for 1% of the time, Pallas kernels for 5%

profile of v12, /device:TPU:0, one launch (start us, length us, event | category | flops | bytes accessed | tf_op | source)
XLA Modules:
  0.0 89.7 jit_solution(8033120656107808258)
XLA Ops:
  0.7 1.2 %copy-done = f32[7,16,16,128]{3,2,1,0:T(8,128)S(1)} copy-done((f32[7,16,16,128]{3,2,1,0:T(8,128)S(1)}, f32[7,16,16,128]{3,2,1,0:T(8,128)}, u32[]{:S(2)}) %copy-start) | copy-done | bytes 917528
  1.8 0.9 %copy-done.2 = f32[16,16,128]{2,1,0:T(8,128)S(1)} copy-done((f32[16,16,128]{2,1,0:T(8,128)S(1)}, f32[16,16,128]{2,1,0:T(8,128)}, u32[]{:S(2)}) %copy-start.2) | copy-done | bytes 131096
  3.4 5.7 %collective-permute-start.32 = (f32[10,16,128]{2,1,0:T(8,128)S(1)}, f32[10,16,128]{2,1,0:T(8,128)S(1)}, u32[]{:S(2)}, u32[]{:S(2)}) collective-permute-start(f32[10,16,128]{2,1,0:T(8,128)S(1)} %get-tuple-element.75), channel_id=1, source_target_pairs={{0,15},{1,2},{2,1},{3,4},{4,3},{5,6},{6,5},{7,8},{8,7},{9,10},{10,... | collective-permute-start | bytes 245768 | tf_op jit(solution)/shard_map/ppermute | solution.py:400
  9.9 1.3 %collective-permute-done.32 = f32[10,16,128]{2,1,0:T(8,128)S(1)} collective-permute-done((f32[10,16,128]{2,1,0:T(8,128)S(1)}, f32[10,16,128]{2,1,0:T(8,128)S(1)}, u32[]{:S(2)}, u32[]{:S(2)}) %collective-permute-start.32) | collective-permute-done | bytes 81952 | tf_op jit(solution)/shard_map/ppermute | solution.py:400
  11.3 1.6 %collective-permute-start.34 = (f32[11,16,128]{2,1,0:T(8,128)S(1)}, f32[11,16,128]{2,1,0:T(8,128)S(1)}, u32[]{:S(2)}, u32[]{:S(2)}) collective-permute-start(f32[11,16,128]{2,1,0:T(8,128)S(1)} %get-tuple-element.71), channel_id=1, source_target_pairs={{0,16},{16,0},{1,17},{17,1},{2,18},{18,2},{3,19},{19,3},{4,20},{20... | collective-permute-start | bytes 270344 | tf_op jit(solution)/shard_map/ppermute | solution.py:429
  12.9 1.8 %collective-permute-start.49 = (f32[1,4,4,16,128]{4,3,2,1,0:T(8,128)S(1)}, f32[1,4,4,16,128]{4,3,2,1,0:T(8,128)S(1)}, u32[]{:S(2)}, u32[]{:S(2)}) collective-permute-start(f32[1,4,4,16,128]{4,3,2,1,0:T(8,128)S(1)} %get-tuple-element.51), channel_id=1, source_target_pairs={{0,12},{1,13},{2,14},{3,15},{4,8},{5,9},{6,10},{7,11},{8,4},{9,5},... | collective-permute-start | bytes 393224 | tf_op jit(solution)/shard_map/ppermute | solution.py:161
  14.8 18.1 %conditional.1 = (f32[11,16,128]{2,1,0:T(8,128)}, f32[11,16,128]{2,1,0:T(8,128)}) conditional(s32[]{:T(128)} %clamp.3, f32[11,16,128]{2,1,0:T(8,128)S(1)} %get-tuple-element.70, f32[11,16,128]{2,1,0:T(8,128)S(1)} %get-tuple-element.70, f32[11,16,128]{2,1,0:T(8,128)S(1)} %get-tuple-element.70, ...), branch_computations={%region_0.1_spmd, %region_1.2_spmd, %region_2.3_spmd, %region_3.4_... | conditional | bytes 720992 | solution.py:437
  14.8 2.9 %collective-permute-start.15 = (f32[11,16,128]{2,1,0:T(8,128)S(1)}, f32[11,16,128]{2,1,0:T(8,128)}, u32[]{:S(2)}, u32[]{:S(2)}) collective-permute-start(f32[11,16,128]{2,1,0:T(8,128)S(1)} %param.7), channel_id=1, source_target_pairs={{16,8},{17,9},{18,10},{19,11},{20,12},{21,13},{22,14},{23,15},{24,... | collective-permute-start | bytes 270344 | tf_op jit(solution)/shard_map/cond/branch_7_fun/ppermute | solution.py:417
  17.7 15.1 %collective-permute-done.15 = f32[11,16,128]{2,1,0:T(8,128)} collective-permute-done((f32[11,16,128]{2,1,0:T(8,128)S(1)}, f32[11,16,128]{2,1,0:T(8,128)}, u32[]{:S(2)}, u32[]{:S(2)}) %collective-permute-start.15) | collective-permute-done | bytes 90144 | tf_op jit(solution)/shard_map/cond/branch_7_fun/ppermute | solution.py:417
  33.4 2.5 %stress_update.1 = f32[16,4,16,128]{3,2,1,0:T(8,128)S(1)} custom-call(s32[4]{0:T(128)S(1)} %pad_add_fusion.info, f32[7,16,16,128]{3,2,1,0:T(8,128)S(1)} %copy-done.1, f32[16,16,128]{2,1,0:T(8,128)S(1)} %copy-done.3, f32[10,16,128]{2,1,0:T(8,128)S(1)} %get-tuple-element.28.head, f32[10,16,128]{2,1,0:T(8,128)S(1)} %get-tuple-element.29.tail, ...), custom_call_target="tpu_custom_call" | custom-call | tf_op jit(solution)/shard_map/stress_update/pallas_call | solution.py:325
  36.0 1.4 %collective-permute-start.37 = (f32[1,4,4,16,128]{4,3,2,1,0:T(8,128)S(1)}, f32[1,4,4,16,128]{4,3,2,1,0:T(8,128)S(1)}, u32[]{:S(2)}, u32[]{:S(2)}) collective-permute-start(f32[1,4,4,16,128]{4,3,2,1,0:T(8,128)S(1)} %get-tuple-element.67), channel_id=1, source_target_pairs={{0,12},{1,13},{2,14},{3,15},{4,8},{5,9},{6,10},{7,11},{8,4},{9,5},... | collective-permute-start | bytes 393224 | tf_op jit(solution)/shard_map/ppermute | solution.py:161
  37.4 1.6 %collective-permute-start.36 = (f32[1,4,4,16,128]{4,3,2,1,0:T(8,128)S(1)}, f32[1,4,4,16,128]{4,3,2,1,0:T(8,128)S(1)}, u32[]{:S(2)}, u32[]{:S(2)}) collective-permute-start(f32[1,4,4,16,128]{4,3,2,1,0:T(8,128)S(1)} %get-tuple-element.68), channel_id=1, source_target_pairs={{0,8},{1,9},{2,10},{3,11},{4,12},{5,13},{6,14},{7,15},{8,0},{9,1},... | collective-permute-start | bytes 393224 | tf_op jit(solution)/shard_map/ppermute | solution.py:161
  39.0 1.4 %collective-permute-start.35 = (f32[1,4,4,16,128]{4,3,2,1,0:T(8,128)S(1)}, f32[1,4,4,16,128]{4,3,2,1,0:T(8,128)S(1)}, u32[]{:S(2)}, u32[]{:S(2)}) collective-permute-start(f32[1,4,4,16,128]{4,3,2,1,0:T(8,128)S(1)} %get-tuple-element.69), channel_id=1, source_target_pairs={{0,4},{1,5},{2,6},{3,7},{4,0},{5,1},{6,2},{7,3},{8,12},{9,13},{10,... | collective-permute-start | bytes 393224 | tf_op jit(solution)/shard_map/ppermute | solution.py:161
  40.6 2.0 %collective-permute-start.51 = (f32[4,1,4,16,128]{4,3,2,0,1:T(8,128)S(1)}, f32[4,1,4,16,128]{4,3,2,0,1:T(8,128)S(1)}, u32[]{:S(2)}, u32[]{:S(2)}) collective-permute-start(f32[4,1,4,16,128]{4,3,2,0,1:T(8,128)S(1)} %get-tuple-element.48), channel_id=1, source_target_pairs={{0,2},{1,3},{2,0},{3,1},{4,6},{5,7},{6,4},{7,5},{8,10},{9,11},{10,... | collective-permute-start | bytes 393224 | tf_op jit(solution)/shard_map/ppermute | solution.py:161
  42.5 1.8 %collective-permute-done.37 = f32[1,4,4,16,128]{4,3,2,1,0:T(8,128)S(1)} collective-permute-done((f32[1,4,4,16,128]{4,3,2,1,0:T(8,128)S(1)}, f32[1,4,4,16,128]{4,3,2,1,0:T(8,128)S(1)}, u32[]{:S(2)}, u32[]{:S(2)}) %collective-permute-start.37) | collective-permute-done | bytes 131104 | tf_op jit(solution)/shard_map/ppermute | solution.py:161
  44.3 7.2 %collective-permute-done.36 = f32[1,4,4,16,128]{4,3,2,1,0:T(8,128)S(1)} collective-permute-done((f32[1,4,4,16,128]{4,3,2,1,0:T(8,128)S(1)}, f32[1,4,4,16,128]{4,3,2,1,0:T(8,128)S(1)}, u32[]{:S(2)}, u32[]{:S(2)}) %collective-permute-start.36) | collective-permute-done | bytes 131104 | tf_op jit(solution)/shard_map/ppermute | solution.py:161
  51.6 1.7 %collective-permute-start.39 = (f32[4,1,4,16,128]{4,3,2,0,1:T(8,128)S(1)}, f32[4,1,4,16,128]{4,3,2,0,1:T(8,128)S(1)}, u32[]{:S(2)}, u32[]{:S(2)}) collective-permute-start(f32[4,1,4,16,128]{4,3,2,0,1:T(8,128)S(1)} %get-tuple-element.64), channel_id=1, source_target_pairs={{0,2},{1,3},{2,0},{3,1},{4,6},{5,7},{6,4},{7,5},{8,10},{9,11},{10,... | collective-permute-start | bytes 393224 | tf_op jit(solution)/shard_map/ppermute | solution.py:161
  54.2 1.0 %move.3 = f32[16,4,16,128]{3,2,1,0:T(8,128)S(1)} custom-call(s32[1]{0:T(128)} %bitcast.rank, s32[16]{0:T(128)S(1)} %copy-done.4, s32[16]{0:T(128)S(1)} %copy-done.5, f32[16,4,16,128]{3,2,1,0:T(8,128)S(1)} %bitcast.150), custom_call_target="tpu_custom_call" | custom-call | tf_op jit(solution)/shard_map/move/pallas_call | solution.py:384
  55.3 1.4 %collective-permute-start.55 = (f32[1,4,4,16,128]{4,3,2,1,0:T(8,128)S(1)}, f32[1,4,4,16,128]{4,3,2,1,0:T(8,128)S(1)}, u32[]{:S(2)}, u32[]{:S(2)}) collective-permute-start(f32[1,4,4,16,128]{4,3,2,1,0:T(8,128)S(1)} %get-tuple-element.43), channel_id=1, source_target_pairs={{0,12},{1,13},{2,14},{3,15},{4,8},{5,9},{6,10},{7,11},{8,4},{9,5},... | collective-permute-start | bytes 393224 | tf_op jit(solution)/shard_map/ppermute | solution.py:161
  57.1 2.6 %collective-permute-start.53 = (f32[1,4,4,16,128]{4,3,2,1,0:T(8,128)S(1)}, f32[1,4,4,16,128]{4,3,2,1,0:T(8,128)S(1)}, u32[]{:S(2)}, u32[]{:S(2)}) collective-permute-start(f32[1,4,4,16,128]{4,3,2,1,0:T(8,128)S(1)} %get-tuple-element.45), channel_id=1, source_target_pairs={{0,4},{1,5},{2,6},{3,7},{4,0},{5,1},{6,2},{7,3},{8,12},{9,13},{10,... | collective-permute-start | bytes 393224 | tf_op jit(solution)/shard_map/ppermute | solution.py:161
  60.3 1.0 %move.2 = f32[16,4,16,128]{3,2,1,0:T(8,128)S(1)} custom-call(s32[1]{0:T(128)} %bitcast.rank, s32[16]{0:T(128)S(1)} %copy-done.4, s32[16]{0:T(128)S(1)} %copy-done.5, f32[16,4,16,128]{3,2,1,0:T(8,128)S(1)} %bitcast.151), custom_call_target="tpu_custom_call" | custom-call | tf_op jit(solution)/shard_map/move/pallas_call | solution.py:384
  61.3 1.0 %collective-permute-start.43 = (f32[1,4,4,16,128]{4,3,2,1,0:T(8,128)S(1)}, f32[1,4,4,16,128]{4,3,2,1,0:T(8,128)S(1)}, u32[]{:S(2)}, u32[]{:S(2)}) collective-permute-start(f32[1,4,4,16,128]{4,3,2,1,0:T(8,128)S(1)} %get-tuple-element.59), channel_id=1, source_target_pairs={{0,12},{1,13},{2,14},{3,15},{4,8},{5,9},{6,10},{7,11},{8,4},{9,5},... | collective-permute-start | bytes 393224 | tf_op jit(solution)/shard_map/ppermute | solution.py:161
  62.4 1.2 %collective-permute-done.55 = f32[1,4,4,16,128]{4,3,2,1,0:T(8,128)S(1)} collective-permute-done((f32[1,4,4,16,128]{4,3,2,1,0:T(8,128)S(1)}, f32[1,4,4,16,128]{4,3,2,1,0:T(8,128)S(1)}, u32[]{:S(2)}, u32[]{:S(2)}) %collective-permute-start.55) | collective-permute-done | bytes 131104 | tf_op jit(solution)/shard_map/ppermute | solution.py:161
  63.6 2.2 %collective-permute-start.41 = (f32[1,4,4,16,128]{4,3,2,1,0:T(8,128)S(1)}, f32[1,4,4,16,128]{4,3,2,1,0:T(8,128)S(1)}, u32[]{:S(2)}, u32[]{:S(2)}) collective-permute-start(f32[1,4,4,16,128]{4,3,2,1,0:T(8,128)S(1)} %get-tuple-element.61), channel_id=1, source_target_pairs={{0,4},{1,5},{2,6},{3,7},{4,0},{5,1},{6,2},{7,3},{8,12},{9,13},{10,... | collective-permute-start | bytes 393224 | tf_op jit(solution)/shard_map/ppermute | solution.py:161
  65.8 3.5 %collective-permute-done.54 = f32[1,4,4,16,128]{4,3,2,1,0:T(8,128)S(1)} collective-permute-done((f32[1,4,4,16,128]{4,3,2,1,0:T(8,128)S(1)}, f32[1,4,4,16,128]{4,3,2,1,0:T(8,128)S(1)}, u32[]{:S(2)}, u32[]{:S(2)}) %collective-permute-start.54) | collective-permute-done | bytes 131104 | tf_op jit(solution)/shard_map/ppermute | solution.py:161
  69.4 1.5 %collective-permute-start.57 = (f32[4,1,4,16,128]{4,3,2,0,1:T(8,128)S(1)}, f32[4,1,4,16,128]{4,3,2,0,1:T(8,128)S(1)}, u32[]{:S(2)}, u32[]{:S(2)}) collective-permute-start(f32[4,1,4,16,128]{4,3,2,0,1:T(8,128)S(1)} %get-tuple-element.40), channel_id=1, source_target_pairs={{0,2},{1,3},{2,0},{3,1},{4,6},{5,7},{6,4},{7,5},{8,10},{9,11},{10,... | collective-permute-start | bytes 393224 | tf_op jit(solution)/shard_map/ppermute | solution.py:161
  70.9 1.2 %collective-permute-done.43 = f32[1,4,4,16,128]{4,3,2,1,0:T(8,128)S(1)} collective-permute-done((f32[1,4,4,16,128]{4,3,2,1,0:T(8,128)S(1)}, f32[1,4,4,16,128]{4,3,2,1,0:T(8,128)S(1)}, u32[]{:S(2)}, u32[]{:S(2)}) %collective-permute-start.43) | collective-permute-done | bytes 131104 | tf_op jit(solution)/shard_map/ppermute | solution.py:161
  72.1 7.8 %collective-permute-done.42 = f32[1,4,4,16,128]{4,3,2,1,0:T(8,128)S(1)} collective-permute-done((f32[1,4,4,16,128]{4,3,2,1,0:T(8,128)S(1)}, f32[1,4,4,16,128]{4,3,2,1,0:T(8,128)S(1)}, u32[]{:S(2)}, u32[]{:S(2)}) %collective-permute-start.42) | collective-permute-done | bytes 131104 | tf_op jit(solution)/shard_map/ppermute | solution.py:161
  80.0 1.7 %collective-permute-start.45 = (f32[4,1,4,16,128]{4,3,2,0,1:T(8,128)S(1)}, f32[4,1,4,16,128]{4,3,2,0,1:T(8,128)S(1)}, u32[]{:S(2)}, u32[]{:S(2)}) collective-permute-start(f32[4,1,4,16,128]{4,3,2,0,1:T(8,128)S(1)} %get-tuple-element.56), channel_id=1, source_target_pairs={{0,2},{1,3},{2,0},{3,1},{4,6},{5,7},{6,4},{7,5},{8,10},{9,11},{10,... | collective-permute-start | bytes 393224 | tf_op jit(solution)/shard_map/ppermute | solution.py:161
  81.9 3.7 %collective-permute-done.46 = f32[4,1,4,16,128]{4,3,2,0,1:T(8,128)S(1)} collective-permute-done((f32[4,1,4,16,128]{4,3,2,0,1:T(8,128)S(1)}, f32[4,1,4,16,128]{4,3,2,0,1:T(8,128)S(1)}, u32[]{:S(2)}, u32[]{:S(2)}) %collective-permute-start.46) | collective-permute-done | bytes 131104 | tf_op jit(solution)/shard_map/ppermute | solution.py:161
  85.6 3.0 %collective-permute-done.45 = f32[4,1,4,16,128]{4,3,2,0,1:T(8,128)S(1)} collective-permute-done((f32[4,1,4,16,128]{4,3,2,0,1:T(8,128)S(1)}, f32[4,1,4,16,128]{4,3,2,0,1:T(8,128)S(1)}, u32[]{:S(2)}, u32[]{:S(2)}) %collective-permute-start.45) | collective-permute-done | bytes 131104 | tf_op jit(solution)/shard_map/ppermute | solution.py:161
  88.7 1.0 %join.1 = (f32[7,16,16,128]{3,2,1,0:T(8,128)}, f32[16,16,128]{2,1,0:T(8,128)}) custom-call(s32[1]{0:T(128)} %bitcast.rank, f32[16,4,16,128]{3,2,1,0:T(8,128)S(1)} %bitcast.147, f32[16,4,16,128]{3,2,1,0:T(8,128)S(1)} %bitcast.146), custom_call_target="tpu_custom_call" | custom-call | tf_op jit(solution)/shard_map/join/pallas_call | solution.py:138
  (69 shorter events, 4.3 us)
Async XLA Ops:
  0.6 1.2 %copy-start = (f32[7,16,16,128]{3,2,1,0:T(8,128)S(1)}, f32[7,16,16,128]{3,2,1,0:T(8,128)}, u32[]{:S(2)}) copy-start(f32[7,16,16,128]{3,2,1,0:T(8,128)} %fields.3) | copy-start | bytes 2752516
  2.9 7.0 %collective-permute-start.33 = (f32[10,16,128]{2,1,0:T(8,128)S(1)}, f32[10,16,128]{2,1,0:T(8,128)S(1)}, u32[]{:S(2)}, u32[]{:S(2)}) collective-permute-start(f32[10,16,128]{2,1,0:T(8,128)S(1)} %get-tuple-element.74), channel_id=1, source_target_pairs={{0,1},{1,0},{2,3},{3,2},{4,5},{5,4},{6,7},{7,6},{8,9},{9,8},{10,11... | collective-permute-start | bytes 245768 | tf_op jit(solution)/shard_map/ppermute | solution.py:401
  3.4 7.8 %collective-permute-start.32 = (f32[10,16,128]{2,1,0:T(8,128)S(1)}, f32[10,16,128]{2,1,0:T(8,128)S(1)}, u32[]{:S(2)}, u32[]{:S(2)}) collective-permute-start(f32[10,16,128]{2,1,0:T(8,128)S(1)} %get-tuple-element.75), channel_id=1, source_target_pairs={{0,15},{1,2},{2,1},{3,4},{4,3},{5,6},{6,5},{7,8},{8,7},{9,10},{10,... | collective-permute-start | bytes 245768 | tf_op jit(solution)/shard_map/ppermute | solution.py:400
  9.8 23.6 %copy-start.1 = (f32[7,16,16,128]{3,2,1,0:T(8,128)S(1)}, f32[7,16,16,128]{3,2,1,0:T(8,128)}, u32[]{:S(2)}) copy-start(f32[7,16,16,128]{3,2,1,0:T(8,128)} %fields.3) | copy-start | bytes 2752516
  11.3 22.1 %collective-permute-start.34 = (f32[11,16,128]{2,1,0:T(8,128)S(1)}, f32[11,16,128]{2,1,0:T(8,128)S(1)}, u32[]{:S(2)}, u32[]{:S(2)}) collective-permute-start(f32[11,16,128]{2,1,0:T(8,128)S(1)} %get-tuple-element.71), channel_id=1, source_target_pairs={{0,16},{16,0},{1,17},{17,1},{2,18},{18,2},{3,19},{19,3},{4,20},{20... | collective-permute-start | bytes 270344 | tf_op jit(solution)/shard_map/ppermute | solution.py:429
  12.9 20.5 %copy-start.3 = (f32[16,16,128]{2,1,0:T(8,128)S(1)}, f32[16,16,128]{2,1,0:T(8,128)}, u32[]{:S(2)}) copy-start(f32[16,16,128]{2,1,0:T(8,128)} %density.3) | copy-start | bytes 393220
  12.9 26.0 %collective-permute-start.49 = (f32[1,4,4,16,128]{4,3,2,1,0:T(8,128)S(1)}, f32[1,4,4,16,128]{4,3,2,1,0:T(8,128)S(1)}, u32[]{:S(2)}, u32[]{:S(2)}) collective-permute-start(f32[1,4,4,16,128]{4,3,2,1,0:T(8,128)S(1)} %get-tuple-element.51), channel_id=1, source_target_pairs={{0,12},{1,13},{2,14},{3,15},{4,8},{5,9},{6,10},{7,11},{8,4},{9,5},... | collective-permute-start | bytes 393224 | tf_op jit(solution)/shard_map/ppermute | solution.py:161
  14.8 25.7 %collective-permute-start.48 = (f32[1,4,4,16,128]{4,3,2,1,0:T(8,128)S(1)}, f32[1,4,4,16,128]{4,3,2,1,0:T(8,128)S(1)}, u32[]{:S(2)}, u32[]{:S(2)}) collective-permute-start(f32[1,4,4,16,128]{4,3,2,1,0:T(8,128)S(1)} %get-tuple-element.52), channel_id=1, source_target_pairs={{0,8},{1,9},{2,10},{3,11},{4,12},{5,13},{6,14},{7,15},{8,0},{9,1},... | collective-permute-start | bytes 393224 | tf_op jit(solution)/shard_map/ppermute | solution.py:161
  14.8 18.1 %collective-permute-start.15 = (f32[11,16,128]{2,1,0:T(8,128)S(1)}, f32[11,16,128]{2,1,0:T(8,128)}, u32[]{:S(2)}, u32[]{:S(2)}) collective-permute-start(f32[11,16,128]{2,1,0:T(8,128)S(1)} %param.7), channel_id=1, source_target_pairs={{16,8},{17,9},{18,10},{19,11},{20,12},{21,13},{22,14},{23,15},{24,... | collective-permute-start | bytes 270344 | tf_op jit(solution)/shard_map/cond/branch_7_fun/ppermute | solution.py:417
  17.7 15.2 %collective-permute-start.14 = (f32[11,16,128]{2,1,0:T(8,128)S(1)}, f32[11,16,128]{2,1,0:T(8,128)}, u32[]{:S(2)}, u32[]{:S(2)}) collective-permute-start(f32[11,16,128]{2,1,0:T(8,128)S(1)} %param.7), channel_id=1, source_target_pairs={{16,7},{17,8},{18,9},{19,10},{20,11},{21,12},{22,13},{23,14},{24,1... | collective-permute-start | bytes 270344 | tf_op jit(solution)/shard_map/cond/branch_7_fun/ppermute | solution.py:417
  32.9 7.6 %collective-permute-start.47 = (f32[1,4,4,16,128]{4,3,2,1,0:T(8,128)S(1)}, f32[1,4,4,16,128]{4,3,2,1,0:T(8,128)S(1)}, u32[]{:S(2)}, u32[]{:S(2)}) collective-permute-start(f32[1,4,4,16,128]{4,3,2,1,0:T(8,128)S(1)} %get-tuple-element.53), channel_id=1, source_target_pairs={{0,4},{1,5},{2,6},{3,7},{4,0},{5,1},{6,2},{7,3},{8,12},{9,13},{10,... | collective-permute-start | bytes 393224 | tf_op jit(solution)/shard_map/ppermute | solution.py:161
  36.0 8.3 %collective-permute-start.37 = (f32[1,4,4,16,128]{4,3,2,1,0:T(8,128)S(1)}, f32[1,4,4,16,128]{4,3,2,1,0:T(8,128)S(1)}, u32[]{:S(2)}, u32[]{:S(2)}) collective-permute-start(f32[1,4,4,16,128]{4,3,2,1,0:T(8,128)S(1)} %get-tuple-element.67), channel_id=1, source_target_pairs={{0,12},{1,13},{2,14},{3,15},{4,8},{5,9},{6,10},{7,11},{8,4},{9,5},... | collective-permute-start | bytes 393224 | tf_op jit(solution)/shard_map/ppermute | solution.py:161
  37.4 14.1 %collective-permute-start.36 = (f32[1,4,4,16,128]{4,3,2,1,0:T(8,128)S(1)}, f32[1,4,4,16,128]{4,3,2,1,0:T(8,128)S(1)}, u32[]{:S(2)}, u32[]{:S(2)}) collective-permute-start(f32[1,4,4,16,128]{4,3,2,1,0:T(8,128)S(1)} %get-tuple-element.68), channel_id=1, source_target_pairs={{0,8},{1,9},{2,10},{3,11},{4,12},{5,13},{6,14},{7,15},{8,0},{9,1},... | collective-permute-start | bytes 393224 | tf_op jit(solution)/shard_map/ppermute | solution.py:161
  39.0 12.5 %collective-permute-start.35 = (f32[1,4,4,16,128]{4,3,2,1,0:T(8,128)S(1)}, f32[1,4,4,16,128]{4,3,2,1,0:T(8,128)S(1)}, u32[]{:S(2)}, u32[]{:S(2)}) collective-permute-start(f32[1,4,4,16,128]{4,3,2,1,0:T(8,128)S(1)} %get-tuple-element.69), channel_id=1, source_target_pairs={{0,4},{1,5},{2,6},{3,7},{4,0},{5,1},{6,2},{7,3},{8,12},{9,13},{10,... | collective-permute-start | bytes 393224 | tf_op jit(solution)/shard_map/ppermute | solution.py:161
  40.5 12.9 %collective-permute-start.52 = (f32[4,1,4,16,128]{4,3,2,0,1:T(8,128)S(1)}, f32[4,1,4,16,128]{4,3,2,0,1:T(8,128)S(1)}, u32[]{:S(2)}, u32[]{:S(2)}) collective-permute-start(f32[4,1,4,16,128]{4,3,2,0,1:T(8,128)S(1)} %get-tuple-element.47), channel_id=1, source_target_pairs={{0,3},{1,2},{2,1},{3,0},{4,7},{5,6},{6,5},{7,4},{8,11},{9,10},{10,... | collective-permute-start | bytes 393224 | tf_op jit(solution)/shard_map/ppermute | solution.py:161
  40.6 12.9 %collective-permute-start.51 = (f32[4,1,4,16,128]{4,3,2,0,1:T(8,128)S(1)}, f32[4,1,4,16,128]{4,3,2,0,1:T(8,128)S(1)}, u32[]{:S(2)}, u32[]{:S(2)}) collective-permute-start(f32[4,1,4,16,128]{4,3,2,0,1:T(8,128)S(1)} %get-tuple-element.48), channel_id=1, source_target_pairs={{0,2},{1,3},{2,0},{3,1},{4,6},{5,7},{6,4},{7,5},{8,10},{9,11},{10,... | collective-permute-start | bytes 393224 | tf_op jit(solution)/shard_map/ppermute | solution.py:161
  44.3 9.2 %collective-permute-start.50 = (f32[4,1,4,16,128]{4,3,2,0,1:T(8,128)S(1)}, f32[4,1,4,16,128]{4,3,2,0,1:T(8,128)S(1)}, u32[]{:S(2)}, u32[]{:S(2)}) collective-permute-start(f32[4,1,4,16,128]{4,3,2,0,1:T(8,128)S(1)} %get-tuple-element.49), channel_id=1, source_target_pairs={{0,1},{1,0},{2,3},{3,2},{4,5},{5,4},{6,7},{7,6},{8,9},{9,8},{10,11... | collective-permute-start | bytes 393224 | tf_op jit(solution)/shard_map/ppermute | solution.py:161
  51.6 5.6 %collective-permute-start.40 = (f32[4,1,4,16,128]{4,3,2,0,1:T(8,128)S(1)}, f32[4,1,4,16,128]{4,3,2,0,1:T(8,128)S(1)}, u32[]{:S(2)}, u32[]{:S(2)}) collective-permute-start(f32[4,1,4,16,128]{4,3,2,0,1:T(8,128)S(1)} %get-tuple-element.63), channel_id=1, source_target_pairs={{0,3},{1,2},{2,1},{3,0},{4,7},{5,6},{6,5},{7,4},{8,11},{9,10},{10,... | collective-permute-start | bytes 393224 | tf_op jit(solution)/shard_map/ppermute | solution.py:161
  51.6 8.6 %collective-permute-start.39 = (f32[4,1,4,16,128]{4,3,2,0,1:T(8,128)S(1)}, f32[4,1,4,16,128]{4,3,2,0,1:T(8,128)S(1)}, u32[]{:S(2)}, u32[]{:S(2)}) collective-permute-start(f32[4,1,4,16,128]{4,3,2,0,1:T(8,128)S(1)} %get-tuple-element.64), channel_id=1, source_target_pairs={{0,2},{1,3},{2,0},{3,1},{4,6},{5,7},{6,4},{7,5},{8,10},{9,11},{10,... | collective-permute-start | bytes 393224 | tf_op jit(solution)/shard_map/ppermute | solution.py:161
  53.4 6.9 %collective-permute-start.38 = (f32[4,1,4,16,128]{4,3,2,0,1:T(8,128)S(1)}, f32[4,1,4,16,128]{4,3,2,0,1:T(8,128)S(1)}, u32[]{:S(2)}, u32[]{:S(2)}) collective-permute-start(f32[4,1,4,16,128]{4,3,2,0,1:T(8,128)S(1)} %get-tuple-element.65), channel_id=1, source_target_pairs={{0,1},{1,0},{2,3},{3,2},{4,5},{5,4},{6,7},{7,6},{8,9},{9,8},{10,11... | collective-permute-start | bytes 393224 | tf_op jit(solution)/shard_map/ppermute | solution.py:161
  55.3 8.3 %collective-permute-start.55 = (f32[1,4,4,16,128]{4,3,2,1,0:T(8,128)S(1)}, f32[1,4,4,16,128]{4,3,2,1,0:T(8,128)S(1)}, u32[]{:S(2)}, u32[]{:S(2)}) collective-permute-start(f32[1,4,4,16,128]{4,3,2,1,0:T(8,128)S(1)} %get-tuple-element.43), channel_id=1, source_target_pairs={{0,12},{1,13},{2,14},{3,15},{4,8},{5,9},{6,10},{7,11},{8,4},{9,5},... | collective-permute-start | bytes 393224 | tf_op jit(solution)/shard_map/ppermute | solution.py:161
  56.7 12.6 %collective-permute-start.54 = (f32[1,4,4,16,128]{4,3,2,1,0:T(8,128)S(1)}, f32[1,4,4,16,128]{4,3,2,1,0:T(8,128)S(1)}, u32[]{:S(2)}, u32[]{:S(2)}) collective-permute-start(f32[1,4,4,16,128]{4,3,2,1,0:T(8,128)S(1)} %get-tuple-element.44), channel_id=1, source_target_pairs={{0,8},{1,9},{2,10},{3,11},{4,12},{5,13},{6,14},{7,15},{8,0},{9,1},... | collective-permute-start | bytes 393224 | tf_op jit(solution)/shard_map/ppermute | solution.py:161
  57.1 12.1 %collective-permute-start.53 = (f32[1,4,4,16,128]{4,3,2,1,0:T(8,128)S(1)}, f32[1,4,4,16,128]{4,3,2,1,0:T(8,128)S(1)}, u32[]{:S(2)}, u32[]{:S(2)}) collective-permute-start(f32[1,4,4,16,128]{4,3,2,1,0:T(8,128)S(1)} %get-tuple-element.45), channel_id=1, source_target_pairs={{0,4},{1,5},{2,6},{3,7},{4,0},{5,1},{6,2},{7,3},{8,12},{9,13},{10,... | collective-permute-start | bytes 393224 | tf_op jit(solution)/shard_map/ppermute | solution.py:161
  61.3 10.8 %collective-permute-start.43 = (f32[1,4,4,16,128]{4,3,2,1,0:T(8,128)S(1)}, f32[1,4,4,16,128]{4,3,2,1,0:T(8,128)S(1)}, u32[]{:S(2)}, u32[]{:S(2)}) collective-permute-start(f32[1,4,4,16,128]{4,3,2,1,0:T(8,128)S(1)} %get-tuple-element.59), channel_id=1, source_target_pairs={{0,12},{1,13},{2,14},{3,15},{4,8},{5,9},{6,10},{7,11},{8,4},{9,5},... | collective-permute-start | bytes 393224 | tf_op jit(solution)/shard_map/ppermute | solution.py:161
  62.3 17.5 %collective-permute-start.42 = (f32[1,4,4,16,128]{4,3,2,1,0:T(8,128)S(1)}, f32[1,4,4,16,128]{4,3,2,1,0:T(8,128)S(1)}, u32[]{:S(2)}, u32[]{:S(2)}) collective-permute-start(f32[1,4,4,16,128]{4,3,2,1,0:T(8,128)S(1)} %get-tuple-element.60), channel_id=1, source_target_pairs={{0,8},{1,9},{2,10},{3,11},{4,12},{5,13},{6,14},{7,15},{8,0},{9,1},... | collective-permute-start | bytes 393224 | tf_op jit(solution)/shard_map/ppermute | solution.py:161
  63.6 16.2 %collective-permute-start.41 = (f32[1,4,4,16,128]{4,3,2,1,0:T(8,128)S(1)}, f32[1,4,4,16,128]{4,3,2,1,0:T(8,128)S(1)}, u32[]{:S(2)}, u32[]{:S(2)}) collective-permute-start(f32[1,4,4,16,128]{4,3,2,1,0:T(8,128)S(1)} %get-tuple-element.61), channel_id=1, source_target_pairs={{0,4},{1,5},{2,6},{3,7},{4,0},{5,1},{6,2},{7,3},{8,12},{9,13},{10,... | collective-permute-start | bytes 393224 | tf_op jit(solution)/shard_map/ppermute | solution.py:161
  69.4 12.3 %collective-permute-start.58 = (f32[4,1,4,16,128]{4,3,2,0,1:T(8,128)S(1)}, f32[4,1,4,16,128]{4,3,2,0,1:T(8,128)S(1)}, u32[]{:S(2)}, u32[]{:S(2)}) collective-permute-start(f32[4,1,4,16,128]{4,3,2,0,1:T(8,128)S(1)} %get-tuple-element.39), channel_id=1, source_target_pairs={{0,3},{1,2},{2,1},{3,0},{4,7},{5,6},{6,5},{7,4},{8,11},{9,10},{10,... | collective-permute-start | bytes 393224 | tf_op jit(solution)/shard_map/ppermute | solution.py:161
  69.4 12.4 %collective-permute-start.57 = (f32[4,1,4,16,128]{4,3,2,0,1:T(8,128)S(1)}, f32[4,1,4,16,128]{4,3,2,0,1:T(8,128)S(1)}, u32[]{:S(2)}, u32[]{:S(2)}) collective-permute-start(f32[4,1,4,16,128]{4,3,2,0,1:T(8,128)S(1)} %get-tuple-element.40), channel_id=1, source_target_pairs={{0,2},{1,3},{2,0},{3,1},{4,6},{5,7},{6,4},{7,5},{8,10},{9,11},{10,... | collective-permute-start | bytes 393224 | tf_op jit(solution)/shard_map/ppermute | solution.py:161
  72.1 9.8 %collective-permute-start.56 = (f32[4,1,4,16,128]{4,3,2,0,1:T(8,128)S(1)}, f32[4,1,4,16,128]{4,3,2,0,1:T(8,128)S(1)}, u32[]{:S(2)}, u32[]{:S(2)}) collective-permute-start(f32[4,1,4,16,128]{4,3,2,0,1:T(8,128)S(1)} %get-tuple-element.41), channel_id=1, source_target_pairs={{0,1},{1,0},{2,3},{3,2},{4,5},{5,4},{6,7},{7,6},{8,9},{9,8},{10,11... | collective-permute-start | bytes 393224 | tf_op jit(solution)/shard_map/ppermute | solution.py:161
  79.9 5.6 %collective-permute-start.46 = (f32[4,1,4,16,128]{4,3,2,0,1:T(8,128)S(1)}, f32[4,1,4,16,128]{4,3,2,0,1:T(8,128)S(1)}, u32[]{:S(2)}, u32[]{:S(2)}) collective-permute-start(f32[4,1,4,16,128]{4,3,2,0,1:T(8,128)S(1)} %get-tuple-element.55), channel_id=1, source_target_pairs={{0,3},{1,2},{2,1},{3,0},{4,7},{5,6},{6,5},{7,4},{8,11},{9,10},{10,... | collective-permute-start | bytes 393224 | tf_op jit(solution)/shard_map/ppermute | solution.py:161
  80.0 8.6 %collective-permute-start.45 = (f32[4,1,4,16,128]{4,3,2,0,1:T(8,128)S(1)}, f32[4,1,4,16,128]{4,3,2,0,1:T(8,128)S(1)}, u32[]{:S(2)}, u32[]{:S(2)}) collective-permute-start(f32[4,1,4,16,128]{4,3,2,0,1:T(8,128)S(1)} %get-tuple-element.56), channel_id=1, source_target_pairs={{0,2},{1,3},{2,0},{3,1},{4,6},{5,7},{6,4},{7,5},{8,10},{9,11},{10,... | collective-permute-start | bytes 393224 | tf_op jit(solution)/shard_map/ppermute | solution.py:161
  81.7 6.9 %collective-permute-start.44 = (f32[4,1,4,16,128]{4,3,2,0,1:T(8,128)S(1)}, f32[4,1,4,16,128]{4,3,2,0,1:T(8,128)S(1)}, u32[]{:S(2)}, u32[]{:S(2)}) collective-permute-start(f32[4,1,4,16,128]{4,3,2,0,1:T(8,128)S(1)} %get-tuple-element.57), channel_id=1, source_target_pairs={{0,1},{1,0},{2,3},{3,2},{4,5},{5,4},{6,7},{7,6},{8,9},{9,8},{10,11... | collective-permute-start | bytes 393224 | tf_op jit(solution)/shard_map/ppermute | solution.py:161
  (3 other events, 2.2 us)
